TPU v7x, 32 devices: a whole 2x2x4 slice. The times are simulated.
32 devices in a mesh: dp: 4 (over x, core), head: 2 (over y), ctx: 4 (over z).
Axes of the slice: x: 2, y: 2, z: 4, core: 2. Of those that a mesh axis runs over, the one named last changes fastest.
Arguments:
- q_latent: bfloat16 [4, 64, 1536], P('dp'), may hold values from -6 to 6
- hidden: bfloat16 [4, 64, 7168], P('dp'), may hold values from -96 to 96
- main_queries: bfloat16 [4, 64, 128, 576], P('dp', 'ctx', 'head'), may hold values from -36 to 36
- main_keys: bfloat16 [4, 4096, 576], P('dp', 'ctx'), may hold values from -6 to 6
- index_keys: bfloat16 [4, 4096, 128], P('dp', 'ctx'), may hold values from -96 to 96
- positions: int32 [4, 64], P('dp'), may hold values from 2048 to 4095, as said below
- w_query: bfloat16 [1536, 8192], P('ctx', 'head'), may hold values from -0.15625 to 0.15625
- w_weights: bfloat16 [7168, 64], P('ctx', 'head'), may hold values from -0.0625 to 0.0625
Outputs:
- grad_query: float32 [1536, 8192], P('ctx', 'head')
- grad_weights: float32 [7168, 64], P('ctx', 'head')
- cross_entropy: float32 [4, 64], P('dp')
Inputs may be any that keep to these rules, and one draw needn't show every extreme that they name: `positions`: in each sequence some query sits at the last key and some at the lowest position.
All inputs are finite; a program needn't handle non-finite values.
Results may differ from a plain program's by a relative error of at most 0.0075.
The roundings to bfloat16 on the way count: a program that leaves them out, or rounds other values in their place, can miss the bound.
Values may be sent and summed in bfloat16 or wider, within the bound.
No kernel may reach another device: no remote copies, remote signals or barrier semaphores. Data moves between devices by JAX's collectives and lax.ppermute only.
A program may use at most 128 MiB of HBM per device.

v0:
```python
import jax
import jax.numpy as jnp
from jax import lax
from jax.sharding import PartitionSpec as P

HI = 64
DI = 128
HM = 128
DL = 576


score_scale = 192.0 ** (-0.5)
masked_floor = -1e30


def merged(x, axis, combine):
    everything = jax.tree.map(lambda part: lax.all_gather(part, axis), x)
    initial = jax.tree.map(lambda part: part[0], everything)

    def turn(k, so_far):
        return combine(so_far, jax.tree.map(lambda part: part[k], everything))

    return lax.fori_loop(1, lax.axis_size(axis), turn, initial)


def pair_merge(first, second):
    joined = jnp.maximum(first[0], second[0])
    return (joined, first[1] * jnp.exp(first[0] - joined) + second[1] * jnp.exp(second[0] - joined))


def per_device(
    q_latent, hidden, main_queries, main_keys, index_keys, positions, w_query, w_weights
):
    index_scale = (HI * DI) ** (-0.5)
    ctx_index = lax.axis_index("ctx")
    latent = q_latent[0]
    activations = hidden[0]
    key_main = main_keys[0]
    key_index = index_keys[0]
    query_pos = positions[0]
    ctx_rows = key_main.shape[0]
    rows_latent = w_query.shape[0]
    rows_hidden = w_weights.shape[0]
    heads_here = w_weights.shape[1]
    query_count = latent.shape[0]
    own_latent = lax.dynamic_slice_in_dim(latent, ctx_index * rows_latent, rows_latent, 1)
    own_hidden = lax.dynamic_slice_in_dim(activations, ctx_index * rows_hidden, rows_hidden, 1)
    columns = latent
    query_sum = jnp.dot(
        columns,
        lax.all_gather(w_query, "ctx", axis=0, tiled=True),
        preferred_element_type=jnp.float32,
    )
    columns = activations
    weight_sum = jnp.dot(
        columns,
        lax.all_gather(w_weights, "ctx", axis=0, tiled=True),
        preferred_element_type=jnp.float32,
    )
    index_query = query_sum.astype(jnp.bfloat16).reshape(query_count, heads_here, DI)
    key_positions = ctx_index * ctx_rows + jnp.arange(ctx_rows, dtype=jnp.int32)
    visible = key_positions[None, :] <= query_pos[:, None]
    affinity = jnp.einsum("qjd,sd->qjs", index_query, key_index, preferred_element_type=jnp.float32)
    partial_logits = (
        jnp.sum(weight_sum[:, :, None] * jnp.maximum(affinity, 0.0), axis=1) * index_scale
    )
    logits = lax.psum(partial_logits, "head")
    gathered = lax.all_gather(main_queries[0], "ctx", axis=0, tiled=True)
    block_count = gathered.shape[1] // 8
    blocks = gathered.reshape(query_count, block_count, 8, DL).transpose(1, 0, 2, 3)

    def block_scores(block):
        scores = (
            jnp.einsum("qhd,sd->qhs", block, key_main, preferred_element_type=jnp.float32)
            * score_scale
        )
        return jnp.where(visible[:, None, :], scores, masked_floor)

    def local_moments(block):
        scores = block_scores(block)
        local_max = jnp.max(scores, axis=2)
        shifted = jnp.where(visible[:, None, :], jnp.exp(scores - local_max[:, :, None]), 0.0)
        return (local_max, jnp.sum(shifted, axis=2))

    local_max, local_sum = lax.map(local_moments, blocks)
    index_local = jnp.max(jnp.where(visible, logits, masked_floor), axis=1)
    index_total = jnp.sum(jnp.where(visible, jnp.exp(logits - index_local[:, None]), 0.0), axis=1)
    main_max, main_sum = merged((local_max, local_sum), "ctx", pair_merge)
    index_max, index_sum = merged((index_local, index_total), "ctx", pair_merge)

    def add_probs(running, inputs):
        block, block_max, block_sum = inputs
        scores = block_scores(block)
        shifted = jnp.where(visible[:, None, :], jnp.exp(scores - block_max[:, :, None]), 0.0)
        return (running + jnp.sum(shifted / block_sum[:, :, None], axis=1), None)

    target_part, _ = lax.scan(
        add_probs, jnp.zeros((query_count, ctx_rows), jnp.float32), (blocks, main_max, main_sum)
    )
    target = lax.psum(target_part, "head") / HM
    shifted = jnp.where(visible, jnp.exp(logits - index_max[:, None]), 0.0)
    index_probs = shifted / index_sum[:, None]
    log_probs = logits - (index_max + jnp.log(index_sum))[:, None]
    loss_part = -jnp.sum(jnp.where(visible, target * log_probs, 0.0), axis=1)
    delta = jnp.where(visible, index_probs - target, 0.0)
    score_grad = jnp.where(
        affinity > 0, delta[:, None, :] * weight_sum[:, :, None] * index_scale, 0.0
    ).astype(jnp.bfloat16)
    query_grad = jnp.einsum(
        "qjs,sd->qjd", score_grad, key_index, preferred_element_type=jnp.float32
    )
    weight_grad = jnp.sum(delta[:, None, :] * jnp.maximum(affinity, 0.0), axis=2) * index_scale
    query_grad, weight_grad, cross_entropy = lax.psum((query_grad, weight_grad, loss_part), "ctx")
    query_bf = query_grad.reshape(query_count, heads_here * DI).astype(jnp.bfloat16)
    weight_bf = weight_grad.astype(jnp.bfloat16)
    grad_query = jnp.einsum("qr,qc->rc", own_latent, query_bf, preferred_element_type=jnp.float32)
    grad_weights = jnp.einsum(
        "qr,qc->rc", own_hidden, weight_bf, preferred_element_type=jnp.float32
    )
    grad_query, grad_weights = lax.psum((grad_query, grad_weights), "dp")
    return (grad_query, grad_weights, cross_entropy[None, :])


def solution(mesh):
    return jax.shard_map(
        per_device,
        mesh=mesh,
        in_specs=(
            P("dp", None, None),
            P("dp", None, None),
            P("dp", "ctx", "head", None),
            P("dp", "ctx", None),
            P("dp", "ctx", None),
            P("dp", None),
            P("ctx", "head"),
            P("ctx", "head"),
        ),
        out_specs=(P("ctx", "head"), P("ctx", "head"), P("dp", None)),
        check_vma=False,
    )
```

profile of v0, /device:TPU:0, one launch (start us, length us, event | category | flops | bytes accessed | tf_op | source)
XLA Modules:
  0.0 579.3 jit_solution(8820875455184810470)
XLA Ops:
  8.8 18.3 %all_gather.34 = bf16[7168,32]{0,1:T(8,128)(2,1)S(1)} all-gather(bf16[1792,32]{0,1:T(8,128)(2,1)S(1)} %copy-done.6), channel_id=1, replica_groups=mesh['dp'=4,'head'=2,'ctx'=4] {'ctx'}, dimensions={0}, use_global_device_ids=true | all-gather | bytes 573440 | tf_op jit(solution)/shard_map/all_gather | solution.py:57
  27.4 83.4 %all-gather.10.cloned.1.call-done = bf16[1,64,64,576]{3,2,0,1:T(8,128)(2,1)} async-done(((bf16[1,16,64,576]{3,2,0,1:T(8,128)(2,1)}), bf16[1,64,64,576]{3,2,0,1:T(8,128)(2,1)}) %all-gather.10.cloned.1.call-update) | async-done | bytes 4718608 | tf_op jit(solution)/shard_map/all_gather | solution.py:68
  110.9 5.4 copy.30
  116.3 27.3 %while.60 = (s32[]{:T(128)}, f32[8,64,8]{1,2,0:T(8,128)S(1)}, f32[8,64,8]{1,2,0:T(8,128)S(1)}, bf16[8,64,8,576]{3,2,1,0:T(8,128)(2,1)}, bf16[1024,576]{0,1:T(8,1...) while((s32[]{:T(128)}, f32[8,64,8]{1,2,0:T(8,128)S(1)}, ...), condition=%wide.region_9.10_spmd.clone, body=%wide.region_6.9_spmd.clone.sunk | while | flops 608238592 | bytes 6261593 | solution.py:85
  116.4 2.4 fusion.57
  118.8 0.8 select_reduce_fusion.2
  119.9 2.4 fusion.57
  122.3 0.8 select_reduce_fusion.2
  123.4 2.4 fusion.57
  125.7 0.8 select_reduce_fusion.2
  126.8 2.4 fusion.57
  129.2 0.8 select_reduce_fusion.2
  130.2 2.3 fusion.57
  132.5 0.8 select_reduce_fusion.2
  133.6 2.3 fusion.57
  135.9 0.8 select_reduce_fusion.2
  137.0 2.3 fusion.57
  139.3 0.8 select_reduce_fusion.2
  140.3 2.3 fusion.57
  142.7 0.8 select_reduce_fusion.2
  143.6 19.4 %all-gather.3 = f32[32,64,8]{1,2,0:T(8,128)S(1)} all-gather(f32[8,64,8]{1,2,0:T(8,128)S(1)} %get-tuple-element.341), channel_id=5, replica_groups=mesh['dp'=4,'head'=2,'ctx'=4] {'ctx'}, dimensions={0}, use_global_device_ids=true | all-gather | bytes 81920 | tf_op jit(solution)/shard_map/all_gather | solution.py:17
  163.0 19.0 %all-gather.4 = f32[32,64,8]{1,2,0:T(8,128)S(1)} all-gather(f32[8,64,8]{1,2,0:T(8,128)S(1)} %get-tuple-element.342), channel_id=6, replica_groups=mesh['dp'=4,'head'=2,'ctx'=4] {'ctx'}, dimensions={0}, use_global_device_ids=true | all-gather | bytes 81920 | tf_op jit(solution)/shard_map/all_gather | solution.py:17
  182.1 27.4 %while.61 = (s32[]{:T(128)}, f32[64,1024]{1,0:T(8,128)S(1)}, bf16[8,64,8,576]{3,2,1,0:T(8,128)(2,1)}, bf16[1024,576]{0,1:T(8,128)(2,1)S(1)}, f32[8,64,8]{1,2,0:T...) while((s32[]{:T(128)}, f32[64,1024]{1,0:T(8,128)S(1)}, ...), condition=%wide.region_14.15_spmd.clone, body=%wide.region_12.14_spmd.clone.sunk | while | flops 607256576 | bytes 3040115 | solution.py:97
  182.4 3.0 fusion.60
  185.8 3.0 fusion.60
  189.3 3.0 fusion.60
  192.7 3.0 fusion.60
  196.1 3.0 fusion.60
  199.5 3.0 fusion.60
  203.0 3.0 fusion.60
  206.4 3.0 fusion.60
  209.5 123.9 %all-gather.8.cloned.1.call-done = bf16[1536,4096]{1,0:T(8,128)(2,1)} async-done(((bf16[384,4096]{1,0:T(8,128)(2,1)}), bf16[1536,4096]{1,0:T(8,128)(2,1)}) %all-gather.8.cloned.1.call-update) | async-done | bytes 12582928 | tf_op jit(solution)/shard_map/all_gather | solution.py:51
  333.4 6.9 %fusion.20 = bf16[8,8,32,128]{3,1,2,0:T(8,128)(2,1)S(1)} fusion(bf16[1536,4096]{1,0:T(8,128)(2,1)} %all-gather.8.cloned.1.call-done, bf16[1,64,1536]{2,1,0:T(8,128)(2,1)S(1)} %copy-done.3), kind=kOutput, calls=%fused_computation.39 | convolution fusion | flops 805568512 | bytes 13303808 | tf_op jit(solution)/shard_map/dot_general | solution.py:49
  340.4 4.0 multiply_reduce_fusion.1
  344.4 0.7 broadcast_multiply_fusion
  346.5 25.9 %all-reduce.12.cloned.1.call-done = (f32[64,1024]{1,0:T(8,128)}, f32[64,1024]{1,0:T(8,128)}) async-done(((f32[64,1024]{1,0:T(8,128)}, f32[64,1024]{1,0:T(8,128)}), (f32[64,1024]{1,0:T(8,128)}, f32[64,1024]{1,0:T(8,128)})) %all-reduce.12.cloned.1.call-update) | async-done | bytes 524304 | tf_op jit(solution)/shard_map/psum | solution.py:67
  372.4 1.1 fusion.26
  373.5 1.2 fusion.27
  375.2 11.7 %all-reduce.3 = (f32[256]{0:T(256)S(1)}, f32[256]{0:T(256)S(1)}) all-reduce(f32[256]{0:T(256)S(1)} %dynamic-update-slice, f32[256]{0:T(256)S(1)} %dynamic-update-slice.1), channel_id=2, replica_groups=mesh['dp'=4,'head'=2,'ctx'=4] {'ctx'}, use_global_device_ids=true, to_apply=%add | all-reduce | flops 512 | bytes 4096
  387.1 1.4 fusion.30
  388.5 4.5 multiply_reduce_fusion
  393.0 1.3 copy-done.1
  394.3 1.6 fusion.19
  395.9 42.6 %all-reduce.13 = (bf16[64,32,128]{2,1,0:T(8,128)(2,1)S(1)}, bf16[64,32]{1,0:T(8,128)(2,1)S(1)}, f32[1,64]{1,0:T(1,128)}) all-reduce(f32[64,32,128]{2,1,0:T(8,128)S(1)} %fusion.19, f32[64,32]{1,0:T(8,128)S(1)} %broadcast_multiply_fusion.1, f32[1,64]{1,0:T(1,128)S(1)} %negate_bitcast_fusion), channel_id=1, replica_groups=mesh['dp'=4,'head'=2,'ctx'=4] {'ctx'}, use_global_device_ids=true, to_apply=%region_16.17 | all-reduce | flops 264256 | bytes 1585664 | tf_op jit(solution)/shard_map/psum | solution.py:113
  438.5 3.7 fusion.23
  442.2 0.9 fusion.34
  443.2 122.7 %all-reduce.10.cloned.1.call-done = (f32[384,4096]{1,0:T(8,128)}, f32[1792,32]{0,1:T(8,128)}) async-done(((f32[384,4096]{1,0:T(8,128)}, f32[1792,32]{0,1:T(8,128)}), (f32[384,4096]{1,0:T(8,128)}, f32[1792,32]{0,1:T(8,128)})) %all-reduce.10.cloned.1.call-update) | async-done | bytes 6520848 | tf_op jit(solution)/shard_map/psum | solution.py:120
  565.8 6.2 %copy.104 = f32[384,4096]{1,0:T(8,128)} copy(f32[384,4096]{1,0:T(8,128)} %get-tuple-element.799) | data formatting | bytes 12582912
  (128 shorter events, 9.3 us)
Async XLA Ops:
  7.2 19.9 %copy-start = (bf16[1,64,7168]{2,1,0:T(8,128)(2,1)S(1)}, bf16[1,64,7168]{2,1,0:T(8,128)(2,1)}, u32[]{:S(2)}) copy-start(bf16[1,64,7168]{2,1,0:T(8,128)(2,1)} %param.17) | copy-start | bytes 2752516
  7.2 1.6 copy-start.6
  7.2 103.7 %all-gather.10.cloned.1.call-start = ((), (), s32[]{:S(2)}) async-start(), calls=%async_computation.1 | async-start | bytes 6553600 | tf_op jit(solution)/shard_map/all_gather | solution.py:68
  7.9 325.5 %all-gather.8.cloned.1.call-start = ((), (), s32[]{:S(2)}) async-start(), calls=%async_computation | async-start | bytes 15728640 | tf_op jit(solution)/shard_map/all_gather | solution.py:51
  8.7 363.7 %all-reduce.12.cloned.1.call-start = ((), (), s32[]{:S(2)}) async-start(), calls=%async_computation.3 | async-start | bytes 1048576 | tf_op jit(solution)/shard_map/psum | solution.py:67
  110.9 5.4 copy-start.7
  110.9 5.4 copy-start.8
  182.1 151.3 %copy-start.3 = (bf16[1,64,1536]{2,1,0:T(8,128)(2,1)S(1)}, bf16[1,64,1536]{2,1,0:T(8,128)(2,1)}, u32[]{:S(2)}) copy-start(bf16[1,64,1536]{2,1,0:T(8,128)(2,1)} %param.16) | copy-start | bytes 589828
  209.5 130.8 %copy-start.2 = (f32[64,1024]{1,0:T(8,128)}, f32[64,1024]{1,0:T(8,128)S(1)}, u32[]{:S(2)}) copy-start(f32[64,1024]{1,0:T(8,128)S(1)} %get-tuple-element.345) | copy-start | bytes 786436
  209.5 130.9 %copy-start.4 = (bf16[1,1024,128]{2,1,0:T(8,128)(2,1)S(1)}, bf16[1,1024,128]{2,1,0:T(8,128)(2,1)}, u32[]{:S(2)}) copy-start(bf16[1,1024,128]{2,1,0:T(8,128)(2,1)} %param.20) | copy-start | bytes 786436
  340.4 4.8 copy-start.9
  345.2 220.7 %all-reduce.10.cloned.1.call-start = ((), (), s32[]{:S(2)}) async-start(), calls=%async_computation.2 | async-start | bytes 13041664 | tf_op jit(solution)/shard_map/psum | solution.py:120
  388.5 5.8 copy-start.1
  565.8 6.2 %copy-start.5 = (f32[1792,32]{0,1:T(8,128)S(1)}, f32[1792,32]{0,1:T(8,128)}, u32[]{:S(2)}) copy-start(f32[1792,32]{0,1:T(8,128)} %get-tuple-element.800) | copy-start | bytes 688132
Sparse Core Ops, SparseCore 0:
  9.6 101.2 all-gather.9
  112.4 220.9 all-gather.7
  345.3 27.0 all-reduce.11
  443.3 122.5 all-reduce.9
where the time goes:
time: 580 us; the launch traced here: 579 us
  waiting for transfers between devices  357 us (62%)
  blocking collectives  111 us (19%)
  matrix products  60.4 us (10%)
  other arithmetic  17.9 us (3%)
  local copies, waits for them, and re-layouts  17.4 us (3%)
  between operations  14.7 us (3%)
    all_gather x1, waiting for transfers between devices, per_device(): lax.all_gather(w_query, 'ctx', axis=0, tiled=True)  124 us
    psum x1, waiting for transfers between devices, per_device(): grad_query, grad_weights = lax.psum((grad_query, grad_weights), 'dp')  123 us
    all_gather x1, waiting for transfers between devices, per_device(): gathered = lax.all_gather(main_queries[0], 'ctx', axis=0, tiled=True)  83.4 us
    dot_general x16, matrix products, block_scores(): jnp.einsum('qhd,sd->qhs', block, key_main, preferred_element_type=jnp.flo...  42.9 us
    psum x1, blocking collectives, per_device(): lax.psum((query_grad, weight_grad, loss_part), 'ctx')  42.6 us
    all_gather x2, blocking collectives, merged(): everything = jax.tree.map(lambda part: lax.all_gather(part, axis), x)  38.3 us
    psum x1, waiting for transfers between devices, per_device(): logits = lax.psum(partial_logits, 'head')  25.9 us
    all_gather x1, blocking collectives, per_device(): lax.all_gather(w_weights, 'ctx', axis=0, tiled=True)  18.3 us
  transfers between devices with their start and end apart: 4, of which 4 were waited for; matrix products, arithmetic and copies ran while one was open for 10% of the time, Pallas kernels for 0%

commit v1 on v0

v1 whole, which is shorter than its diff:
```python
import jax
import jax.numpy as jnp
from jax import lax
from jax.sharding import PartitionSpec as P

HI = 64
DI = 128
HM = 128

score_scale = 192.0 ** (-0.5)
index_scale = (HI * DI) ** (-0.5)
masked_floor = -1e30


def folded_ring(size):
    return list(range(0, 1)) + list(range(1, size, 2)) + list(range(2, size, 2))[::-1]


def per_device(
    q_latent, hidden, main_queries, main_keys, index_keys, positions, w_query, w_weights
):
    n = lax.axis_size("ctx")
    z = lax.axis_index("ctx")
    y = lax.axis_index("head")
    dp_size = lax.axis_size("dp")
    dp = lax.axis_index("dp")
    ring = folded_ring(n)
    place_of = [ring.index(k) for k in range(n)]
    ring_table = jnp.array(ring, jnp.int32)
    place = jnp.array(place_of, jnp.int32)[z]
    ring_pairs = [(ring[k], ring[(k + 1) % n]) for k in range(n)]

    def at_place(k):
        return ring_table[lax.rem(k + 2 * n, n)]

    def onward(x):
        return lax.ppermute(x, "ctx", ring_pairs)

    def swap_head(x):
        return lax.ppermute(x, "head", [(0, 1), (1, 0)])

    latent = q_latent[0]
    activations = hidden[0]
    rows = main_keys.shape[1]
    half = rows // 2
    rows_latent = w_query.shape[0]
    rows_hidden = w_weights.shape[0]
    heads_here = w_weights.shape[1]
    queries_here = main_queries.shape[1]
    query_pos = lax.dynamic_slice_in_dim(positions[0], z * queries_here, queries_here)
    own_latent = lax.dynamic_slice_in_dim(latent, z * rows_latent, rows_latent, 1)
    own_hidden = lax.dynamic_slice_in_dim(activations, z * rows_hidden, rows_hidden, 1)

    key_part = lax.dynamic_slice_in_dim(main_keys[0], y * half, half)
    index_part = lax.dynamic_slice_in_dim(index_keys[0], y * half, half)
    other_queries = swap_head(main_queries[0])
    index_mine = [index_part]
    for _ in range(n - 1):
        index_mine.append(onward(index_mine[-1]))
    keys_mine = [key_part]
    for _ in range(n - 1):
        keys_mine.append(onward(keys_mine[-1]))
    index_own = jnp.concatenate(index_mine)
    index_other = swap_head(index_own)
    sources = jnp.stack([at_place(place - t) for t in range(n)])
    base = sources[:, None] * rows + jnp.arange(half, dtype=jnp.int32)[None, :]
    pos_own = (base + y * half).reshape(-1)
    pos_other = (base + (1 - y) * half).reshape(-1)
    visible_own = pos_own[None, :] <= query_pos[:, None]
    visible_other = pos_other[None, :] <= query_pos[:, None]

    query_sum = jnp.dot(own_latent, w_query, preferred_element_type=jnp.float32)
    weight_sum = jnp.dot(own_hidden, w_weights, preferred_element_type=jnp.float32)
    weight_sum = jnp.pad(weight_sum, ((0, 0), (0, 128 - heads_here)))
    partial = jnp.concatenate([query_sum, weight_sum], axis=1)
    width = query_sum.shape[1]

    def partial_of(k):
        return lax.dynamic_slice_in_dim(partial, at_place(k) * queries_here, queries_here)

    total = partial_of(place - 1)
    for t in range(1, n):
        total = onward(total) + partial_of(place - t - 1)
    index_query = total[:, :width].astype(jnp.bfloat16).reshape(queries_here, heads_here, DI)
    head_weights = total[:, width : width + heads_here]

    def affinity_to(keys):
        return jnp.einsum("qjd,sd->qjs", index_query, keys, preferred_element_type=jnp.float32)

    def part_logits(keys):
        reached = jnp.maximum(affinity_to(keys), 0.0)
        return jnp.sum(head_weights[:, :, None] * reached, axis=1) * index_scale

    part_own, part_other = part_logits(index_own), part_logits(index_other)
    from_other, from_own = swap_head((part_own, part_other))
    logits_own = part_own + from_own
    logits_other = part_other + from_other

    all_queries = jnp.concatenate([main_queries[0], other_queries], axis=1)
    scores = jnp.concatenate(
        [
            jnp.einsum("qhd,sd->qhs", all_queries, k, preferred_element_type=jnp.float32)
            for k in keys_mine
        ],
        axis=2,
    )
    scores = jnp.where(visible_own[:, None, :], scores * score_scale, masked_floor)
    top = jnp.max(scores, axis=2)
    shifted = jnp.exp(scores - top[:, :, None])
    mass = jnp.sum(shifted, axis=2)
    half_heads = main_queries.shape[2]
    other_top, other_mass = swap_head((top, mass))
    other_top = jnp.concatenate([other_top[:, half_heads:], other_top[:, :half_heads]], axis=1)
    other_mass = jnp.concatenate([other_mass[:, half_heads:], other_mass[:, :half_heads]], axis=1)
    joint = jnp.maximum(top, other_top)
    mass = mass * jnp.exp(top - joint) + other_mass * jnp.exp(other_top - joint)
    factor = jnp.exp(top - joint) / mass / HM
    target_own = jnp.sum(shifted * factor[:, :, None], axis=1)
    target_own = jnp.where(visible_own, target_own, 0.0)
    target_other = swap_head(target_own)

    floor_own = jnp.where(visible_own, logits_own, masked_floor)
    floor_other = jnp.where(visible_other, logits_other, masked_floor)
    high = jnp.maximum(jnp.max(floor_own, axis=1), jnp.max(floor_other, axis=1))
    exp_own = jnp.exp(floor_own - high[:, None])
    exp_other = jnp.exp(floor_other - high[:, None])
    index_total = jnp.sum(exp_own, axis=1) + jnp.sum(exp_other, axis=1)
    level = (high + jnp.log(index_total))[:, None]

    def loss_part(visible, target, logits):
        return jnp.sum(jnp.where(visible, target * (logits - level), 0.0), axis=1)

    loss = -(
        loss_part(visible_own, target_own, logits_own)
        + loss_part(visible_other, target_other, logits_other)
    )
    delta_own = jnp.where(visible_own, exp_own / index_total[:, None] - target_own, 0.0)
    delta_other = jnp.where(visible_other, exp_other / index_total[:, None] - target_other, 0.0)

    def grads(delta, keys):
        affinity = affinity_to(keys)
        score_grad = jnp.where(
            affinity > 0, delta[:, None, :] * head_weights[:, :, None] * index_scale, 0.0
        ).astype(jnp.bfloat16)
        query_grad = jnp.einsum("qjs,sd->qjd", score_grad, keys, preferred_element_type=jnp.float32)
        weight_grad = jnp.sum(delta[:, None, :] * jnp.maximum(affinity, 0.0), axis=2)
        return query_grad, weight_grad

    query_a, weight_a = grads(delta_own, index_own)
    query_b, weight_b = grads(delta_other, index_other)
    query_grad = (query_a + query_b).reshape(queries_here, width).astype(jnp.bfloat16)
    weight_grad = ((weight_a + weight_b) * index_scale).astype(jnp.bfloat16)
    loss_high = loss.astype(jnp.bfloat16)
    loss_low = (loss - loss_high.astype(jnp.float32)).astype(jnp.bfloat16)
    tail = jnp.concatenate([weight_grad, loss_high[:, None], loss_low[:, None]], axis=1)
    tail = jnp.pad(tail, ((0, 0), (0, 128 - tail.shape[1])))
    piece = jnp.concatenate([query_grad, tail], axis=1)

    pieces = [piece]
    for t in range(1, n):
        pairs = [(k, (k + t) % n) for k in range(n)]
        pieces.append(lax.ppermute(piece, "ctx", pairs))
    stacked = jnp.stack(pieces)
    sequence = jnp.concatenate(
        [lax.dynamic_index_in_dim(stacked, lax.rem(z - k + n, n), 0, False) for k in range(n)]
    )

    def across_dp(x):
        whole, bit = x[None], dp_size // 2
        while bit:
            other = lax.ppermute(whole, "dp", [(k, k ^ bit) for k in range(dp_size)])
            upper = (dp & bit) != 0
            whole = jnp.concatenate([jnp.where(upper, other, whole), jnp.where(upper, whole, other)])
            bit //= 2
        return whole

    latents = across_dp(own_latent)
    hiddens = across_dp(own_hidden)
    everything = across_dp(sequence)
    grad_query = jnp.einsum(
        "bqr,bqc->rc", latents, everything[:, :, :width], preferred_element_type=jnp.float32
    )
    grad_weights = jnp.einsum(
        "bqr,bqc->rc",
        hiddens,
        everything[:, :, width : width + heads_here],
        preferred_element_type=jnp.float32,
    )
    low = sequence[:, width + heads_here : width + heads_here + 2].astype(jnp.float32)
    cross_entropy = low[:, 0] + low[:, 1]
    return (grad_query, grad_weights, cross_entropy[None, :])


def solution(mesh):
    return jax.shard_map(
        per_device,
        mesh=mesh,
        in_specs=(
            P("dp", None, None),
            P("dp", None, None),
            P("dp", "ctx", "head", None),
            P("dp", "ctx", None),
            P("dp", "ctx", None),
            P("dp", None),
            P("ctx", "head"),
            P("ctx", "head"),
        ),
        out_specs=(P("ctx", "head"), P("ctx", "head"), P("dp", None)),
        check_vma=False,
    )
```

time: 580 us -> 184 us (0.32)
  waiting for transfers between devices: 357 us -> 67.1 us
  blocking collectives: 111 us -> 0 us
  matrix products: 60.4 us -> 21.7 us
  starting transfers between devices: 0.16 us -> 37 us
  other arithmetic: 17.9 us -> 32.3 us
  between operations: 14.7 us -> 7.09 us
    all_gather x2 -> x0, waiting for transfers between devices: 207 us -> none  [the longest x1 124 us: per_device(): lax.all_gather(w_query, 'ctx', axis=0, tiled=True)]
    psum x2 -> x0, waiting for transfers between devices: 149 us -> none  [the longest x1 123 us: per_device(): grad_query, grad_weights = lax.psum((grad_query, grad_weights), 'dp')]
    ppermute x0 -> x25, waiting for transfers between devices: none -> 67.1 us  [the longest x7 36.9 us: swap_head(): return lax.ppermute(x, 'head', [(0, 1), (1, 0)])]
    all_gather x3 -> x0, blocking collectives: 56.6 us -> none  [the longest x2 38.3 us: merged(): everything = jax.tree.map(lambda part: lax.all_gather(part, axis), x)]
    psum x1 -> x0, blocking collectives: 42.6 us -> none  [per_device(): lax.psum((query_grad, weight_grad, loss_part), 'ctx')]
    dot_general x22 -> x12, matrix products: 60.4 us -> 21.7 us  [the longest x4 9.51 us: per_device(): jnp.einsum('qhd,sd->qhs', all_queries, k, preferred_element_type=jnp.floa...]
    ppermute x0 -> x25, starting transfers between devices: none -> 37 us  [the longest x9 18.5 us: onward(): return lax.ppermute(x, 'ctx', ring_pairs)]
    unnamed x1 -> x0, blocking collectives: 11.7 us -> none
  transfers between devices with their start and end apart: 4 -> 25, of which waited for: 4 -> 14; matrix products, arithmetic and copies ran while one was open for 10% -> 34% of each run, Pallas kernels for 0% -> 0%
where the time goes in v1:
time: 184 us; the launch traced here: 183 us
  waiting for transfers between devices  67.1 us (36%)
  starting transfers between devices  37 us (20%)
  other arithmetic  32.3 us (18%)
  matrix products  21.7 us (12%)
  local copies, waits for them, and re-layouts  17.4 us (9%)
  between operations  7.09 us (4%)
    ppermute x7, waiting for transfers between devices, swap_head(): return lax.ppermute(x, 'head', [(0, 1), (1, 0)])  36.9 us
    ppermute x9, starting transfers between devices, onward(): return lax.ppermute(x, 'ctx', ring_pairs)  18.5 us
    ppermute x9, waiting for transfers between devices, onward(): return lax.ppermute(x, 'ctx', ring_pairs)  17.8 us
    dot_general x4, matrix products, per_device(): jnp.einsum('qhd,sd->qhs', all_queries, k, preferred_element_type=jnp.floa...  9.51 us
    ppermute x7, starting transfers between devices, swap_head(): return lax.ppermute(x, 'head', [(0, 1), (1, 0)])  9.04 us
    ppermute x6, waiting for transfers between devices, across_dp(): other = lax.ppermute(whole, 'dp', [(k, k ^ bit) for k in range(dp_size)])  7.92 us
    reduce_sum x1, other arithmetic, per_device(): target_own = jnp.sum(shifted * factor[:, :, None], axis=1)  5.6 us
    unnamed x50, local copies, waits for them, and re-layouts  5.19 us
  transfers between devices with their start and end apart: 25, of which 14 were waited for; matrix products, arithmetic and copies ran while one was open for 34% of the time, Pallas kernels for 0%

profile of v1, /device:TPU:0, one launch (start us, length us, event | category | flops | bytes accessed | tf_op | source)
XLA Modules:
  0.0 182.7 jit_solution(11498104097907918956)
XLA Ops:
  1.8 3.0 %collective-permute-start.23 = (bf16[1,64,1792]{2,1,0:T(8,128)(2,1)S(1)}, bf16[1,64,1792]{2,1,0:T(8,128)(2,1)}, u32[]{:S(2)}, u32[]{:S(2)}) collective-permute-start(bf16[1,64,1792]{2,1,0:T(8,128)(2,1)S(1)} %constant_dynamic-slice_fusion.2), channel_id=1, source_target_pairs={{0,16},{8,24},{16,0},{24,8},{1,17},{9,25},{17,1},{25,9},{2,18},{10... | collective-permute-start | bytes 688136 | tf_op jit(solution)/shard_map/ppermute | solution.py:171
  4.8 1.4 constant_dynamic-slice_fusion.3
  6.2 1.2 dynamic_slice.73
  10.7 1.5 fusion.77
  12.9 2.5 %fusion.43 = f32[64,4096]{1,0:T(8,128)} fusion(bf16[384,4096]{1,0:T(8,128)(2,1)S(1)} %copy-done, bf16[1,64,384]{2,1,0:T(8,128)(2,1)} %constant_dynamic-slice_fusion.3), kind=kOutput, calls=%fused_computation.104 | convolution fusion | flops 201326592 | bytes 4243456 | tf_op jit(solution)/shard_map/dot_general | solution.py:72
  15.5 1.3 select_maximum_fusion
  16.9 2.1 %collective-permute-start.2 = (f32[16,4224]{1,0:T(8,128)S(1)}, f32[16,4224]{1,0:T(8,128)S(1)}, u32[]{:S(2)}, u32[]{:S(2)}) collective-permute-start(f32[16,4224]{1,0:T(8,128)S(1)} %constant_dynamic-slice_fusion.1), channel_id=1, source_target_pairs={{0,1},{1,3},{3,2},{2,0},{4,5},{5,7},{7,6},{6,4},{8,9},{9,11},{11,1... | collective-permute-start | bytes 811016 | tf_op jit(solution)/shard_map/ppermute | solution.py:37
  19.9 2.6 %collective-permute-start.5 = (bf16[512,128]{1,0:T(8,128)(2,1)S(1)}, bf16[512,128]{1,0:T(8,128)(2,1)S(1)}, u32[]{:S(2)}, u32[]{:S(2)}) collective-permute-start(bf16[512,128]{1,0:T(8,128)(2,1)S(1)} %dynamic-slice_bitcast_fusion.5), channel_id=1, source_target_pairs={{0,1},{1,3},{3,2},{2,0},{4,5},{5,7},{7,6},{6,4},{8,9},{9,11},{11,1... | collective-permute-start | bytes 393224 | tf_op jit(solution)/shard_map/ppermute | solution.py:37
  22.6 1.9 %dynamic-slice_bitcast_fusion = bf16[512,576]{0,1:T(8,128)(2,1)} fusion(bf16[1,1024,576]{1,2,0:T(8,128)(2,1)} %param.13, s32[]{:T(128)S(6)} %select_n.183), kind=kLoop, calls=%fused_computation.58 | loop fusion | bytes 1179652 | tf_op jit(solution)/shard_map/dynamic_slice | solution.py:54
  25.6 2.6 %add_multiply_fusion = s32[4]{0:T(128)S(1)} fusion(s32[1]{0:T(128)} %get-tuple-element.43, s32[1]{0:T(128)} %get-tuple-element.44, s32[1]{0:T(128)} %get-tuple-element.45, s32[1]{0:T(128)} %get-tuple-element.46), kind=kLoop, calls=%fused_computation.136 | loop fusion | flops 16 | bytes 32 | tf_op jit(solution)/shard_map/mul | solution.py:66
  28.2 2.1 %collective-permute-done.5 = bf16[512,128]{1,0:T(8,128)(2,1)S(1)} collective-permute-done((bf16[512,128]{1,0:T(8,128)(2,1)S(1)}, bf16[512,128]{1,0:T(8,128)(2,1)S(1)}, u32[]{:S(2)}, u32[]{:S(2)}) %collective-permute-start.5) | collective-permute-done | bytes 131104 | tf_op jit(solution)/shard_map/ppermute | solution.py:37
  30.2 1.1 collective-permute-start.6
  31.4 3.4 %collective-permute-start.3 = (f32[16,4224]{1,0:T(8,128)S(1)}, f32[16,4224]{1,0:T(8,128)S(1)}, u32[]{:S(2)}, u32[]{:S(2)}) collective-permute-start(f32[16,4224]{1,0:T(8,128)S(1)} %dynamic-slice_add_fusion.2), channel_id=1, source_target_pairs={{0,1},{1,3},{3,2},{2,0},{4,5},{5,7},{7,6},{6,4},{8,9},{9,11},{11,1... | collective-permute-start | bytes 811016 | tf_op jit(solution)/shard_map/ppermute | solution.py:37
  35.7 10.0 %collective-permute-done.6 = bf16[512,128]{1,0:T(8,128)(2,1)S(1)} collective-permute-done((bf16[512,128]{1,0:T(8,128)(2,1)S(1)}, bf16[512,128]{1,0:T(8,128)(2,1)S(1)}, u32[]{:S(2)}, u32[]{:S(2)}) %collective-permute-start.6) | collective-permute-done | bytes 131104 | tf_op jit(solution)/shard_map/ppermute | solution.py:37
  45.7 1.1 collective-permute-start.7
  46.8 4.6 %collective-permute-done.3 = f32[16,4224]{1,0:T(8,128)S(1)} collective-permute-done((f32[16,4224]{1,0:T(8,128)S(1)}, f32[16,4224]{1,0:T(8,128)S(1)}, u32[]{:S(2)}, u32[]{:S(2)}) %collective-permute-start.3) | collective-permute-done | bytes 270368 | tf_op jit(solution)/shard_map/ppermute | solution.py:37
  53.8 3.4 %copy.24 = bf16[1,16,64,576]{2,3,1,0:T(8,128)(2,1)S(1)} copy(bf16[1,16,64,576]{3,2,1,0:T(8,128)(2,1)} %param.12) | data formatting | bytes 2359296 | tf_op args[2]
  57.2 1.6 collective-permute-start.11
  60.4 3.1 %collective-permute-start.13 = (bf16[512,576]{0,1:T(8,128)(2,1)}, bf16[512,576]{0,1:T(8,128)(2,1)}, u32[]{:S(2)}, u32[]{:S(2)}) collective-permute-start(bf16[512,576]{0,1:T(8,128)(2,1)} %collective-permute-done.12), channel_id=1, source_target_pairs={{0,1},{1,3},{3,2},{2,0},{4,5},{5,7},{7,6},{6,4},{8,9},{9,11},{11,1... | collective-permute-start | bytes 1769480 | tf_op jit(solution)/shard_map/ppermute | solution.py:37
  64.6 31.4 %collective-permute-done.8 = bf16[2048,128]{1,0:T(8,128)(2,1)S(1)} collective-permute-done((bf16[2048,128]{1,0:T(8,128)(2,1)S(1)}, bf16[2048,128]{1,0:T(8,128)(2,1)S(1)}, u32[]{:S(2)}, u32[]{:S(2)}) %collective-permute-start.8) | collective-permute-done | bytes 524320 | tf_op jit(solution)/shard_map/ppermute | solution.py:40
  96.1 1.4 fusion.5
  97.4 1.6 multiply_reduce_fusion.4
  99.5 1.6 collective-permute-start.10
  102.0 1.6 collective-permute-start.9
  103.6 3.7 %copy.26 = bf16[16,64,576]{1,2,0:T(8,128)(2,1)} copy(bf16[16,64,576]{2,1,0:T(8,128)(2,1)} %collective-permute-done.11) | data formatting | bytes 2359296 | tf_op jit(solution)/shard_map/ppermute | solution.py:40
  107.2 3.0 %pad_maximum_fusion = bf16[16,128,576]{1,2,0:T(8,128)(2,1)S(1)} fusion(bf16[16,64,576]{1,2,0:T(8,128)(2,1)} %copy.26, bf16[16,64,576]{1,2,0:T(8,128)(2,1)S(1)} %bitcast.99), kind=kLoop, calls=%fused_computation.17 | loop fusion | flops 4718592 | bytes 4718592 | tf_op jit(solution)/shard_map/concatenate | solution.py:99
  110.2 3.6 %collective-permute-start.14 = (bf16[512,576]{0,1:T(8,128)(2,1)}, bf16[512,576]{0,1:T(8,128)(2,1)S(1)}, u32[]{:S(2)}, u32[]{:S(2)}) collective-permute-start(bf16[512,576]{0,1:T(8,128)(2,1)} %collective-permute-done.13), channel_id=1, source_target_pairs={{0,1},{1,3},{3,2},{2,0},{4,5},{5,7},{7,6},{6,4},{8,9},{9,11},{11,1... | collective-permute-start | bytes 1769480 | tf_op jit(solution)/shard_map/ppermute | solution.py:37
  113.8 2.9 %fusion.17 = f32[16,128,512]{2,1,0:T(8,128)S(1)} fusion(bf16[16,128,576]{1,2,0:T(8,128)(2,1)S(1)} %pad_maximum_fusion, bf16[512,576]{0,1:T(8,128)(2,1)} %collective-permute-done.13), kind=kOutput, calls=%fused_computation.40 | convolution fusion | flops 1207959552 | bytes 7143424 | tf_op jit(solution)/shard_map/qhd,sd->qhs/dot_general | solution.py:102
  116.8 1.8 %fusion.21 = f32[16,128,512]{2,1,0:T(8,128)S(1)} fusion(bf16[16,128,576]{1,2,0:T(8,128)(2,1)S(1)} %pad_maximum_fusion, bf16[1,1024,576]{1,2,0:T(8,128)(2,1)S(1)} %copy-done.7, s32[]{:T(128)S(6)} %select_n.183), kind=kOutput, calls=%fused_computation.44 | convolution fusion | flops 1207959552 | bytes 7143428 | tf_op jit(solution)/shard_map/qhd,sd->qhs/dot_general | solution.py:102
  118.6 2.9 %fusion.19 = f32[16,128,512]{2,1,0:T(8,128)S(1)} fusion(bf16[16,128,576]{1,2,0:T(8,128)(2,1)S(1)} %pad_maximum_fusion, bf16[512,576]{0,1:T(8,128)(2,1)} %collective-permute-done.12), kind=kOutput, calls=%fused_computation.42 | convolution fusion | flops 1207959552 | bytes 7143424 | tf_op jit(solution)/shard_map/qhd,sd->qhs/dot_general | solution.py:102
  122.4 1.8 %fusion.15 = f32[16,128,512]{2,1,0:T(8,128)S(1)} fusion(bf16[16,128,576]{1,2,0:T(8,128)(2,1)S(1)} %pad_maximum_fusion, bf16[512,576]{0,1:T(8,128)(2,1)S(1)} %collective-permute-done.14), kind=kOutput, calls=%fused_computation.38 | convolution fusion | flops 1207959552 | bytes 7143424 | tf_op jit(solution)/shard_map/qhd,sd->qhs/dot_general | solution.py:102
  124.2 2.7 %fusion.71 = f32[16,128]{1,0:T(8,128)S(1)} fusion(f32[16,128,512]{2,1,0:T(8,128)S(1)} %fusion.15, f32[16,128,512]{2,1,0:T(8,128)S(1)} %fusion.17, f32[16,128,512]{2,1,0:T(8,128)S(1)} %fusion.19, f32[16,128,512]{2,1,0:T(8,128)S(1)} %fusion.21, pred[16,2048]{1,0:T(8,128)(4,1)S(1)} %broadcast_compare_fusion), kind=kLoop, calls=%fused_computation.153 | loop fusion | flops 25163776 | bytes 16818176 | tf_op jit(solution)/shard_map/reduce_max | solution.py:108
  126.9 4.1 %fusion.1 = f32[16,128]{1,0:T(8,128)S(1)} fusion(f32[16,128]{1,0:T(8,128)S(1)} %fusion.71, f32[16,128,512]{2,1,0:T(8,128)S(1)} %fusion.15, f32[16,128,512]{2,1,0:T(8,128)S(1)} %fusion.17, f32[16,128,512]{2,1,0:T(8,128)S(1)} %fusion.19, f32[16,128,512]{2,1,0:T(8,128)S(1)} %fusion.21, pred[16,2048]{1,0:T(8,128)(4,1)S(1)} %broadcast_compare_fusion), kind=kLoop, calls=%fused_computation.4 | loop fusion | flops 29358080 | bytes 16826368 | tf_op jit(solution)/shard_map/reduce_sum | solution.py:110
  131.7 1.2 fusion.41
  132.8 1.6 collective-permute-start.15
  134.9 1.7 collective-permute-done.15
  136.7 5.6 %multiply_reduce_fusion = f32[16,2048]{1,0:T(8,128)S(1)} fusion(f32[16,128]{1,0:T(8,128)S(1)} %fusion.51, f32[16,128]{1,0:T(8,128)S(1)} %fusion.71, f32[16,128,512]{2,1,0:T(8,128)S(1)} %fusion.15, f32[16,128,512]{2,1,0:T(8,128)S(1)} %fusion.17, f32[16,128,512]{2,1,0:T(8,128)S(1)} %fusion.19, f32[16,128,512]{2,1,0:T(8,128)S(1)} %fusion.21, ...), kind=kLoop, calls=%fused_computation.2 | loop fusion | flops 33521664 | bytes 16957440 | tf_op jit(solution)/shard_map/reduce_sum | solution.py:118
  142.6 1.6 collective-permute-start.17
  144.2 3.4 %collective-permute-done.17 = f32[16,2048]{1,0:T(8,128)S(1)} collective-permute-done((f32[16,2048]{1,0:T(8,128)S(1)}, f32[16,2048]{1,0:T(8,128)S(1)}, u32[]{:S(2)}, u32[]{:S(2)}) %collective-permute-start.17) | collective-permute-done | bytes 131104 | tf_op jit(solution)/shard_map/ppermute | solution.py:40
  151.3 2.4 %collective-permute-start.18 = (bf16[16,4224]{1,0:T(8,128)(2,1)S(1)}, bf16[16,4224]{1,0:T(8,128)(2,1)S(1)}, u32[]{:S(2)}, u32[]{:S(2)}) collective-permute-start(bf16[16,4224]{1,0:T(8,128)(2,1)S(1)} %get-tuple-element.34), channel_id=1, source_target_pairs={{0,1},{1,2},{2,3},{3,0},{4,5},{5,6},{6,7},{7,4},{8,9},{9,10},{10,1... | collective-permute-start | bytes 405512 | tf_op jit(solution)/shard_map/ppermute | solution.py:162
  153.8 1.5 collective-permute-start.19
  158.2 3.0 %collective-permute-done.19 = bf16[16,4224]{1,0:T(8,128)(2,1)S(1)} collective-permute-done((bf16[16,4224]{1,0:T(8,128)(2,1)S(1)}, bf16[16,4224]{1,0:T(8,128)(2,1)S(1)}, u32[]{:S(2)}, u32[]{:S(2)}) %collective-permute-start.19) | collective-permute-done | bytes 135200 | tf_op jit(solution)/shard_map/ppermute | solution.py:162
  161.9 1.6 collective-permute-start.21
  163.4 1.1 broadcast_select_fusion.7
  165.4 6.8 %collective-permute-done.21 = bf16[1,64,4224]{2,1,0:T(8,128)(2,1)S(1)} collective-permute-done((bf16[1,64,4224]{2,1,0:T(8,128)(2,1)S(1)}, bf16[1,64,4224]{2,1,0:T(8,128)(2,1)S(1)}, u32[]{:S(2)}, u32[]{:S(2)}) %collective-permute-start.21) | collective-permute-done | bytes 540704 | tf_op jit(solution)/shard_map/ppermute | solution.py:171
  175.4 1.1 collective-permute-done.22
  176.5 1.5 broadcast_select_fusion
  179.0 3.7 %convolution_bitcast_fusion = f32[384,4096]{1,0:T(8,128)} fusion(bf16[2,64,4224]{2,1,0:T(8,128)(2,1)S(1)} %get-tuple-element.16, bf16[2,64,4224]{2,1,0:T(8,128)(2,1)S(1)} %get-tuple-element.15, bf16[2,64,384]{2,1,0:T(8,128)(2,1)S(1)} %get-tuple-element.32, bf16[2,64,384]{2,1,0:T(8,128)(2,1)S(1)} %get-tuple-element.31), kind=kOutput, calls=%fused_computation.5 | convolution fusion | flops 806453248 | bytes 8650752 | tf_op jit(solution)/shard_map/bqr,bqc->rc/dot_general | solution.py:180
  (119 shorter events, 23.2 us)
Async XLA Ops:
  0.6 12.2 %copy-start = (bf16[384,4096]{1,0:T(8,128)(2,1)S(1)}, bf16[384,4096]{1,0:T(8,128)(2,1)}, u32[]{:S(2)}) copy-start(bf16[384,4096]{1,0:T(8,128)(2,1)} %param.16) | copy-start | bytes 9437188
  0.6 14.7 %copy-start.16 = (bf16[1792,32]{0,1:T(8,128)(2,1)S(1)}, bf16[1792,32]{0,1:T(8,128)(2,1)}, u32[]{:S(2)}) copy-start(bf16[1792,32]{0,1:T(8,128)(2,1)} %param.17) | copy-start | bytes 344068
  1.8 161.7 %collective-permute-start.23 = (bf16[1,64,1792]{2,1,0:T(8,128)(2,1)S(1)}, bf16[1,64,1792]{2,1,0:T(8,128)(2,1)}, u32[]{:S(2)}, u32[]{:S(2)}) collective-permute-start(bf16[1,64,1792]{2,1,0:T(8,128)(2,1)S(1)} %constant_dynamic-slice_fusion.2), channel_id=1, source_target_pairs={{0,16},{8,24},{16,0},{24,8},{1,17},{9,25},{17,1},{25,9},{2,18},{10... | collective-permute-start | bytes 688136 | tf_op jit(solution)/shard_map/ppermute | solution.py:171
  6.2 150.0 %collective-permute-start = (bf16[1,64,384]{2,1,0:T(8,128)(2,1)}, bf16[1,64,384]{2,1,0:T(8,128)(2,1)}, u32[]{:S(2)}, u32[]{:S(2)}) collective-permute-start(bf16[1,64,384]{2,1,0:T(8,128)(2,1)} %constant_dynamic-slice_fusion.3), channel_id=1, source_target_pairs={{0,16},{8,24},{16,0},{24,8},{1,17},{9,25},{17,1},{25,9},{2,18},{10... | collective-permute-start | bytes 147464 | tf_op jit(solution)/shard_map/ppermute | solution.py:171
  12.9 22.7 %copy-start.21 = (s32[1,64]{1,0:T(1,128)S(1)}, s32[1,64]{1,0:T(1,128)}, u32[]{:S(2)}) copy-start(s32[1,64]{1,0:T(1,128)} %param.15) | copy-start | bytes 772
  16.8 36.9 %copy-start.6 = (f32[64,4224]{1,0:T(8,128)}, f32[64,4224]{1,0:T(8,128)S(1)}, u32[]{:S(2)}) copy-start(f32[64,4224]{1,0:T(8,128)S(1)} %select_maximum_fusion) | copy-start | bytes 3244036
  16.9 14.5 %collective-permute-start.2 = (f32[16,4224]{1,0:T(8,128)S(1)}, f32[16,4224]{1,0:T(8,128)S(1)}, u32[]{:S(2)}, u32[]{:S(2)}) collective-permute-start(f32[16,4224]{1,0:T(8,128)S(1)} %constant_dynamic-slice_fusion.1), channel_id=1, source_target_pairs={{0,1},{1,3},{3,2},{2,0},{4,5},{5,7},{7,6},{6,4},{8,9},{9,11},{11,1... | collective-permute-start | bytes 811016 | tf_op jit(solution)/shard_map/ppermute | solution.py:37
  19.9 10.3 %collective-permute-start.5 = (bf16[512,128]{1,0:T(8,128)(2,1)S(1)}, bf16[512,128]{1,0:T(8,128)(2,1)S(1)}, u32[]{:S(2)}, u32[]{:S(2)}) collective-permute-start(bf16[512,128]{1,0:T(8,128)(2,1)S(1)} %dynamic-slice_bitcast_fusion.5), channel_id=1, source_target_pairs={{0,1},{1,3},{3,2},{2,0},{4,5},{5,7},{7,6},{6,4},{8,9},{9,11},{11,1... | collective-permute-start | bytes 393224 | tf_op jit(solution)/shard_map/ppermute | solution.py:37
  24.5 34.3 %collective-permute-start.12 = (bf16[512,576]{0,1:T(8,128)(2,1)}, bf16[512,576]{0,1:T(8,128)(2,1)}, u32[]{:S(2)}, u32[]{:S(2)}) collective-permute-start(bf16[512,576]{0,1:T(8,128)(2,1)} %dynamic-slice_bitcast_fusion), channel_id=1, source_target_pairs={{0,1},{1,3},{3,2},{2,0},{4,5},{5,7},{7,6},{6,4},{8,9},{9,11},{11,1... | collective-permute-start | bytes 1769480 | tf_op jit(solution)/shard_map/ppermute | solution.py:37
  30.2 15.4 %collective-permute-start.6 = (bf16[512,128]{1,0:T(8,128)(2,1)S(1)}, bf16[512,128]{1,0:T(8,128)(2,1)S(1)}, u32[]{:S(2)}, u32[]{:S(2)}) collective-permute-start(bf16[512,128]{1,0:T(8,128)(2,1)S(1)} %collective-permute-done.5), channel_id=1, source_target_pairs={{0,1},{1,3},{3,2},{2,0},{4,5},{5,7},{7,6},{6,4},{8,9},{9,11},{11,1... | collective-permute-start | bytes 393224 | tf_op jit(solution)/shard_map/ppermute | solution.py:37
  31.4 20.0 %collective-permute-start.3 = (f32[16,4224]{1,0:T(8,128)S(1)}, f32[16,4224]{1,0:T(8,128)S(1)}, u32[]{:S(2)}, u32[]{:S(2)}) collective-permute-start(f32[16,4224]{1,0:T(8,128)S(1)} %dynamic-slice_add_fusion.2), channel_id=1, source_target_pairs={{0,1},{1,3},{3,2},{2,0},{4,5},{5,7},{7,6},{6,4},{8,9},{9,11},{11,1... | collective-permute-start | bytes 811016 | tf_op jit(solution)/shard_map/ppermute | solution.py:37
  35.7 61.8 %copy-start.19 = (s32[16]{0:T(128)}, s32[16]{0:T(128)S(1)}, u32[]{:S(2)}) copy-start(s32[16]{0:T(128)S(1)} %fusion.58) | copy-start | bytes 196
  45.7 51.8 %copy-start.8 = (bf16[512,128]{1,0:T(8,128)(2,1)}, bf16[512,128]{1,0:T(8,128)(2,1)S(1)}, u32[]{:S(2)}) copy-start(bf16[512,128]{1,0:T(8,128)(2,1)S(1)} %collective-permute-done.6) | copy-start | bytes 393220
  45.7 11.5 %collective-permute-start.7 = (bf16[512,128]{1,0:T(8,128)(2,1)S(1)}, bf16[512,128]{1,0:T(8,128)(2,1)S(1)}, u32[]{:S(2)}, u32[]{:S(2)}) collective-permute-start(bf16[512,128]{1,0:T(8,128)(2,1)S(1)} %collective-permute-done.6), channel_id=1, source_target_pairs={{0,1},{1,3},{3,2},{2,0},{4,5},{5,7},{7,6},{6,4},{8,9},{9,11},{11,1... | collective-permute-start | bytes 393224 | tf_op jit(solution)/shard_map/ppermute | solution.py:37
  52.1 7.6 %collective-permute-start.4 = (f32[16,4224]{1,0:T(8,128)}, f32[16,4224]{1,0:T(8,128)S(1)}, u32[]{:S(2)}, u32[]{:S(2)}) collective-permute-start(f32[16,4224]{1,0:T(8,128)} %dynamic-slice_add_fusion.1), channel_id=1, source_target_pairs={{0,1},{1,3},{3,2},{2,0},{4,5},{5,7},{7,6},{6,4},{8,9},{9,11},{11,1... | collective-permute-start | bytes 811016 | tf_op jit(solution)/shard_map/ppermute | solution.py:37
  57.2 41.9 %copy-start.10 = (bf16[512,128]{1,0:T(8,128)(2,1)}, bf16[512,128]{1,0:T(8,128)(2,1)S(1)}, u32[]{:S(2)}) copy-start(bf16[512,128]{1,0:T(8,128)(2,1)S(1)} %collective-permute-done.7) | copy-start | bytes 393220
  57.2 44.8 %collective-permute-start.11 = (bf16[16,64,576]{2,1,0:T(8,128)(2,1)}, bf16[16,64,576]{2,1,0:T(8,128)(2,1)}, u32[]{:S(2)}, u32[]{:S(2)}) collective-permute-start(bf16[16,64,576]{2,1,0:T(8,128)(2,1)} %bitcast.100), channel_id=1, source_target_pairs={{0,4},{4,0},{1,5},{5,1},{2,6},{6,2},{3,7},{7,3},{8,12},{12,8},{9,1... | collective-permute-start | bytes 3538952 | tf_op jit(solution)/shard_map/ppermute | solution.py:40
  58.8 37.2 %collective-permute-start.8 = (bf16[2048,128]{1,0:T(8,128)(2,1)S(1)}, bf16[2048,128]{1,0:T(8,128)(2,1)S(1)}, u32[]{:S(2)}, u32[]{:S(2)}) collective-permute-start(bf16[2048,128]{1,0:T(8,128)(2,1)S(1)} %pad_maximum_fusion.4), channel_id=1, source_target_pairs={{0,4},{4,0},{1,5},{5,1},{2,6},{6,2},{3,7},{7,3},{8,12},{12,8},{9,1... | collective-permute-start | bytes 1572872 | tf_op jit(solution)/shard_map/ppermute | solution.py:40
  59.7 0.7 copy-start.14
  60.4 49.8 %collective-permute-start.13 = (bf16[512,576]{0,1:T(8,128)(2,1)}, bf16[512,576]{0,1:T(8,128)(2,1)}, u32[]{:S(2)}, u32[]{:S(2)}) collective-permute-start(bf16[512,576]{0,1:T(8,128)(2,1)} %collective-permute-done.12), channel_id=1, source_target_pairs={{0,1},{1,3},{3,2},{2,0},{4,5},{5,7},{7,6},{6,4},{8,9},{9,11},{11,1... | collective-permute-start | bytes 1769480 | tf_op jit(solution)/shard_map/ppermute | solution.py:37
  64.6 34.5 %copy-start.17 = (f32[16,32]{1,0:T(8,128)}, f32[16,32]{1,0:T(8,128)S(1)}, u32[]{:S(2)}) copy-start(f32[16,32]{1,0:T(8,128)S(1)} %slice.46) | copy-start | bytes 6148
  96.0 1.4 copy-start.12
  97.4 2.0 %copy-start.2 = (f32[16,32,2048]{2,1,0:T(8,128)}, f32[16,32,2048]{2,1,0:T(8,128)S(1)}, u32[]{:S(2)}) copy-start(f32[16,32,2048]{2,1,0:T(8,128)S(1)} %get-tuple-element.51) | copy-start | bytes 12582916
  99.5 2.0 %copy-start.4 = (f32[16,32,2048]{2,1,0:T(8,128)}, f32[16,32,2048]{2,1,0:T(8,128)S(1)}, u32[]{:S(2)}) copy-start(f32[16,32,2048]{2,1,0:T(8,128)S(1)} %get-tuple-element.49) | copy-start | bytes 12582916
  99.5 32.2 %collective-permute-start.10 = (f32[16,2048]{1,0:T(8,128)S(1)}, f32[16,2048]{1,0:T(8,128)}, u32[]{:S(2)}, u32[]{:S(2)}) collective-permute-start(f32[16,2048]{1,0:T(8,128)S(1)} %broadcast_multiply_fusion.1), channel_id=1, source_target_pairs={{0,4},{4,0},{1,5},{5,1},{2,6},{6,2},{3,7},{7,3},{8,12},{12,8},{9,1... | collective-permute-start | bytes 393224 | tf_op jit(solution)/shard_map/ppermute | solution.py:40
  102.0 29.7 %collective-permute-start.9 = (f32[16,2048]{1,0:T(8,128)S(1)}, f32[16,2048]{1,0:T(8,128)}, u32[]{:S(2)}, u32[]{:S(2)}) collective-permute-start(f32[16,2048]{1,0:T(8,128)S(1)} %broadcast_multiply_fusion), channel_id=1, source_target_pairs={{0,4},{4,0},{1,5},{5,1},{2,6},{6,2},{3,7},{7,3},{8,12},{12,8},{9,1... | collective-permute-start | bytes 393224 | tf_op jit(solution)/shard_map/ppermute | solution.py:40
  110.2 6.6 %copy-start.7 = (bf16[1,1024,576]{1,2,0:T(8,128)(2,1)S(1)}, bf16[1,1024,576]{1,2,0:T(8,128)(2,1)}, u32[]{:S(2)}) copy-start(bf16[1,1024,576]{1,2,0:T(8,128)(2,1)} %param.13) | copy-start | bytes 3538948
  110.2 12.2 %collective-permute-start.14 = (bf16[512,576]{0,1:T(8,128)(2,1)}, bf16[512,576]{0,1:T(8,128)(2,1)S(1)}, u32[]{:S(2)}, u32[]{:S(2)}) collective-permute-start(bf16[512,576]{0,1:T(8,128)(2,1)} %collective-permute-done.13), channel_id=1, source_target_pairs={{0,1},{1,3},{3,2},{2,0},{4,5},{5,7},{7,6},{6,4},{8,9},{9,11},{11,1... | collective-permute-start | bytes 1769480 | tf_op jit(solution)/shard_map/ppermute | solution.py:37
  126.9 4.7 %copy-start.20 = (s32[16]{0:T(128)S(1)}, s32[16]{0:T(128)}, u32[]{:S(2)}) copy-start(s32[16]{0:T(128)} %copy-done.19) | copy-start | bytes 196
  131.1 3.7 %collective-permute-start.16 = (f32[16,128]{1,0:T(8,128)S(1)}, f32[16,128]{1,0:T(8,128)S(1)}, u32[]{:S(2)}, u32[]{:S(2)}) collective-permute-start(f32[16,128]{1,0:T(8,128)S(1)} %fusion.1), channel_id=1, source_target_pairs={{0,4},{4,0},{1,5},{5,1},{2,6},{6,2},{3,7},{7,3},{8,12},{12,8},{9,1... | collective-permute-start | bytes 24584 | tf_op jit(solution)/shard_map/ppermute | solution.py:40
  132.8 3.7 %collective-permute-start.15 = (f32[16,128]{1,0:T(8,128)S(1)}, f32[16,128]{1,0:T(8,128)S(1)}, u32[]{:S(2)}, u32[]{:S(2)}) collective-permute-start(f32[16,128]{1,0:T(8,128)S(1)} %fusion.71), channel_id=1, source_target_pairs={{0,4},{4,0},{1,5},{5,1},{2,6},{6,2},{3,7},{7,3},{8,12},{12,8},{9,1... | collective-permute-start | bytes 24584 | tf_op jit(solution)/shard_map/ppermute | solution.py:40
  136.7 11.3 %copy-start.3 = (f32[16,32,2048]{2,1,0:T(8,128)S(1)}, f32[16,32,2048]{2,1,0:T(8,128)}, u32[]{:S(2)}) copy-start(f32[16,32,2048]{2,1,0:T(8,128)} %copy-done.2) | copy-start | bytes 12582916
  136.7 11.2 %copy-start.5 = (f32[16,32,2048]{2,1,0:T(8,128)S(1)}, f32[16,32,2048]{2,1,0:T(8,128)}, u32[]{:S(2)}) copy-start(f32[16,32,2048]{2,1,0:T(8,128)} %copy-done.4) | copy-start | bytes 12582916
  142.6 5.0 %collective-permute-start.17 = (f32[16,2048]{1,0:T(8,128)S(1)}, f32[16,2048]{1,0:T(8,128)S(1)}, u32[]{:S(2)}, u32[]{:S(2)}) collective-permute-start(f32[16,2048]{1,0:T(8,128)S(1)} %get-tuple-element.37), channel_id=1, source_target_pairs={{0,4},{4,0},{1,5},{5,1},{2,6},{6,2},{3,7},{7,3},{8,12},{12,8},{9,1... | collective-permute-start | bytes 393224 | tf_op jit(solution)/shard_map/ppermute | solution.py:40
  148.0 1.0 copy-start.13
  148.0 1.1 copy-start.15
  148.0 1.0 copy-start.18
  149.1 0.9 copy-start.9
  149.1 1.0 copy-start.11
  151.3 6.9 %collective-permute-start.18 = (bf16[16,4224]{1,0:T(8,128)(2,1)S(1)}, bf16[16,4224]{1,0:T(8,128)(2,1)S(1)}, u32[]{:S(2)}, u32[]{:S(2)}) collective-permute-start(bf16[16,4224]{1,0:T(8,128)(2,1)S(1)} %get-tuple-element.34), channel_id=1, source_target_pairs={{0,1},{1,2},{2,3},{3,0},{4,5},{5,6},{6,7},{7,4},{8,9},{9,10},{10,1... | collective-permute-start | bytes 405512 | tf_op jit(solution)/shard_map/ppermute | solution.py:162
  153.8 7.4 %collective-permute-start.19 = (bf16[16,4224]{1,0:T(8,128)(2,1)S(1)}, bf16[16,4224]{1,0:T(8,128)(2,1)S(1)}, u32[]{:S(2)}, u32[]{:S(2)}) collective-permute-start(bf16[16,4224]{1,0:T(8,128)(2,1)S(1)} %get-tuple-element.34), channel_id=1, source_target_pairs={{0,2},{1,3},{2,0},{3,1},{4,6},{5,7},{6,4},{7,5},{8,10},{9,11},{10,... | collective-permute-start | bytes 405512 | tf_op jit(solution)/shard_map/ppermute | solution.py:162
  155.2 6.4 %collective-permute-start.20 = (bf16[16,4224]{1,0:T(8,128)(2,1)S(1)}, bf16[16,4224]{1,0:T(8,128)(2,1)S(1)}, u32[]{:S(2)}, u32[]{:S(2)}) collective-permute-start(bf16[16,4224]{1,0:T(8,128)(2,1)S(1)} %get-tuple-element.34), channel_id=1, source_target_pairs={{0,3},{1,0},{2,1},{3,2},{4,7},{5,4},{6,5},{7,6},{8,11},{9,8},{10,9... | collective-permute-start | bytes 405512 | tf_op jit(solution)/shard_map/ppermute | solution.py:162
  157.1 16.4 %collective-permute-start.1 = (bf16[2,64,384]{2,1,0:T(8,128)(2,1)S(1)}, bf16[2,64,384]{2,1,0:T(8,128)(2,1)S(1)}, u32[]{:S(2)}, u32[]{:S(2)}) collective-permute-start(bf16[2,64,384]{2,1,0:T(8,128)(2,1)S(1)} %pad_maximum_fusion.7), channel_id=1, source_target_pairs={{0,8},{8,0},{16,24},{24,16},{1,9},{9,1},{17,25},{25,17},{2,10},{10... | collective-permute-start | bytes 294920 | tf_op jit(solution)/shard_map/ppermute | solution.py:171
  161.9 10.3 %collective-permute-start.21 = (bf16[1,64,4224]{2,1,0:T(8,128)(2,1)S(1)}, bf16[1,64,4224]{2,1,0:T(8,128)(2,1)S(1)}, u32[]{:S(2)}, u32[]{:S(2)}) collective-permute-start(bf16[1,64,4224]{2,1,0:T(8,128)(2,1)S(1)} %get-tuple-element.22), channel_id=1, source_target_pairs={{0,16},{8,24},{16,0},{24,8},{1,17},{9,25},{17,1},{25,9},{2,18},{10... | collective-permute-start | bytes 1622024 | tf_op jit(solution)/shard_map/ppermute | solution.py:171
  165.4 8.1 %collective-permute-start.24 = (bf16[2,64,1792]{2,1,0:T(8,128)(2,1)}, bf16[2,64,1792]{2,1,0:T(8,128)(2,1)}, u32[]{:S(2)}, u32[]{:S(2)}) collective-permute-start(bf16[2,64,1792]{2,1,0:T(8,128)(2,1)} %pad_maximum_fusion.5), channel_id=1, source_target_pairs={{0,8},{8,0},{16,24},{24,16},{1,9},{9,1},{17,25},{25,17},{2,10},{10... | collective-permute-start | bytes 1376264 | tf_op jit(solution)/shard_map/ppermute | solution.py:171
  173.4 3.0 %collective-permute-start.22 = (bf16[2,64,4224]{2,1,0:T(8,128)(2,1)}, bf16[2,64,4224]{2,1,0:T(8,128)(2,1)}, u32[]{:S(2)}, u32[]{:S(2)}) collective-permute-start(bf16[2,64,4224]{2,1,0:T(8,128)(2,1)} %pad_maximum_fusion.1), channel_id=1, source_target_pairs={{0,8},{8,0},{16,24},{24,16},{1,9},{9,1},{17,25},{25,17},{2,10},{10... | collective-permute-start | bytes 3244040 | tf_op jit(solution)/shard_map/ppermute | solution.py:171
  179.0 3.7 %copy-start.1 = (bf16[384,4096]{1,0:T(8,128)(2,1)S(1)}, bf16[384,4096]{1,0:T(8,128)(2,1)}, u32[]{:S(2)}) copy-start(bf16[384,4096]{1,0:T(8,128)(2,1)} %param.16) | copy-start | bytes 9437188

commit v2 on v1

v2 whole, which is shorter than its diff:
```python
import functools
import math

import jax
import jax.numpy as jnp
from jax import lax
from jax.experimental import pallas as pl
from jax.experimental.pallas import tpu as pltpu
from jax.sharding import PartitionSpec as P

HI = 64
DI = 128
HM = 128

index_scale = (HI * DI) ** (-0.5)
exponent_scale = 192.0 ** (-0.5) / math.log(2.0)
masked_floor = -1e30
lanes = 128
f32 = jnp.float32
bf16 = jnp.bfloat16
vmem_limit = 56 * 2**20


def folded_ring(size):
    return [0] + list(range(1, size, 2)) + list(range(2, size, 2))[::-1]


def params():
    return pltpu.CompilerParams(vmem_limit_bytes=vmem_limit)


def in_smem():
    return pl.BlockSpec(memory_space=pltpu.SMEM)


def in_vmem():
    return pl.BlockSpec(memory_space=pltpu.VMEM)


def times(a, b, axis_a, axis_b):
    return lax.dot_general(a, b, (((axis_a,), (axis_b,)), ((), ())), preferred_element_type=f32)


def project_kernel(latent, weight, hidden, hidden_weight, out):
    width = weight.shape[1]
    heads = hidden_weight.shape[0]
    for at in range(0, width, 512):
        out[:, at : at + 512] = times(latent[...], weight[:, at : at + 512], 1, 0)
    mixed = times(hidden[...], hidden_weight[...], 1, 1)
    out[:, width : width + heads] = mixed
    out[:, width + heads :] = jnp.zeros((out.shape[0], lanes - heads), f32)


def project(latent, weight, hidden, hidden_weight):
    count, width = latent.shape[0], weight.shape[1]
    return pl.pallas_call(
        project_kernel,
        out_shape=jax.ShapeDtypeStruct((count, width + lanes), f32),
        in_specs=[in_vmem()] * 4,
        out_specs=in_vmem(),
        compiler_params=params(),
        cost_estimate=pl.CostEstimate(
            flops=2 * count * weight.size, bytes_accessed=2 * weight.size, transcendentals=0
        ),
        name="project",
    )(latent, weight, hidden, hidden_weight)


def score_kernel(first, limits, mine, other, keys, top_before, mass_before, weights, top, top_all, mass_all, mass):
    count, heads, depth = mine.shape
    span = keys.shape[1]
    key_at = lax.broadcasted_iota(jnp.int32, (1, span), 1)
    row_at = lax.broadcasted_iota(jnp.int32, (heads, lanes), 0)
    lane_at = lax.broadcasted_iota(jnp.int32, (heads, lanes), 1)
    group = min(8, count)
    for at in range(0, count, group):
        for source, offset in ((mine, 0), (other, heads)):
            rows = source[at : at + group].reshape(group * heads, depth)
            scores = times(rows, keys[...], 1, 0)
            diagonal = lane_at == row_at + offset
            for k in range(group):
                q = at + k
                visible = key_at <= limits[q]
                one = jnp.where(visible, scores[k * heads : (k + 1) * heads], masked_floor)
                high = jnp.max(one, axis=1, keepdims=True)
                shifted = jnp.exp2((one - high) * exponent_scale)
                total = jnp.sum(shifted, axis=1, keepdims=True)
                weights[q, offset : offset + heads] = shifted.astype(bf16)
                high_row = jnp.sum(jnp.where(diagonal, high, 0.0), axis=0, keepdims=True)
                total_row = jnp.sum(jnp.where(diagonal, total, 0.0), axis=0, keepdims=True)
                if offset == 0:
                    top[q : q + 1, :] = high_row
                    mass[q : q + 1, :] = total_row
                else:
                    top[q : q + 1, :] += high_row
                    mass[q : q + 1, :] += total_row
    if first:
        top_all[...] = top[...]
        mass_all[...] = mass[...]
    else:
        before, now = top_before[...], top[...]
        joint = jnp.maximum(before, now)
        top_all[...] = joint
        mass_all[...] = mass_before[...] * jnp.exp2((before - joint) * exponent_scale) + mass[
            ...
        ] * jnp.exp2((now - joint) * exponent_scale)


def score(limits, mine, other, keys, before):
    count, heads, depth = mine.shape
    span = keys.shape[1]
    stats = jax.ShapeDtypeStruct((count, lanes), f32)
    first = before is None
    if first:
        before = (jnp.zeros((count, lanes), f32),) * 2
    return pl.pallas_call(
        functools.partial(score_kernel, first),
        out_shape=(jax.ShapeDtypeStruct((count, 2 * heads, span), bf16), stats, stats, stats),
        in_specs=[in_smem()] + [in_vmem()] * 5,
        out_specs=(in_vmem(),) * 4,
        scratch_shapes=[pltpu.VMEM((count, lanes), f32)],
        compiler_params=params(),
        cost_estimate=pl.CostEstimate(
            flops=4 * count * heads * depth * span,
            bytes_accessed=2 * (2 * mine.size + keys.size + 2 * count * heads * span),
            transcendentals=2 * count * heads * span,
        ),
        name="score",
    )(limits, mine, other, keys, *before)


def target_kernel(blocks, *refs):
    weights, tops = refs[:blocks], refs[blocks : 2 * blocks]
    top, mass, other_top, other_mass, out = refs[2 * blocks :]
    count, heads, span = weights[0].shape
    far_top = pltpu.roll(other_top[...], heads // 2, 1)
    far_mass = pltpu.roll(other_mass[...], heads // 2, 1)
    joint = jnp.maximum(top[...], far_top)
    total = mass[...] * jnp.exp2((top[...] - joint) * exponent_scale) + far_mass * jnp.exp2(
        (far_top - joint) * exponent_scale
    )
    row_at = lax.broadcasted_iota(jnp.int32, (heads, lanes), 0)
    lane_at = lax.broadcasted_iota(jnp.int32, (heads, lanes), 1)
    diagonal = row_at == lane_at
    inverse = 1.0 / (total * HM)
    for t in range(blocks):
        factor = jnp.exp2((tops[t][...] - joint) * exponent_scale) * inverse
        for q in range(count):
            column = jnp.sum(
                jnp.where(diagonal, factor[q : q + 1, :], 0.0), axis=1, keepdims=True
            )
            mixed = weights[t][q].astype(f32) * column
            out[q : q + 1, t * span : (t + 1) * span] = jnp.sum(mixed, axis=0, keepdims=True)


def make_target(weights, tops, top, mass, other_top, other_mass):
    blocks = len(weights)
    count, heads, span = weights[0].shape
    group = min(8, count)

    def stat_spec():
        return pl.BlockSpec((group, lanes), lambda i: (i, 0))

    return pl.pallas_call(
        functools.partial(target_kernel, blocks),
        grid=(count // group,),
        out_shape=jax.ShapeDtypeStruct((count, blocks * span), f32),
        in_specs=[pl.BlockSpec((group, heads, span), lambda i: (i, 0, 0))] * blocks
        + [stat_spec() for _ in range(blocks + 4)],
        out_specs=pl.BlockSpec((group, blocks * span), lambda i: (i, 0)),
        compiler_params=params(),
        cost_estimate=pl.CostEstimate(
            flops=2 * blocks * count * heads * span,
            bytes_accessed=2 * blocks * count * heads * span,
            transcendentals=0,
        ),
        name="target",
    )(*weights, *tops, top, mass, other_top, other_mass)


def query_rows(total, heads):
    return jnp.concatenate(
        [total[:, j * DI : (j + 1) * DI].astype(bf16) for j in range(heads)], axis=0
    )


def logits_kernel(heads, total, own, other, out):
    count = total.shape[0]
    query = query_rows(total, heads)
    columns = [total[:, heads * DI + j : heads * DI + j + 1] for j in range(heads)]
    span = 512
    for part, keys in enumerate((own, other)):
        for at in range(0, keys.shape[0], span):
            affinity = times(query, keys[at : at + span, :], 1, 1)
            running = jnp.zeros((count, span), f32)
            for j in range(heads):
                reached = jnp.maximum(affinity[j * count : (j + 1) * count], 0.0)
                running = running + columns[j] * reached
            out[part, :, at : at + span] = running * index_scale


def make_logits(heads, total, own, other):
    count, length = total.shape[0], own.shape[0]
    return pl.pallas_call(
        functools.partial(logits_kernel, heads),
        out_shape=jax.ShapeDtypeStruct((2, count, length), f32),
        in_specs=[in_vmem()] * 3,
        out_specs=in_vmem(),
        compiler_params=params(),
        cost_estimate=pl.CostEstimate(
            flops=4 * count * heads * DI * length,
            bytes_accessed=4 * (total.size + 2 * count * length) + 4 * length * DI,
            transcendentals=0,
        ),
        name="logits",
    )(total, own, other)


def gradient_kernel(
    heads, blocks, bases, positions, total, own, other, part, far, target_own, target_other, out, logit, flow
):
    count = total.shape[0]
    span = own.shape[0] // blocks
    query = query_rows(total, heads)
    position = positions[:, 0:1]
    key_at = lax.broadcasted_iota(jnp.int32, (count, span), 1)
    sides = ((own, target_own), (other, target_other))

    def seen(side, t):
        return key_at + bases[side, t] <= position

    highs = []
    for side in range(2):
        high = jnp.full((count, span), masked_floor, f32)
        for t in range(blocks):
            at = slice(t * span, (t + 1) * span)
            value = part[side, :, at] + far[1 - side, :, at]
            logit[side, :, at] = value
            high = jnp.maximum(high, jnp.where(seen(side, t), value, masked_floor))
        highs.append(jnp.max(high, axis=1, keepdims=True))
    high = jnp.maximum(highs[0], highs[1])
    sums = []
    for side in range(2):
        running = jnp.zeros((count, span), f32)
        for t in range(blocks):
            at = slice(t * span, (t + 1) * span)
            grown = jnp.exp(logit[side, :, at] - high)
            running = running + jnp.where(seen(side, t), grown, 0.0)
        sums.append(jnp.sum(running, axis=1, keepdims=True))
    mass = sums[0] + sums[1]
    level = high + jnp.log(mass)
    inverse = 1.0 / mass
    columns = [
        total[:, heads * DI + j : heads * DI + j + 1] * index_scale for j in range(heads)
    ]
    losses = []
    query_sum = jnp.zeros((heads * count, DI), f32)
    flow[...] = jnp.zeros(flow.shape, f32)
    for side, (keys, target) in enumerate(sides):
        running = jnp.zeros((count, span), f32)
        for t in range(blocks):
            at = slice(t * span, (t + 1) * span)
            visible = seen(side, t)
            value = logit[side, :, at]
            wanted = target[:, at]
            running = running + jnp.where(visible, wanted * (value - level), 0.0)
            grown = jnp.exp(value - high) * inverse
            delta = jnp.where(visible, grown - wanted, 0.0)
            affinity = times(query, keys[at, :], 1, 1)
            grads = []
            for j in range(heads):
                rows = slice(j * count, (j + 1) * count)
                one = affinity[rows]
                grads.append(jnp.where(one > 0, delta * columns[j], 0.0).astype(bf16))
                product = delta * jnp.maximum(one, 0.0)
                folded = product[:, :lanes]
                for k in range(lanes, span, lanes):
                    folded = folded + product[:, k : k + lanes]
                flow[rows, :] += folded
            query_sum = query_sum + times(jnp.concatenate(grads, axis=0), keys[at, :], 1, 0)
        losses.append(jnp.sum(running, axis=1, keepdims=True))
    loss = -(losses[0] + losses[1])
    lane_at = lax.broadcasted_iota(jnp.int32, (count, lanes), 1)
    tail = jnp.zeros((count, lanes), f32)
    for j in range(heads):
        rows = slice(j * count, (j + 1) * count)
        out[:, j * DI : (j + 1) * DI] = query_sum[rows].astype(bf16)
        column = jnp.sum(flow[rows, :], axis=1, keepdims=True) * index_scale
        tail = jnp.where(lane_at == j, column, tail)
    loss_high = loss.astype(bf16).astype(f32)
    tail = jnp.where(lane_at == heads, loss_high, tail)
    tail = jnp.where(lane_at == heads + 1, loss - loss_high, tail)
    out[:, heads * DI :] = tail.astype(bf16)


def gradients(heads, blocks, bases, positions, total, own, other, part, far, target_own, target_other):
    count, length = total.shape[0], own.shape[0]
    return pl.pallas_call(
        functools.partial(gradient_kernel, heads, blocks),
        out_shape=jax.ShapeDtypeStruct((count, heads * DI + lanes), bf16),
        in_specs=[in_smem()] + [in_vmem()] * 8,
        out_specs=in_vmem(),
        scratch_shapes=[
            pltpu.VMEM((2, count, length), f32),
            pltpu.VMEM((heads * count, lanes), f32),
        ],
        compiler_params=params(),
        cost_estimate=pl.CostEstimate(
            flops=8 * count * heads * DI * length,
            bytes_accessed=4 * (total.size + 6 * count * length) + 4 * length * DI,
            transcendentals=4 * count * length,
        ),
        name="gradient",
    )(bases, positions, total, own, other, part, far, target_own, target_other)


def outer_kernel(parts, blocks, place, latents, hiddens, *refs):
    bodies, tails = refs[:parts], refs[parts : 2 * parts]
    grad, grad_mixed, rows, tail_rows = refs[2 * parts :]
    count = bodies[0].shape[1]
    for k in range(parts):
        for t in range(blocks):
            to = pl.ds(pl.multiple_of(place[k, t] * count, count), count)
            rows[to, :] = bodies[k][t]

    grad[...] = times(latents[...], rows[...], 0, 0)

    @pl.when(pl.program_id(0) == 0)
    def _():
        for k in range(parts):
            for t in range(blocks):
                to = pl.ds(pl.multiple_of(place[k, t] * count, count), count)
                tail_rows[to, :] = tails[k][t]
        mixed = times(tail_rows[...], hiddens[...], 0, 0)
        grad_mixed[...] = mixed[: grad_mixed.shape[0]]


def outer(heads, place, latents, hiddens, parts):
    blocks, count, _ = parts[0].shape
    total = latents.shape[0]
    width = heads * DI
    span = 512
    row_count, hidden_count = latents.shape[1], hiddens.shape[1]
    body = [pl.BlockSpec((blocks, count, span), lambda i: (0, 0, i)) for _ in parts]
    tail = [
        pl.BlockSpec((blocks, count, lanes), lambda i: (0, 0, width // lanes)) for _ in parts
    ]
    return pl.pallas_call(
        functools.partial(outer_kernel, len(parts), blocks),
        grid=(width // span,),
        out_shape=(
            jax.ShapeDtypeStruct((row_count, width), f32),
            jax.ShapeDtypeStruct((heads, hidden_count), f32),
        ),
        in_specs=[
            in_smem(),
            pl.BlockSpec((total, row_count), lambda i: (0, 0)),
            pl.BlockSpec((total, hidden_count), lambda i: (0, 0)),
        ]
        + body
        + tail,
        out_specs=(
            pl.BlockSpec((row_count, span), lambda i: (0, i)),
            pl.BlockSpec((heads, hidden_count), lambda i: (0, 0)),
        ),
        scratch_shapes=[pltpu.VMEM((total, span), bf16), pltpu.VMEM((total, lanes), bf16)],
        compiler_params=params(),
        cost_estimate=pl.CostEstimate(
            flops=2 * total * row_count * width,
            bytes_accessed=4 * row_count * width + 2 * total * width,
            transcendentals=0,
        ),
        name="outer",
    )(place, latents, hiddens, *parts, *parts)


def per_device(
    q_latent, hidden, main_queries, main_keys, index_keys, positions, w_query, w_weights
):
    n = lax.axis_size("ctx")
    z = lax.axis_index("ctx")
    y = lax.axis_index("head")
    dp_size = lax.axis_size("dp")
    dp = lax.axis_index("dp")
    ring = folded_ring(n)
    place_of = [ring.index(k) for k in range(n)]
    ring_table = jnp.array(ring, jnp.int32)
    place = jnp.array(place_of, jnp.int32)[z]
    ring_pairs = [(ring[k], ring[(k + 1) % n]) for k in range(n)]

    def at_place(k):
        return ring_table[lax.rem(k + 2 * n, n)]

    def onward(x):
        return lax.ppermute(x, "ctx", ring_pairs)

    def swap_head(x):
        return lax.ppermute(x, "head", [(0, 1), (1, 0)])

    rows = main_keys.shape[1]
    half = rows // 2
    rows_latent = w_query.shape[0]
    rows_hidden = w_weights.shape[0]
    heads_here = w_weights.shape[1]
    width = heads_here * DI
    queries_here = main_queries.shape[1]
    query_pos = lax.dynamic_slice_in_dim(positions[0], z * queries_here, queries_here)
    own_latent = lax.dynamic_slice_in_dim(q_latent[0], z * rows_latent, rows_latent, 1)
    own_hidden = lax.dynamic_slice_in_dim(hidden[0], z * rows_hidden, rows_hidden, 1)

    queries = main_queries[0]
    other_queries = swap_head(queries)
    key_part = lax.dynamic_slice_in_dim(main_keys[0].T, y * half, half, 1)
    keys_mine = [key_part]
    for _ in range(n - 1):
        keys_mine.append(onward(keys_mine[-1]))
    index_mine = [lax.dynamic_slice_in_dim(index_keys[0], y * half, half)]
    for _ in range(n - 1):
        index_mine.append(onward(index_mine[-1]))
    index_own = jnp.concatenate(index_mine)
    index_other = swap_head(index_own)
    sources = jnp.stack([at_place(place - t) for t in range(n)]) * rows
    base_own = sources + y * half
    bases = jnp.stack([base_own, sources + (1 - y) * half])

    partial = project(own_latent, w_query, own_hidden, w_weights.T)

    def partial_of(k):
        return lax.dynamic_slice_in_dim(partial, at_place(k) * queries_here, queries_here)

    total = partial_of(place - 1)
    for t in range(1, n):
        total = onward(total) + partial_of(place - t - 1)

    part = make_logits(heads_here, total, index_own, index_other)
    far = swap_head(part)

    weights, tops, before = [], [], None
    for t in range(n):
        limits = query_pos - base_own[t]
        numer, top, *before = score(limits, queries, other_queries, keys_mine[t], before)
        weights.append(numer)
        tops.append(top)
    far_top, far_mass = swap_head(jnp.stack(before))
    target_own = make_target(weights, tops, *before, far_top, far_mass)
    target_other = swap_head(target_own)

    position_rows = jnp.broadcast_to(query_pos[:, None], (queries_here, lanes))
    piece = gradients(
        heads_here,
        n,
        bases,
        position_rows,
        total,
        index_own,
        index_other,
        part,
        far,
        target_own,
        target_other,
    )

    pieces = [piece]
    for t in range(1, n):
        pairs = [(k, (k + t) % n) for k in range(n)]
        pieces.append(lax.ppermute(piece, "ctx", pairs))
    sequence = jnp.stack(pieces)

    def swap_dp(x, bit):
        return lax.ppermute(x, "dp", [(k, k ^ bit) for k in range(dp_size)])

    gathered = [sequence]
    bit = dp_size // 2
    while bit:
        gathered = gathered + [swap_dp(x, bit) for x in gathered]
        bit //= 2
    flips = [0]
    bit = dp_size // 2
    while bit:
        flips = flips + [k ^ bit for k in flips]
        bit //= 2
    steps = lax.rem(z - jnp.arange(n, dtype=jnp.int32) + n, n)
    where_from = jnp.stack([(dp ^ k) * n + steps for k in flips])
    both = lax.all_gather(jnp.concatenate([own_latent, own_hidden], axis=1), "dp")
    both = both.reshape(-1, rows_latent + rows_hidden)
    if queries_here % 16:
        flat = jnp.concatenate(gathered)
        order = jnp.argsort(where_from.reshape(-1))
        gathered = [flat[order].reshape(1, -1, flat.shape[2])]
        where_from = jnp.zeros((1, 1), jnp.int32)
    grad_query, grad_weights = outer(
        heads_here, where_from, both[:, :rows_latent], both[:, rows_latent:], gathered
    )
    low = sequence[:, :, width + heads_here : width + heads_here + 2].astype(f32)
    low = low[:, :, 0] + low[:, :, 1]
    losses = jnp.concatenate([low[steps[k]] for k in range(n)])
    return (grad_query, grad_weights.T, losses[None, :])


def solution(mesh):
    return jax.shard_map(
        per_device,
        mesh=mesh,
        in_specs=(
            P("dp", None, None),
            P("dp", None, None),
            P("dp", "ctx", "head", None),
            P("dp", "ctx", None),
            P("dp", "ctx", None),
            P("dp", None),
            P("ctx", "head"),
            P("ctx", "head"),
        ),
        out_specs=(P("ctx", "head"), P("ctx", "head"), P("dp", None)),
        check_vma=False,
    )
```

time: 184 us -> 164 us (0.89)
  Pallas kernels: 0 us -> 46.7 us
  waiting for transfers between devices: 67.1 us -> 31.4 us
  matrix products: 21.7 us -> 0 us
  between operations: 7.09 us -> 27.7 us
  other arithmetic: 32.3 us -> 15 us
  starting transfers between devices: 37 us -> 26 us
    pallas_call x0 -> x9, Pallas kernels: none -> 46.7 us  [the longest x4 20.9 us: score(): pl.pallas_call(functools.partial(score_kernel, first), out_shape=(jax.Sha...]
    ppermute x7 -> x5, waiting for transfers between devices: 36.9 us -> 3.06 us  [swap_head(): return lax.ppermute(x, 'head', [(0, 1), (1, 0)])]
    dot_general x12 -> x0, matrix products: 21.7 us -> none  [the longest x4 9.51 us: per_device(): jnp.einsum('qhd,sd->qhs', all_queries, k, preferred_element_type=jnp.floa...]
    reduce_sum x5 -> x0, other arithmetic: 11.2 us -> none  [the longest x1 5.6 us: per_device(): target_own = jnp.sum(shifted * factor[:, :, None], axis=1)]
    ppermute x9, starting transfers between devices: 18.5 us -> 11.8 us  [onward(): return lax.ppermute(x, 'ctx', ring_pairs)]
    ppermute x6 -> x3, waiting for transfers between devices: 7.92 us -> 1.29 us  [swap_dp(): return lax.ppermute(x, 'dp', [(k, k ^ bit) for k in range(dp_size)])]
    concatenate x7 -> x1, other arithmetic: 6.35 us -> 0.75 us  [per_device(): jnp.concatenate([own_latent, own_hidden], axis=1)]
    slice x3 -> x4, local copies, waits for them, and re-layouts: 0.15 us -> 5.04 us  [the longest x1 2.18 us: per_device(): both[:, rows_latent:]]
  transfers between devices with their start and end apart: 25 -> 21, of which waited for: 14 -> 10; matrix products, arithmetic and copies ran while one was open for 34% -> 17% of each run, Pallas kernels for 0% -> 24%
where the time goes in v2:
time: 164 us; the launch traced here: 163 us
  Pallas kernels  46.7 us (28%)
  waiting for transfers between devices  31.4 us (19%)
  between operations  27.7 us (17%)
  starting transfers between devices  26 us (16%)
  local copies, waits for them, and re-layouts  15.6 us (10%)
  other arithmetic  15 us (9%)
    ppermute x9, waiting for transfers between devices, onward(): return lax.ppermute(x, 'ctx', ring_pairs)  21.1 us
    pallas_call x4, Pallas kernels, score(): pl.pallas_call(functools.partial(score_kernel, first), out_shape=(jax.Sha...  20.9 us
    ppermute x9, starting transfers between devices, onward(): return lax.ppermute(x, 'ctx', ring_pairs)  11.8 us
    pallas_call x1, Pallas kernels, outer(): pl.pallas_call(functools.partial(outer_kernel, len(parts), blocks), grid=...  8.28 us
    ppermute x5, starting transfers between devices, swap_head(): return lax.ppermute(x, 'head', [(0, 1), (1, 0)])  8.24 us
    ppermute x3, waiting for transfers between devices, per_device(): pieces.append(lax.ppermute(piece, 'ctx', pairs))  5.98 us
    pallas_call x1, Pallas kernels, make_target(): pl.pallas_call(functools.partial(target_kernel, blocks), grid=(count // g...  5.45 us
    add x2, other arithmetic, per_device(): base_own = sources + y * half  5.15 us
  transfers between devices with their start and end apart: 21, of which 10 were waited for; matrix products, arithmetic and copies ran while one was open for 17% of the time, Pallas kernels for 24%

profile of v2, /device:TPU:0, one launch (start us, length us, event | category | flops | bytes accessed | tf_op | source)
XLA Modules:
  0.0 162.5 jit_solution(17682339116440556431)
XLA Ops:
  7.2 3.0 %collective-permute-start.8 = (bf16[16,64,576]{2,1,0:T(8,128)(2,1)}, bf16[16,64,576]{2,1,0:T(8,128)(2,1)}, u32[]{:S(2)}, u32[]{:S(2)}) collective-permute-start(bf16[16,64,576]{2,1,0:T(8,128)(2,1)} %bitcast.56), channel_id=1, source_target_pairs={{0,4},{4,0},{1,5},{5,1},{2,6},{6,2},{3,7},{7,3},{8,12},{12,8},{9,1... | collective-permute-start | bytes 3538952 | tf_op jit(solution)/shard_map/ppermute | solution.py:398
  10.3 1.6 %collective-permute-start.9 = (bf16[576,512]{1,0:T(8,128)(2,1)S(1)}, bf16[576,512]{1,0:T(8,128)(2,1)}, u32[]{:S(2)}, u32[]{:S(2)}) collective-permute-start(bf16[576,512]{1,0:T(8,128)(2,1)S(1)} %dynamic-slice_bitcast_fusion.keys), channel_id=1, source_target_pairs={{0,1},{1,3},{3,2},{2,0},{4,5},{5,7},{7,6},{6,4},{8,9},{9,11},{11,1... | collective-permute-start | bytes 1769480 | tf_op jit(solution)/shard_map/ppermute | solution.py:395
  12.0 1.2 dynamic_slice.70
  17.8 1.6 %dynamic-slice_bitcast_fusion.1.hidden = bf16[64,1792]{1,0:T(8,128)(2,1)} fusion(bf16[1,64,7168]{2,1,0:T(8,128)(2,1)} %param.11, s32[]{:T(128)S(6)} %select_n.59), kind=kLoop, calls=%fused_computation.7 | loop fusion | bytes 458756 | tf_op jit(solution)/shard_map/dynamic_slice | solution.py:409
  19.5 1.4 dynamic-slice_bitcast_fusion.3.latent
  20.9 3.7 %project.1 = f32[64,4224]{1,0:T(8,128)} custom-call(bf16[64,384]{1,0:T(8,128)(2,1)} %dynamic-slice_bitcast_fusion.3.latent, bf16[384,4096]{1,0:T(8,128)(2,1)} %weight.1, bf16[64,1792]{1,0:T(8,128)(2,1)} %dynamic-slice_bitcast_fusion.1.hidden, bf16[32,1792]{1,0:T(8,128)(2,1)} %bitcast.53), custom_call_target="tpu_custom_call" | custom-call | flops 201326592 | bytes 3145728 | tf_op jit(solution)/shard_map/project/pallas_call | solution.py:56
  24.6 1.1 constant_dynamic-slice_fusion
  25.7 2.6 %collective-permute-start = (f32[16,4224]{1,0:T(8,128)S(1)}, f32[16,4224]{1,0:T(8,128)S(1)}, u32[]{:S(2)}, u32[]{:S(2)}) collective-permute-start(f32[16,4224]{1,0:T(8,128)S(1)} %constant_dynamic-slice_fusion), channel_id=1, source_target_pairs={{0,1},{1,3},{3,2},{2,0},{4,5},{5,7},{7,6},{6,4},{8,9},{9,11},{11,1... | collective-permute-start | bytes 811016 | tf_op jit(solution)/shard_map/ppermute | solution.py:395
  30.2 2.6 %fusion.3 = s32[4]{0:T(128)S(1)} fusion(s32[1]{0:T(128)} %get-tuple-element.64, s32[1]{0:T(128)} %get-tuple-element.61, s32[1]{0:T(128)} %get-tuple-element.62, s32[1]{0:T(128)} %get-tuple-element.63, s32[]{:T(128)S(6)} %mul.76), kind=kLoop, calls=%fused_computation.32 | loop fusion | flops 20 | bytes 36 | tf_op jit(solution)/shard_map/add | solution.py:423
  33.4 2.3 %collective-permute-done = f32[16,4224]{1,0:T(8,128)S(1)} collective-permute-done((f32[16,4224]{1,0:T(8,128)S(1)}, f32[16,4224]{1,0:T(8,128)S(1)}, u32[]{:S(2)}, u32[]{:S(2)}) %collective-permute-start) | collective-permute-done | bytes 270368 | tf_op jit(solution)/shard_map/ppermute | solution.py:395
  35.7 1.9 %collective-permute-start.1 = (f32[16,4224]{1,0:T(8,128)S(1)}, f32[16,4224]{1,0:T(8,128)S(1)}, u32[]{:S(2)}, u32[]{:S(2)}) collective-permute-start(f32[16,4224]{1,0:T(8,128)S(1)} %dynamic-slice_add_fusion.2), channel_id=1, source_target_pairs={{0,1},{1,3},{3,2},{2,0},{4,5},{5,7},{7,6},{6,4},{8,9},{9,11},{11,1... | collective-permute-start | bytes 811016 | tf_op jit(solution)/shard_map/ppermute | solution.py:395
  37.7 1.2 broadcast_subtract_fusion
  39.5 1.2 collective-permute-start.4
  40.7 2.4 %broadcast_subtract_fusion.1 = (s32[16]{0:T(128)}, s32[16]{0:T(128)}, s32[16]{0:T(128)}) fusion(s32[16]{0:T(128)S(1)} %get-tuple-element.44, s32[]{:T(128)} %bitcast.24, s32[]{:T(128)} %bitcast.22, s32[]{:T(128)} %bitcast.18), kind=kLoop, calls=%fused_computation.35 | loop fusion | flops 48 | bytes 268 | tf_op jit(solution)/shard_map/sub | solution.py:440
  43.1 2.7 %collective-permute-done.4 = bf16[512,128]{1,0:T(8,128)(2,1)} collective-permute-done((bf16[512,128]{1,0:T(8,128)(2,1)}, bf16[512,128]{1,0:T(8,128)(2,1)}, u32[]{:S(2)}, u32[]{:S(2)}) %collective-permute-start.4) | collective-permute-done | bytes 131104 | tf_op jit(solution)/shard_map/ppermute | solution.py:395
  45.8 1.7 %collective-permute-start.5 = (bf16[512,128]{1,0:T(8,128)(2,1)}, bf16[512,128]{1,0:T(8,128)(2,1)}, u32[]{:S(2)}, u32[]{:S(2)}) collective-permute-start(bf16[512,128]{1,0:T(8,128)(2,1)} %collective-permute-done.4), channel_id=1, source_target_pairs={{0,1},{1,3},{3,2},{2,0},{4,5},{5,7},{7,6},{6,4},{8,9},{9,11},{11,1... | collective-permute-start | bytes 393224 | tf_op jit(solution)/shard_map/ppermute | solution.py:395
  47.5 1.4 collective-permute-start.10
  49.0 2.6 %broadcast_add_fusion.1 = (s32[1,4]{1,0:T(1,128)S(1)}, s32[1,4]{1,0:T(1,128)S(1)}) fusion(s32[]{:T(128)S(6)} %mul.76, s32[1,1]{1,0:T(1,128)} %bitcast.9, s32[1,1]{1,0:T(1,128)} %bitcast.7, s32[1,1]{1,0:T(1,128)} %bitcast.5, s32[1,1]{1,0:T(1,128)} %bitcast.3), kind=kLoop, calls=%fused_computation.39 | loop fusion | flops 20 | bytes 52 | tf_op jit(solution)/shard_map/add | solution.py:423
  52.2 1.3 collective-permute-done.5
  53.5 1.1 pad_maximum_fusion.1.own
  54.6 1.6 collective-permute-start.6
  56.1 10.0 %collective-permute-done.10.keys = bf16[576,512]{1,0:T(8,128)(2,1)} collective-permute-done((bf16[576,512]{1,0:T(8,128)(2,1)}, bf16[576,512]{1,0:T(8,128)(2,1)}, u32[]{:S(2)}, u32[]{:S(2)}) %collective-permute-start.10) | collective-permute-done | bytes 589856 | tf_op jit(solution)/shard_map/ppermute | solution.py:395
  66.1 0.8 collective-permute-start.11
  66.9 4.9 %collective-permute-done.2 = f32[16,4224]{1,0:T(8,128)S(1)} collective-permute-done((f32[16,4224]{1,0:T(8,128)S(1)}, f32[16,4224]{1,0:T(8,128)S(1)}, u32[]{:S(2)}, u32[]{:S(2)}) %collective-permute-start.2) | collective-permute-done | bytes 270368 | tf_op jit(solution)/shard_map/ppermute | solution.py:395
  73.2 5.2 %score.4 = (bf16[16,128,512]{2,1,0:T(8,128)(2,1)}, f32[16,128]{1,0:T(8,128)}, f32[16,128]{1,0:T(8,128)}, f32[16,128]{1,0:T(8,128)}) custom-call(s32[16]{0:T(128)} %get-tuple-element.55.limits, bf16[16,64,576]{2,1,0:T(8,128)(2,1)} %bitcast.57, bf16[16,64,576]{2,1,0:T(8,128)(2,1)} %collective-permute-done.8.other, bf16[576,512]{1,0:T(8,128)(2,1)} %copy-done.7, ...), custom_call_target="tpu_custom_call" | custom-call | flops 1207959552 | bytes 5046272 | tf_op jit(solution)/shard_map/score/pallas_call | solution.py:116
  78.3 5.2 %score.5 = (bf16[16,128,512]{2,1,0:T(8,128)(2,1)}, f32[16,128]{1,0:T(8,128)}, f32[16,128]{1,0:T(8,128)}, f32[16,128]{1,0:T(8,128)}) custom-call(s32[16]{0:T(128)} %get-tuple-element.54.limits, bf16[16,64,576]{2,1,0:T(8,128)(2,1)} %bitcast.58, bf16[16,64,576]{2,1,0:T(8,128)(2,1)} %collective-permute-done.8.other, ...), custom_call_target="tpu_custom_call" | custom-call | flops 1207959552 | bytes 5046272 | tf_op jit(solution)/shard_map/score/pallas_call | solution.py:116
  83.6 5.2 %score.6 = (bf16[16,128,512]{2,1,0:T(8,128)(2,1)}, f32[16,128]{1,0:T(8,128)}, f32[16,128]{1,0:T(8,128)}, f32[16,128]{1,0:T(8,128)}) custom-call(s32[16]{0:T(128)} %get-tuple-element.53.limits, bf16[16,64,576]{2,1,0:T(8,128)(2,1)} %bitcast.59, bf16[16,64,576]{2,1,0:T(8,128)(2,1)} %collective-permute-done.8.other, ...), custom_call_target="tpu_custom_call" | custom-call | flops 1207959552 | bytes 5046272 | tf_op jit(solution)/shard_map/score/pallas_call | solution.py:116
  88.8 0.8 copy-done.13
  89.6 5.3 %score.7 = (bf16[16,128,512]{2,1,0:T(8,128)(2,1)}, f32[16,128]{1,0:T(8,128)}, f32[16,128]{1,0:T(8,128)}, f32[16,128]{1,0:T(8,128)}) custom-call(s32[16]{0:T(128)} %get-tuple-element.43.limits, bf16[16,64,576]{2,1,0:T(8,128)(2,1)} %bitcast.60, bf16[16,64,576]{2,1,0:T(8,128)(2,1)} %collective-permute-done.8.other, bf16[576,512]{1,0:T(8,128)(2,1)} %copy-done.13, ...), custom_call_target="tpu_custom_call" | custom-call | flops 1207959552 | bytes 5046272 | tf_op jit(solution)/shard_map/score/pallas_call | solution.py:116
  95.5 1.5 collective-permute-start.12
  97.1 0.8 copy-done.14
  97.9 3.2 %logits.1.part = f32[2,16,2048]{2,1,0:T(8,128)} custom-call(f32[16,4224]{1,0:T(8,128)} %dynamic-slice_add_fusion.total, bf16[2048,128]{1,0:T(8,128)(2,1)} %copy-done.8, bf16[2048,128]{1,0:T(8,128)(2,1)} %copy-done.14), custom_call_target="tpu_custom_call" | custom-call | flops 536870912 | bytes 1581056 | tf_op jit(solution)/shard_map/logits/pallas_call | solution.py:204
  102.2 5.5 %target.1.target_own = f32[16,2048]{1,0:T(8,128)} custom-call(bf16[16,128,512]{2,1,0:T(8,128)(2,1)} %get-tuple-element.21.refs_0_, bf16[16,128,512]{2,1,0:T(8,128)(2,1)} %get-tuple-element.24.refs_1_, bf16[16,128,512]{2,1,0:T(8,128)(2,1)} %get-tuple-element.27.refs_2_, bf16[16,128,512]{2,1,0:T(8,128)(2,1)} %get-tuple-element.30.refs_3_, ...), custom_call_target="tpu_custom_call" | custom-call | flops 8388608 | bytes 8388608 | tf_op jit(solution)/shard_map/target/pallas_call | solution.py:164
  107.7 1.6 collective-permute-start.13
  109.9 3.0 %collective-permute-done.13.target_other = f32[16,2048]{1,0:T(8,128)S(1)} collective-permute-done((f32[16,2048]{1,0:T(8,128)}, f32[16,2048]{1,0:T(8,128)S(1)}, u32[]{:S(2)}, u32[]{:S(2)}) %collective-permute-start.13) | collective-permute-done | bytes 131104 | tf_op jit(solution)/shard_map/ppermute | solution.py:398
  113.6 5.1 %gradient.1 = bf16[16,4224]{1,0:T(8,128)(2,1)} custom-call(s32[2,4]{1,0:T(2,128)} %pad_add_fusion.1.bases, s32[16,128]{1,0:T(8,128)} %broadcast_in_dim.15.positions, f32[16,4224]{1,0:T(8,128)} %dynamic-slice_add_fusion.total, bf16[2048,128]{1,0:T(8,128)(2,1)} %copy-done.8, bf16[2048,128]{1,0:T(8,128)(2,1)} %copy-done.14, f32[2,16,2048]{2,1,0:T(8,128)} %logits.1.part, ...), custom_call_target="tpu_custom_call" | custom-call | flops 1073741824 | bytes 2105344 | tf_op jit(solution)/shard_map/gradient/pallas_call | solution.py:298
  118.7 0.8 collective-permute-start.14
  119.5 2.2 %collective-permute-start.15 = (bf16[16,4224]{1,0:T(8,128)(2,1)}, bf16[16,4224]{1,0:T(8,128)(2,1)S(1)}, u32[]{:S(2)}, u32[]{:S(2)}) collective-permute-start(bf16[16,4224]{1,0:T(8,128)(2,1)} %gradient.1), channel_id=1, source_target_pairs={{0,2},{1,3},{2,0},{3,1},{4,6},{5,7},{6,4},{7,5},{8,10},{9,11},{10,... | collective-permute-start | bytes 405512 | tf_op jit(solution)/shard_map/ppermute | solution.py:466
  121.7 0.8 collective-permute-start.16
  122.5 3.3 %collective-permute-done.14 = bf16[16,4224]{1,0:T(8,128)(2,1)S(1)} collective-permute-done((bf16[16,4224]{1,0:T(8,128)(2,1)}, bf16[16,4224]{1,0:T(8,128)(2,1)S(1)}, u32[]{:S(2)}, u32[]{:S(2)}) %collective-permute-start.14) | collective-permute-done | bytes 135200 | tf_op jit(solution)/shard_map/ppermute | solution.py:466
  125.8 2.7 %collective-permute-done.15 = bf16[16,4224]{1,0:T(8,128)(2,1)S(1)} collective-permute-done((bf16[16,4224]{1,0:T(8,128)(2,1)}, bf16[16,4224]{1,0:T(8,128)(2,1)S(1)}, u32[]{:S(2)}, u32[]{:S(2)}) %collective-permute-start.15) | collective-permute-done | bytes 135200 | tf_op jit(solution)/shard_map/ppermute | solution.py:466
  128.5 1.0 pad_maximum_fusion.refs_0_.refs_4_
  129.5 1.6 collective-permute-start.17
  140.0 2.2 %slice.53.hiddens = bf16[256,1792]{1,0:T(8,128)(2,1)} slice(bf16[256,2176]{1,0:T(8,128)(2,1)} %all-gather.3.cloned.1.call-done), slice={[0:256], [384:2176]} | slice | bytes 1835008 | tf_op jit(solution)/shard_map/slice | solution.py:492
  142.2 1.6 slice.52.latents
  145.8 0.8 collective-permute-done.19.refs_3_.refs_7_
  146.6 0.8 copy-done.5
  147.4 8.3 %outer.1 = (f32[384,4096]{1,0:T(8,128)}, f32[32,1792]{1,0:T(8,128)}) custom-call(s32[4,4]{1,0:T(4,128)} %pad_add_fusion.place, bf16[256,384]{1,0:T(8,128)(2,1)} %slice.52.latents, bf16[256,1792]{1,0:T(8,128)(2,1)} %slice.53.hiddens, bf16[4,16,4224]{2,1,0:T(8,128)(2,1)} %copy-done.1, bf16[4,16,4224]{2,1,0:T(8,128)(2,1)} %copy-done.3, ...), custom_call_target="tpu_custom_call" | custom-call | flops 805306368 | bytes 8388608 | tf_op jit(solution)/shard_map/outer/pallas_call | solution.py:348
  (73 shorter events, 10.5 us)
Async XLA Ops:
  7.2 3.1 %copy-start = (bf16[1,1024,576]{1,2,0:T(8,128)(2,1)S(1)}, bf16[1,1024,576]{1,2,0:T(8,128)(2,1)}, u32[]{:S(2)}) copy-start(bf16[1,1024,576]{1,2,0:T(8,128)(2,1)} %param.13) | copy-start | bytes 3538948
  7.2 9.3 %copy-start.11 = (s32[4]{0:T(128)S(1)}, s32[4]{0:T(128)}, u32[]{:S(2)}) copy-start(s32[4]{0:T(128)} %constant.100.clone) | copy-start | bytes 52
  7.2 132.8 %all-gather.3.cloned.1.call-start = ((), (), s32[]{:S(2)}) async-start(), calls=%async_computation | async-start | bytes 1392640 | tf_op jit(solution)/shard_map/all_gather | solution.py:484
  7.2 65.3 %collective-permute-start.8 = (bf16[16,64,576]{2,1,0:T(8,128)(2,1)}, bf16[16,64,576]{2,1,0:T(8,128)(2,1)}, u32[]{:S(2)}, u32[]{:S(2)}) collective-permute-start(bf16[16,64,576]{2,1,0:T(8,128)(2,1)} %bitcast.56), channel_id=1, source_target_pairs={{0,4},{4,0},{1,5},{5,1},{2,6},{6,2},{3,7},{7,3},{8,12},{12,8},{9,1... | collective-permute-start | bytes 3538952 | tf_op jit(solution)/shard_map/ppermute | solution.py:398
  10.3 14.3 %copy-start.7 = (bf16[576,512]{1,0:T(8,128)(2,1)}, bf16[576,512]{1,0:T(8,128)(2,1)S(1)}, u32[]{:S(2)}) copy-start(bf16[576,512]{1,0:T(8,128)(2,1)S(1)} %dynamic-slice_bitcast_fusion.keys) | copy-start | bytes 1769476
  10.3 37.2 %collective-permute-start.9 = (bf16[576,512]{1,0:T(8,128)(2,1)S(1)}, bf16[576,512]{1,0:T(8,128)(2,1)}, u32[]{:S(2)}, u32[]{:S(2)}) collective-permute-start(bf16[576,512]{1,0:T(8,128)(2,1)S(1)} %dynamic-slice_bitcast_fusion.keys), channel_id=1, source_target_pairs={{0,1},{1,3},{3,2},{2,0},{4,5},{5,7},{7,6},{6,4},{8,9},{9,11},{11,1... | collective-permute-start | bytes 1769480 | tf_op jit(solution)/shard_map/ppermute | solution.py:395
  20.9 7.4 %copy-start.10 = (bf16[1,1024,128]{2,1,0:T(8,128)(2,1)S(1)}, bf16[1,1024,128]{2,1,0:T(8,128)(2,1)}, u32[]{:S(2)}) copy-start(bf16[1,1024,128]{2,1,0:T(8,128)(2,1)} %param.14) | copy-start | bytes 786436
  20.9 8.0 %copy-start.6 = (bf16[64,1792]{1,0:T(8,128)(2,1)S(1)}, bf16[64,1792]{1,0:T(8,128)(2,1)}, u32[]{:S(2)}) copy-start(bf16[64,1792]{1,0:T(8,128)(2,1)} %dynamic-slice_bitcast_fusion.1.hidden) | copy-start | bytes 688132
  20.9 8.0 %copy-start.9 = (bf16[64,384]{1,0:T(8,128)(2,1)S(1)}, bf16[64,384]{1,0:T(8,128)(2,1)}, u32[]{:S(2)}) copy-start(bf16[64,384]{1,0:T(8,128)(2,1)} %dynamic-slice_bitcast_fusion.3.latent) | copy-start | bytes 147460
  24.6 11.1 %copy-start.2 = (f32[64,4224]{1,0:T(8,128)S(1)}, f32[64,4224]{1,0:T(8,128)}, u32[]{:S(2)}) copy-start(f32[64,4224]{1,0:T(8,128)} %project.1) | copy-start | bytes 3244036
  24.6 13.1 %copy-start.12 = (s32[1,64]{1,0:T(1,128)S(1)}, s32[1,64]{1,0:T(1,128)}, u32[]{:S(2)}) copy-start(s32[1,64]{1,0:T(1,128)} %param.15) | copy-start | bytes 772
  25.7 10.0 %collective-permute-start = (f32[16,4224]{1,0:T(8,128)S(1)}, f32[16,4224]{1,0:T(8,128)S(1)}, u32[]{:S(2)}, u32[]{:S(2)}) collective-permute-start(f32[16,4224]{1,0:T(8,128)S(1)} %constant_dynamic-slice_fusion), channel_id=1, source_target_pairs={{0,1},{1,3},{3,2},{2,0},{4,5},{5,7},{7,6},{6,4},{8,9},{9,11},{11,1... | collective-permute-start | bytes 811016 | tf_op jit(solution)/shard_map/ppermute | solution.py:395
  28.4 11.1 %collective-permute-start.3 = (bf16[512,128]{1,0:T(8,128)(2,1)S(1)}, bf16[512,128]{1,0:T(8,128)(2,1)}, u32[]{:S(2)}, u32[]{:S(2)}) collective-permute-start(bf16[512,128]{1,0:T(8,128)(2,1)S(1)} %dynamic-slice_bitcast_fusion.2), channel_id=1, source_target_pairs={{0,1},{1,3},{3,2},{2,0},{4,5},{5,7},{7,6},{6,4},{8,9},{9,11},{11,1... | collective-permute-start | bytes 393224 | tf_op jit(solution)/shard_map/ppermute | solution.py:395
  35.7 13.1 %collective-permute-start.1 = (f32[16,4224]{1,0:T(8,128)S(1)}, f32[16,4224]{1,0:T(8,128)S(1)}, u32[]{:S(2)}, u32[]{:S(2)}) collective-permute-start(f32[16,4224]{1,0:T(8,128)S(1)} %dynamic-slice_add_fusion.2), channel_id=1, source_target_pairs={{0,1},{1,3},{3,2},{2,0},{4,5},{5,7},{7,6},{6,4},{8,9},{9,11},{11,1... | collective-permute-start | bytes 811016 | tf_op jit(solution)/shard_map/ppermute | solution.py:395
  39.5 6.3 %collective-permute-start.4 = (bf16[512,128]{1,0:T(8,128)(2,1)}, bf16[512,128]{1,0:T(8,128)(2,1)}, u32[]{:S(2)}, u32[]{:S(2)}) collective-permute-start(bf16[512,128]{1,0:T(8,128)(2,1)} %collective-permute-done.3), channel_id=1, source_target_pairs={{0,1},{1,3},{3,2},{2,0},{4,5},{5,7},{7,6},{6,4},{8,9},{9,11},{11,1... | collective-permute-start | bytes 393224 | tf_op jit(solution)/shard_map/ppermute | solution.py:395
  45.8 7.7 %collective-permute-start.5 = (bf16[512,128]{1,0:T(8,128)(2,1)}, bf16[512,128]{1,0:T(8,128)(2,1)}, u32[]{:S(2)}, u32[]{:S(2)}) collective-permute-start(bf16[512,128]{1,0:T(8,128)(2,1)} %collective-permute-done.4), channel_id=1, source_target_pairs={{0,1},{1,3},{3,2},{2,0},{4,5},{5,7},{7,6},{6,4},{8,9},{9,11},{11,1... | collective-permute-start | bytes 393224 | tf_op jit(solution)/shard_map/ppermute | solution.py:395
  47.5 18.6 %collective-permute-start.10 = (bf16[576,512]{1,0:T(8,128)(2,1)}, bf16[576,512]{1,0:T(8,128)(2,1)}, u32[]{:S(2)}, u32[]{:S(2)}) collective-permute-start(bf16[576,512]{1,0:T(8,128)(2,1)} %collective-permute-done.9.keys), channel_id=1, source_target_pairs={{0,1},{1,3},{3,2},{2,0},{4,5},{5,7},{7,6},{6,4},{8,9},{9,11},{11,1... | collective-permute-start | bytes 1769480 | tf_op jit(solution)/shard_map/ppermute | solution.py:395
  48.9 22.9 %collective-permute-start.2 = (f32[16,4224]{1,0:T(8,128)S(1)}, f32[16,4224]{1,0:T(8,128)S(1)}, u32[]{:S(2)}, u32[]{:S(2)}) collective-permute-start(f32[16,4224]{1,0:T(8,128)S(1)} %dynamic-slice_add_fusion.1), channel_id=1, source_target_pairs={{0,1},{1,3},{3,2},{2,0},{4,5},{5,7},{7,6},{6,4},{8,9},{9,11},{11,1... | collective-permute-start | bytes 811016 | tf_op jit(solution)/shard_map/ppermute | solution.py:395
  54.5 23.8 %copy-start.8 = (bf16[2048,128]{1,0:T(8,128)(2,1)}, bf16[2048,128]{1,0:T(8,128)(2,1)S(1)}, u32[]{:S(2)}) copy-start(bf16[2048,128]{1,0:T(8,128)(2,1)S(1)} %pad_maximum_fusion.1.own) | copy-start | bytes 1572868
  54.6 42.5 %collective-permute-start.6 = (bf16[2048,128]{1,0:T(8,128)(2,1)S(1)}, bf16[2048,128]{1,0:T(8,128)(2,1)S(1)}, u32[]{:S(2)}, u32[]{:S(2)}) collective-permute-start(bf16[2048,128]{1,0:T(8,128)(2,1)S(1)} %pad_maximum_fusion.1.own), channel_id=1, source_target_pairs={{0,4},{4,0},{1,5},{5,1},{2,6},{6,2},{3,7},{7,3},{8,12},{12,8},{9,1... | collective-permute-start | bytes 1572872 | tf_op jit(solution)/shard_map/ppermute | solution.py:398
  66.1 22.7 %collective-permute-start.11 = (bf16[576,512]{1,0:T(8,128)(2,1)}, bf16[576,512]{1,0:T(8,128)(2,1)S(1)}, u32[]{:S(2)}, u32[]{:S(2)}) collective-permute-start(bf16[576,512]{1,0:T(8,128)(2,1)} %collective-permute-done.10.keys), channel_id=1, source_target_pairs={{0,1},{1,3},{3,2},{2,0},{4,5},{5,7},{7,6},{6,4},{8,9},{9,11},{11,1... | collective-permute-start | bytes 1769480 | tf_op jit(solution)/shard_map/ppermute | solution.py:395
  88.8 0.8 copy-start.13
  95.5 6.1 %collective-permute-start.12 = (f32[2,16,128]{2,1,0:T(8,128)S(1)}, f32[2,16,128]{2,1,0:T(8,128)S(1)}, u32[]{:S(2)}, u32[]{:S(2)}) collective-permute-start(f32[2,16,128]{2,1,0:T(8,128)S(1)} %pad_maximum_fusion.3), channel_id=1, source_target_pairs={{0,4},{4,0},{1,5},{5,1},{2,6},{6,2},{3,7},{7,3},{8,12},{12,8},{9,1... | collective-permute-start | bytes 49160 | tf_op jit(solution)/shard_map/ppermute | solution.py:398
  97.1 0.8 copy-start.14
  101.1 8.8 %collective-permute-start.7 = (f32[2,16,2048]{2,1,0:T(8,128)}, f32[2,16,2048]{2,1,0:T(8,128)S(1)}, u32[]{:S(2)}, u32[]{:S(2)}) collective-permute-start(f32[2,16,2048]{2,1,0:T(8,128)} %logits.1.part), channel_id=1, source_target_pairs={{0,4},{4,0},{1,5},{5,1},{2,6},{6,2},{3,7},{7,3},{8,12},{12,8},{9,1... | collective-permute-start | bytes 786440 | tf_op jit(solution)/shard_map/ppermute | solution.py:398
  107.7 5.2 %collective-permute-start.13 = (f32[16,2048]{1,0:T(8,128)}, f32[16,2048]{1,0:T(8,128)S(1)}, u32[]{:S(2)}, u32[]{:S(2)}) collective-permute-start(f32[16,2048]{1,0:T(8,128)} %target.1.target_own), channel_id=1, source_target_pairs={{0,4},{4,0},{1,5},{5,1},{2,6},{6,2},{3,7},{7,3},{8,12},{12,8},{9,1... | collective-permute-start | bytes 393224 | tf_op jit(solution)/shard_map/ppermute | solution.py:398
  109.9 3.7 %copy-start.15 = (f32[2,16,2048]{2,1,0:T(8,128)}, f32[2,16,2048]{2,1,0:T(8,128)S(1)}, u32[]{:S(2)}) copy-start(f32[2,16,2048]{2,1,0:T(8,128)S(1)} %collective-permute-done.7.far) | copy-start | bytes 786436
  112.9 0.7 copy-start.16
  118.7 7.1 %collective-permute-start.14 = (bf16[16,4224]{1,0:T(8,128)(2,1)}, bf16[16,4224]{1,0:T(8,128)(2,1)S(1)}, u32[]{:S(2)}, u32[]{:S(2)}) collective-permute-start(bf16[16,4224]{1,0:T(8,128)(2,1)} %gradient.1), channel_id=1, source_target_pairs={{0,1},{1,2},{2,3},{3,0},{4,5},{5,6},{6,7},{7,4},{8,9},{9,10},{10,1... | collective-permute-start | bytes 405512 | tf_op jit(solution)/shard_map/ppermute | solution.py:466
  119.5 9.0 %collective-permute-start.15 = (bf16[16,4224]{1,0:T(8,128)(2,1)}, bf16[16,4224]{1,0:T(8,128)(2,1)S(1)}, u32[]{:S(2)}, u32[]{:S(2)}) collective-permute-start(bf16[16,4224]{1,0:T(8,128)(2,1)} %gradient.1), channel_id=1, source_target_pairs={{0,2},{1,3},{2,0},{3,1},{4,6},{5,7},{6,4},{7,5},{8,10},{9,11},{10,... | collective-permute-start | bytes 405512 | tf_op jit(solution)/shard_map/ppermute | solution.py:466
  121.7 6.8 %collective-permute-start.16 = (bf16[16,4224]{1,0:T(8,128)(2,1)}, bf16[16,4224]{1,0:T(8,128)(2,1)S(1)}, u32[]{:S(2)}, u32[]{:S(2)}) collective-permute-start(bf16[16,4224]{1,0:T(8,128)(2,1)} %gradient.1), channel_id=1, source_target_pairs={{0,3},{1,0},{2,1},{3,2},{4,7},{5,4},{6,5},{7,6},{8,11},{9,8},{10,9... | collective-permute-start | bytes 405512 | tf_op jit(solution)/shard_map/ppermute | solution.py:466
  129.5 17.0 %copy-start.1 = (bf16[4,16,4224]{2,1,0:T(8,128)(2,1)}, bf16[4,16,4224]{2,1,0:T(8,128)(2,1)S(1)}, u32[]{:S(2)}) copy-start(bf16[4,16,4224]{2,1,0:T(8,128)(2,1)S(1)} %pad_maximum_fusion.refs_0_.refs_4_) | copy-start | bytes 1622020
  129.5 14.3 %collective-permute-start.17 = (bf16[4,16,4224]{2,1,0:T(8,128)(2,1)S(1)}, bf16[4,16,4224]{2,1,0:T(8,128)(2,1)S(1)}, u32[]{:S(2)}, u32[]{:S(2)}) collective-permute-start(bf16[4,16,4224]{2,1,0:T(8,128)(2,1)S(1)} %pad_maximum_fusion.refs_0_.refs_4_), channel_id=1, source_target_pairs={{0,16},{8,24},{16,0},{24,8},{1,17},{9,25},{17,1},{25,9},{2,18},{10... | collective-permute-start | bytes 1622024 | tf_op jit(solution)/shard_map/ppermute | solution.py:470
  143.8 1.9 %collective-permute-start.18 = (bf16[4,16,4224]{2,1,0:T(8,128)(2,1)S(1)}, bf16[4,16,4224]{2,1,0:T(8,128)(2,1)S(1)}, u32[]{:S(2)}, u32[]{:S(2)}) collective-permute-start(bf16[4,16,4224]{2,1,0:T(8,128)(2,1)S(1)} %pad_maximum_fusion.refs_0_.refs_4_), channel_id=1, source_target_pairs={{0,8},{8,0},{16,24},{24,16},{1,9},{9,1},{17,25},{25,17},{2,10},{10... | collective-permute-start | bytes 1622024 | tf_op jit(solution)/shard_map/ppermute | solution.py:470
  143.8 2.7 %copy-start.3 = (bf16[4,16,4224]{2,1,0:T(8,128)(2,1)}, bf16[4,16,4224]{2,1,0:T(8,128)(2,1)S(1)}, u32[]{:S(2)}) copy-start(bf16[4,16,4224]{2,1,0:T(8,128)(2,1)S(1)} %collective-permute-done.17.refs_1_.refs_5_) | copy-start | bytes 1622020
  143.8 2.7 %collective-permute-start.19 = (bf16[4,16,4224]{2,1,0:T(8,128)(2,1)S(1)}, bf16[4,16,4224]{2,1,0:T(8,128)(2,1)S(1)}, u32[]{:S(2)}, u32[]{:S(2)}) collective-permute-start(bf16[4,16,4224]{2,1,0:T(8,128)(2,1)S(1)} %collective-permute-done.17.refs_1_.refs_5_), channel_id=1, source_target_pairs={{0,8},{8,0},{16,24},{24,16},{1,9},{9,1},{17,25},{25,17},{2,10},{10... | collective-permute-start | bytes 1622024 | tf_op jit(solution)/shard_map/ppermute | solution.py:470
  145.8 0.8 copy-start.4
  146.6 0.8 copy-start.5
Sparse Core Ops, SparseCore 0:
  29.8 16.8 all-gather.2

commit v3 on v2

--- a/solution.py
+++ b/solution.py
@@ -3,6 +3,7 @@
 
 import jax
 import jax.numpy as jnp
+import numpy as np
 from jax import lax
 from jax.experimental import pallas as pl
 from jax.experimental.pallas import tpu as pltpu
@@ -18,7 +19,7 @@
 lanes = 128
 f32 = jnp.float32
 bf16 = jnp.bfloat16
-vmem_limit = 56 * 2**20
+vmem_limit = 24 * 2**20
 
 
 def folded_ring(size):
@@ -41,33 +42,101 @@
     return lax.dot_general(a, b, (((axis_a,), (axis_b,)), ((), ())), preferred_element_type=f32)
 
 
-def project_kernel(latent, weight, hidden, hidden_weight, out):
+def device_table(n, heads, dp_size, rows):
+    ring = folded_ring(n)
+    half = rows // heads
+    flips = dp_flips(dp_size)
+    table = []
+    for z in range(n):
+        place = ring.index(z)
+        behind = [ring[(place - t) % n] for t in range(n)]
+        for y in range(heads):
+            for dp in range(dp_size):
+                row = [z] + [ring[(place - 1 - t) % n] for t in range(n)]
+                row += [k * rows + y * half for k in behind]
+                row += [k * rows + (1 - y) * half for k in behind]
+                row += [(dp ^ k) * n + (z - t) % n for k in flips for t in range(n)]
+                row += [flips.index(dp ^ b) for b in range(dp_size)]
+                table.append(row)
+    return np.array(table, np.int32)
+
+
+def dp_flips(dp_size):
+    flips, bit = [0], dp_size // 2
+    while bit:
+        flips, bit = flips + [k ^ bit for k in flips], bit // 2
+    return flips
+
+
+def project_kernel(aligned, info, latent, weight, hidden, hidden_weight, *outs):
+    *parts, kept = outs
     width = weight.shape[1]
     heads = hidden_weight.shape[0]
+    count = parts[0].shape[0]
+    if aligned:
+        starts = [pl.multiple_of(info[1 + k] * count, count) for k in range(len(parts))]
+        rows = jnp.concatenate([latent[pl.ds(k, count), :] for k in starts], axis=0)
+        mixed_rows = jnp.concatenate([hidden[pl.ds(k, count), :] for k in starts], axis=0)
+    else:
+        rows, mixed_rows = latent[...], hidden[...]
     for at in range(0, width, 512):
-        out[:, at : at + 512] = times(latent[...], weight[:, at : at + 512], 1, 0)
-    mixed = times(hidden[...], hidden_weight[...], 1, 1)
-    out[:, width : width + heads] = mixed
-    out[:, width + heads :] = jnp.zeros((out.shape[0], lanes - heads), f32)
-
-
-def project(latent, weight, hidden, hidden_weight):
-    count, width = latent.shape[0], weight.shape[1]
-    return pl.pallas_call(
-        project_kernel,
-        out_shape=jax.ShapeDtypeStruct((count, width + lanes), f32),
-        in_specs=[in_vmem()] * 4,
-        out_specs=in_vmem(),
+        product = times(rows, weight[:, at : at + 512], 1, 0)
+        for k, out in enumerate(parts):
+            out[:, at : at + 512] = product[k * count : (k + 1) * count]
+    mixed = times(mixed_rows, hidden_weight[...], 1, 1)
+    for k, out in enumerate(parts):
+        out[:, width : width + heads] = mixed[k * count : (k + 1) * count]
+        out[:, width + heads :] = jnp.zeros((count, lanes - heads), f32)
+    kept[:, : latent.shape[1]] = latent[...]
+    kept[:, latent.shape[1] :] = hidden[...]
+
+
+def project(info, count, latent, weight, hidden, hidden_weight):
+    queries, width = latent.shape[0], weight.shape[1]
+    depth, hidden_depth = weight.shape[0], hidden_weight.shape[1]
+    blocks = queries // count
+    aligned = count % 16 == 0 and depth % lanes == 0 and hidden_depth % lanes == 0
+    columns = lambda i, info: (0, info[0])
+    whole = lambda i, info: (0, 0)
+    kept = None
+    if not aligned:
+        latent = lax.dynamic_slice_in_dim(latent, info[0] * depth, depth, 1)
+        hidden = lax.dynamic_slice_in_dim(hidden, info[0] * hidden_depth, hidden_depth, 1)
+        kept = jnp.concatenate([latent, hidden], axis=1)
+        order = info[1 : 1 + blocks]
+        latent = latent.reshape(blocks, count, depth)[order].reshape(queries, depth)
+        hidden = hidden.reshape(blocks, count, hidden_depth)[order].reshape(queries, hidden_depth)
+        columns = whole
+    *parts, kept_here = pl.pallas_call(
+        functools.partial(project_kernel, aligned),
+        grid_spec=pltpu.PrefetchScalarGridSpec(
+            num_scalar_prefetch=1,
+            grid=(1,),
+            in_specs=[
+                pl.BlockSpec((queries, depth), columns),
+                pl.BlockSpec((depth, width), whole),
+                pl.BlockSpec((queries, hidden_depth), columns),
+                pl.BlockSpec(hidden_weight.shape, whole),
+            ],
+            out_specs=[pl.BlockSpec((count, width + lanes), whole)] * blocks
+            + [pl.BlockSpec((queries, depth + hidden_depth), whole)],
+        ),
+        out_shape=[jax.ShapeDtypeStruct((count, width + lanes), f32)] * blocks
+        + [jax.ShapeDtypeStruct((queries, depth + hidden_depth), bf16)],
         compiler_params=params(),
         cost_estimate=pl.CostEstimate(
-            flops=2 * count * weight.size, bytes_accessed=2 * weight.size, transcendentals=0
+            flops=2 * queries * weight.size, bytes_accessed=2 * weight.size, transcendentals=0
         ),
         name="project",
-    )(latent, weight, hidden, hidden_weight)
-
-
-def score_kernel(first, limits, mine, other, keys, top_before, mass_before, weights, top, top_all, mass_all, mass):
+    )(info, latent, weight, hidden, hidden_weight)
+    return parts, kept_here if aligned else kept
+
+
+def score_kernel(
+    t, base_at, info, positions, mine, other, keys, top_before, mass_before, weights, top, top_all, mass_all, mass
+):
     count, heads, depth = mine.shape
+    limits = [positions[info[0] * count + q] - info[base_at] for q in range(count)]
     span = keys.shape[1]
     key_at = lax.broadcasted_iota(jnp.int32, (1, span), 1)
     row_at = lax.broadcasted_iota(jnp.int32, (heads, lanes), 0)
@@ -94,7 +163,7 @@
                 else:
                     top[q : q + 1, :] += high_row
                     mass[q : q + 1, :] += total_row
-    if first:
+    if t == 0:
         top_all[...] = top[...]
         mass_all[...] = mass[...]
     else:
@@ -106,17 +175,16 @@
         ] * jnp.exp2((now - joint) * exponent_scale)
 
 
-def score(limits, mine, other, keys, before):
+def score(t, n, info, positions, mine, other, keys, before):
     count, heads, depth = mine.shape
     span = keys.shape[1]
     stats = jax.ShapeDtypeStruct((count, lanes), f32)
-    first = before is None
-    if first:
+    if before is None:
         before = (jnp.zeros((count, lanes), f32),) * 2
     return pl.pallas_call(
-        functools.partial(score_kernel, first),
+        functools.partial(score_kernel, t, 1 + n + t),
         out_shape=(jax.ShapeDtypeStruct((count, 2 * heads, span), bf16), stats, stats, stats),
-        in_specs=[in_smem()] + [in_vmem()] * 5,
+        in_specs=[in_smem()] * 2 + [in_vmem()] * 5,
         out_specs=(in_vmem(),) * 4,
         scratch_shapes=[pltpu.VMEM((count, lanes), f32)],
         compiler_params=params(),
@@ -126,7 +194,7 @@
             transcendentals=2 * count * heads * span,
         ),
         name="score",
-    )(limits, mine, other, keys, *before)
+    )(info, positions, mine, other, keys, *before)
 
 
 def target_kernel(blocks, *refs):
@@ -184,8 +252,9 @@
     )
 
 
-def logits_kernel(heads, total, own, other, out):
-    count = total.shape[0]
+def logits_kernel(heads, received, here, own, other, out):
+    count = received.shape[0]
+    total = received[...] + here[...]
     query = query_rows(total, heads)
     columns = [total[:, heads * DI + j : heads * DI + j + 1] for j in range(heads)]
     span = 512
@@ -199,35 +268,40 @@
             out[part, :, at : at + span] = running * index_scale
 
 
-def make_logits(heads, total, own, other):
-    count, length = total.shape[0], own.shape[0]
+def make_logits(heads, received, here, own, other):
+    count, length = received.shape[0], own.shape[0]
     return pl.pallas_call(
         functools.partial(logits_kernel, heads),
         out_shape=jax.ShapeDtypeStruct((2, count, length), f32),
-        in_specs=[in_vmem()] * 3,
+        in_specs=[in_vmem()] * 4,
         out_specs=in_vmem(),
         compiler_params=params(),
         cost_estimate=pl.CostEstimate(
             flops=4 * count * heads * DI * length,
-            bytes_accessed=4 * (total.size + 2 * count * length) + 4 * length * DI,
+            bytes_accessed=4 * (2 * received.size + 2 * count * length) + 4 * length * DI,
             transcendentals=0,
         ),
         name="logits",
-    )(total, own, other)
+    )(received, here, own, other)
 
 
 def gradient_kernel(
-    heads, blocks, bases, positions, total, own, other, part, far, target_own, target_other, out, logit, flow
+    heads, blocks, info, positions, received, here, own, other, part, far, target_own, target_other, out, logit, flow
 ):
-    count = total.shape[0]
+    count = received.shape[0]
+    total = received[...] + here[...]
     span = own.shape[0] // blocks
     query = query_rows(total, heads)
-    position = positions[:, 0:1]
+    row_at = lax.broadcasted_iota(jnp.int32, (count, lanes), 0)
+    position = jnp.zeros((count, lanes), jnp.int32)
+    for q in range(count):
+        position = jnp.where(row_at == q, positions[info[0] * count + q], position)
+    position = position[:, 0:1]
     key_at = lax.broadcasted_iota(jnp.int32, (count, span), 1)
     sides = ((own, target_own), (other, target_other))
 
     def seen(side, t):
-        return key_at + bases[side, t] <= position
+        return key_at + info[1 + (1 + side) * blocks + t] <= position
 
     highs = []
     for side in range(2):
@@ -293,12 +367,12 @@
     out[:, heads * DI :] = tail.astype(bf16)
 
 
-def gradients(heads, blocks, bases, positions, total, own, other, part, far, target_own, target_other):
-    count, length = total.shape[0], own.shape[0]
+def gradients(heads, blocks, info, positions, received, here, own, other, part, far, target_own, target_other):
+    count, length = received.shape[0], own.shape[0]
     return pl.pallas_call(
         functools.partial(gradient_kernel, heads, blocks),
         out_shape=jax.ShapeDtypeStruct((count, heads * DI + lanes), bf16),
-        in_specs=[in_smem()] + [in_vmem()] * 8,
+        in_specs=[in_smem()] * 2 + [in_vmem()] * 8,
         out_specs=in_vmem(),
         scratch_shapes=[
             pltpu.VMEM((2, count, length), f32),
@@ -307,46 +381,46 @@
         compiler_params=params(),
         cost_estimate=pl.CostEstimate(
             flops=8 * count * heads * DI * length,
-            bytes_accessed=4 * (total.size + 6 * count * length) + 4 * length * DI,
+            bytes_accessed=4 * (2 * received.size + 6 * count * length) + 4 * length * DI,
             transcendentals=4 * count * length,
         ),
         name="gradient",
-    )(bases, positions, total, own, other, part, far, target_own, target_other)
-
-
-def outer_kernel(parts, blocks, place, latents, hiddens, *refs):
+    )(info, positions, received, here, own, other, part, far, target_own, target_other)
+
+
+def outer_kernel(parts, blocks, at, info, latents, hiddens, *refs):
     bodies, tails = refs[:parts], refs[parts : 2 * parts]
     grad, grad_mixed, rows, tail_rows = refs[2 * parts :]
     count = bodies[0].shape[1]
     for k in range(parts):
         for t in range(blocks):
-            to = pl.ds(pl.multiple_of(place[k, t] * count, count), count)
+            to = pl.ds(pl.multiple_of(info[at + k * blocks + t] * count, count), count)
             rows[to, :] = bodies[k][t]
 
-    grad[...] = times(latents[...], rows[...], 0, 0)
+    grad[...] = times(latents[...], rows[...], 1, 0)
 
     @pl.when(pl.program_id(0) == 0)
     def _():
         for k in range(parts):
             for t in range(blocks):
-                to = pl.ds(pl.multiple_of(place[k, t] * count, count), count)
+                to = pl.ds(pl.multiple_of(info[at + k * blocks + t] * count, count), count)
                 tail_rows[to, :] = tails[k][t]
         mixed = times(tail_rows[...], hiddens[...], 0, 0)
         grad_mixed[...] = mixed[: grad_mixed.shape[0]]
 
 
-def outer(heads, place, latents, hiddens, parts):
+def outer(heads, at, info, latents, hiddens, parts):
     blocks, count, _ = parts[0].shape
-    total = latents.shape[0]
+    row_count, total = latents.shape
     width = heads * DI
     span = 512
-    row_count, hidden_count = latents.shape[1], hiddens.shape[1]
+    hidden_count = hiddens.shape[1]
     body = [pl.BlockSpec((blocks, count, span), lambda i: (0, 0, i)) for _ in parts]
     tail = [
         pl.BlockSpec((blocks, count, lanes), lambda i: (0, 0, width // lanes)) for _ in parts
     ]
     return pl.pallas_call(
-        functools.partial(outer_kernel, len(parts), blocks),
+        functools.partial(outer_kernel, len(parts), blocks, at),
         grid=(width // span,),
         out_shape=(
             jax.ShapeDtypeStruct((row_count, width), f32),
@@ -354,7 +428,7 @@
         ),
         in_specs=[
             in_smem(),
-            pl.BlockSpec((total, row_count), lambda i: (0, 0)),
+            pl.BlockSpec((row_count, total), lambda i: (0, 0)),
             pl.BlockSpec((total, hidden_count), lambda i: (0, 0)),
         ]
         + body
@@ -371,7 +445,7 @@
             transcendentals=0,
         ),
         name="outer",
-    )(place, latents, hiddens, *parts, *parts)
+    )(info, latents, hiddens, *parts, *parts)
 
 
 def per_device(
@@ -379,79 +453,90 @@
 ):
     n = lax.axis_size("ctx")
     z = lax.axis_index("ctx")
+    head_size = lax.axis_size("head")
     y = lax.axis_index("head")
     dp_size = lax.axis_size("dp")
     dp = lax.axis_index("dp")
     ring = folded_ring(n)
-    place_of = [ring.index(k) for k in range(n)]
-    ring_table = jnp.array(ring, jnp.int32)
-    place = jnp.array(place_of, jnp.int32)[z]
-    ring_pairs = [(ring[k], ring[(k + 1) % n]) for k in range(n)]
-
-    def at_place(k):
-        return ring_table[lax.rem(k + 2 * n, n)]
-
-    def onward(x):
-        return lax.ppermute(x, "ctx", ring_pairs)
-
-    def swap_head(x):
-        return lax.ppermute(x, "head", [(0, 1), (1, 0)])
-
     rows = main_keys.shape[1]
-    half = rows // 2
+    half = rows // head_size
     rows_latent = w_query.shape[0]
-    rows_hidden = w_weights.shape[0]
     heads_here = w_weights.shape[1]
     width = heads_here * DI
     queries_here = main_queries.shape[1]
-    query_pos = lax.dynamic_slice_in_dim(positions[0], z * queries_here, queries_here)
-    own_latent = lax.dynamic_slice_in_dim(q_latent[0], z * rows_latent, rows_latent, 1)
-    own_hidden = lax.dynamic_slice_in_dim(hidden[0], z * rows_hidden, rows_hidden, 1)
-
+    sequence_positions = positions[0]
+
+    def onward(x, t=1):
+        return lax.ppermute(x, "ctx", [(ring[k], ring[(k + t) % n]) for k in range(n)])
+
+    def swap_head(x):
+        return lax.ppermute(x, "head", [(0, 1), (1, 0)])
+
+    def swap_dp(x, bit):
+        return lax.ppermute(x, "dp", [(k, k ^ bit) for k in range(dp_size)])
+
+    def over_dp(x):
+        gathered, bit = [x], dp_size // 2
+        while bit:
+            gathered, bit = gathered + [swap_dp(one, bit) for one in gathered], bit // 2
+        return gathered
+
+    table = jnp.array(device_table(n, head_size, dp_size, rows))
+    info = lax.dynamic_index_in_dim(table, (z * head_size + y) * dp_size + dp, 0, False)
+
+    keys_mine = [lax.dynamic_slice_in_dim(main_keys[0].T, y * half, half, 1)]
+    keys_mine.append(onward(keys_mine[0]))
     queries = main_queries[0]
     other_queries = swap_head(queries)
-    key_part = lax.dynamic_slice_in_dim(main_keys[0].T, y * half, half, 1)
-    keys_mine = [key_part]
-    for _ in range(n - 1):
-        keys_mine.append(onward(keys_mine[-1]))
-    index_mine = [lax.dynamic_slice_in_dim(index_keys[0], y * half, half)]
-    for _ in range(n - 1):
-        index_mine.append(onward(index_mine[-1]))
-    index_own = jnp.concatenate(index_mine)
+    index_part = lax.dynamic_slice_in_dim(index_keys[0], y * half, half)
+    index_own = jnp.concatenate([index_part] + [onward(index_part, t) for t in range(1, n)])
     index_other = swap_head(index_own)
-    sources = jnp.stack([at_place(place - t) for t in range(n)]) * rows
-    base_own = sources + y * half
-    bases = jnp.stack([base_own, sources + (1 - y) * half])
-
-    partial = project(own_latent, w_query, own_hidden, w_weights.T)
-
-    def partial_of(k):
-        return lax.dynamic_slice_in_dim(partial, at_place(k) * queries_here, queries_here)
-
-    total = partial_of(place - 1)
-    for t in range(1, n):
-        total = onward(total) + partial_of(place - t - 1)
-
-    part = make_logits(heads_here, total, index_own, index_other)
-    far = swap_head(part)
-
+    parts, kept = project(
+        info, queries_here, q_latent[0], w_query, hidden[0], w_weights.T
+    )
+    received = onward(parts[0])
     weights, tops, before = [], [], None
-    for t in range(n):
-        limits = query_pos - base_own[t]
-        numer, top, *before = score(limits, queries, other_queries, keys_mine[t], before)
+
+    def score_next(keys):
+        nonlocal before
+        t = len(weights)
+        numer, top, *before = score(
+            t, n, info, sequence_positions, queries, other_queries, keys, before
+        )
         weights.append(numer)
         tops.append(top)
+
+    for t in range(1, n - 1):
+        summed = received + parts[t]
+        if t == 2:
+            score_next(keys_mine[0])
+            keys, summed, before = lax.optimization_barrier((keys_mine[t], summed, before))
+        else:
+            keys, summed = lax.optimization_barrier((keys_mine[t], summed))
+        keys_mine[t] = keys
+        keys_mine.append(onward(keys))
+        received = onward(summed)
+    while len(weights) < n - 1:
+        score_next(keys_mine[len(weights)])
+
+    part = make_logits(heads_here, received, parts[n - 1], index_own, index_other)
+    far = swap_head(part)
+    latents = jnp.stack(over_dp(kept))
+    from_dp = info[1 + 3 * n + n * dp_size :]
+    latents = jnp.concatenate([latents[from_dp[b]] for b in range(dp_size)])
+    latents, hiddens = latents[:, :rows_latent].T, latents[:, rows_latent:]
+
+    score_next(keys_mine[n - 1])
     far_top, far_mass = swap_head(jnp.stack(before))
     target_own = make_target(weights, tops, *before, far_top, far_mass)
     target_other = swap_head(target_own)
-
-    position_rows = jnp.broadcast_to(query_pos[:, None], (queries_here, lanes))
     piece = gradients(
         heads_here,
         n,
-        bases,
-        position_rows,
-        total,
+        info,
+        sequence_positions,
+        received,
+        parts[n - 1],
         index_own,
         index_other,
         part,
@@ -465,34 +550,22 @@
         pairs = [(k, (k + t) % n) for k in range(n)]
         pieces.append(lax.ppermute(piece, "ctx", pairs))
     sequence = jnp.stack(pieces)
-
-    def swap_dp(x, bit):
-        return lax.ppermute(x, "dp", [(k, k ^ bit) for k in range(dp_size)])
-
-    gathered = [sequence]
-    bit = dp_size // 2
-    while bit:
-        gathered = gathered + [swap_dp(x, bit) for x in gathered]
-        bit //= 2
-    flips = [0]
-    bit = dp_size // 2
-    while bit:
-        flips = flips + [k ^ bit for k in flips]
-        bit //= 2
-    steps = lax.rem(z - jnp.arange(n, dtype=jnp.int32) + n, n)
-    where_from = jnp.stack([(dp ^ k) * n + steps for k in flips])
-    both = lax.all_gather(jnp.concatenate([own_latent, own_hidden], axis=1), "dp")
-    both = both.reshape(-1, rows_latent + rows_hidden)
+    gathered = over_dp(sequence)
+    order_at = 1 + 3 * n
     if queries_here % 16:
         flat = jnp.concatenate(gathered)
-        order = jnp.argsort(where_from.reshape(-1))
+        order = jnp.argsort(info[order_at : order_at + n * dp_size])
+        outer_info = jnp.zeros((1,), jnp.int32)
         gathered = [flat[order].reshape(1, -1, flat.shape[2])]
-        where_from = jnp.zeros((1, 1), jnp.int32)
+        order_at = 0
+    else:
+        outer_info = info
     grad_query, grad_weights = outer(
-        heads_here, where_from, both[:, :rows_latent], both[:, rows_latent:], gathered
+        heads_here, order_at, outer_info, latents, hiddens, gathered
     )
     low = sequence[:, :, width + heads_here : width + heads_here + 2].astype(f32)
     low = low[:, :, 0] + low[:, :, 1]
+    steps = lax.rem(z - jnp.arange(n, dtype=jnp.int32) + n, n)
     losses = jnp.concatenate([low[steps[k]] for k in range(n)])
     return (grad_query, grad_weights.T, losses[None, :])
 

time: 164 us -> 142 us (0.87)
  waiting for transfers between devices: 31.4 us -> 52.8 us
  Pallas kernels: 46.7 us -> 29.1 us
  other arithmetic: 15 us -> 3.25 us
  between operations: 27.7 us -> 16.2 us
  local copies, waits for them, and re-layouts: 15.6 us -> 6.89 us
  starting transfers between devices: 26 us -> 31.8 us
    ppermute x9, waiting for transfers between devices: 21.1 us -> 34.4 us  [onward(): lax.ppermute(x, 'ctx', [(ring[k], ring[(k + t) % n]) for k in range(n)])]
    ppermute x3 -> x6, waiting for transfers between devices: 1.29 us -> 12.7 us  [swap_dp(): return lax.ppermute(x, 'dp', [(k, k ^ bit) for k in range(dp_size)])]
    pallas_call x6, Pallas kernels: 32.9 us -> 21.5 us  [the longest x4 13.8 us: score(): pl.pallas_call(functools.partial(score_kernel, t, 1 + n + t), out_shape=(...]
    add x8 -> x2, other arithmetic: 5.98 us -> 0.06 us  [per_device(): summed = received + parts[t]]
    dynamic_slice x7 -> x3, local copies, waits for them, and re-layouts: 6.1 us -> 0.74 us  [the longest x1 0.69 us: per_device(): lax.dynamic_index_in_dim(table, (z * head_size + y) * dp_size + dp, 0, Fa...]
    slice x3 -> x1, local copies, waits for them, and re-layouts: 4.44 us -> 0.66 us  [per_device(): latents = jnp.concatenate([latents[from_dp[b]] for b in range(dp_size)])]
    sub x2 -> x0, other arithmetic: 3.59 us -> none  [per_device(): limits = query_pos - base_own[t]]
    pallas_call x1, Pallas kernels: 5.45 us -> 2.36 us  [make_target(): pl.pallas_call(functools.partial(target_kernel, blocks), grid=(count // g...]
  transfers between devices with their start and end apart: 21 -> 23, of which waited for: 10 -> 8; matrix products, arithmetic and copies ran while one was open for 17% -> 4% of each run, Pallas kernels for 24% -> 16%
where the time goes in v3:
time: 142 us; the launch traced here: 140 us
  waiting for transfers between devices  52.8 us (37%)
  starting transfers between devices  31.8 us (22%)
  Pallas kernels  29.1 us (20%)
  between operations  16.2 us (11%)
  local copies, waits for them, and re-layouts  6.89 us (5%)
  other arithmetic  3.25 us (2%)
    ppermute x9, waiting for transfers between devices, onward(): lax.ppermute(x, 'ctx', [(ring[k], ring[(k + t) % n]) for k in range(n)])  34.4 us
    ppermute x9, starting transfers between devices, onward(): lax.ppermute(x, 'ctx', [(ring[k], ring[(k + t) % n]) for k in range(n)])  14.6 us
    pallas_call x4, Pallas kernels, score(): pl.pallas_call(functools.partial(score_kernel, t, 1 + n + t), out_shape=(...  13.8 us
    ppermute x6, waiting for transfers between devices, swap_dp(): return lax.ppermute(x, 'dp', [(k, k ^ bit) for k in range(dp_size)])  12.7 us
    ppermute x5, starting transfers between devices, swap_head(): return lax.ppermute(x, 'head', [(0, 1), (1, 0)])  8.25 us
    pallas_call x1, Pallas kernels, outer(): pl.pallas_call(functools.partial(outer_kernel, len(parts), blocks, at), g...  6.43 us
    ppermute x3, starting transfers between devices, per_device(): pieces.append(lax.ppermute(piece, 'ctx', pairs))  5.82 us
    ppermute x3, waiting for transfers between devices, per_device(): pieces.append(lax.ppermute(piece, 'ctx', pairs))  5.42 us
  transfers between devices with their start and end apart: 23, of which 8 were waited for; matrix products, arithmetic and copies ran while one was open for 4% of the time, Pallas kernels for 16%

profile of v3, /device:TPU:0, one launch (start us, length us, event | category | flops | bytes accessed | tf_op | source)
XLA Modules:
  0.0 140.0 jit_solution(13309394367418868243)
XLA Ops:
  0.7 3.0 %collective-permute-start.7 = (bf16[16,64,576]{2,1,0:T(8,128)(2,1)}, bf16[16,64,576]{2,1,0:T(8,128)(2,1)}, u32[]{:S(2)}, u32[]{:S(2)}) collective-permute-start(bf16[16,64,576]{2,1,0:T(8,128)(2,1)} %bitcast.55), channel_id=1, source_target_pairs={{0,4},{4,0},{1,5},{5,1},{2,6},{6,2},{3,7},{7,3},{8,12},{12,8},{9,1... | collective-permute-start | bytes 3538952 | tf_op jit(solution)/shard_map/ppermute | solution.py:473
  3.7 1.6 %collective-permute-start.3 = (bf16[576,512]{1,0:T(8,128)(2,1)S(1)}, bf16[576,512]{1,0:T(8,128)(2,1)}, u32[]{:S(2)}, u32[]{:S(2)}) collective-permute-start(bf16[576,512]{1,0:T(8,128)(2,1)S(1)} %dynamic-slice_bitcast_fusion.keys), channel_id=1, source_target_pairs={{0,1},{1,3},{3,2},{2,0},{4,5},{5,7},{7,6},{6,4},{8,9},{9,11},{11,1... | collective-permute-start | bytes 1769480 | tf_op jit(solution)/shard_map/ppermute | solution.py:470
  5.4 0.7 constant_dynamic-slice_fusion
  6.1 1.9 %copy-done.1 = bf16[384,4096]{1,0:T(8,128)(2,1)S(1)} copy-done((bf16[384,4096]{1,0:T(8,128)(2,1)S(1)}, bf16[384,4096]{1,0:T(8,128)(2,1)}, u32[]{:S(2)}) %copy-start.1) | copy-done | bytes 3145752
  8.0 0.9 copy-done.3
  8.9 0.9 copy-done.4
  9.8 1.3 project.1
  11.1 2.6 %collective-permute-start.4 = (f32[16,4224]{1,0:T(8,128)S(1)}, f32[16,4224]{1,0:T(8,128)S(1)}, u32[]{:S(2)}, u32[]{:S(2)}) collective-permute-start(f32[16,4224]{1,0:T(8,128)S(1)} %get-tuple-element.33), channel_id=1, source_target_pairs={{0,1},{1,3},{3,2},{2,0},{4,5},{5,7},{7,6},{6,4},{8,9},{9,11},{11,1... | collective-permute-start | bytes 811016 | tf_op jit(solution)/shard_map/ppermute | solution.py:470
  13.8 11.5 %collective-permute-done.4 = f32[16,4224]{1,0:T(8,128)S(1)} collective-permute-done((f32[16,4224]{1,0:T(8,128)S(1)}, f32[16,4224]{1,0:T(8,128)S(1)}, u32[]{:S(2)}, u32[]{:S(2)}) %collective-permute-start.4) | collective-permute-done | bytes 270368 | tf_op jit(solution)/shard_map/ppermute | solution.py:470
  25.3 0.8 collective-permute-start.5
  26.2 3.4 %collective-permute-start.6 = (f32[16,4224]{1,0:T(8,128)S(1)}, f32[16,4224]{1,0:T(8,128)S(1)}, u32[]{:S(2)}, u32[]{:S(2)}) collective-permute-start(f32[16,4224]{1,0:T(8,128)S(1)} %add.59), channel_id=1, source_target_pairs={{0,1},{1,3},{3,2},{2,0},{4,5},{5,7},{7,6},{6,4},{8,9},{9,11},{11,1... | collective-permute-start | bytes 811016 | tf_op jit(solution)/shard_map/ppermute | solution.py:470
  29.5 0.3 collective-permute-start.10
  29.8 1.3 collective-permute-start.11
  31.1 22.8 %collective-permute-done.6 = f32[16,4224]{1,0:T(8,128)S(1)} collective-permute-done((f32[16,4224]{1,0:T(8,128)S(1)}, f32[16,4224]{1,0:T(8,128)S(1)}, u32[]{:S(2)}, u32[]{:S(2)}) %collective-permute-start.6) | collective-permute-done | bytes 270368 | tf_op jit(solution)/shard_map/ppermute | solution.py:470
  54.0 1.0 collective-permute-start.9
  55.1 3.4 %score.4 = (bf16[16,128,512]{2,1,0:T(8,128)(2,1)S(1)}, f32[16,128]{1,0:T(8,128)S(1)}, f32[16,128]{1,0:T(8,128)S(1)}, f32[16,128]{1,0:T(8,128)S(1)}) custom-call(s32[33]{0:T(128)S(1)} %get-tuple-element.72.info, s32[64]{0:T(128)S(1)} %bitcast.60, bf16[16,64,576]{2,1,0:T(8,128)(2,1)S(1)} %bitcast.56, bf16[16,64,576]{2,1,0:T(8,128)(2,1)} %collective-permute-done.7.other, ...), custom_call_target="tpu_custom_call" | custom-call | flops 1207959552 | bytes 5046272 | tf_op jit(solution)/shard_map/score/pallas_call | solution.py:184
  58.5 3.4 %collective-permute-start.14 = (bf16[576,512]{1,0:T(8,128)(2,1)S(1)}, bf16[576,512]{1,0:T(8,128)(2,1)S(1)}, u32[]{:S(2)}, u32[]{:S(2)}) collective-permute-start(bf16[576,512]{1,0:T(8,128)(2,1)S(1)} %collective-permute-done.5.keys), channel_id=1, source_target_pairs={{0,1},{1,3},{3,2},{2,0},{4,5},{5,7},{7,6},{6,4},{8,9},{9,11},{11,1... | collective-permute-start | bytes 1769480 | tf_op jit(solution)/shard_map/ppermute | solution.py:470
  61.9 1.5 %collective-permute-start = (bf16[64,2176]{1,0:T(8,128)(2,1)S(1)}, bf16[64,2176]{1,0:T(8,128)(2,1)}, u32[]{:S(2)}, u32[]{:S(2)}) collective-permute-start(bf16[64,2176]{1,0:T(8,128)(2,1)S(1)} %get-tuple-element.32), channel_id=1, source_target_pairs={{0,16},{8,24},{16,0},{24,8},{1,17},{9,25},{17,1},{25,9},{2,18},{10... | collective-permute-start | bytes 835592 | tf_op jit(solution)/shard_map/ppermute | solution.py:476
  63.5 1.5 %collective-permute-start.12 = (bf16[2048,128]{1,0:T(8,128)(2,1)S(1)}, bf16[2048,128]{1,0:T(8,128)(2,1)S(1)}, u32[]{:S(2)}, u32[]{:S(2)}) collective-permute-start(bf16[2048,128]{1,0:T(8,128)(2,1)S(1)} %pad_maximum_fusion.5.own), channel_id=1, source_target_pairs={{0,4},{4,0},{1,5},{5,1},{2,6},{6,2},{3,7},{7,3},{8,12},{12,8},{9,1... | collective-permute-start | bytes 1572872 | tf_op jit(solution)/shard_map/ppermute | solution.py:473
  65.0 3.6 %collective-permute-done = bf16[64,2176]{1,0:T(8,128)(2,1)} collective-permute-done((bf16[64,2176]{1,0:T(8,128)(2,1)S(1)}, bf16[64,2176]{1,0:T(8,128)(2,1)}, u32[]{:S(2)}, u32[]{:S(2)}) %collective-permute-start) | collective-permute-done | bytes 278560 | tf_op jit(solution)/shard_map/ppermute | solution.py:476
  68.7 3.5 %score.5 = (bf16[16,128,512]{2,1,0:T(8,128)(2,1)S(1)}, f32[16,128]{1,0:T(8,128)S(1)}, f32[16,128]{1,0:T(8,128)S(1)}, f32[16,128]{1,0:T(8,128)S(1)}) custom-call(s32[33]{0:T(128)S(1)} %get-tuple-element.72.info, s32[64]{0:T(128)S(1)} %bitcast.61, bf16[16,64,576]{2,1,0:T(8,128)(2,1)S(1)} %bitcast.57, bf16[16,64,576]{2,1,0:T(8,128)(2,1)} %collective-permute-done.7.other, ...), custom_call_target="tpu_custom_call" | custom-call | flops 1207959552 | bytes 5046272 | tf_op jit(solution)/shard_map/score/pallas_call | solution.py:184
  72.2 3.4 %score.6 = (bf16[16,128,512]{2,1,0:T(8,128)(2,1)S(1)}, f32[16,128]{1,0:T(8,128)S(1)}, f32[16,128]{1,0:T(8,128)S(1)}, f32[16,128]{1,0:T(8,128)S(1)}) custom-call(s32[33]{0:T(128)S(1)} %get-tuple-element.72.info, s32[64]{0:T(128)S(1)} %bitcast.62, bf16[16,64,576]{2,1,0:T(8,128)(2,1)S(1)} %bitcast.58, bf16[16,64,576]{2,1,0:T(8,128)(2,1)} %collective-permute-done.7.other, ...), custom_call_target="tpu_custom_call" | custom-call | flops 1207959552 | bytes 5046272 | tf_op jit(solution)/shard_map/score/pallas_call | solution.py:184
  75.6 3.4 %score.7 = (bf16[16,128,512]{2,1,0:T(8,128)(2,1)S(1)}, f32[16,128]{1,0:T(8,128)S(1)}, f32[16,128]{1,0:T(8,128)S(1)}, f32[16,128]{1,0:T(8,128)S(1)}) custom-call(s32[33]{0:T(128)S(1)} %get-tuple-element.72.info, s32[64]{0:T(128)S(1)} %bitcast.63, bf16[16,64,576]{2,1,0:T(8,128)(2,1)S(1)} %bitcast.59, bf16[16,64,576]{2,1,0:T(8,128)(2,1)} %collective-permute-done.7.other, ...), custom_call_target="tpu_custom_call" | custom-call | flops 1207959552 | bytes 5046272 | tf_op jit(solution)/shard_map/score/pallas_call | solution.py:184
  79.1 1.5 %collective-permute-start.15 = (f32[2,16,128]{2,1,0:T(8,128)S(1)}, f32[2,16,128]{2,1,0:T(8,128)S(1)}, u32[]{:S(2)}, u32[]{:S(2)}) collective-permute-start(f32[2,16,128]{2,1,0:T(8,128)S(1)} %pad_maximum_fusion.6), channel_id=1, source_target_pairs={{0,4},{4,0},{1,5},{5,1},{2,6},{6,2},{3,7},{7,3},{8,12},{12,8},{9,1... | collective-permute-start | bytes 49160 | tf_op jit(solution)/shard_map/ppermute | solution.py:473
  80.6 1.3 logits.1.part
  81.9 0.6 collective-permute-start.13
  82.5 0.4 collective-permute-done.15
  82.9 2.4 %target.1.target_own = f32[16,2048]{1,0:T(8,128)S(1)} custom-call(bf16[16,128,512]{2,1,0:T(8,128)(2,1)S(1)} %get-tuple-element.42.refs_0_, bf16[16,128,512]{2,1,0:T(8,128)(2,1)S(1)} %get-tuple-element.45.refs_1_, bf16[16,128,512]{2,1,0:T(8,128)(2,1)S(1)} %get-tuple-element.49.refs_2_, bf16[16,128,512]{2,1,0:T(8,128)(2,1)S(1)} %get-tuple-element.52.refs_3_, ...), custom_call_target="tpu_custom_call" | custom-call | flops 8388608 | bytes 8388608 | tf_op jit(solution)/shard_map/target/pallas_call | solution.py:232
  85.2 1.5 %collective-permute-start.16 = (f32[16,2048]{1,0:T(8,128)S(1)}, f32[16,2048]{1,0:T(8,128)}, u32[]{:S(2)}, u32[]{:S(2)}) collective-permute-start(f32[16,2048]{1,0:T(8,128)S(1)} %target.1.target_own), channel_id=1, source_target_pairs={{0,4},{4,0},{1,5},{5,1},{2,6},{6,2},{3,7},{7,3},{8,12},{12,8},{9,1... | collective-permute-start | bytes 393224 | tf_op jit(solution)/shard_map/ppermute | solution.py:473
  86.8 0.7 fusion.2
  92.4 0.7 fusion.3
  103.4 3.9 %gradient.1 = bf16[16,4224]{1,0:T(8,128)(2,1)S(1)} custom-call(s32[33]{0:T(128)S(1)} %get-tuple-element.72.info, s32[64]{0:T(128)S(1)} %bitcast.64, f32[16,4224]{1,0:T(8,128)S(1)} %collective-permute-done.8.received, f32[16,4224]{1,0:T(8,128)S(1)} %get-tuple-element.41.here, bf16[2048,128]{1,0:T(8,128)(2,1)S(1)} %pad_maximum_fusion.5.own, ...), custom_call_target="tpu_custom_call" | custom-call | flops 1073741824 | bytes 2375680 | tf_op jit(solution)/shard_map/gradient/pallas_call | solution.py:372
  107.4 2.9 %collective-permute-start.18 = (bf16[16,4224]{1,0:T(8,128)(2,1)S(1)}, bf16[16,4224]{1,0:T(8,128)(2,1)S(1)}, u32[]{:S(2)}, u32[]{:S(2)}) collective-permute-start(bf16[16,4224]{1,0:T(8,128)(2,1)S(1)} %gradient.1), channel_id=1, source_target_pairs={{0,2},{1,3},{2,0},{3,1},{4,6},{5,7},{6,4},{7,5},{8,10},{9,11},{10,... | collective-permute-start | bytes 405512 | tf_op jit(solution)/shard_map/ppermute | solution.py:551
  110.3 2.8 %collective-permute-start.19 = (bf16[16,4224]{1,0:T(8,128)(2,1)S(1)}, bf16[16,4224]{1,0:T(8,128)(2,1)S(1)}, u32[]{:S(2)}, u32[]{:S(2)}) collective-permute-start(bf16[16,4224]{1,0:T(8,128)(2,1)S(1)} %gradient.1), channel_id=1, source_target_pairs={{0,3},{1,0},{2,1},{3,2},{4,7},{5,4},{6,5},{7,6},{8,11},{9,8},{10,9... | collective-permute-start | bytes 405512 | tf_op jit(solution)/shard_map/ppermute | solution.py:551
  113.1 1.3 pad_maximum_fusion
  114.4 1.3 collective-permute-done.17
  115.7 4.1 %collective-permute-done.18 = bf16[16,4224]{1,0:T(8,128)(2,1)S(1)} collective-permute-done((bf16[16,4224]{1,0:T(8,128)(2,1)S(1)}, bf16[16,4224]{1,0:T(8,128)(2,1)S(1)}, u32[]{:S(2)}, u32[]{:S(2)}) %collective-permute-start.18) | collective-permute-done | bytes 135200 | tf_op jit(solution)/shard_map/ppermute | solution.py:551
  119.9 0.1 pad_maximum_fusion.4.refs_0_.refs_4_
  119.9 1.6 %collective-permute-start.20 = (bf16[4,16,4224]{2,1,0:T(8,128)(2,1)S(1)}, bf16[4,16,4224]{2,1,0:T(8,128)(2,1)S(1)}, u32[]{:S(2)}, u32[]{:S(2)}) collective-permute-start(bf16[4,16,4224]{2,1,0:T(8,128)(2,1)S(1)} %pad_maximum_fusion.4.refs_0_.refs_4_), channel_id=1, source_target_pairs={{0,16},{8,24},{16,0},{24,8},{1,17},{9,25},{17,1},{25,9},{2,18},{10... | collective-permute-start | bytes 1622024 | tf_op jit(solution)/shard_map/ppermute | solution.py:476
  121.5 0.1 dynamic-slice_bitcast_fusion.4
  121.6 0.7 copy-done.7
  122.3 0.1 copy.13.latents
  122.5 1.0 pad_maximum_fusion.1.hiddens
  123.6 8.1 %collective-permute-done.20.refs_1_.refs_5_ = bf16[4,16,4224]{2,1,0:T(8,128)(2,1)S(1)} collective-permute-done((bf16[4,16,4224]{2,1,0:T(8,128)(2,1)S(1)}, bf16[4,16,4224]{2,1,0:T(8,128)(2,1)S(1)}, u32[]{:S(2)}, u32[]{:S(2)}) %collective-permute-start.20) | collective-permute-done | bytes 540704 | tf_op jit(solution)/shard_map/ppermute | solution.py:476
  131.8 0.2 dynamic-slice_reduce_fusion.3
  132.0 0.6 maximum_bitcast_fusion.1
  132.5 1.0 collective-permute-done.22.refs_3_.refs_7_
  133.6 6.4 %outer.1 = (f32[384,4096]{1,0:T(8,128)}, f32[32,1792]{1,0:T(8,128)}) custom-call(s32[33]{0:T(128)S(1)} %get-tuple-element.72.info, bf16[384,256]{1,0:T(8,128)(2,1)S(1)} %copy.13.latents, bf16[256,1792]{1,0:T(8,128)(2,1)S(1)} %pad_maximum_fusion.1.hiddens, bf16[4,16,4224]{2,1,0:T(8,128)(2,1)S(1)} %pad_maximum_fusion.4.refs_0_.refs_4_, ...), custom_call_target="tpu_custom_call" | custom-call | flops 805306368 | bytes 8388608 | tf_op jit(solution)/shard_map/outer/pallas_call | solution.py:422
  (47 shorter events, 0.6 us)
Async XLA Ops:
  0.6 3.1 %copy-start = (bf16[1,1024,576]{1,2,0:T(8,128)(2,1)S(1)}, bf16[1,1024,576]{1,2,0:T(8,128)(2,1)}, u32[]{:S(2)}) copy-start(bf16[1,1024,576]{1,2,0:T(8,128)(2,1)} %param.12) | copy-start | bytes 3538948
  0.6 5.4 %copy-start.2 = (bf16[1,64,7168]{2,1,0:T(8,128)(2,1)S(1)}, bf16[1,64,7168]{2,1,0:T(8,128)(2,1)}, u32[]{:S(2)}) copy-start(bf16[1,64,7168]{2,1,0:T(8,128)(2,1)} %param.10) | copy-start | bytes 2752516
  0.7 54.4 %collective-permute-start.7 = (bf16[16,64,576]{2,1,0:T(8,128)(2,1)}, bf16[16,64,576]{2,1,0:T(8,128)(2,1)}, u32[]{:S(2)}, u32[]{:S(2)}) collective-permute-start(bf16[16,64,576]{2,1,0:T(8,128)(2,1)} %bitcast.55), channel_id=1, source_target_pairs={{0,4},{4,0},{1,5},{5,1},{2,6},{6,2},{3,7},{7,3},{8,12},{12,8},{9,1... | collective-permute-start | bytes 3538952 | tf_op jit(solution)/shard_map/ppermute | solution.py:473
  3.7 21.6 %collective-permute-start.3 = (bf16[576,512]{1,0:T(8,128)(2,1)S(1)}, bf16[576,512]{1,0:T(8,128)(2,1)}, u32[]{:S(2)}, u32[]{:S(2)}) collective-permute-start(bf16[576,512]{1,0:T(8,128)(2,1)S(1)} %dynamic-slice_bitcast_fusion.keys), channel_id=1, source_target_pairs={{0,1},{1,3},{3,2},{2,0},{4,5},{5,7},{7,6},{6,4},{8,9},{9,11},{11,1... | collective-permute-start | bytes 1769480 | tf_op jit(solution)/shard_map/ppermute | solution.py:470
  6.1 1.9 %copy-start.1 = (bf16[384,4096]{1,0:T(8,128)(2,1)S(1)}, bf16[384,4096]{1,0:T(8,128)(2,1)}, u32[]{:S(2)}) copy-start(bf16[384,4096]{1,0:T(8,128)(2,1)} %weight.1) | copy-start | bytes 9437188
  8.0 0.9 copy-start.3
  8.9 0.9 copy-start.4
  9.8 19.8 %copy-start.8 = (bf16[1,1024,128]{2,1,0:T(8,128)(2,1)S(1)}, bf16[1,1024,128]{2,1,0:T(8,128)(2,1)}, u32[]{:S(2)}) copy-start(bf16[1,1024,128]{2,1,0:T(8,128)(2,1)} %param.13) | copy-start | bytes 786436
  11.1 43.9 %copy-start.5 = (bf16[1,16,64,576]{3,2,1,0:T(8,128)(2,1)S(1)}, bf16[1,16,64,576]{3,2,1,0:T(8,128)(2,1)}, u32[]{:S(2)}) copy-start(bf16[1,16,64,576]{3,2,1,0:T(8,128)(2,1)} %param.11) | copy-start | bytes 3538948
  11.1 43.9 %copy-start.6 = (s32[1,64]{1,0:T(1,128)S(1)}, s32[1,64]{1,0:T(1,128)}, u32[]{:S(2)}) copy-start(s32[1,64]{1,0:T(1,128)} %param.14) | copy-start | bytes 772
  11.1 14.2 %collective-permute-start.4 = (f32[16,4224]{1,0:T(8,128)S(1)}, f32[16,4224]{1,0:T(8,128)S(1)}, u32[]{:S(2)}, u32[]{:S(2)}) collective-permute-start(f32[16,4224]{1,0:T(8,128)S(1)} %get-tuple-element.33), channel_id=1, source_target_pairs={{0,1},{1,3},{3,2},{2,0},{4,5},{5,7},{7,6},{6,4},{8,9},{9,11},{11,1... | collective-permute-start | bytes 811016 | tf_op jit(solution)/shard_map/ppermute | solution.py:470
  25.3 33.2 %collective-permute-start.5 = (bf16[576,512]{1,0:T(8,128)(2,1)}, bf16[576,512]{1,0:T(8,128)(2,1)S(1)}, u32[]{:S(2)}, u32[]{:S(2)}) collective-permute-start(bf16[576,512]{1,0:T(8,128)(2,1)} %collective-permute-done.3.keys), channel_id=1, source_target_pairs={{0,1},{1,3},{3,2},{2,0},{4,5},{5,7},{7,6},{6,4},{8,9},{9,11},{11,1... | collective-permute-start | bytes 1769480 | tf_op jit(solution)/shard_map/ppermute | solution.py:470
  26.2 27.8 %collective-permute-start.6 = (f32[16,4224]{1,0:T(8,128)S(1)}, f32[16,4224]{1,0:T(8,128)S(1)}, u32[]{:S(2)}, u32[]{:S(2)}) collective-permute-start(f32[16,4224]{1,0:T(8,128)S(1)} %add.59), channel_id=1, source_target_pairs={{0,1},{1,3},{3,2},{2,0},{4,5},{5,7},{7,6},{6,4},{8,9},{9,11},{11,1... | collective-permute-start | bytes 811016 | tf_op jit(solution)/shard_map/ppermute | solution.py:470
  29.5 33.9 %collective-permute-start.10 = (bf16[512,128]{1,0:T(8,128)(2,1)S(1)}, bf16[512,128]{1,0:T(8,128)(2,1)S(1)}, u32[]{:S(2)}, u32[]{:S(2)}) collective-permute-start(bf16[512,128]{1,0:T(8,128)(2,1)S(1)} %dynamic-slice_bitcast_fusion.5), channel_id=1, source_target_pairs={{0,3},{1,2},{3,0},{2,1},{4,7},{5,6},{7,4},{6,5},{8,11},{9,10},{11,... | collective-permute-start | bytes 393224 | tf_op jit(solution)/shard_map/ppermute | solution.py:470
  29.8 33.6 %collective-permute-start.11 = (bf16[512,128]{1,0:T(8,128)(2,1)S(1)}, bf16[512,128]{1,0:T(8,128)(2,1)S(1)}, u32[]{:S(2)}, u32[]{:S(2)}) collective-permute-start(bf16[512,128]{1,0:T(8,128)(2,1)S(1)} %dynamic-slice_bitcast_fusion.5), channel_id=1, source_target_pairs={{0,2},{1,0},{3,1},{2,3},{4,6},{5,4},{7,5},{6,7},{8,10},{9,8},{11,9... | collective-permute-start | bytes 393224 | tf_op jit(solution)/shard_map/ppermute | solution.py:470
  54.0 9.4 %collective-permute-start.9 = (bf16[512,128]{1,0:T(8,128)(2,1)S(1)}, bf16[512,128]{1,0:T(8,128)(2,1)S(1)}, u32[]{:S(2)}, u32[]{:S(2)}) collective-permute-start(bf16[512,128]{1,0:T(8,128)(2,1)S(1)} %dynamic-slice_bitcast_fusion.5), channel_id=1, source_target_pairs={{0,1},{1,3},{3,2},{2,0},{4,5},{5,7},{7,6},{6,4},{8,9},{9,11},{11,1... | collective-permute-start | bytes 393224 | tf_op jit(solution)/shard_map/ppermute | solution.py:470
  58.5 17.1 %collective-permute-start.14 = (bf16[576,512]{1,0:T(8,128)(2,1)S(1)}, bf16[576,512]{1,0:T(8,128)(2,1)S(1)}, u32[]{:S(2)}, u32[]{:S(2)}) collective-permute-start(bf16[576,512]{1,0:T(8,128)(2,1)S(1)} %collective-permute-done.5.keys), channel_id=1, source_target_pairs={{0,1},{1,3},{3,2},{2,0},{4,5},{5,7},{7,6},{6,4},{8,9},{9,11},{11,1... | collective-permute-start | bytes 1769480 | tf_op jit(solution)/shard_map/ppermute | solution.py:470
  61.9 6.7 %collective-permute-start = (bf16[64,2176]{1,0:T(8,128)(2,1)S(1)}, bf16[64,2176]{1,0:T(8,128)(2,1)}, u32[]{:S(2)}, u32[]{:S(2)}) collective-permute-start(bf16[64,2176]{1,0:T(8,128)(2,1)S(1)} %get-tuple-element.32), channel_id=1, source_target_pairs={{0,16},{8,24},{16,0},{24,8},{1,17},{9,25},{17,1},{25,9},{2,18},{10... | collective-permute-start | bytes 835592 | tf_op jit(solution)/shard_map/ppermute | solution.py:476
  63.4 49.7 %collective-permute-start.1 = (bf16[64,2176]{1,0:T(8,128)(2,1)S(1)}, bf16[64,2176]{1,0:T(8,128)(2,1)}, u32[]{:S(2)}, u32[]{:S(2)}) collective-permute-start(bf16[64,2176]{1,0:T(8,128)(2,1)S(1)} %get-tuple-element.32), channel_id=1, source_target_pairs={{0,8},{8,0},{16,24},{24,16},{1,9},{9,1},{17,25},{25,17},{2,10},{10... | collective-permute-start | bytes 835592 | tf_op jit(solution)/shard_map/ppermute | solution.py:476
  63.5 17.1 %collective-permute-start.12 = (bf16[2048,128]{1,0:T(8,128)(2,1)S(1)}, bf16[2048,128]{1,0:T(8,128)(2,1)S(1)}, u32[]{:S(2)}, u32[]{:S(2)}) collective-permute-start(bf16[2048,128]{1,0:T(8,128)(2,1)S(1)} %pad_maximum_fusion.5.own), channel_id=1, source_target_pairs={{0,4},{4,0},{1,5},{5,1},{2,6},{6,2},{3,7},{7,3},{8,12},{12,8},{9,1... | collective-permute-start | bytes 1572872 | tf_op jit(solution)/shard_map/ppermute | solution.py:473
  68.6 44.6 %collective-permute-start.2 = (bf16[64,2176]{1,0:T(8,128)(2,1)}, bf16[64,2176]{1,0:T(8,128)(2,1)}, u32[]{:S(2)}, u32[]{:S(2)}) collective-permute-start(bf16[64,2176]{1,0:T(8,128)(2,1)} %collective-permute-done), channel_id=1, source_target_pairs={{0,8},{8,0},{16,24},{24,16},{1,9},{9,1},{17,25},{25,17},{2,10},{10... | collective-permute-start | bytes 835592 | tf_op jit(solution)/shard_map/ppermute | solution.py:476
  68.6 12.0 %collective-permute-start.8 = (f32[16,4224]{1,0:T(8,128)S(1)}, f32[16,4224]{1,0:T(8,128)S(1)}, u32[]{:S(2)}, u32[]{:S(2)}) collective-permute-start(f32[16,4224]{1,0:T(8,128)S(1)} %add.60), channel_id=1, source_target_pairs={{0,1},{1,3},{3,2},{2,0},{4,5},{5,7},{7,6},{6,4},{8,9},{9,11},{11,1... | collective-permute-start | bytes 811016 | tf_op jit(solution)/shard_map/ppermute | solution.py:470
  79.1 3.8 %collective-permute-start.15 = (f32[2,16,128]{2,1,0:T(8,128)S(1)}, f32[2,16,128]{2,1,0:T(8,128)S(1)}, u32[]{:S(2)}, u32[]{:S(2)}) collective-permute-start(f32[2,16,128]{2,1,0:T(8,128)S(1)} %pad_maximum_fusion.6), channel_id=1, source_target_pairs={{0,4},{4,0},{1,5},{5,1},{2,6},{6,2},{3,7},{7,3},{8,12},{12,8},{9,1... | collective-permute-start | bytes 49160 | tf_op jit(solution)/shard_map/ppermute | solution.py:473
  81.9 21.5 %collective-permute-start.13 = (f32[2,16,2048]{2,1,0:T(8,128)S(1)}, f32[2,16,2048]{2,1,0:T(8,128)}, u32[]{:S(2)}, u32[]{:S(2)}) collective-permute-start(f32[2,16,2048]{2,1,0:T(8,128)S(1)} %logits.1.part), channel_id=1, source_target_pairs={{0,4},{4,0},{1,5},{5,1},{2,6},{6,2},{3,7},{7,3},{8,12},{12,8},{9,1... | collective-permute-start | bytes 786440 | tf_op jit(solution)/shard_map/ppermute | solution.py:473
  85.2 18.1 %collective-permute-start.16 = (f32[16,2048]{1,0:T(8,128)S(1)}, f32[16,2048]{1,0:T(8,128)}, u32[]{:S(2)}, u32[]{:S(2)}) collective-permute-start(f32[16,2048]{1,0:T(8,128)S(1)} %target.1.target_own), channel_id=1, source_target_pairs={{0,4},{4,0},{1,5},{5,1},{2,6},{6,2},{3,7},{7,3},{8,12},{12,8},{9,1... | collective-permute-start | bytes 393224 | tf_op jit(solution)/shard_map/ppermute | solution.py:473
  107.3 8.4 %collective-permute-start.17 = (bf16[16,4224]{1,0:T(8,128)(2,1)S(1)}, bf16[16,4224]{1,0:T(8,128)(2,1)S(1)}, u32[]{:S(2)}, u32[]{:S(2)}) collective-permute-start(bf16[16,4224]{1,0:T(8,128)(2,1)S(1)} %gradient.1), channel_id=1, source_target_pairs={{0,1},{1,2},{2,3},{3,0},{4,5},{5,6},{6,7},{7,4},{8,9},{9,10},{10,1... | collective-permute-start | bytes 405512 | tf_op jit(solution)/shard_map/ppermute | solution.py:551
  107.4 12.5 %collective-permute-start.18 = (bf16[16,4224]{1,0:T(8,128)(2,1)S(1)}, bf16[16,4224]{1,0:T(8,128)(2,1)S(1)}, u32[]{:S(2)}, u32[]{:S(2)}) collective-permute-start(bf16[16,4224]{1,0:T(8,128)(2,1)S(1)} %gradient.1), channel_id=1, source_target_pairs={{0,2},{1,3},{2,0},{3,1},{4,6},{5,7},{6,4},{7,5},{8,10},{9,11},{10,... | collective-permute-start | bytes 405512 | tf_op jit(solution)/shard_map/ppermute | solution.py:551
  110.3 9.6 %collective-permute-start.19 = (bf16[16,4224]{1,0:T(8,128)(2,1)S(1)}, bf16[16,4224]{1,0:T(8,128)(2,1)S(1)}, u32[]{:S(2)}, u32[]{:S(2)}) collective-permute-start(bf16[16,4224]{1,0:T(8,128)(2,1)S(1)} %gradient.1), channel_id=1, source_target_pairs={{0,3},{1,0},{2,1},{3,2},{4,7},{5,4},{6,5},{7,6},{8,11},{9,8},{10,9... | collective-permute-start | bytes 405512 | tf_op jit(solution)/shard_map/ppermute | solution.py:551
  119.9 11.7 %collective-permute-start.20 = (bf16[4,16,4224]{2,1,0:T(8,128)(2,1)S(1)}, bf16[4,16,4224]{2,1,0:T(8,128)(2,1)S(1)}, u32[]{:S(2)}, u32[]{:S(2)}) collective-permute-start(bf16[4,16,4224]{2,1,0:T(8,128)(2,1)S(1)} %pad_maximum_fusion.4.refs_0_.refs_4_), channel_id=1, source_target_pairs={{0,16},{8,24},{16,0},{24,8},{1,17},{9,25},{17,1},{25,9},{2,18},{10... | collective-permute-start | bytes 1622024 | tf_op jit(solution)/shard_map/ppermute | solution.py:476
  121.6 0.7 copy-start.7
  123.5 9.1 %collective-permute-start.21 = (bf16[4,16,4224]{2,1,0:T(8,128)(2,1)S(1)}, bf16[4,16,4224]{2,1,0:T(8,128)(2,1)S(1)}, u32[]{:S(2)}, u32[]{:S(2)}) collective-permute-start(bf16[4,16,4224]{2,1,0:T(8,128)(2,1)S(1)} %pad_maximum_fusion.4.refs_0_.refs_4_), channel_id=1, source_target_pairs={{0,8},{8,0},{16,24},{24,16},{1,9},{9,1},{17,25},{25,17},{2,10},{10... | collective-permute-start | bytes 1622024 | tf_op jit(solution)/shard_map/ppermute | solution.py:476
  131.6 1.9 %collective-permute-start.22 = (bf16[4,16,4224]{2,1,0:T(8,128)(2,1)S(1)}, bf16[4,16,4224]{2,1,0:T(8,128)(2,1)S(1)}, u32[]{:S(2)}, u32[]{:S(2)}) collective-permute-start(bf16[4,16,4224]{2,1,0:T(8,128)(2,1)S(1)} %collective-permute-done.20.refs_1_.refs_5_), channel_id=1, source_target_pairs={{0,8},{8,0},{16,24},{24,16},{1,9},{9,1},{17,25},{25,17},{2,10},{10... | collective-permute-start | bytes 1622024 | tf_op jit(solution)/shard_map/ppermute | solution.py:476

commit v4 on v3

--- a/solution.py
+++ b/solution.py
@@ -56,7 +56,7 @@
                 row += [k * rows + y * half for k in behind]
                 row += [k * rows + (1 - y) * half for k in behind]
                 row += [(dp ^ k) * n + (z - t) % n for k in flips for t in range(n)]
-                row += [flips.index(dp ^ b) for b in range(dp_size)]
+                row += [dp ^ k for k in flips]
                 table.append(row)
     return np.array(table, np.int32)
 
@@ -147,16 +147,19 @@
             rows = source[at : at + group].reshape(group * heads, depth)
             scores = times(rows, keys[...], 1, 0)
             diagonal = lane_at == row_at + offset
+            blocks = [scores[k * heads : (k + 1) * heads] for k in range(group)]
+            seen = [key_at <= limits[at + k] for k in range(group)]
+            blocks = [jnp.where(seen[k], blocks[k], masked_floor) for k in range(group)]
+            highs = [jnp.max(one, axis=1, keepdims=True) for one in blocks]
+            totals = []
+            for k in range(group):
+                shifted = jnp.exp2((blocks[k] - highs[k]) * exponent_scale)
+                weights[at + k, offset : offset + heads] = shifted.astype(bf16)
+                totals.append(jnp.sum(shifted, axis=1, keepdims=True))
             for k in range(group):
                 q = at + k
-                visible = key_at <= limits[q]
-                one = jnp.where(visible, scores[k * heads : (k + 1) * heads], masked_floor)
-                high = jnp.max(one, axis=1, keepdims=True)
-                shifted = jnp.exp2((one - high) * exponent_scale)
-                total = jnp.sum(shifted, axis=1, keepdims=True)
-                weights[q, offset : offset + heads] = shifted.astype(bf16)
-                high_row = jnp.sum(jnp.where(diagonal, high, 0.0), axis=0, keepdims=True)
-                total_row = jnp.sum(jnp.where(diagonal, total, 0.0), axis=0, keepdims=True)
+                high_row = jnp.sum(jnp.where(diagonal, highs[k], 0.0), axis=0, keepdims=True)
+                total_row = jnp.sum(jnp.where(diagonal, totals[k], 0.0), axis=0, keepdims=True)
                 if offset == 0:
                     top[q : q + 1, :] = high_row
                     mass[q : q + 1, :] = total_row
@@ -199,10 +202,10 @@
 
 def target_kernel(blocks, *refs):
     weights, tops = refs[:blocks], refs[blocks : 2 * blocks]
-    top, mass, other_top, other_mass, out = refs[2 * blocks :]
+    top, mass, far, out, held = refs[2 * blocks :]
     count, heads, span = weights[0].shape
-    far_top = pltpu.roll(other_top[...], heads // 2, 1)
-    far_mass = pltpu.roll(other_mass[...], heads // 2, 1)
+    far_top = pltpu.roll(far[0], heads // 2, 1)
+    far_mass = pltpu.roll(far[1], heads // 2, 1)
     joint = jnp.maximum(top[...], far_top)
     total = mass[...] * jnp.exp2((top[...] - joint) * exponent_scale) + far_mass * jnp.exp2(
         (far_top - joint) * exponent_scale
@@ -218,24 +221,19 @@
                 jnp.where(diagonal, factor[q : q + 1, :], 0.0), axis=1, keepdims=True
             )
             mixed = weights[t][q].astype(f32) * column
-            out[q : q + 1, t * span : (t + 1) * span] = jnp.sum(mixed, axis=0, keepdims=True)
-
-
-def make_target(weights, tops, top, mass, other_top, other_mass):
+            held[q : q + 1, t * span : (t + 1) * span] = jnp.sum(mixed, axis=0, keepdims=True)
+    out[...] = held[...].astype(bf16)
+
+
+def make_target(weights, tops, top, mass, far):
     blocks = len(weights)
     count, heads, span = weights[0].shape
-    group = min(8, count)
-
-    def stat_spec():
-        return pl.BlockSpec((group, lanes), lambda i: (i, 0))
-
     return pl.pallas_call(
         functools.partial(target_kernel, blocks),
-        grid=(count // group,),
-        out_shape=jax.ShapeDtypeStruct((count, blocks * span), f32),
-        in_specs=[pl.BlockSpec((group, heads, span), lambda i: (i, 0, 0))] * blocks
-        + [stat_spec() for _ in range(blocks + 4)],
-        out_specs=pl.BlockSpec((group, blocks * span), lambda i: (i, 0)),
+        out_shape=jax.ShapeDtypeStruct((count, blocks * span), bf16),
+        in_specs=[in_vmem()] * (2 * blocks + 3),
+        out_specs=in_vmem(),
+        scratch_shapes=[pltpu.VMEM((count, blocks * span), f32)],
         compiler_params=params(),
         cost_estimate=pl.CostEstimate(
             flops=2 * blocks * count * heads * span,
@@ -243,7 +241,7 @@
             transcendentals=0,
         ),
         name="target",
-    )(*weights, *tops, top, mass, other_top, other_mass)
+    )(*weights, *tops, top, mass, far)
 
 
 def query_rows(total, heads):
@@ -336,7 +334,7 @@
             at = slice(t * span, (t + 1) * span)
             visible = seen(side, t)
             value = logit[side, :, at]
-            wanted = target[:, at]
+            wanted = target[:, at].astype(f32)
             running = running + jnp.where(visible, wanted * (value - level), 0.0)
             grown = jnp.exp(value - high) * inverse
             delta = jnp.where(visible, grown - wanted, 0.0)
@@ -345,8 +343,9 @@
             for j in range(heads):
                 rows = slice(j * count, (j + 1) * count)
                 one = affinity[rows]
-                grads.append(jnp.where(one > 0, delta * columns[j], 0.0).astype(bf16))
-                product = delta * jnp.maximum(one, 0.0)
+                reached = jnp.where(one > 0, delta, 0.0)
+                grads.append((reached * columns[j]).astype(bf16))
+                product = reached * one
                 folded = product[:, :lanes]
                 for k in range(lanes, span, lanes):
                     folded = folded + product[:, k : k + lanes]
@@ -388,56 +387,85 @@
     )(info, positions, received, here, own, other, part, far, target_own, target_other)
 
 
-def outer_kernel(parts, blocks, at, info, latents, hiddens, *refs):
-    bodies, tails = refs[:parts], refs[parts : 2 * parts]
-    grad, grad_mixed, rows, tail_rows = refs[2 * parts :]
-    count = bodies[0].shape[1]
-    for k in range(parts):
-        for t in range(blocks):
-            to = pl.ds(pl.multiple_of(info[at + k * blocks + t] * count, count), count)
-            rows[to, :] = bodies[k][t]
-
-    grad[...] = times(latents[...], rows[...], 1, 0)
-
-    @pl.when(pl.program_id(0) == 0)
+def arrange_kernel(at, info, *refs):
+    kept, (latents, hiddens, held) = refs[:-3], refs[-3:]
+    queries, depth = kept[0].shape[0], latents.shape[0]
+    for k, one in enumerate(kept):
+        to = pl.ds(pl.multiple_of(info[at + k] * queries, queries), queries)
+        held[to, :] = one[:, :depth].astype(f32)
+        hiddens[to, :] = one[:, depth:]
+    latents[...] = held[...].T.astype(bf16)
+
+
+def arrange(at, info, depth, kept):
+    queries, width = kept[0].shape
+    total = queries * len(kept)
+    return pl.pallas_call(
+        functools.partial(arrange_kernel, at),
+        out_shape=(
+            jax.ShapeDtypeStruct((depth, total), bf16),
+            jax.ShapeDtypeStruct((total, width - depth), bf16),
+        ),
+        in_specs=[in_smem()] + [in_vmem()] * len(kept),
+        out_specs=(in_vmem(),) * 2,
+        scratch_shapes=[pltpu.VMEM((total, depth), f32)],
+        compiler_params=params(),
+        cost_estimate=pl.CostEstimate(
+            flops=0, bytes_accessed=4 * total * width, transcendentals=0
+        ),
+        name="arrange",
+    )(info, *kept)
+
+
+def outer_kernel(heads, order, dp_at, info, latents, hiddens, *refs):
+    parts, (grad, grad_mixed, losses, rows) = refs[:-4], refs[-4:]
+    count = parts[0].shape[-2]
+    width = heads * DI
+    span = grad.shape[1]
+    step = pl.program_id(0)
+
+    @pl.when(step == 0)
     def _():
-        for k in range(parts):
-            for t in range(blocks):
-                to = pl.ds(pl.multiple_of(info[at + k * blocks + t] * count, count), count)
-                tail_rows[to, :] = tails[k][t]
-        mixed = times(tail_rows[...], hiddens[...], 0, 0)
-        grad_mixed[...] = mixed[: grad_mixed.shape[0]]
-
-
-def outer(heads, at, info, latents, hiddens, parts):
-    blocks, count, _ = parts[0].shape
+        k = 0
+        for part in parts:
+            for t in range(part.shape[0]):
+                to = 0 if order is None else pl.multiple_of(info[order[k]] * count, count)
+                rows[pl.ds(to, count), :] = part[t]
+                k += 1
+        tails = rows[:, width:]
+        grad_mixed[...] = times(tails, hiddens[...], 0, 0)[:heads]
+        own = losses.shape[1]
+        from_own = rows[pl.ds(pl.multiple_of(info[dp_at] * own, own), own), width:].astype(f32)
+        column = from_own[:, heads : heads + 1] + from_own[:, heads + 1 : heads + 2]
+        diagonal = lax.broadcasted_iota(jnp.int32, (own, own), 0) == lax.broadcasted_iota(
+            jnp.int32, (own, own), 1
+        )
+        losses[...] = jnp.sum(jnp.where(diagonal, column, 0.0), axis=0, keepdims=True)
+
+    at = pl.ds(pl.multiple_of(step * span, span), span)
+    grad[...] = times(latents[...], rows[:, at], 1, 0)
+
+
+def outer(heads, order, dp_at, queries, info, latents, hiddens, parts):
     row_count, total = latents.shape
     width = heads * DI
     span = 512
     hidden_count = hiddens.shape[1]
-    body = [pl.BlockSpec((blocks, count, span), lambda i: (0, 0, i)) for _ in parts]
-    tail = [
-        pl.BlockSpec((blocks, count, lanes), lambda i: (0, 0, width // lanes)) for _ in parts
-    ]
     return pl.pallas_call(
-        functools.partial(outer_kernel, len(parts), blocks, at),
+        functools.partial(outer_kernel, heads, order, dp_at),
         grid=(width // span,),
         out_shape=(
             jax.ShapeDtypeStruct((row_count, width), f32),
             jax.ShapeDtypeStruct((heads, hidden_count), f32),
-        ),
-        in_specs=[
-            in_smem(),
-            pl.BlockSpec((row_count, total), lambda i: (0, 0)),
-            pl.BlockSpec((total, hidden_count), lambda i: (0, 0)),
-        ]
-        + body
-        + tail,
+            jax.ShapeDtypeStruct((1, queries), f32),
+        ),
+        in_specs=[in_smem()] + [in_vmem()] * (2 + len(parts)),
         out_specs=(
             pl.BlockSpec((row_count, span), lambda i: (0, i)),
             pl.BlockSpec((heads, hidden_count), lambda i: (0, 0)),
-        ),
-        scratch_shapes=[pltpu.VMEM((total, span), bf16), pltpu.VMEM((total, lanes), bf16)],
+            pl.BlockSpec((1, queries), lambda i: (0, 0)),
+        ),
+        scratch_shapes=[pltpu.VMEM((total, width + lanes), bf16)],
         compiler_params=params(),
         cost_estimate=pl.CostEstimate(
             flops=2 * total * row_count * width,
@@ -445,7 +473,7 @@
             transcendentals=0,
         ),
         name="outer",
-    )(info, latents, hiddens, *parts, *parts)
+    )(info, latents, hiddens, *parts)
 
 
 def per_device(
@@ -462,7 +490,6 @@
     half = rows // head_size
     rows_latent = w_query.shape[0]
     heads_here = w_weights.shape[1]
-    width = heads_here * DI
     queries_here = main_queries.shape[1]
     sequence_positions = positions[0]
 
@@ -490,7 +517,6 @@
     other_queries = swap_head(queries)
     index_part = lax.dynamic_slice_in_dim(index_keys[0], y * half, half)
     index_own = jnp.concatenate([index_part] + [onward(index_part, t) for t in range(1, n)])
-    index_other = swap_head(index_own)
     parts, kept = project(
         info, queries_here, q_latent[0], w_query, hidden[0], w_weights.T
     )
@@ -508,9 +534,9 @@
 
     for t in range(1, n - 1):
         summed = received + parts[t]
-        if t == 2:
-            score_next(keys_mine[0])
-            keys, summed, before = lax.optimization_barrier((keys_mine[t], summed, before))
+        if t == 1:
+            keys, summed, index_own = lax.optimization_barrier((keys_mine[t], summed, index_own))
+            index_other = swap_head(index_own)
         else:
             keys, summed = lax.optimization_barrier((keys_mine[t], summed))
         keys_mine[t] = keys
@@ -521,14 +547,12 @@
 
     part = make_logits(heads_here, received, parts[n - 1], index_own, index_other)
     far = swap_head(part)
-    latents = jnp.stack(over_dp(kept))
-    from_dp = info[1 + 3 * n + n * dp_size :]
-    latents = jnp.concatenate([latents[from_dp[b]] for b in range(dp_size)])
-    latents, hiddens = latents[:, :rows_latent].T, latents[:, rows_latent:]
+    order_at = 1 + 3 * n
+    dp_at = order_at + n * dp_size
+    latents, hiddens = arrange(dp_at, info, rows_latent, over_dp(kept))
 
     score_next(keys_mine[n - 1])
-    far_top, far_mass = swap_head(jnp.stack(before))
-    target_own = make_target(weights, tops, *before, far_top, far_mass)
+    target_own = make_target(weights, tops, *before, swap_head(jnp.stack(before)))
     target_other = swap_head(target_own)
     piece = gradients(
         heads_here,
@@ -543,31 +567,33 @@
         far,
         target_own,
         target_other,
-    )
-
-    pieces = [piece]
+    )[None]
+
+    brought = []
     for t in range(1, n):
         pairs = [(k, (k + t) % n) for k in range(n)]
-        pieces.append(lax.ppermute(piece, "ctx", pairs))
-    sequence = jnp.stack(pieces)
-    gathered = over_dp(sequence)
-    order_at = 1 + 3 * n
+        brought.append(lax.ppermute(piece, "ctx", pairs))
+    own_pieces = over_dp(piece)
+    brought = over_dp(jnp.concatenate(brought))
     if queries_here % 16:
-        flat = jnp.concatenate(gathered)
+        flat = jnp.concatenate([jnp.concatenate([a, b]) for a, b in zip(own_pieces, brought)])
         order = jnp.argsort(info[order_at : order_at + n * dp_size])
-        outer_info = jnp.zeros((1,), jnp.int32)
-        gathered = [flat[order].reshape(1, -1, flat.shape[2])]
-        order_at = 0
+        parts_in, order = [flat[order].reshape(1, -1, flat.shape[2])], None
     else:
-        outer_info = info
-    grad_query, grad_weights = outer(
-        heads_here, order_at, outer_info, latents, hiddens, gathered
+        parts_in, order = own_pieces + brought, []
+        order += [order_at + k * n for k in range(dp_size)]
+        order += [order_at + k * n + t for k in range(dp_size) for t in range(1, n)]
+    grad_query, grad_weights, losses = outer(
+        heads_here,
+        order,
+        dp_at,
+        q_latent.shape[1],
+        info,
+        latents,
+        hiddens,
+        parts_in,
     )
-    low = sequence[:, :, width + heads_here : width + heads_here + 2].astype(f32)
-    low = low[:, :, 0] + low[:, :, 1]
-    steps = lax.rem(z - jnp.arange(n, dtype=jnp.int32) + n, n)
-    losses = jnp.concatenate([low[steps[k]] for k in range(n)])
-    return (grad_query, grad_weights.T, losses[None, :])
+    return (grad_query, grad_weights.T, losses)
 
 
 def solution(mesh):

time: 142 us -> 132 us (0.930); the launches traced: 140 us -> 131 us
  between operations: 16.2 us -> 0.82 us
  waiting for transfers between devices: 52.8 us -> 60.3 us
  other arithmetic: 3.25 us -> 0.1 us
  starting transfers between devices: 31.8 us -> 34.6 us
    ppermute x9, starting transfers between devices: 14.6 us -> 20.3 us  [onward(): lax.ppermute(x, 'ctx', [(ring[k], ring[(k + t) % n]) for k in range(n)])]
    ppermute x5, waiting for transfers between devices: 0.37 us -> 5.82 us  [swap_head(): return lax.ppermute(x, 'head', [(0, 1), (1, 0)])]
    ppermute x5, starting transfers between devices: 8.25 us -> 6.15 us  [swap_head(): return lax.ppermute(x, 'head', [(0, 1), (1, 0)])]
    ppermute x3, starting transfers between devices: 5.82 us -> 3.87 us  [per_device(): brought.append(lax.ppermute(piece, 'ctx', pairs))]
    ppermute x9, waiting for transfers between devices: 34.4 us -> 36 us  [onward(): lax.ppermute(x, 'ctx', [(ring[k], ring[(k + t) % n]) for k in range(n)])]
    ppermute x6 -> x9, starting transfers between devices: 3.13 us -> 4.32 us  [swap_dp(): return lax.ppermute(x, 'dp', [(k, k ^ bit) for k in range(dp_size)])]
    ppermute x6 -> x9, waiting for transfers between devices: 12.7 us -> 13.4 us  [swap_dp(): return lax.ppermute(x, 'dp', [(k, k ^ bit) for k in range(dp_size)])]
    unnamed x18 -> x16, local copies, waits for them, and re-layouts: 4.45 us -> 5.01 us
  transfers between devices with their start and end apart: 23 -> 26, of which waited for: 8 -> 12; matrix products, arithmetic and copies ran while one was open for 4% -> 1% of each run, Pallas kernels for 16% -> 15%
where the time goes in v4:
time: 132 us; the launch traced here: 131 us
  waiting for transfers between devices  60.3 us (46%)
  starting transfers between devices  34.6 us (26%)
  Pallas kernels  28.9 us (22%)
  local copies, waits for them, and re-layouts  6.68 us (5%)
    ppermute x9, waiting for transfers between devices, onward(): lax.ppermute(x, 'ctx', [(ring[k], ring[(k + t) % n]) for k in range(n)])  36 us
    ppermute x9, starting transfers between devices, onward(): lax.ppermute(x, 'ctx', [(ring[k], ring[(k + t) % n]) for k in range(n)])  20.3 us
    pallas_call x4, Pallas kernels, score(): pl.pallas_call(functools.partial(score_kernel, t, 1 + n + t), out_shape=(...  13.9 us
    ppermute x9, waiting for transfers between devices, swap_dp(): return lax.ppermute(x, 'dp', [(k, k ^ bit) for k in range(dp_size)])  13.4 us
    ppermute x5, starting transfers between devices, swap_head(): return lax.ppermute(x, 'head', [(0, 1), (1, 0)])  6.15 us
    pallas_call x1, Pallas kernels, outer(): pl.pallas_call(functools.partial(outer_kernel, heads, order, dp_at), grid...  5.94 us
    ppermute x5, waiting for transfers between devices, swap_head(): return lax.ppermute(x, 'head', [(0, 1), (1, 0)])  5.82 us
    ppermute x3, waiting for transfers between devices, per_device(): brought.append(lax.ppermute(piece, 'ctx', pairs))  5.05 us
  transfers between devices with their start and end apart: 26, of which 12 were waited for; matrix products, arithmetic and copies ran while one was open for 1% of the time, Pallas kernels for 15%

profile of v4, /device:TPU:0, one launch (start us, length us, event | category | flops | bytes accessed | tf_op | source)
XLA Modules:
  0.0 131.4 jit_solution(9529329714029229614)
XLA Ops:
  0.7 1.2 copy-done
  2.0 3.1 %collective-permute-start.3 = (bf16[576,512]{1,0:T(8,128)(2,1)S(1)}, bf16[576,512]{1,0:T(8,128)(2,1)}, u32[]{:S(2)}, u32[]{:S(2)}) collective-permute-start(bf16[576,512]{1,0:T(8,128)(2,1)S(1)} %dynamic-slice_bitcast_fusion.keys), channel_id=1, source_target_pairs={{0,1},{1,3},{3,2},{2,0},{4,5},{5,7},{7,6},{6,4},{8,9},{9,11},{11,1... | collective-permute-start | bytes 1769480 | tf_op jit(solution)/shard_map/ppermute | solution.py:497
  5.0 0.9 dynamic-slice_bitcast_fusion.1
  5.9 2.6 %collective-permute-start.5 = (bf16[512,128]{1,0:T(8,128)(2,1)S(1)}, bf16[512,128]{1,0:T(8,128)(2,1)S(1)}, u32[]{:S(2)}, u32[]{:S(2)}) collective-permute-start(bf16[512,128]{1,0:T(8,128)(2,1)S(1)} %dynamic-slice_bitcast_fusion.1), channel_id=1, source_target_pairs={{0,1},{1,3},{3,2},{2,0},{4,5},{5,7},{7,6},{6,4},{8,9},{9,11},{11,1... | collective-permute-start | bytes 393224 | tf_op jit(solution)/shard_map/ppermute | solution.py:497
  8.6 1.9 %collective-permute-start.7 = (bf16[512,128]{1,0:T(8,128)(2,1)S(1)}, bf16[512,128]{1,0:T(8,128)(2,1)S(1)}, u32[]{:S(2)}, u32[]{:S(2)}) collective-permute-start(bf16[512,128]{1,0:T(8,128)(2,1)S(1)} %dynamic-slice_bitcast_fusion.1), channel_id=1, source_target_pairs={{0,2},{1,0},{3,1},{2,3},{4,6},{5,4},{7,5},{6,7},{8,10},{9,8},{11,9... | collective-permute-start | bytes 393224 | tf_op jit(solution)/shard_map/ppermute | solution.py:497
  10.5 1.5 %collective-permute-start.13 = (bf16[16,64,576]{2,1,0:T(8,128)(2,1)}, bf16[16,64,576]{2,1,0:T(8,128)(2,1)}, u32[]{:S(2)}, u32[]{:S(2)}) collective-permute-start(bf16[16,64,576]{2,1,0:T(8,128)(2,1)} %bitcast.28), channel_id=1, source_target_pairs={{0,4},{4,0},{1,5},{5,1},{2,6},{6,2},{3,7},{7,3},{8,12},{12,8},{9,1... | collective-permute-start | bytes 3538952 | tf_op jit(solution)/shard_map/ppermute | solution.py:500
  12.0 0.7 fusion.info
  12.7 1.9 %copy-done.1 = bf16[384,4096]{1,0:T(8,128)(2,1)S(1)} copy-done((bf16[384,4096]{1,0:T(8,128)(2,1)S(1)}, bf16[384,4096]{1,0:T(8,128)(2,1)}, u32[]{:S(2)}) %copy-start.1) | copy-done | bytes 3145752
  14.6 0.9 copy-done.3
  15.5 0.9 copy-done.4
  16.4 1.3 project.1
  17.8 6.1 %collective-permute-done.5 = bf16[512,128]{1,0:T(8,128)(2,1)S(1)} collective-permute-done((bf16[512,128]{1,0:T(8,128)(2,1)S(1)}, bf16[512,128]{1,0:T(8,128)(2,1)S(1)}, u32[]{:S(2)}, u32[]{:S(2)}) %collective-permute-start.5) | collective-permute-done | bytes 131104 | tf_op jit(solution)/shard_map/ppermute | solution.py:497
  23.9 5.9 %collective-permute-start.4 = (f32[16,4224]{1,0:T(8,128)S(1)}, f32[16,4224]{1,0:T(8,128)S(1)}, u32[]{:S(2)}, u32[]{:S(2)}) collective-permute-start(f32[16,4224]{1,0:T(8,128)S(1)} %get-tuple-element.37), channel_id=1, source_target_pairs={{0,1},{1,3},{3,2},{2,0},{4,5},{5,7},{7,6},{6,4},{8,9},{9,11},{11,1... | collective-permute-start | bytes 811016 | tf_op jit(solution)/shard_map/ppermute | solution.py:497
  29.9 6.6 %collective-permute-done.4 = f32[16,4224]{1,0:T(8,128)S(1)} collective-permute-done((f32[16,4224]{1,0:T(8,128)S(1)}, f32[16,4224]{1,0:T(8,128)S(1)}, u32[]{:S(2)}, u32[]{:S(2)}) %collective-permute-start.4) | collective-permute-done | bytes 270368 | tf_op jit(solution)/shard_map/ppermute | solution.py:497
  36.5 0.9 collective-permute-start.8
  37.4 3.4 %collective-permute-start.9 = (f32[16,4224]{1,0:T(8,128)S(1)}, f32[16,4224]{1,0:T(8,128)S(1)}, u32[]{:S(2)}, u32[]{:S(2)}) collective-permute-start(f32[16,4224]{1,0:T(8,128)S(1)} %add.24), channel_id=1, source_target_pairs={{0,1},{1,3},{3,2},{2,0},{4,5},{5,7},{7,6},{6,4},{8,9},{9,11},{11,1... | collective-permute-start | bytes 811016 | tf_op jit(solution)/shard_map/ppermute | solution.py:497
  40.8 17.2 %collective-permute-done.9 = f32[16,4224]{1,0:T(8,128)S(1)} collective-permute-done((f32[16,4224]{1,0:T(8,128)S(1)}, f32[16,4224]{1,0:T(8,128)S(1)}, u32[]{:S(2)}, u32[]{:S(2)}) %collective-permute-start.9) | collective-permute-done | bytes 270368 | tf_op jit(solution)/shard_map/ppermute | solution.py:497
  58.0 0.1 collective-permute-start.14
  58.1 1.3 %collective-permute-start.11 = (bf16[2048,128]{1,0:T(8,128)(2,1)S(1)}, bf16[2048,128]{1,0:T(8,128)(2,1)S(1)}, u32[]{:S(2)}, u32[]{:S(2)}) collective-permute-start(bf16[2048,128]{1,0:T(8,128)(2,1)S(1)} %pad_maximum_fusion.own), channel_id=1, source_target_pairs={{0,4},{4,0},{1,5},{5,1},{2,6},{6,2},{3,7},{7,3},{8,12},{12,8},{9,1... | collective-permute-start | bytes 1572872 | tf_op jit(solution)/shard_map/ppermute | solution.py:500
  59.4 2.4 %collective-permute-start.10 = (f32[16,4224]{1,0:T(8,128)S(1)}, f32[16,4224]{1,0:T(8,128)S(1)}, u32[]{:S(2)}, u32[]{:S(2)}) collective-permute-start(f32[16,4224]{1,0:T(8,128)S(1)} %add.25), channel_id=1, source_target_pairs={{0,1},{1,3},{3,2},{2,0},{4,5},{5,7},{7,6},{6,4},{8,9},{9,11},{11,1... | collective-permute-start | bytes 811016 | tf_op jit(solution)/shard_map/ppermute | solution.py:497
  61.8 3.5 %score.4 = (bf16[16,128,512]{2,1,0:T(8,128)(2,1)S(1)}, f32[16,128]{1,0:T(8,128)S(1)}, f32[16,128]{1,0:T(8,128)S(1)}, f32[16,128]{1,0:T(8,128)S(1)}) custom-call(s32[33]{0:T(128)S(1)} %fusion.info, s32[64]{0:T(128)S(1)} %bitcast.33, bf16[16,64,576]{2,1,0:T(8,128)(2,1)S(1)} %bitcast.29, bf16[16,64,576]{2,1,0:T(8,128)(2,1)} %collective-permute-done.13.other, ...), custom_call_target="tpu_custom_call" | custom-call | flops 1207959552 | bytes 5046272 | tf_op jit(solution)/shard_map/score/pallas_call | solution.py:187
  65.2 3.6 %score.5 = (bf16[16,128,512]{2,1,0:T(8,128)(2,1)S(1)}, f32[16,128]{1,0:T(8,128)S(1)}, f32[16,128]{1,0:T(8,128)S(1)}, f32[16,128]{1,0:T(8,128)S(1)}) custom-call(s32[33]{0:T(128)S(1)} %fusion.info, s32[64]{0:T(128)S(1)} %bitcast.34, bf16[16,64,576]{2,1,0:T(8,128)(2,1)S(1)} %bitcast.30, bf16[16,64,576]{2,1,0:T(8,128)(2,1)} %collective-permute-done.13.other, ...), custom_call_target="tpu_custom_call" | custom-call | flops 1207959552 | bytes 5046272 | tf_op jit(solution)/shard_map/score/pallas_call | solution.py:187
  68.8 3.5 %score.6 = (bf16[16,128,512]{2,1,0:T(8,128)(2,1)S(1)}, f32[16,128]{1,0:T(8,128)S(1)}, f32[16,128]{1,0:T(8,128)S(1)}, f32[16,128]{1,0:T(8,128)S(1)}) custom-call(s32[33]{0:T(128)S(1)} %fusion.info, s32[64]{0:T(128)S(1)} %bitcast.35, bf16[16,64,576]{2,1,0:T(8,128)(2,1)S(1)} %bitcast.31, bf16[16,64,576]{2,1,0:T(8,128)(2,1)} %collective-permute-done.13.other, ...), custom_call_target="tpu_custom_call" | custom-call | flops 1207959552 | bytes 5046272 | tf_op jit(solution)/shard_map/score/pallas_call | solution.py:187
  72.3 6.1 %collective-permute-done.10.received = f32[16,4224]{1,0:T(8,128)S(1)} collective-permute-done((f32[16,4224]{1,0:T(8,128)S(1)}, f32[16,4224]{1,0:T(8,128)S(1)}, u32[]{:S(2)}, u32[]{:S(2)}) %collective-permute-start.10) | collective-permute-done | bytes 270368 | tf_op jit(solution)/shard_map/ppermute | solution.py:497
  78.3 1.3 logits.1.part
  79.6 1.0 collective-permute-start.12
  80.6 3.4 %score.7 = (bf16[16,128,512]{2,1,0:T(8,128)(2,1)S(1)}, f32[16,128]{1,0:T(8,128)S(1)}, f32[16,128]{1,0:T(8,128)S(1)}, f32[16,128]{1,0:T(8,128)S(1)}) custom-call(s32[33]{0:T(128)S(1)} %fusion.info, s32[64]{0:T(128)S(1)} %bitcast.36, bf16[16,64,576]{2,1,0:T(8,128)(2,1)S(1)} %bitcast.32, bf16[16,64,576]{2,1,0:T(8,128)(2,1)} %collective-permute-done.13.other, ...), custom_call_target="tpu_custom_call" | custom-call | flops 1207959552 | bytes 5046272 | tf_op jit(solution)/shard_map/score/pallas_call | solution.py:187
  84.1 1.2 collective-permute-start.15
  85.2 2.6 %collective-permute-done.15.refs_10_ = f32[2,16,128]{2,1,0:T(8,128)S(1)} collective-permute-done((f32[2,16,128]{2,1,0:T(8,128)S(1)}, f32[2,16,128]{2,1,0:T(8,128)S(1)}, u32[]{:S(2)}, u32[]{:S(2)}) %collective-permute-start.15) | collective-permute-done | bytes 16416 | tf_op jit(solution)/shard_map/ppermute | solution.py:500
  87.9 2.2 %target.1.target_own = bf16[16,2048]{1,0:T(8,128)(2,1)S(1)} custom-call(bf16[16,128,512]{2,1,0:T(8,128)(2,1)S(1)} %get-tuple-element.45.refs_0_, bf16[16,128,512]{2,1,0:T(8,128)(2,1)S(1)} %get-tuple-element.48.refs_1_, bf16[16,128,512]{2,1,0:T(8,128)(2,1)S(1)} %get-tuple-element.52.refs_2_, bf16[16,128,512]{2,1,0:T(8,128)(2,1)S(1)} %get-tuple-element.55.refs_3_, ...), custom_call_target="tpu_custom_call" | custom-call | flops 8388608 | bytes 8388608 | tf_op jit(solution)/shard_map/target/pallas_call | solution.py:231
  90.1 1.2 collective-permute-start.16
  91.2 3.2 %collective-permute-done.16.target_other = bf16[16,2048]{1,0:T(8,128)(2,1)S(1)} collective-permute-done((bf16[16,2048]{1,0:T(8,128)(2,1)S(1)}, bf16[16,2048]{1,0:T(8,128)(2,1)S(1)}, u32[]{:S(2)}, u32[]{:S(2)}) %collective-permute-start.16) | collective-permute-done | bytes 65568 | tf_op jit(solution)/shard_map/ppermute | solution.py:500
  94.4 3.6 %gradient.1 = bf16[16,4224]{1,0:T(8,128)(2,1)S(1)} custom-call(s32[33]{0:T(128)S(1)} %fusion.info, s32[64]{0:T(128)S(1)} %bitcast.37, f32[16,4224]{1,0:T(8,128)S(1)} %collective-permute-done.10.received, f32[16,4224]{1,0:T(8,128)S(1)} %get-tuple-element.43.here, bf16[2048,128]{1,0:T(8,128)(2,1)S(1)} %pad_maximum_fusion.own, ...), custom_call_target="tpu_custom_call" | custom-call | flops 1073741824 | bytes 2375680 | tf_op jit(solution)/shard_map/gradient/pallas_call | solution.py:371
  98.0 0.8 collective-permute-start.21
  98.8 3.0 %collective-permute-start.22 = (bf16[1,16,4224]{2,1,0:T(8,128)(2,1)S(1)}, bf16[1,16,4224]{2,1,0:T(8,128)(2,1)S(1)}, u32[]{:S(2)}, u32[]{:S(2)}) collective-permute-start(bf16[1,16,4224]{2,1,0:T(8,128)(2,1)S(1)} %bitcast.21), channel_id=1, source_target_pairs={{0,3},{1,0},{2,1},{3,2},{4,7},{5,4},{6,5},{7,6},{8,11},{9,8},{10,9... | collective-permute-start | bytes 405512 | tf_op jit(solution)/shard_map/ppermute | solution.py:575
  101.9 3.2 %collective-permute-done.20 = bf16[1,16,4224]{2,1,0:T(8,128)(2,1)S(1)} collective-permute-done((bf16[1,16,4224]{2,1,0:T(8,128)(2,1)S(1)}, bf16[1,16,4224]{2,1,0:T(8,128)(2,1)S(1)}, u32[]{:S(2)}, u32[]{:S(2)}) %collective-permute-start.20) | collective-permute-done | bytes 135200 | tf_op jit(solution)/shard_map/ppermute | solution.py:575
  105.1 1.9 %collective-permute-done.21 = bf16[1,16,4224]{2,1,0:T(8,128)(2,1)S(1)} collective-permute-done((bf16[1,16,4224]{2,1,0:T(8,128)(2,1)S(1)}, bf16[1,16,4224]{2,1,0:T(8,128)(2,1)S(1)}, u32[]{:S(2)}, u32[]{:S(2)}) %collective-permute-start.21) | collective-permute-done | bytes 135200 | tf_op jit(solution)/shard_map/ppermute | solution.py:575
  107.0 1.6 %collective-permute-start.23 = (bf16[3,16,4224]{2,1,0:T(8,128)(2,1)S(1)}, bf16[3,16,4224]{2,1,0:T(8,128)(2,1)S(1)}, u32[]{:S(2)}, u32[]{:S(2)}) collective-permute-start(bf16[3,16,4224]{2,1,0:T(8,128)(2,1)S(1)} %constant_dynamic-update-slice_fusion.refs_4_), channel_id=1, source_target_pairs={{0,16},{8,24},{16,0},{24,8},{1,17},{9,25},{17,1},{25,9},{2,18},{10... | collective-permute-start | bytes 1216520 | tf_op jit(solution)/shard_map/ppermute | solution.py:503
  108.5 0.5 collective-permute-start
  109.1 0.5 collective-permute-start.24
  109.6 5.6 %collective-permute-done.23.refs_5_ = bf16[3,16,4224]{2,1,0:T(8,128)(2,1)S(1)} collective-permute-done((bf16[3,16,4224]{2,1,0:T(8,128)(2,1)S(1)}, bf16[3,16,4224]{2,1,0:T(8,128)(2,1)S(1)}, u32[]{:S(2)}, u32[]{:S(2)}) %collective-permute-start.23) | collective-permute-done | bytes 405536 | tf_op jit(solution)/shard_map/ppermute | solution.py:503
  115.2 3.0 %collective-permute-done.refs_1_ = bf16[64,2176]{1,0:T(8,128)(2,1)S(1)} collective-permute-done((bf16[64,2176]{1,0:T(8,128)(2,1)S(1)}, bf16[64,2176]{1,0:T(8,128)(2,1)S(1)}, u32[]{:S(2)}, u32[]{:S(2)}) %collective-permute-start) | collective-permute-done | bytes 278560 | tf_op jit(solution)/shard_map/ppermute | solution.py:503
  118.1 1.5 %collective-permute-start.17 = (bf16[1,16,4224]{2,1,0:T(8,128)(2,1)S(1)}, bf16[1,16,4224]{2,1,0:T(8,128)(2,1)S(1)}, u32[]{:S(2)}, u32[]{:S(2)}) collective-permute-start(bf16[1,16,4224]{2,1,0:T(8,128)(2,1)S(1)} %bitcast.22), channel_id=1, source_target_pairs={{0,16},{8,24},{16,0},{24,8},{1,17},{9,25},{17,1},{25,9},{2,18},{10... | collective-permute-start | bytes 405512 | tf_op jit(solution)/shard_map/ppermute | solution.py:503
  119.6 0.2 collective-permute-start.18
  119.9 4.3 %collective-permute-done.17.refs_1_ = bf16[1,16,4224]{2,1,0:T(8,128)(2,1)S(1)} collective-permute-done((bf16[1,16,4224]{2,1,0:T(8,128)(2,1)S(1)}, bf16[1,16,4224]{2,1,0:T(8,128)(2,1)S(1)}, u32[]{:S(2)}, u32[]{:S(2)}) %collective-permute-start.17) | collective-permute-done | bytes 135200 | tf_op jit(solution)/shard_map/ppermute | solution.py:503
  124.1 0.8 arrange.1
  124.9 0.6 collective-permute-done.19.refs_3_
  125.5 5.9 %outer.1 = (f32[384,4096]{1,0:T(8,128)}, f32[32,1792]{1,0:T(8,128)}, f32[1,64]{1,0:T(1,128)}) custom-call(s32[33]{0:T(128)S(1)} %fusion.info, bf16[384,256]{1,0:T(8,128)(2,1)S(1)} %get-tuple-element.35.latents, bf16[256,1792]{1,0:T(8,128)(2,1)S(1)} %get-tuple-element.36.hiddens, bf16[1,16,4224]{2,1,0:T(8,128)(2,1)S(1)} %bitcast.24, ...), custom_call_target="tpu_custom_call" | custom-call | flops 805306368 | bytes 8388608 | tf_op jit(solution)/shard_map/outer/pallas_call | solution.py:454
  (39 shorter events, 0.3 us)
Async XLA Ops:
  0.6 1.3 copy-start
  0.6 12.1 %copy-start.2 = (bf16[1,64,7168]{2,1,0:T(8,128)(2,1)S(1)}, bf16[1,64,7168]{2,1,0:T(8,128)(2,1)}, u32[]{:S(2)}) copy-start(bf16[1,64,7168]{2,1,0:T(8,128)(2,1)} %param.10) | copy-start | bytes 2752516
  2.0 34.5 %collective-permute-start.3 = (bf16[576,512]{1,0:T(8,128)(2,1)S(1)}, bf16[576,512]{1,0:T(8,128)(2,1)}, u32[]{:S(2)}, u32[]{:S(2)}) collective-permute-start(bf16[576,512]{1,0:T(8,128)(2,1)S(1)} %dynamic-slice_bitcast_fusion.keys), channel_id=1, source_target_pairs={{0,1},{1,3},{3,2},{2,0},{4,5},{5,7},{7,6},{6,4},{8,9},{9,11},{11,1... | collective-permute-start | bytes 1769480 | tf_op jit(solution)/shard_map/ppermute | solution.py:497
  5.9 17.9 %collective-permute-start.5 = (bf16[512,128]{1,0:T(8,128)(2,1)S(1)}, bf16[512,128]{1,0:T(8,128)(2,1)S(1)}, u32[]{:S(2)}, u32[]{:S(2)}) collective-permute-start(bf16[512,128]{1,0:T(8,128)(2,1)S(1)} %dynamic-slice_bitcast_fusion.1), channel_id=1, source_target_pairs={{0,1},{1,3},{3,2},{2,0},{4,5},{5,7},{7,6},{6,4},{8,9},{9,11},{11,1... | collective-permute-start | bytes 393224 | tf_op jit(solution)/shard_map/ppermute | solution.py:497
  8.6 21.2 %collective-permute-start.6 = (bf16[512,128]{1,0:T(8,128)(2,1)S(1)}, bf16[512,128]{1,0:T(8,128)(2,1)S(1)}, u32[]{:S(2)}, u32[]{:S(2)}) collective-permute-start(bf16[512,128]{1,0:T(8,128)(2,1)S(1)} %dynamic-slice_bitcast_fusion.1), channel_id=1, source_target_pairs={{0,3},{1,2},{3,0},{2,1},{4,7},{5,6},{7,4},{6,5},{8,11},{9,10},{11,... | collective-permute-start | bytes 393224 | tf_op jit(solution)/shard_map/ppermute | solution.py:497
  8.6 21.2 %collective-permute-start.7 = (bf16[512,128]{1,0:T(8,128)(2,1)S(1)}, bf16[512,128]{1,0:T(8,128)(2,1)S(1)}, u32[]{:S(2)}, u32[]{:S(2)}) collective-permute-start(bf16[512,128]{1,0:T(8,128)(2,1)S(1)} %dynamic-slice_bitcast_fusion.1), channel_id=1, source_target_pairs={{0,2},{1,0},{3,1},{2,3},{4,6},{5,4},{7,5},{6,7},{8,10},{9,8},{11,9... | collective-permute-start | bytes 393224 | tf_op jit(solution)/shard_map/ppermute | solution.py:497
  10.5 51.3 %collective-permute-start.13 = (bf16[16,64,576]{2,1,0:T(8,128)(2,1)}, bf16[16,64,576]{2,1,0:T(8,128)(2,1)}, u32[]{:S(2)}, u32[]{:S(2)}) collective-permute-start(bf16[16,64,576]{2,1,0:T(8,128)(2,1)} %bitcast.28), channel_id=1, source_target_pairs={{0,4},{4,0},{1,5},{5,1},{2,6},{6,2},{3,7},{7,3},{8,12},{12,8},{9,1... | collective-permute-start | bytes 3538952 | tf_op jit(solution)/shard_map/ppermute | solution.py:500
  12.7 1.9 %copy-start.1 = (bf16[384,4096]{1,0:T(8,128)(2,1)S(1)}, bf16[384,4096]{1,0:T(8,128)(2,1)}, u32[]{:S(2)}) copy-start(bf16[384,4096]{1,0:T(8,128)(2,1)} %weight.1) | copy-start | bytes 9437188
  14.6 0.9 copy-start.3
  15.5 0.9 copy-start.4
  17.7 44.0 %copy-start.5 = (bf16[1,16,64,576]{3,2,1,0:T(8,128)(2,1)S(1)}, bf16[1,16,64,576]{3,2,1,0:T(8,128)(2,1)}, u32[]{:S(2)}) copy-start(bf16[1,16,64,576]{3,2,1,0:T(8,128)(2,1)} %param.11) | copy-start | bytes 3538948
  17.8 44.0 %copy-start.6 = (s32[1,64]{1,0:T(1,128)S(1)}, s32[1,64]{1,0:T(1,128)}, u32[]{:S(2)}) copy-start(s32[1,64]{1,0:T(1,128)} %param.14) | copy-start | bytes 772
  23.9 12.6 %collective-permute-start.4 = (f32[16,4224]{1,0:T(8,128)S(1)}, f32[16,4224]{1,0:T(8,128)S(1)}, u32[]{:S(2)}, u32[]{:S(2)}) collective-permute-start(f32[16,4224]{1,0:T(8,128)S(1)} %get-tuple-element.37), channel_id=1, source_target_pairs={{0,1},{1,3},{3,2},{2,0},{4,5},{5,7},{7,6},{6,4},{8,9},{9,11},{11,1... | collective-permute-start | bytes 811016 | tf_op jit(solution)/shard_map/ppermute | solution.py:497
  36.5 21.5 %collective-permute-start.8 = (bf16[576,512]{1,0:T(8,128)(2,1)}, bf16[576,512]{1,0:T(8,128)(2,1)S(1)}, u32[]{:S(2)}, u32[]{:S(2)}) collective-permute-start(bf16[576,512]{1,0:T(8,128)(2,1)} %collective-permute-done.3.keys), channel_id=1, source_target_pairs={{0,1},{1,3},{3,2},{2,0},{4,5},{5,7},{7,6},{6,4},{8,9},{9,11},{11,1... | collective-permute-start | bytes 1769480 | tf_op jit(solution)/shard_map/ppermute | solution.py:497
  37.4 20.6 %collective-permute-start.9 = (f32[16,4224]{1,0:T(8,128)S(1)}, f32[16,4224]{1,0:T(8,128)S(1)}, u32[]{:S(2)}, u32[]{:S(2)}) collective-permute-start(f32[16,4224]{1,0:T(8,128)S(1)} %add.24), channel_id=1, source_target_pairs={{0,1},{1,3},{3,2},{2,0},{4,5},{5,7},{7,6},{6,4},{8,9},{9,11},{11,1... | collective-permute-start | bytes 811016 | tf_op jit(solution)/shard_map/ppermute | solution.py:497
  58.0 22.6 %collective-permute-start.14 = (bf16[576,512]{1,0:T(8,128)(2,1)S(1)}, bf16[576,512]{1,0:T(8,128)(2,1)S(1)}, u32[]{:S(2)}, u32[]{:S(2)}) collective-permute-start(bf16[576,512]{1,0:T(8,128)(2,1)S(1)} %collective-permute-done.8.keys), channel_id=1, source_target_pairs={{0,1},{1,3},{3,2},{2,0},{4,5},{5,7},{7,6},{6,4},{8,9},{9,11},{11,1... | collective-permute-start | bytes 1769480 | tf_op jit(solution)/shard_map/ppermute | solution.py:497
  58.1 14.2 %collective-permute-start.11 = (bf16[2048,128]{1,0:T(8,128)(2,1)S(1)}, bf16[2048,128]{1,0:T(8,128)(2,1)S(1)}, u32[]{:S(2)}, u32[]{:S(2)}) collective-permute-start(bf16[2048,128]{1,0:T(8,128)(2,1)S(1)} %pad_maximum_fusion.own), channel_id=1, source_target_pairs={{0,4},{4,0},{1,5},{5,1},{2,6},{6,2},{3,7},{7,3},{8,12},{12,8},{9,1... | collective-permute-start | bytes 1572872 | tf_op jit(solution)/shard_map/ppermute | solution.py:500
  59.4 19.0 %collective-permute-start.10 = (f32[16,4224]{1,0:T(8,128)S(1)}, f32[16,4224]{1,0:T(8,128)S(1)}, u32[]{:S(2)}, u32[]{:S(2)}) collective-permute-start(f32[16,4224]{1,0:T(8,128)S(1)} %add.25), channel_id=1, source_target_pairs={{0,1},{1,3},{3,2},{2,0},{4,5},{5,7},{7,6},{6,4},{8,9},{9,11},{11,1... | collective-permute-start | bytes 811016 | tf_op jit(solution)/shard_map/ppermute | solution.py:497
  79.6 11.6 %collective-permute-start.12 = (f32[2,16,2048]{2,1,0:T(8,128)S(1)}, f32[2,16,2048]{2,1,0:T(8,128)S(1)}, u32[]{:S(2)}, u32[]{:S(2)}) collective-permute-start(f32[2,16,2048]{2,1,0:T(8,128)S(1)} %logits.1.part), channel_id=1, source_target_pairs={{0,4},{4,0},{1,5},{5,1},{2,6},{6,2},{3,7},{7,3},{8,12},{12,8},{9,1... | collective-permute-start | bytes 786440 | tf_op jit(solution)/shard_map/ppermute | solution.py:500
  84.1 3.8 %collective-permute-start.15 = (f32[2,16,128]{2,1,0:T(8,128)S(1)}, f32[2,16,128]{2,1,0:T(8,128)S(1)}, u32[]{:S(2)}, u32[]{:S(2)}) collective-permute-start(f32[2,16,128]{2,1,0:T(8,128)S(1)} %pad_maximum_fusion.1), channel_id=1, source_target_pairs={{0,4},{4,0},{1,5},{5,1},{2,6},{6,2},{3,7},{7,3},{8,12},{12,8},{9,1... | collective-permute-start | bytes 49160 | tf_op jit(solution)/shard_map/ppermute | solution.py:500
  90.1 4.3 %collective-permute-start.16 = (bf16[16,2048]{1,0:T(8,128)(2,1)S(1)}, bf16[16,2048]{1,0:T(8,128)(2,1)S(1)}, u32[]{:S(2)}, u32[]{:S(2)}) collective-permute-start(bf16[16,2048]{1,0:T(8,128)(2,1)S(1)} %target.1.target_own), channel_id=1, source_target_pairs={{0,4},{4,0},{1,5},{5,1},{2,6},{6,2},{3,7},{7,3},{8,12},{12,8},{9,1... | collective-permute-start | bytes 196616 | tf_op jit(solution)/shard_map/ppermute | solution.py:500
  98.0 7.1 %collective-permute-start.20 = (bf16[1,16,4224]{2,1,0:T(8,128)(2,1)S(1)}, bf16[1,16,4224]{2,1,0:T(8,128)(2,1)S(1)}, u32[]{:S(2)}, u32[]{:S(2)}) collective-permute-start(bf16[1,16,4224]{2,1,0:T(8,128)(2,1)S(1)} %bitcast.19), channel_id=1, source_target_pairs={{0,1},{1,2},{2,3},{3,0},{4,5},{5,6},{6,7},{7,4},{8,9},{9,10},{10,1... | collective-permute-start | bytes 405512 | tf_op jit(solution)/shard_map/ppermute | solution.py:575
  98.0 8.9 %collective-permute-start.21 = (bf16[1,16,4224]{2,1,0:T(8,128)(2,1)S(1)}, bf16[1,16,4224]{2,1,0:T(8,128)(2,1)S(1)}, u32[]{:S(2)}, u32[]{:S(2)}) collective-permute-start(bf16[1,16,4224]{2,1,0:T(8,128)(2,1)S(1)} %bitcast.20), channel_id=1, source_target_pairs={{0,2},{1,3},{2,0},{3,1},{4,6},{5,7},{6,4},{7,5},{8,10},{9,11},{10,... | collective-permute-start | bytes 405512 | tf_op jit(solution)/shard_map/ppermute | solution.py:575
  98.8 8.1 %collective-permute-start.22 = (bf16[1,16,4224]{2,1,0:T(8,128)(2,1)S(1)}, bf16[1,16,4224]{2,1,0:T(8,128)(2,1)S(1)}, u32[]{:S(2)}, u32[]{:S(2)}) collective-permute-start(bf16[1,16,4224]{2,1,0:T(8,128)(2,1)S(1)} %bitcast.21), channel_id=1, source_target_pairs={{0,3},{1,0},{2,1},{3,2},{4,7},{5,4},{6,5},{7,6},{8,11},{9,8},{10,9... | collective-permute-start | bytes 405512 | tf_op jit(solution)/shard_map/ppermute | solution.py:575
  107.0 8.2 %collective-permute-start.23 = (bf16[3,16,4224]{2,1,0:T(8,128)(2,1)S(1)}, bf16[3,16,4224]{2,1,0:T(8,128)(2,1)S(1)}, u32[]{:S(2)}, u32[]{:S(2)}) collective-permute-start(bf16[3,16,4224]{2,1,0:T(8,128)(2,1)S(1)} %constant_dynamic-update-slice_fusion.refs_4_), channel_id=1, source_target_pairs={{0,16},{8,24},{16,0},{24,8},{1,17},{9,25},{17,1},{25,9},{2,18},{10... | collective-permute-start | bytes 1216520 | tf_op jit(solution)/shard_map/ppermute | solution.py:503
  108.5 9.6 %collective-permute-start = (bf16[64,2176]{1,0:T(8,128)(2,1)S(1)}, bf16[64,2176]{1,0:T(8,128)(2,1)S(1)}, u32[]{:S(2)}, u32[]{:S(2)}) collective-permute-start(bf16[64,2176]{1,0:T(8,128)(2,1)S(1)} %get-tuple-element.34.refs_0_), channel_id=1, source_target_pairs={{0,16},{8,24},{16,0},{24,8},{1,17},{9,25},{17,1},{25,9},{2,18},{10... | collective-permute-start | bytes 835592 | tf_op jit(solution)/shard_map/ppermute | solution.py:503
  109.1 10.6 %collective-permute-start.1 = (bf16[64,2176]{1,0:T(8,128)(2,1)S(1)}, bf16[64,2176]{1,0:T(8,128)(2,1)S(1)}, u32[]{:S(2)}, u32[]{:S(2)}) collective-permute-start(bf16[64,2176]{1,0:T(8,128)(2,1)S(1)} %get-tuple-element.34.refs_0_), channel_id=1, source_target_pairs={{0,8},{8,0},{16,24},{24,16},{1,9},{9,1},{17,25},{25,17},{2,10},{10... | collective-permute-start | bytes 835592 | tf_op jit(solution)/shard_map/ppermute | solution.py:503
  109.1 16.4 %collective-permute-start.24 = (bf16[3,16,4224]{2,1,0:T(8,128)(2,1)S(1)}, bf16[3,16,4224]{2,1,0:T(8,128)(2,1)S(1)}, u32[]{:S(2)}, u32[]{:S(2)}) collective-permute-start(bf16[3,16,4224]{2,1,0:T(8,128)(2,1)S(1)} %constant_dynamic-update-slice_fusion.refs_4_), channel_id=1, source_target_pairs={{0,8},{8,0},{16,24},{24,16},{1,9},{9,1},{17,25},{25,17},{2,10},{10... | collective-permute-start | bytes 1216520 | tf_op jit(solution)/shard_map/ppermute | solution.py:503
  115.2 10.3 %collective-permute-start.25 = (bf16[3,16,4224]{2,1,0:T(8,128)(2,1)S(1)}, bf16[3,16,4224]{2,1,0:T(8,128)(2,1)S(1)}, u32[]{:S(2)}, u32[]{:S(2)}) collective-permute-start(bf16[3,16,4224]{2,1,0:T(8,128)(2,1)S(1)} %collective-permute-done.23.refs_5_), channel_id=1, source_target_pairs={{0,8},{8,0},{16,24},{24,16},{1,9},{9,1},{17,25},{25,17},{2,10},{10... | collective-permute-start | bytes 1216520 | tf_op jit(solution)/shard_map/ppermute | solution.py:503
  118.1 6.0 %collective-permute-start.2 = (bf16[64,2176]{1,0:T(8,128)(2,1)S(1)}, bf16[64,2176]{1,0:T(8,128)(2,1)S(1)}, u32[]{:S(2)}, u32[]{:S(2)}) collective-permute-start(bf16[64,2176]{1,0:T(8,128)(2,1)S(1)} %collective-permute-done.refs_1_), channel_id=1, source_target_pairs={{0,8},{8,0},{16,24},{24,16},{1,9},{9,1},{17,25},{25,17},{2,10},{10... | collective-permute-start | bytes 835592 | tf_op jit(solution)/shard_map/ppermute | solution.py:503
  118.1 6.0 %collective-permute-start.17 = (bf16[1,16,4224]{2,1,0:T(8,128)(2,1)S(1)}, bf16[1,16,4224]{2,1,0:T(8,128)(2,1)S(1)}, u32[]{:S(2)}, u32[]{:S(2)}) collective-permute-start(bf16[1,16,4224]{2,1,0:T(8,128)(2,1)S(1)} %bitcast.22), channel_id=1, source_target_pairs={{0,16},{8,24},{16,0},{24,8},{1,17},{9,25},{17,1},{25,9},{2,18},{10... | collective-permute-start | bytes 405512 | tf_op jit(solution)/shard_map/ppermute | solution.py:503
  119.6 5.3 %collective-permute-start.18 = (bf16[1,16,4224]{2,1,0:T(8,128)(2,1)S(1)}, bf16[1,16,4224]{2,1,0:T(8,128)(2,1)S(1)}, u32[]{:S(2)}, u32[]{:S(2)}) collective-permute-start(bf16[1,16,4224]{2,1,0:T(8,128)(2,1)S(1)} %bitcast.23), channel_id=1, source_target_pairs={{0,8},{8,0},{16,24},{24,16},{1,9},{9,1},{17,25},{25,17},{2,10},{10... | collective-permute-start | bytes 405512 | tf_op jit(solution)/shard_map/ppermute | solution.py:503
  124.1 1.4 %collective-permute-start.19 = (bf16[1,16,4224]{2,1,0:T(8,128)(2,1)S(1)}, bf16[1,16,4224]{2,1,0:T(8,128)(2,1)S(1)}, u32[]{:S(2)}, u32[]{:S(2)}) collective-permute-start(bf16[1,16,4224]{2,1,0:T(8,128)(2,1)S(1)} %collective-permute-done.17.refs_1_), channel_id=1, source_target_pairs={{0,8},{8,0},{16,24},{24,16},{1,9},{9,1},{17,25},{25,17},{2,10},{10... | collective-permute-start | bytes 405512 | tf_op jit(solution)/shard_map/ppermute | solution.py:503

commit v5 on v4

--- a/solution.py
+++ b/solution.py
@@ -20,6 +20,7 @@
 f32 = jnp.float32
 bf16 = jnp.bfloat16
 vmem_limit = 24 * 2**20
+group_size = 4
 
 
 def folded_ring(size):
@@ -133,7 +134,22 @@
 
 
 def score_kernel(
-    t, base_at, info, positions, mine, other, keys, top_before, mass_before, weights, top, top_all, mass_all, mass
+    t,
+    base_at,
+    info,
+    positions,
+    mine,
+    other,
+    keys,
+    top_before,
+    mass_before,
+    weights,
+    top,
+    top_all,
+    mass_all,
+    mass,
+    even,
+    odd,
 ):
     count, heads, depth = mine.shape
     limits = [positions[info[0] * count + q] - info[base_at] for q in range(count)]
@@ -141,31 +157,39 @@
     key_at = lax.broadcasted_iota(jnp.int32, (1, span), 1)
     row_at = lax.broadcasted_iota(jnp.int32, (heads, lanes), 0)
     lane_at = lax.broadcasted_iota(jnp.int32, (heads, lanes), 1)
-    group = min(8, count)
-    for at in range(0, count, group):
-        for source, offset in ((mine, 0), (other, heads)):
-            rows = source[at : at + group].reshape(group * heads, depth)
-            scores = times(rows, keys[...], 1, 0)
-            diagonal = lane_at == row_at + offset
-            blocks = [scores[k * heads : (k + 1) * heads] for k in range(group)]
-            seen = [key_at <= limits[at + k] for k in range(group)]
-            blocks = [jnp.where(seen[k], blocks[k], masked_floor) for k in range(group)]
-            highs = [jnp.max(one, axis=1, keepdims=True) for one in blocks]
-            totals = []
-            for k in range(group):
-                shifted = jnp.exp2((blocks[k] - highs[k]) * exponent_scale)
-                weights[at + k, offset : offset + heads] = shifted.astype(bf16)
-                totals.append(jnp.sum(shifted, axis=1, keepdims=True))
-            for k in range(group):
-                q = at + k
-                high_row = jnp.sum(jnp.where(diagonal, highs[k], 0.0), axis=0, keepdims=True)
-                total_row = jnp.sum(jnp.where(diagonal, totals[k], 0.0), axis=0, keepdims=True)
-                if offset == 0:
-                    top[q : q + 1, :] = high_row
-                    mass[q : q + 1, :] = total_row
-                else:
-                    top[q : q + 1, :] += high_row
-                    mass[q : q + 1, :] += total_row
+    group = min(group_size, count)
+    work = [(at, k) for at in range(0, count, group) for k in range(2)]
+    held = (even, odd)
+
+    def multiply(step):
+        at, k = work[step]
+        rows = (mine, other)[k][at : at + group].reshape(group * heads, depth)
+        held[step % 2][...] = times(rows, keys[...], 1, 0)
+
+    multiply(0)
+    for step, (at, k) in enumerate(work):
+        if step + 1 < len(work):
+            multiply(step + 1)
+        scores = held[step % 2]
+        offset = k * heads
+        diagonal = lane_at == row_at + offset
+        for i in range(group):
+            q = at + i
+            one = jnp.where(
+                key_at <= limits[q], scores[i * heads : (i + 1) * heads, :], masked_floor
+            )
+            high = jnp.max(one, axis=1, keepdims=True)
+            shifted = jnp.exp2((one - high) * exponent_scale)
+            total = jnp.sum(shifted, axis=1, keepdims=True)
+            weights[q, offset : offset + heads] = shifted.astype(bf16)
+            high_row = jnp.sum(jnp.where(diagonal, high, 0.0), axis=0, keepdims=True)
+            total_row = jnp.sum(jnp.where(diagonal, total, 0.0), axis=0, keepdims=True)
+            if k == 0:
+                top[q : q + 1, :] = high_row
+                mass[q : q + 1, :] = total_row
+            else:
+                top[q : q + 1, :] += high_row
+                mass[q : q + 1, :] += total_row
     if t == 0:
         top_all[...] = top[...]
         mass_all[...] = mass[...]
@@ -189,7 +213,8 @@
         out_shape=(jax.ShapeDtypeStruct((count, 2 * heads, span), bf16), stats, stats, stats),
         in_specs=[in_smem()] * 2 + [in_vmem()] * 5,
         out_specs=(in_vmem(),) * 4,
-        scratch_shapes=[pltpu.VMEM((count, lanes), f32)],
+        scratch_shapes=[pltpu.VMEM((count, lanes), f32)]
+        + [pltpu.VMEM((min(group_size, count) * heads, span), f32)] * 2,
         compiler_params=params(),
         cost_estimate=pl.CostEstimate(
             flops=4 * count * heads * depth * span,
@@ -200,9 +225,9 @@
     )(info, positions, mine, other, keys, *before)
 
 
-def target_kernel(blocks, *refs):
+def delta_kernel(blocks, *refs):
     weights, tops = refs[:blocks], refs[blocks : 2 * blocks]
-    top, mass, far, out, held = refs[2 * blocks :]
+    top, mass, far, probs, out, sent, held = refs[2 * blocks :]
     count, heads, span = weights[0].shape
     far_top = pltpu.roll(far[0], heads // 2, 1)
     far_mass = pltpu.roll(far[1], heads // 2, 1)
@@ -222,17 +247,22 @@
             )
             mixed = weights[t][q].astype(f32) * column
             held[q : q + 1, t * span : (t + 1) * span] = jnp.sum(mixed, axis=0, keepdims=True)
-    out[...] = held[...].astype(bf16)
-
-
-def make_target(weights, tops, top, mass, far):
+    delta = probs[0] - held[...]
+    out[...] = delta
+    sent[...] = delta.astype(bf16)
+
+
+def make_delta(weights, tops, top, mass, far, probs):
     blocks = len(weights)
     count, heads, span = weights[0].shape
     return pl.pallas_call(
-        functools.partial(target_kernel, blocks),
-        out_shape=jax.ShapeDtypeStruct((count, blocks * span), bf16),
-        in_specs=[in_vmem()] * (2 * blocks + 3),
-        out_specs=in_vmem(),
+        functools.partial(delta_kernel, blocks),
+        out_shape=(
+            jax.ShapeDtypeStruct((count, blocks * span), f32),
+            jax.ShapeDtypeStruct((count, blocks * span), bf16),
+        ),
+        in_specs=[in_vmem()] * (2 * blocks + 4),
+        out_specs=(in_vmem(),) * 2,
         scratch_shapes=[pltpu.VMEM((count, blocks * span), f32)],
         compiler_params=params(),
         cost_estimate=pl.CostEstimate(
@@ -240,8 +270,8 @@
             bytes_accessed=2 * blocks * count * heads * span,
             transcendentals=0,
         ),
-        name="target",
-    )(*weights, *tops, top, mass, far)
+        name="delta",
+    )(*weights, *tops, top, mass, far, probs)
 
 
 def query_rows(total, heads):
@@ -283,20 +313,15 @@
     )(received, here, own, other)
 
 
-def gradient_kernel(
-    heads, blocks, info, positions, received, here, own, other, part, far, target_own, target_other, out, logit, flow
-):
-    count = received.shape[0]
-    total = received[...] + here[...]
-    span = own.shape[0] // blocks
-    query = query_rows(total, heads)
+def softmax_kernel(blocks, info, positions, part, far, probs, log_probs):
+    _, count, length = part.shape
+    span = length // blocks
     row_at = lax.broadcasted_iota(jnp.int32, (count, lanes), 0)
     position = jnp.zeros((count, lanes), jnp.int32)
     for q in range(count):
         position = jnp.where(row_at == q, positions[info[0] * count + q], position)
     position = position[:, 0:1]
     key_at = lax.broadcasted_iota(jnp.int32, (count, span), 1)
-    sides = ((own, target_own), (other, target_other))
 
     def seen(side, t):
         return key_at + info[1 + (1 + side) * blocks + t] <= position
@@ -307,7 +332,7 @@
         for t in range(blocks):
             at = slice(t * span, (t + 1) * span)
             value = part[side, :, at] + far[1 - side, :, at]
-            logit[side, :, at] = value
+            log_probs[side, :, at] = value
             high = jnp.maximum(high, jnp.where(seen(side, t), value, masked_floor))
         highs.append(jnp.max(high, axis=1, keepdims=True))
     high = jnp.maximum(highs[0], highs[1])
@@ -316,48 +341,103 @@
         running = jnp.zeros((count, span), f32)
         for t in range(blocks):
             at = slice(t * span, (t + 1) * span)
-            grown = jnp.exp(logit[side, :, at] - high)
-            running = running + jnp.where(seen(side, t), grown, 0.0)
+            grown = jnp.where(seen(side, t), jnp.exp(log_probs[side, :, at] - high), 0.0)
+            probs[side, :, at] = grown
+            running = running + grown
         sums.append(jnp.sum(running, axis=1, keepdims=True))
     mass = sums[0] + sums[1]
     level = high + jnp.log(mass)
     inverse = 1.0 / mass
+    for side in range(2):
+        for t in range(blocks):
+            at = slice(t * span, (t + 1) * span)
+            probs[side, :, at] = probs[side, :, at] * inverse
+            log_probs[side, :, at] = jnp.where(seen(side, t), log_probs[side, :, at] - level, 0.0)
+
+
+def make_softmax(blocks, info, positions, part, far):
+    return pl.pallas_call(
+        functools.partial(softmax_kernel, blocks),
+        out_shape=(jax.ShapeDtypeStruct(part.shape, f32),) * 2,
+        in_specs=[in_smem()] * 2 + [in_vmem()] * 2,
+        out_specs=(in_vmem(),) * 2,
+        compiler_params=params(),
+        cost_estimate=pl.CostEstimate(
+            flops=8 * part.size, bytes_accessed=16 * part.size, transcendentals=part.size
+        ),
+        name="softmax",
+    )(info, positions, part, far)
+
+
+def gradient_kernel(
+    heads,
+    blocks,
+    received,
+    here,
+    own,
+    other,
+    probs,
+    log_probs,
+    delta_own,
+    sent,
+    brought,
+    out,
+    flow,
+    query_sum,
+    grads,
+    even,
+    odd,
+):
+    count = received.shape[0]
+    total = received[...] + here[...]
+    span = own.shape[0] // blocks
+    query = query_rows(total, heads)
     columns = [
         total[:, heads * DI + j : heads * DI + j + 1] * index_scale for j in range(heads)
     ]
-    losses = []
-    query_sum = jnp.zeros((heads * count, DI), f32)
+    work = [(side, t) for side in range(2) for t in range(blocks)]
+    held = (even, odd)
+
+    def multiply(step):
+        side, t = work[step]
+        keys = (own, other)[side][t * span : (t + 1) * span, :]
+        held[step % 2][...] = times(query, keys, 1, 1)
+
+    multiply(0)
     flow[...] = jnp.zeros(flow.shape, f32)
-    for side, (keys, target) in enumerate(sides):
-        running = jnp.zeros((count, span), f32)
-        for t in range(blocks):
-            at = slice(t * span, (t + 1) * span)
-            visible = seen(side, t)
-            value = logit[side, :, at]
-            wanted = target[:, at].astype(f32)
-            running = running + jnp.where(visible, wanted * (value - level), 0.0)
-            grown = jnp.exp(value - high) * inverse
-            delta = jnp.where(visible, grown - wanted, 0.0)
-            affinity = times(query, keys[at, :], 1, 1)
-            grads = []
-            for j in range(heads):
-                rows = slice(j * count, (j + 1) * count)
-                one = affinity[rows]
-                reached = jnp.where(one > 0, delta, 0.0)
-                grads.append((reached * columns[j]).astype(bf16))
-                product = reached * one
-                folded = product[:, :lanes]
-                for k in range(lanes, span, lanes):
-                    folded = folded + product[:, k : k + lanes]
-                flow[rows, :] += folded
-            query_sum = query_sum + times(jnp.concatenate(grads, axis=0), keys[at, :], 1, 0)
-        losses.append(jnp.sum(running, axis=1, keepdims=True))
+    running = [jnp.zeros((count, span), f32)] * 2
+    for step, (side, t) in enumerate(work):
+        if step + 1 < len(work):
+            multiply(step + 1)
+        at = slice(t * span, (t + 1) * span)
+        affinity = held[step % 2]
+        rounded = (sent, brought)[side][:, at].astype(f32)
+        delta = delta_own[:, at] if side == 0 else rounded
+        wanted = probs[side, :, at] - rounded
+        running[side] = running[side] + wanted * log_probs[side, :, at]
+        for j in range(heads):
+            rows = slice(j * count, (j + 1) * count)
+            one = affinity[rows, :]
+            reached = jnp.where(one > 0, delta, 0.0)
+            grads[rows, :] = (reached * columns[j]).astype(bf16)
+            product = reached * one
+            folded = product[:, :lanes]
+            for k in range(lanes, span, lanes):
+                folded = folded + product[:, k : k + lanes]
+            flow[rows, :] += folded
+        keys = (own, other)[side][at, :]
+        product = times(grads[...], keys, 1, 0)
+        if step == 0:
+            query_sum[...] = product
+        else:
+            query_sum[...] += product
+    losses = [jnp.sum(one, axis=1, keepdims=True) for one in running]
     loss = -(losses[0] + losses[1])
     lane_at = lax.broadcasted_iota(jnp.int32, (count, lanes), 1)
     tail = jnp.zeros((count, lanes), f32)
     for j in range(heads):
         rows = slice(j * count, (j + 1) * count)
-        out[:, j * DI : (j + 1) * DI] = query_sum[rows].astype(bf16)
+        out[:, j * DI : (j + 1) * DI] = query_sum[rows, :].astype(bf16)
         column = jnp.sum(flow[rows, :], axis=1, keepdims=True) * index_scale
         tail = jnp.where(lane_at == j, column, tail)
     loss_high = loss.astype(bf16).astype(f32)
@@ -366,25 +446,29 @@
     out[:, heads * DI :] = tail.astype(bf16)
 
 
-def gradients(heads, blocks, info, positions, received, here, own, other, part, far, target_own, target_other):
+def gradients(heads, blocks, received, here, own, other, probs, log_probs, delta_own, sent, brought):
     count, length = received.shape[0], own.shape[0]
+    span = length // blocks
     return pl.pallas_call(
         functools.partial(gradient_kernel, heads, blocks),
         out_shape=jax.ShapeDtypeStruct((count, heads * DI + lanes), bf16),
-        in_specs=[in_smem()] * 2 + [in_vmem()] * 8,
+        in_specs=[in_vmem()] * 9,
         out_specs=in_vmem(),
         scratch_shapes=[
-            pltpu.VMEM((2, count, length), f32),
             pltpu.VMEM((heads * count, lanes), f32),
+            pltpu.VMEM((heads * count, DI), f32),
+            pltpu.VMEM((heads * count, span), bf16),
+            pltpu.VMEM((heads * count, span), f32),
+            pltpu.VMEM((heads * count, span), f32),
         ],
         compiler_params=params(),
         cost_estimate=pl.CostEstimate(
             flops=8 * count * heads * DI * length,
             bytes_accessed=4 * (2 * received.size + 6 * count * length) + 4 * length * DI,
-            transcendentals=4 * count * length,
+            transcendentals=0,
         ),
         name="gradient",
-    )(info, positions, received, here, own, other, part, far, target_own, target_other)
+    )(received, here, own, other, probs, log_probs, delta_own, sent, brought)
 
 
 def arrange_kernel(at, info, *refs):
@@ -418,54 +502,54 @@
 
 
 def outer_kernel(heads, order, dp_at, info, latents, hiddens, *refs):
-    parts, (grad, grad_mixed, losses, rows) = refs[:-4], refs[-4:]
+    parts, (grad, grad_mixed, losses, rows, blocks, sems) = refs[:-6], refs[-6:]
     count = parts[0].shape[-2]
     width = heads * DI
-    span = grad.shape[1]
-    step = pl.program_id(0)
-
-    @pl.when(step == 0)
-    def _():
-        k = 0
-        for part in parts:
-            for t in range(part.shape[0]):
-                to = 0 if order is None else pl.multiple_of(info[order[k]] * count, count)
-                rows[pl.ds(to, count), :] = part[t]
-                k += 1
-        tails = rows[:, width:]
-        grad_mixed[...] = times(tails, hiddens[...], 0, 0)[:heads]
-        own = losses.shape[1]
-        from_own = rows[pl.ds(pl.multiple_of(info[dp_at] * own, own), own), width:].astype(f32)
-        column = from_own[:, heads : heads + 1] + from_own[:, heads + 1 : heads + 2]
-        diagonal = lax.broadcasted_iota(jnp.int32, (own, own), 0) == lax.broadcasted_iota(
-            jnp.int32, (own, own), 1
-        )
-        losses[...] = jnp.sum(jnp.where(diagonal, column, 0.0), axis=0, keepdims=True)
-
-    at = pl.ds(pl.multiple_of(step * span, span), span)
-    grad[...] = times(latents[...], rows[:, at], 1, 0)
+    steps, _, span = blocks.shape
+    k = 0
+    for part in parts:
+        for t in range(part.shape[0]):
+            to = 0 if order is None else pl.multiple_of(info[order[k]] * count, count)
+            rows[pl.ds(to, count), :] = part[t]
+            k += 1
+    copies = []
+    for i in range(steps):
+        at = slice(i * span, (i + 1) * span)
+        blocks[i] = times(latents[...], rows[:, at], 1, 0)
+        copies.append(pltpu.make_async_copy(blocks.at[i], grad.at[:, at], sems.at[i]))
+        copies[-1].start()
+    tails = rows[:, width:]
+    grad_mixed[...] = times(tails, hiddens[...], 0, 0)[:heads]
+    own = losses.shape[1]
+    from_own = rows[pl.ds(pl.multiple_of(info[dp_at] * own, own), own), width:].astype(f32)
+    column = from_own[:, heads : heads + 1] + from_own[:, heads + 1 : heads + 2]
+    diagonal = lax.broadcasted_iota(jnp.int32, (own, own), 0) == lax.broadcasted_iota(
+        jnp.int32, (own, own), 1
+    )
+    losses[...] = jnp.sum(jnp.where(diagonal, column, 0.0), axis=0, keepdims=True)
+    for copy in copies:
+        copy.wait()
 
 
 def outer(heads, order, dp_at, queries, info, latents, hiddens, parts):
     row_count, total = latents.shape
     width = heads * DI
-    span = 512
+    steps = 8
     hidden_count = hiddens.shape[1]
     return pl.pallas_call(
         functools.partial(outer_kernel, heads, order, dp_at),
-        grid=(width // span,),
         out_shape=(
             jax.ShapeDtypeStruct((row_count, width), f32),
             jax.ShapeDtypeStruct((heads, hidden_count), f32),
             jax.ShapeDtypeStruct((1, queries), f32),
         ),
         in_specs=[in_smem()] + [in_vmem()] * (2 + len(parts)),
-        out_specs=(
-            pl.BlockSpec((row_count, span), lambda i: (0, i)),
-            pl.BlockSpec((heads, hidden_count), lambda i: (0, 0)),
-            pl.BlockSpec((1, queries), lambda i: (0, 0)),
-        ),
-        scratch_shapes=[pltpu.VMEM((total, width + lanes), bf16)],
+        out_specs=(pl.BlockSpec(memory_space=pl.ANY), in_vmem(), in_vmem()),
+        scratch_shapes=[
+            pltpu.VMEM((total, width + lanes), bf16),
+            pltpu.VMEM((steps, row_count, width // steps), f32),
+            pltpu.SemaphoreType.DMA((steps,)),
+        ],
         compiler_params=params(),
         cost_estimate=pl.CostEstimate(
             flops=2 * total * row_count * width,
@@ -515,12 +599,12 @@
     keys_mine.append(onward(keys_mine[0]))
     queries = main_queries[0]
     other_queries = swap_head(queries)
-    index_part = lax.dynamic_slice_in_dim(index_keys[0], y * half, half)
-    index_own = jnp.concatenate([index_part] + [onward(index_part, t) for t in range(1, n)])
-    parts, kept = project(
-        info, queries_here, q_latent[0], w_query, hidden[0], w_weights.T
-    )
+    index_parts = [lax.dynamic_slice_in_dim(index_keys[0], y * half, half)]
+    index_parts += [onward(index_parts[0], t) for t in range(1, n - 1)]
+    parts, kept = project(info, queries_here, q_latent[0], w_query, hidden[0], w_weights.T)
     received = onward(parts[0])
+    order_at = 1 + 3 * n
+    dp_at = order_at + n * dp_size
     weights, tops, before = [], [], None
 
     def score_next(keys):
@@ -532,9 +616,16 @@
         weights.append(numer)
         tops.append(top)
 
+    index_own = index_other = None
     for t in range(1, n - 1):
         summed = received + parts[t]
         if t == 1:
+            keys, summed, index_parts = lax.optimization_barrier(
+                (keys_mine[t], summed, index_parts)
+            )
+            index_parts.append(onward(index_parts[0], n - 1))
+        elif t == 2:
+            index_own = jnp.concatenate(index_parts)
             keys, summed, index_own = lax.optimization_barrier((keys_mine[t], summed, index_own))
             index_other = swap_head(index_own)
         else:
@@ -542,31 +633,29 @@
         keys_mine[t] = keys
         keys_mine.append(onward(keys))
         received = onward(summed)
-    while len(weights) < n - 1:
+    while len(weights) < n - 2:
         score_next(keys_mine[len(weights)])
+    latents, hiddens = arrange(dp_at, info, rows_latent, over_dp(kept))
+    before, latents, hiddens = lax.optimization_barrier((before, latents, hiddens))
+    score_next(keys_mine[n - 2])
 
     part = make_logits(heads_here, received, parts[n - 1], index_own, index_other)
-    far = swap_head(part)
-    order_at = 1 + 3 * n
-    dp_at = order_at + n * dp_size
-    latents, hiddens = arrange(dp_at, info, rows_latent, over_dp(kept))
+    probs, log_probs = make_softmax(n, info, sequence_positions, part, swap_head(part))
 
     score_next(keys_mine[n - 1])
-    target_own = make_target(weights, tops, *before, swap_head(jnp.stack(before)))
-    target_other = swap_head(target_own)
+    delta_own, sent = make_delta(weights, tops, *before, swap_head(jnp.stack(before)), probs)
     piece = gradients(
         heads_here,
         n,
-        info,
-        sequence_positions,
         received,
         parts[n - 1],
         index_own,
         index_other,
-        part,
-        far,
-        target_own,
-        target_other,
+        probs,
+        log_probs,
+        delta_own,
+        sent,
+        swap_head(sent),
     )[None]
 
     brought = []
@@ -574,7 +663,8 @@
         pairs = [(k, (k + t) % n) for k in range(n)]
         brought.append(lax.ppermute(piece, "ctx", pairs))
     own_pieces = over_dp(piece)
-    brought = over_dp(jnp.concatenate(brought))
+    brought, own_pieces = lax.optimization_barrier((jnp.concatenate(brought), own_pieces))
+    brought = over_dp(brought)
     if queries_here % 16:
         flat = jnp.concatenate([jnp.concatenate([a, b]) for a, b in zip(own_pieces, brought)])
         order = jnp.argsort(info[order_at : order_at + n * dp_size])

time: 132 us -> 131 us (level); the launches traced: 131 us -> 128 us
  waiting for transfers between devices: 60.3 us -> 67.5 us
  starting transfers between devices: 34.6 us -> 28.6 us
  Pallas kernels: 28.9 us -> 24.1 us
    ppermute x9, waiting for transfers between devices: 36 us -> 47.8 us  [onward(): lax.ppermute(x, 'ctx', [(ring[k], ring[(k + t) % n]) for k in range(n)])]
    ppermute x9, starting transfers between devices: 20.3 us -> 13.7 us  [onward(): lax.ppermute(x, 'ctx', [(ring[k], ring[(k + t) % n]) for k in range(n)])]
    ppermute x9, waiting for transfers between devices: 13.4 us -> 9.25 us  [swap_dp(): return lax.ppermute(x, 'dp', [(k, k ^ bit) for k in range(dp_size)])]
    pallas_call x4, Pallas kernels: 13.9 us -> 10.7 us  [score(): pl.pallas_call(functools.partial(score_kernel, t, 1 + n + t), out_shape=(...]
    ppermute x5, waiting for transfers between devices: 5.82 us -> 4.15 us  [swap_head(): return lax.ppermute(x, 'head', [(0, 1), (1, 0)])]
    pallas_call x2 -> x3, Pallas kernels: 8.11 us -> 7.36 us  [the longest x1 4.38 us: outer(): pl.pallas_call(functools.partial(outer_kernel, heads, order, dp_at), out_...]
  transfers between devices with their start and end apart: 26 -> 26, of which waited for: 12 -> 14; matrix products, arithmetic and copies ran while one was open for 1% -> 1% of each run, Pallas kernels for 15% -> 12%
where the time goes in v5:
time: 131 us; the launch traced here: 128 us
  waiting for transfers between devices  67.5 us (52%)
  starting transfers between devices  28.6 us (22%)
  Pallas kernels  24.1 us (18%)
  local copies, waits for them, and re-layouts  6.92 us (5%)
    ppermute x9, waiting for transfers between devices, onward(): lax.ppermute(x, 'ctx', [(ring[k], ring[(k + t) % n]) for k in range(n)])  47.8 us
    ppermute x9, starting transfers between devices, onward(): lax.ppermute(x, 'ctx', [(ring[k], ring[(k + t) % n]) for k in range(n)])  13.7 us
    pallas_call x4, Pallas kernels, score(): pl.pallas_call(functools.partial(score_kernel, t, 1 + n + t), out_shape=(...  10.7 us
    ppermute x9, waiting for transfers between devices, swap_dp(): return lax.ppermute(x, 'dp', [(k, k ^ bit) for k in range(dp_size)])  9.25 us
    ppermute x5, starting transfers between devices, swap_head(): return lax.ppermute(x, 'head', [(0, 1), (1, 0)])  6.85 us
    ppermute x3, waiting for transfers between devices, per_device(): brought.append(lax.ppermute(piece, 'ctx', pairs))  6.26 us
    unnamed x16, local copies, waits for them, and re-layouts  6.17 us
    pallas_call x1, Pallas kernels, outer(): pl.pallas_call(functools.partial(outer_kernel, heads, order, dp_at), out_...  4.38 us
  transfers between devices with their start and end apart: 26, of which 14 were waited for; matrix products, arithmetic and copies ran while one was open for 1% of the time, Pallas kernels for 12%

profile of v5, /device:TPU:0, one launch (start us, length us, event | category | flops | bytes accessed | tf_op | source)
XLA Modules:
  0.0 128.2 jit_solution(12264030850160671293)
XLA Ops:
  0.7 1.3 copy-done
  2.0 3.1 %collective-permute-start.1 = (bf16[576,512]{1,0:T(8,128)(2,1)S(1)}, bf16[576,512]{1,0:T(8,128)(2,1)}, u32[]{:S(2)}, u32[]{:S(2)}) collective-permute-start(bf16[576,512]{1,0:T(8,128)(2,1)S(1)} %dynamic-slice_bitcast_fusion.keys), channel_id=1, source_target_pairs={{0,1},{1,3},{3,2},{2,0},{4,5},{5,7},{7,6},{6,4},{8,9},{9,11},{11,1... | collective-permute-start | bytes 1769480 | tf_op jit(solution)/shard_map/ppermute | solution.py:581
  5.0 1.5 %collective-permute-start = (bf16[16,64,576]{2,1,0:T(8,128)(2,1)}, bf16[16,64,576]{2,1,0:T(8,128)(2,1)S(1)}, u32[]{:S(2)}, u32[]{:S(2)}) collective-permute-start(bf16[16,64,576]{2,1,0:T(8,128)(2,1)} %bitcast.33), channel_id=1, source_target_pairs={{0,4},{4,0},{1,5},{5,1},{2,6},{6,2},{3,7},{7,3},{8,12},{12,8},{9,1... | collective-permute-start | bytes 3538952 | tf_op jit(solution)/shard_map/ppermute | solution.py:584
  6.6 0.7 fusion.info
  7.2 1.9 %copy-done.1 = bf16[384,4096]{1,0:T(8,128)(2,1)S(1)} copy-done((bf16[384,4096]{1,0:T(8,128)(2,1)S(1)}, bf16[384,4096]{1,0:T(8,128)(2,1)}, u32[]{:S(2)}) %copy-start.1) | copy-done | bytes 3145752
  9.1 1.2 copy-done.2
  10.3 0.9 copy-done.3
  11.2 0.9 copy-done.4
  12.1 1.3 %project.1 = (f32[16,4224]{1,0:T(8,128)S(1)}, f32[16,4224]{1,0:T(8,128)S(1)}, f32[16,4224]{1,0:T(8,128)S(1)}, f32[16,4224]{1,0:T(8,128)S(1)}, bf16[64,2176]{1,0:T(8,128)(2,1)S(1)}) custom-call(s32[33]{0:T(128)S(1)} %fusion.info, bf16[64,1536]{1,0:T(8,128)(2,1)S(1)} %bitcast.18, bf16[384,4096]{1,0:T(8,128)(2,1)S(1)} %copy-done.1, ...), custom_call_target="tpu_custom_call" | custom-call | flops 201326592 | bytes 3145728 | tf_op jit(solution)/shard_map/project/pallas_call | solution.py:111
  13.5 2.7 %collective-permute-start.2 = (f32[16,4224]{1,0:T(8,128)S(1)}, f32[16,4224]{1,0:T(8,128)S(1)}, u32[]{:S(2)}, u32[]{:S(2)}) collective-permute-start(f32[16,4224]{1,0:T(8,128)S(1)} %get-tuple-element.50), channel_id=1, source_target_pairs={{0,1},{1,3},{3,2},{2,0},{4,5},{5,7},{7,6},{6,4},{8,9},{9,11},{11,1... | collective-permute-start | bytes 811016 | tf_op jit(solution)/shard_map/ppermute | solution.py:581
  16.1 0.5 collective-permute-start.3
  16.6 1.3 %collective-permute-start.4 = (bf16[512,128]{1,0:T(8,128)(2,1)S(1)}, bf16[512,128]{1,0:T(8,128)(2,1)S(1)}, u32[]{:S(2)}, u32[]{:S(2)}) collective-permute-start(bf16[512,128]{1,0:T(8,128)(2,1)S(1)} %dynamic-slice_bitcast_fusion.1), channel_id=1, source_target_pairs={{0,3},{1,2},{3,0},{2,1},{4,7},{5,6},{7,4},{6,5},{8,11},{9,10},{11,... | collective-permute-start | bytes 393224 | tf_op jit(solution)/shard_map/ppermute | solution.py:581
  18.0 8.0 %collective-permute-done.2 = f32[16,4224]{1,0:T(8,128)S(1)} collective-permute-done((f32[16,4224]{1,0:T(8,128)S(1)}, f32[16,4224]{1,0:T(8,128)S(1)}, u32[]{:S(2)}, u32[]{:S(2)}) %collective-permute-start.2) | collective-permute-done | bytes 270368 | tf_op jit(solution)/shard_map/ppermute | solution.py:581
  26.0 3.6 %collective-permute-done.3 = bf16[512,128]{1,0:T(8,128)(2,1)S(1)} collective-permute-done((bf16[512,128]{1,0:T(8,128)(2,1)S(1)}, bf16[512,128]{1,0:T(8,128)(2,1)S(1)}, u32[]{:S(2)}, u32[]{:S(2)}) %collective-permute-start.3) | collective-permute-done | bytes 131104 | tf_op jit(solution)/shard_map/ppermute | solution.py:581
  29.6 2.5 %collective-permute-done.4 = bf16[512,128]{1,0:T(8,128)(2,1)S(1)} collective-permute-done((bf16[512,128]{1,0:T(8,128)(2,1)S(1)}, bf16[512,128]{1,0:T(8,128)(2,1)S(1)}, u32[]{:S(2)}, u32[]{:S(2)}) %collective-permute-start.4) | collective-permute-done | bytes 131104 | tf_op jit(solution)/shard_map/ppermute | solution.py:581
  32.1 2.7 %collective-permute-start.8 = (bf16[576,512]{1,0:T(8,128)(2,1)}, bf16[576,512]{1,0:T(8,128)(2,1)S(1)}, u32[]{:S(2)}, u32[]{:S(2)}) collective-permute-start(bf16[576,512]{1,0:T(8,128)(2,1)} %collective-permute-done.1.keys), channel_id=1, source_target_pairs={{0,1},{1,3},{3,2},{2,0},{4,5},{5,7},{7,6},{6,4},{8,9},{9,11},{11,1... | collective-permute-start | bytes 1769480 | tf_op jit(solution)/shard_map/ppermute | solution.py:581
  34.7 1.9 %collective-permute-start.10 = (bf16[512,128]{1,0:T(8,128)(2,1)S(1)}, bf16[512,128]{1,0:T(8,128)(2,1)S(1)}, u32[]{:S(2)}, u32[]{:S(2)}) collective-permute-start(bf16[512,128]{1,0:T(8,128)(2,1)S(1)} %dynamic-slice_bitcast_fusion.1), channel_id=1, source_target_pairs={{0,2},{1,0},{3,1},{2,3},{4,6},{5,4},{7,5},{6,7},{8,10},{9,8},{11,9... | collective-permute-start | bytes 393224 | tf_op jit(solution)/shard_map/ppermute | solution.py:581
  36.8 1.5 %collective-permute-start.5 = (bf16[64,2176]{1,0:T(8,128)(2,1)S(1)}, bf16[64,2176]{1,0:T(8,128)(2,1)S(1)}, u32[]{:S(2)}, u32[]{:S(2)}) collective-permute-start(bf16[64,2176]{1,0:T(8,128)(2,1)S(1)} %get-tuple-element.57.refs_0_), channel_id=1, source_target_pairs={{0,16},{8,24},{16,0},{24,8},{1,17},{9,25},{17,1},{25,9},{2,18},{10... | collective-permute-start | bytes 835592 | tf_op jit(solution)/shard_map/ppermute | solution.py:587
  38.3 15.8 %collective-permute-done.10 = bf16[512,128]{1,0:T(8,128)(2,1)S(1)} collective-permute-done((bf16[512,128]{1,0:T(8,128)(2,1)S(1)}, bf16[512,128]{1,0:T(8,128)(2,1)S(1)}, u32[]{:S(2)}, u32[]{:S(2)}) %collective-permute-start.10) | collective-permute-done | bytes 131104 | tf_op jit(solution)/shard_map/ppermute | solution.py:581
  54.1 3.6 %collective-permute-done.9 = f32[16,4224]{1,0:T(8,128)S(1)} collective-permute-done((f32[16,4224]{1,0:T(8,128)S(1)}, f32[16,4224]{1,0:T(8,128)S(1)}, u32[]{:S(2)}, u32[]{:S(2)}) %collective-permute-start.9) | collective-permute-done | bytes 270368 | tf_op jit(solution)/shard_map/ppermute | solution.py:581
  57.7 1.6 %collective-permute-start.12 = (bf16[2048,128]{1,0:T(8,128)(2,1)S(1)}, bf16[2048,128]{1,0:T(8,128)(2,1)S(1)}, u32[]{:S(2)}, u32[]{:S(2)}) collective-permute-start(bf16[2048,128]{1,0:T(8,128)(2,1)S(1)} %pad_maximum_fusion.own), channel_id=1, source_target_pairs={{0,4},{4,0},{1,5},{5,1},{2,6},{6,2},{3,7},{7,3},{8,12},{12,8},{9,1... | collective-permute-start | bytes 1572872 | tf_op jit(solution)/shard_map/ppermute | solution.py:584
  59.3 1.4 %collective-permute-start.11 = (f32[16,4224]{1,0:T(8,128)S(1)}, f32[16,4224]{1,0:T(8,128)S(1)}, u32[]{:S(2)}, u32[]{:S(2)}) collective-permute-start(f32[16,4224]{1,0:T(8,128)S(1)} %add.25), channel_id=1, source_target_pairs={{0,1},{1,3},{3,2},{2,0},{4,5},{5,7},{7,6},{6,4},{8,9},{9,11},{11,1... | collective-permute-start | bytes 811016 | tf_op jit(solution)/shard_map/ppermute | solution.py:581
  60.9 0.8 arrange.1
  61.7 2.5 %score.4 = (bf16[16,128,512]{2,1,0:T(8,128)(2,1)S(1)}, f32[16,128]{1,0:T(8,128)S(1)}, f32[16,128]{1,0:T(8,128)S(1)}, f32[16,128]{1,0:T(8,128)S(1)}) custom-call(s32[33]{0:T(128)S(1)} %fusion.info, s32[64]{0:T(128)S(1)} %bitcast.28, bf16[16,64,576]{2,1,0:T(8,128)(2,1)S(1)} %bitcast.34, bf16[16,64,576]{2,1,0:T(8,128)(2,1)S(1)} %collective-permute-done.other, ...), custom_call_target="tpu_custom_call" | custom-call | flops 1207959552 | bytes 5046272 | tf_op jit(solution)/shard_map/score/pallas_call | solution.py:211
  64.2 3.1 %score.5 = (bf16[16,128,512]{2,1,0:T(8,128)(2,1)S(1)}, f32[16,128]{1,0:T(8,128)S(1)}, f32[16,128]{1,0:T(8,128)S(1)}, f32[16,128]{1,0:T(8,128)S(1)}) custom-call(s32[33]{0:T(128)S(1)} %fusion.info, s32[64]{0:T(128)S(1)} %bitcast.29, bf16[16,64,576]{2,1,0:T(8,128)(2,1)S(1)} %bitcast.35, bf16[16,64,576]{2,1,0:T(8,128)(2,1)S(1)} %collective-permute-done.other, ...), custom_call_target="tpu_custom_call" | custom-call | flops 1207959552 | bytes 5046272 | tf_op jit(solution)/shard_map/score/pallas_call | solution.py:211
  67.3 14.4 %collective-permute-done.11.received = f32[16,4224]{1,0:T(8,128)S(1)} collective-permute-done((f32[16,4224]{1,0:T(8,128)S(1)}, f32[16,4224]{1,0:T(8,128)S(1)}, u32[]{:S(2)}, u32[]{:S(2)}) %collective-permute-start.11) | collective-permute-done | bytes 270368 | tf_op jit(solution)/shard_map/ppermute | solution.py:581
  81.7 1.3 logits.1.part
  83.0 0.6 collective-permute-start.13
  83.6 2.5 %score.6 = (bf16[16,128,512]{2,1,0:T(8,128)(2,1)S(1)}, f32[16,128]{1,0:T(8,128)S(1)}, f32[16,128]{1,0:T(8,128)S(1)}, f32[16,128]{1,0:T(8,128)S(1)}) custom-call(s32[33]{0:T(128)S(1)} %fusion.info, s32[64]{0:T(128)S(1)} %bitcast.30, bf16[16,64,576]{2,1,0:T(8,128)(2,1)S(1)} %bitcast.36, bf16[16,64,576]{2,1,0:T(8,128)(2,1)S(1)} %collective-permute-done.other, ...), custom_call_target="tpu_custom_call" | custom-call | flops 1207959552 | bytes 5046272 | tf_op jit(solution)/shard_map/score/pallas_call | solution.py:211
  86.1 2.5 %score.7 = (bf16[16,128,512]{2,1,0:T(8,128)(2,1)S(1)}, f32[16,128]{1,0:T(8,128)S(1)}, f32[16,128]{1,0:T(8,128)S(1)}, f32[16,128]{1,0:T(8,128)S(1)}) custom-call(s32[33]{0:T(128)S(1)} %fusion.info, s32[64]{0:T(128)S(1)} %bitcast.31, bf16[16,64,576]{2,1,0:T(8,128)(2,1)S(1)} %bitcast.37, bf16[16,64,576]{2,1,0:T(8,128)(2,1)S(1)} %collective-permute-done.other, ...), custom_call_target="tpu_custom_call" | custom-call | flops 1207959552 | bytes 5046272 | tf_op jit(solution)/shard_map/score/pallas_call | solution.py:211
  88.7 1.6 %collective-permute-start.15 = (f32[2,16,128]{2,1,0:T(8,128)S(1)}, f32[2,16,128]{2,1,0:T(8,128)S(1)}, u32[]{:S(2)}, u32[]{:S(2)}) collective-permute-start(f32[2,16,128]{2,1,0:T(8,128)S(1)} %pad_maximum_fusion.2), channel_id=1, source_target_pairs={{0,4},{4,0},{1,5},{5,1},{2,6},{6,2},{3,7},{7,3},{8,12},{12,8},{9,1... | collective-permute-start | bytes 49160 | tf_op jit(solution)/shard_map/ppermute | solution.py:584
  90.3 0.9 collective-permute-done.13.far
  91.2 0.8 softmax.1
  92.0 0.5 collective-permute-done.15.refs_10_
  92.5 2.2 %delta.1 = (f32[16,2048]{1,0:T(8,128)S(1)}, bf16[16,2048]{1,0:T(8,128)(2,1)S(1)}) custom-call(bf16[16,128,512]{2,1,0:T(8,128)(2,1)S(1)} %get-tuple-element.72.refs_0_, bf16[16,128,512]{2,1,0:T(8,128)(2,1)S(1)} %get-tuple-element.73.refs_1_, bf16[16,128,512]{2,1,0:T(8,128)(2,1)S(1)} %get-tuple-element.77.refs_2_, ...), custom_call_target="tpu_custom_call" | custom-call | flops 8388608 | bytes 8388608 | tf_op jit(solution)/shard_map/delta/pallas_call | solution.py:258
  94.7 1.6 %collective-permute-start.16 = (bf16[16,2048]{1,0:T(8,128)(2,1)S(1)}, bf16[16,2048]{1,0:T(8,128)(2,1)S(1)}, u32[]{:S(2)}, u32[]{:S(2)}) collective-permute-start(bf16[16,2048]{1,0:T(8,128)(2,1)S(1)} %get-tuple-element.88.sent), channel_id=1, source_target_pairs={{0,4},{4,0},{1,5},{5,1},{2,6},{6,2},{3,7},{7,3},{8,12},{12,8},{9,1... | collective-permute-start | bytes 196616 | tf_op jit(solution)/shard_map/ppermute | solution.py:584
  96.3 2.7 %collective-permute-done.16.brought = bf16[16,2048]{1,0:T(8,128)(2,1)S(1)} collective-permute-done((bf16[16,2048]{1,0:T(8,128)(2,1)S(1)}, bf16[16,2048]{1,0:T(8,128)(2,1)S(1)}, u32[]{:S(2)}, u32[]{:S(2)}) %collective-permute-start.16) | collective-permute-done | bytes 65568 | tf_op jit(solution)/shard_map/ppermute | solution.py:584
  99.0 2.7 %gradient.1 = bf16[16,4224]{1,0:T(8,128)(2,1)S(1)} custom-call(f32[16,4224]{1,0:T(8,128)S(1)} %collective-permute-done.11.received, f32[16,4224]{1,0:T(8,128)S(1)} %get-tuple-element.68.here, bf16[2048,128]{1,0:T(8,128)(2,1)S(1)} %pad_maximum_fusion.own, bf16[2048,128]{1,0:T(8,128)(2,1)S(1)} %collective-permute-done.12.other, ...), custom_call_target="tpu_custom_call" | custom-call | flops 1073741824 | bytes 2375680 | tf_op jit(solution)/shard_map/gradient/pallas_call | solution.py:452
  101.7 1.6 %collective-permute-start.20 = (bf16[1,16,4224]{2,1,0:T(8,128)(2,1)S(1)}, bf16[1,16,4224]{2,1,0:T(8,128)(2,1)S(1)}, u32[]{:S(2)}, u32[]{:S(2)}) collective-permute-start(bf16[1,16,4224]{2,1,0:T(8,128)(2,1)S(1)} %bitcast.19), channel_id=1, source_target_pairs={{0,16},{8,24},{16,0},{24,8},{1,17},{9,25},{17,1},{25,9},{2,18},{10... | collective-permute-start | bytes 405512 | tf_op jit(solution)/shard_map/ppermute | solution.py:587
  103.2 1.4 %collective-permute-start.18 = (bf16[1,16,4224]{2,1,0:T(8,128)(2,1)S(1)}, bf16[1,16,4224]{2,1,0:T(8,128)(2,1)S(1)}, u32[]{:S(2)}, u32[]{:S(2)}) collective-permute-start(bf16[1,16,4224]{2,1,0:T(8,128)(2,1)S(1)} %bitcast.21), channel_id=1, source_target_pairs={{0,2},{1,3},{2,0},{3,1},{4,6},{5,7},{6,4},{7,5},{8,10},{9,11},{10,... | collective-permute-start | bytes 405512 | tf_op jit(solution)/shard_map/ppermute | solution.py:664
  104.6 2.4 %collective-permute-start.19 = (bf16[1,16,4224]{2,1,0:T(8,128)(2,1)S(1)}, bf16[1,16,4224]{2,1,0:T(8,128)(2,1)S(1)}, u32[]{:S(2)}, u32[]{:S(2)}) collective-permute-start(bf16[1,16,4224]{2,1,0:T(8,128)(2,1)S(1)} %bitcast.22), channel_id=1, source_target_pairs={{0,3},{1,0},{2,1},{3,2},{4,7},{5,4},{6,5},{7,6},{8,11},{9,8},{10,9... | collective-permute-start | bytes 405512 | tf_op jit(solution)/shard_map/ppermute | solution.py:664
  107.1 0.5 collective-permute-start.22
  107.6 3.4 %collective-permute-done.17 = bf16[1,16,4224]{2,1,0:T(8,128)(2,1)S(1)} collective-permute-done((bf16[1,16,4224]{2,1,0:T(8,128)(2,1)S(1)}, bf16[1,16,4224]{2,1,0:T(8,128)(2,1)S(1)}, u32[]{:S(2)}, u32[]{:S(2)}) %collective-permute-start.17) | collective-permute-done | bytes 135200 | tf_op jit(solution)/shard_map/ppermute | solution.py:664
  111.0 2.9 %collective-permute-done.18 = bf16[1,16,4224]{2,1,0:T(8,128)(2,1)S(1)} collective-permute-done((bf16[1,16,4224]{2,1,0:T(8,128)(2,1)S(1)}, bf16[1,16,4224]{2,1,0:T(8,128)(2,1)S(1)}, u32[]{:S(2)}, u32[]{:S(2)}) %collective-permute-start.18) | collective-permute-done | bytes 135200 | tf_op jit(solution)/shard_map/ppermute | solution.py:664
  113.9 0.6 collective-permute-start.23
  114.5 7.4 %collective-permute-done.23.refs_5_ = bf16[3,16,4224]{2,1,0:T(8,128)(2,1)S(1)} collective-permute-done((bf16[3,16,4224]{2,1,0:T(8,128)(2,1)S(1)}, bf16[3,16,4224]{2,1,0:T(8,128)(2,1)S(1)}, u32[]{:S(2)}, u32[]{:S(2)}) %collective-permute-start.23) | collective-permute-done | bytes 405536 | tf_op jit(solution)/shard_map/ppermute | solution.py:587
  121.9 1.7 %collective-permute-done.25.refs_7_ = bf16[3,16,4224]{2,1,0:T(8,128)(2,1)S(1)} collective-permute-done((bf16[3,16,4224]{2,1,0:T(8,128)(2,1)S(1)}, bf16[3,16,4224]{2,1,0:T(8,128)(2,1)S(1)}, u32[]{:S(2)}, u32[]{:S(2)}) %collective-permute-start.25) | collective-permute-done | bytes 405536 | tf_op jit(solution)/shard_map/ppermute | solution.py:587
  123.6 4.4 %outer.1 = (f32[384,4096]{1,0:T(8,128)}, f32[32,1792]{1,0:T(8,128)}, f32[1,64]{1,0:T(1,128)}) custom-call(s32[33]{0:T(128)S(1)} %fusion.info, bf16[384,256]{1,0:T(8,128)(2,1)S(1)} %get-tuple-element.60.latents, bf16[256,1792]{1,0:T(8,128)(2,1)S(1)} %get-tuple-element.61.hiddens, bf16[1,16,4224]{2,1,0:T(8,128)(2,1)S(1)} %bitcast.24, ...), custom_call_target="tpu_custom_call" | custom-call | flops 805306368 | bytes 8388608 | tf_op jit(solution)/shard_map/outer/pallas_call | solution.py:539
  (40 shorter events, 0.5 us)
Async XLA Ops:
  0.6 1.3 copy-start
  2.0 30.1 %collective-permute-start.1 = (bf16[576,512]{1,0:T(8,128)(2,1)S(1)}, bf16[576,512]{1,0:T(8,128)(2,1)}, u32[]{:S(2)}, u32[]{:S(2)}) collective-permute-start(bf16[576,512]{1,0:T(8,128)(2,1)S(1)} %dynamic-slice_bitcast_fusion.keys), channel_id=1, source_target_pairs={{0,1},{1,3},{3,2},{2,0},{4,5},{5,7},{7,6},{6,4},{8,9},{9,11},{11,1... | collective-permute-start | bytes 1769480 | tf_op jit(solution)/shard_map/ppermute | solution.py:581
  5.0 56.6 %collective-permute-start = (bf16[16,64,576]{2,1,0:T(8,128)(2,1)}, bf16[16,64,576]{2,1,0:T(8,128)(2,1)S(1)}, u32[]{:S(2)}, u32[]{:S(2)}) collective-permute-start(bf16[16,64,576]{2,1,0:T(8,128)(2,1)} %bitcast.33), channel_id=1, source_target_pairs={{0,4},{4,0},{1,5},{5,1},{2,6},{6,2},{3,7},{7,3},{8,12},{12,8},{9,1... | collective-permute-start | bytes 3538952 | tf_op jit(solution)/shard_map/ppermute | solution.py:584
  7.2 1.9 %copy-start.1 = (bf16[384,4096]{1,0:T(8,128)(2,1)S(1)}, bf16[384,4096]{1,0:T(8,128)(2,1)}, u32[]{:S(2)}) copy-start(bf16[384,4096]{1,0:T(8,128)(2,1)} %weight.1) | copy-start | bytes 9437188
  9.1 1.2 copy-start.2
  10.3 0.9 copy-start.3
  11.2 0.9 copy-start.4
  12.1 4.0 %copy-start.7 = (bf16[1,1024,128]{2,1,0:T(8,128)(2,1)S(1)}, bf16[1,1024,128]{2,1,0:T(8,128)(2,1)}, u32[]{:S(2)}) copy-start(bf16[1,1024,128]{2,1,0:T(8,128)(2,1)} %param.13) | copy-start | bytes 786436
  13.4 48.2 %copy-start.5 = (s32[1,64]{1,0:T(1,128)S(1)}, s32[1,64]{1,0:T(1,128)}, u32[]{:S(2)}) copy-start(s32[1,64]{1,0:T(1,128)} %param.14) | copy-start | bytes 772
  13.4 48.2 %copy-start.6 = (bf16[1,16,64,576]{3,2,1,0:T(8,128)(2,1)S(1)}, bf16[1,16,64,576]{3,2,1,0:T(8,128)(2,1)}, u32[]{:S(2)}) copy-start(bf16[1,16,64,576]{3,2,1,0:T(8,128)(2,1)} %param.11) | copy-start | bytes 3538948
  13.5 12.5 %collective-permute-start.2 = (f32[16,4224]{1,0:T(8,128)S(1)}, f32[16,4224]{1,0:T(8,128)S(1)}, u32[]{:S(2)}, u32[]{:S(2)}) collective-permute-start(f32[16,4224]{1,0:T(8,128)S(1)} %get-tuple-element.50), channel_id=1, source_target_pairs={{0,1},{1,3},{3,2},{2,0},{4,5},{5,7},{7,6},{6,4},{8,9},{9,11},{11,1... | collective-permute-start | bytes 811016 | tf_op jit(solution)/shard_map/ppermute | solution.py:581
  16.1 13.5 %collective-permute-start.3 = (bf16[512,128]{1,0:T(8,128)(2,1)S(1)}, bf16[512,128]{1,0:T(8,128)(2,1)S(1)}, u32[]{:S(2)}, u32[]{:S(2)}) collective-permute-start(bf16[512,128]{1,0:T(8,128)(2,1)S(1)} %dynamic-slice_bitcast_fusion.1), channel_id=1, source_target_pairs={{0,1},{1,3},{3,2},{2,0},{4,5},{5,7},{7,6},{6,4},{8,9},{9,11},{11,1... | collective-permute-start | bytes 393224 | tf_op jit(solution)/shard_map/ppermute | solution.py:581
  16.6 15.4 %collective-permute-start.4 = (bf16[512,128]{1,0:T(8,128)(2,1)S(1)}, bf16[512,128]{1,0:T(8,128)(2,1)S(1)}, u32[]{:S(2)}, u32[]{:S(2)}) collective-permute-start(bf16[512,128]{1,0:T(8,128)(2,1)S(1)} %dynamic-slice_bitcast_fusion.1), channel_id=1, source_target_pairs={{0,3},{1,2},{3,0},{2,1},{4,7},{5,6},{7,4},{6,5},{8,11},{9,10},{11,... | collective-permute-start | bytes 393224 | tf_op jit(solution)/shard_map/ppermute | solution.py:581
  32.1 25.6 %collective-permute-start.8 = (bf16[576,512]{1,0:T(8,128)(2,1)}, bf16[576,512]{1,0:T(8,128)(2,1)S(1)}, u32[]{:S(2)}, u32[]{:S(2)}) collective-permute-start(bf16[576,512]{1,0:T(8,128)(2,1)} %collective-permute-done.1.keys), channel_id=1, source_target_pairs={{0,1},{1,3},{3,2},{2,0},{4,5},{5,7},{7,6},{6,4},{8,9},{9,11},{11,1... | collective-permute-start | bytes 1769480 | tf_op jit(solution)/shard_map/ppermute | solution.py:581
  34.7 19.3 %collective-permute-start.10 = (bf16[512,128]{1,0:T(8,128)(2,1)S(1)}, bf16[512,128]{1,0:T(8,128)(2,1)S(1)}, u32[]{:S(2)}, u32[]{:S(2)}) collective-permute-start(bf16[512,128]{1,0:T(8,128)(2,1)S(1)} %dynamic-slice_bitcast_fusion.1), channel_id=1, source_target_pairs={{0,2},{1,0},{3,1},{2,3},{4,6},{5,4},{7,5},{6,7},{8,10},{9,8},{11,9... | collective-permute-start | bytes 393224 | tf_op jit(solution)/shard_map/ppermute | solution.py:581
  36.7 21.0 %collective-permute-start.9 = (f32[16,4224]{1,0:T(8,128)S(1)}, f32[16,4224]{1,0:T(8,128)S(1)}, u32[]{:S(2)}, u32[]{:S(2)}) collective-permute-start(f32[16,4224]{1,0:T(8,128)S(1)} %add.24), channel_id=1, source_target_pairs={{0,1},{1,3},{3,2},{2,0},{4,5},{5,7},{7,6},{6,4},{8,9},{9,11},{11,1... | collective-permute-start | bytes 811016 | tf_op jit(solution)/shard_map/ppermute | solution.py:581
  36.8 22.5 %collective-permute-start.5 = (bf16[64,2176]{1,0:T(8,128)(2,1)S(1)}, bf16[64,2176]{1,0:T(8,128)(2,1)S(1)}, u32[]{:S(2)}, u32[]{:S(2)}) collective-permute-start(bf16[64,2176]{1,0:T(8,128)(2,1)S(1)} %get-tuple-element.57.refs_0_), channel_id=1, source_target_pairs={{0,16},{8,24},{16,0},{24,8},{1,17},{9,25},{17,1},{25,9},{2,18},{10... | collective-permute-start | bytes 835592 | tf_op jit(solution)/shard_map/ppermute | solution.py:587
  54.1 5.3 %collective-permute-start.6 = (bf16[64,2176]{1,0:T(8,128)(2,1)S(1)}, bf16[64,2176]{1,0:T(8,128)(2,1)S(1)}, u32[]{:S(2)}, u32[]{:S(2)}) collective-permute-start(bf16[64,2176]{1,0:T(8,128)(2,1)S(1)} %get-tuple-element.57.refs_0_), channel_id=1, source_target_pairs={{0,8},{8,0},{16,24},{24,16},{1,9},{9,1},{17,25},{25,17},{2,10},{10... | collective-permute-start | bytes 835592 | tf_op jit(solution)/shard_map/ppermute | solution.py:587
  57.7 24.0 %collective-permute-start.12 = (bf16[2048,128]{1,0:T(8,128)(2,1)S(1)}, bf16[2048,128]{1,0:T(8,128)(2,1)S(1)}, u32[]{:S(2)}, u32[]{:S(2)}) collective-permute-start(bf16[2048,128]{1,0:T(8,128)(2,1)S(1)} %pad_maximum_fusion.own), channel_id=1, source_target_pairs={{0,4},{4,0},{1,5},{5,1},{2,6},{6,2},{3,7},{7,3},{8,12},{12,8},{9,1... | collective-permute-start | bytes 1572872 | tf_op jit(solution)/shard_map/ppermute | solution.py:584
  59.3 1.6 %collective-permute-start.7 = (bf16[64,2176]{1,0:T(8,128)(2,1)S(1)}, bf16[64,2176]{1,0:T(8,128)(2,1)S(1)}, u32[]{:S(2)}, u32[]{:S(2)}) collective-permute-start(bf16[64,2176]{1,0:T(8,128)(2,1)S(1)} %collective-permute-done.5.refs_1_), channel_id=1, source_target_pairs={{0,8},{8,0},{16,24},{24,16},{1,9},{9,1},{17,25},{25,17},{2,10},{10... | collective-permute-start | bytes 835592 | tf_op jit(solution)/shard_map/ppermute | solution.py:587
  59.3 26.8 %collective-permute-start.14 = (bf16[576,512]{1,0:T(8,128)(2,1)S(1)}, bf16[576,512]{1,0:T(8,128)(2,1)S(1)}, u32[]{:S(2)}, u32[]{:S(2)}) collective-permute-start(bf16[576,512]{1,0:T(8,128)(2,1)S(1)} %collective-permute-done.8.keys), channel_id=1, source_target_pairs={{0,1},{1,3},{3,2},{2,0},{4,5},{5,7},{7,6},{6,4},{8,9},{9,11},{11,1... | collective-permute-start | bytes 1769480 | tf_op jit(solution)/shard_map/ppermute | solution.py:581
  59.3 22.4 %collective-permute-start.11 = (f32[16,4224]{1,0:T(8,128)S(1)}, f32[16,4224]{1,0:T(8,128)S(1)}, u32[]{:S(2)}, u32[]{:S(2)}) collective-permute-start(f32[16,4224]{1,0:T(8,128)S(1)} %add.25), channel_id=1, source_target_pairs={{0,1},{1,3},{3,2},{2,0},{4,5},{5,7},{7,6},{6,4},{8,9},{9,11},{11,1... | collective-permute-start | bytes 811016 | tf_op jit(solution)/shard_map/ppermute | solution.py:581
  83.0 8.2 %collective-permute-start.13 = (f32[2,16,2048]{2,1,0:T(8,128)S(1)}, f32[2,16,2048]{2,1,0:T(8,128)S(1)}, u32[]{:S(2)}, u32[]{:S(2)}) collective-permute-start(f32[2,16,2048]{2,1,0:T(8,128)S(1)} %logits.1.part), channel_id=1, source_target_pairs={{0,4},{4,0},{1,5},{5,1},{2,6},{6,2},{3,7},{7,3},{8,12},{12,8},{9,1... | collective-permute-start | bytes 786440 | tf_op jit(solution)/shard_map/ppermute | solution.py:584
  88.7 3.8 %collective-permute-start.15 = (f32[2,16,128]{2,1,0:T(8,128)S(1)}, f32[2,16,128]{2,1,0:T(8,128)S(1)}, u32[]{:S(2)}, u32[]{:S(2)}) collective-permute-start(f32[2,16,128]{2,1,0:T(8,128)S(1)} %pad_maximum_fusion.2), channel_id=1, source_target_pairs={{0,4},{4,0},{1,5},{5,1},{2,6},{6,2},{3,7},{7,3},{8,12},{12,8},{9,1... | collective-permute-start | bytes 49160 | tf_op jit(solution)/shard_map/ppermute | solution.py:584
  94.7 4.3 %collective-permute-start.16 = (bf16[16,2048]{1,0:T(8,128)(2,1)S(1)}, bf16[16,2048]{1,0:T(8,128)(2,1)S(1)}, u32[]{:S(2)}, u32[]{:S(2)}) collective-permute-start(bf16[16,2048]{1,0:T(8,128)(2,1)S(1)} %get-tuple-element.88.sent), channel_id=1, source_target_pairs={{0,4},{4,0},{1,5},{5,1},{2,6},{6,2},{3,7},{7,3},{8,12},{12,8},{9,1... | collective-permute-start | bytes 196616 | tf_op jit(solution)/shard_map/ppermute | solution.py:584
  101.7 5.4 %collective-permute-start.20 = (bf16[1,16,4224]{2,1,0:T(8,128)(2,1)S(1)}, bf16[1,16,4224]{2,1,0:T(8,128)(2,1)S(1)}, u32[]{:S(2)}, u32[]{:S(2)}) collective-permute-start(bf16[1,16,4224]{2,1,0:T(8,128)(2,1)S(1)} %bitcast.19), channel_id=1, source_target_pairs={{0,16},{8,24},{16,0},{24,8},{1,17},{9,25},{17,1},{25,9},{2,18},{10... | collective-permute-start | bytes 405512 | tf_op jit(solution)/shard_map/ppermute | solution.py:587
  103.2 7.8 %collective-permute-start.17 = (bf16[1,16,4224]{2,1,0:T(8,128)(2,1)S(1)}, bf16[1,16,4224]{2,1,0:T(8,128)(2,1)S(1)}, u32[]{:S(2)}, u32[]{:S(2)}) collective-permute-start(bf16[1,16,4224]{2,1,0:T(8,128)(2,1)S(1)} %bitcast.20), channel_id=1, source_target_pairs={{0,1},{1,2},{2,3},{3,0},{4,5},{5,6},{6,7},{7,4},{8,9},{9,10},{10,1... | collective-permute-start | bytes 405512 | tf_op jit(solution)/shard_map/ppermute | solution.py:664
  103.2 10.6 %collective-permute-start.18 = (bf16[1,16,4224]{2,1,0:T(8,128)(2,1)S(1)}, bf16[1,16,4224]{2,1,0:T(8,128)(2,1)S(1)}, u32[]{:S(2)}, u32[]{:S(2)}) collective-permute-start(bf16[1,16,4224]{2,1,0:T(8,128)(2,1)S(1)} %bitcast.21), channel_id=1, source_target_pairs={{0,2},{1,3},{2,0},{3,1},{4,6},{5,7},{6,4},{7,5},{8,10},{9,11},{10,... | collective-permute-start | bytes 405512 | tf_op jit(solution)/shard_map/ppermute | solution.py:664
  104.6 9.2 %collective-permute-start.19 = (bf16[1,16,4224]{2,1,0:T(8,128)(2,1)S(1)}, bf16[1,16,4224]{2,1,0:T(8,128)(2,1)S(1)}, u32[]{:S(2)}, u32[]{:S(2)}) collective-permute-start(bf16[1,16,4224]{2,1,0:T(8,128)(2,1)S(1)} %bitcast.22), channel_id=1, source_target_pairs={{0,3},{1,0},{2,1},{3,2},{4,7},{5,4},{6,5},{7,6},{8,11},{9,8},{10,9... | collective-permute-start | bytes 405512 | tf_op jit(solution)/shard_map/ppermute | solution.py:664
  107.1 6.8 %collective-permute-start.21 = (bf16[1,16,4224]{2,1,0:T(8,128)(2,1)S(1)}, bf16[1,16,4224]{2,1,0:T(8,128)(2,1)S(1)}, u32[]{:S(2)}, u32[]{:S(2)}) collective-permute-start(bf16[1,16,4224]{2,1,0:T(8,128)(2,1)S(1)} %bitcast.23), channel_id=1, source_target_pairs={{0,8},{8,0},{16,24},{24,16},{1,9},{9,1},{17,25},{25,17},{2,10},{10... | collective-permute-start | bytes 405512 | tf_op jit(solution)/shard_map/ppermute | solution.py:587
  107.1 6.8 %collective-permute-start.22 = (bf16[1,16,4224]{2,1,0:T(8,128)(2,1)S(1)}, bf16[1,16,4224]{2,1,0:T(8,128)(2,1)S(1)}, u32[]{:S(2)}, u32[]{:S(2)}) collective-permute-start(bf16[1,16,4224]{2,1,0:T(8,128)(2,1)S(1)} %collective-permute-done.20.refs_1_), channel_id=1, source_target_pairs={{0,8},{8,0},{16,24},{24,16},{1,9},{9,1},{17,25},{25,17},{2,10},{10... | collective-permute-start | bytes 405512 | tf_op jit(solution)/shard_map/ppermute | solution.py:587
  113.9 8.0 %collective-permute-start.23 = (bf16[3,16,4224]{2,1,0:T(8,128)(2,1)S(1)}, bf16[3,16,4224]{2,1,0:T(8,128)(2,1)S(1)}, u32[]{:S(2)}, u32[]{:S(2)}) collective-permute-start(bf16[3,16,4224]{2,1,0:T(8,128)(2,1)S(1)} %pad_maximum_fusion.1.refs_4_), channel_id=1, source_target_pairs={{0,16},{8,24},{16,0},{24,8},{1,17},{9,25},{17,1},{25,9},{2,18},{10... | collective-permute-start | bytes 1216520 | tf_op jit(solution)/shard_map/ppermute | solution.py:587
  114.5 7.4 %collective-permute-start.24 = (bf16[3,16,4224]{2,1,0:T(8,128)(2,1)S(1)}, bf16[3,16,4224]{2,1,0:T(8,128)(2,1)S(1)}, u32[]{:S(2)}, u32[]{:S(2)}) collective-permute-start(bf16[3,16,4224]{2,1,0:T(8,128)(2,1)S(1)} %pad_maximum_fusion.1.refs_4_), channel_id=1, source_target_pairs={{0,8},{8,0},{16,24},{24,16},{1,9},{9,1},{17,25},{25,17},{2,10},{10... | collective-permute-start | bytes 1216520 | tf_op jit(solution)/shard_map/ppermute | solution.py:587
  121.9 1.7 %collective-permute-start.25 = (bf16[3,16,4224]{2,1,0:T(8,128)(2,1)S(1)}, bf16[3,16,4224]{2,1,0:T(8,128)(2,1)S(1)}, u32[]{:S(2)}, u32[]{:S(2)}) collective-permute-start(bf16[3,16,4224]{2,1,0:T(8,128)(2,1)S(1)} %collective-permute-done.23.refs_5_), channel_id=1, source_target_pairs={{0,8},{8,0},{16,24},{24,16},{1,9},{9,1},{17,25},{25,17},{2,10},{10... | collective-permute-start | bytes 1216520 | tf_op jit(solution)/shard_map/ppermute | solution.py:587

commit v6 on v5

--- a/solution.py
+++ b/solution.py
@@ -23,10 +23,6 @@
 group_size = 4
 
 
-def folded_ring(size):
-    return [0] + list(range(1, size, 2)) + list(range(2, size, 2))[::-1]
-
-
 def params():
     return pltpu.CompilerParams(vmem_limit_bytes=vmem_limit)
 
@@ -43,23 +39,77 @@
     return lax.dot_general(a, b, (((axis_a,), (axis_b,)), ((), ())), preferred_element_type=f32)
 
 
-def device_table(n, heads, dp_size, rows):
-    ring = folded_ring(n)
-    half = rows // heads
-    flips = dp_flips(dp_size)
+at_ctx, at_head, at_dp = 0, 1, 2
+
+
+class Route:
+    def __init__(self, n):
+        self.n = n
+
+    def pairs(self, left, step):
+        n = self.n
+        if left:
+            return [(k, k - 1) for k in range(1, n - step + 1)]
+        return [(k, k + 1) for k in range(step - 1, n - 1)]
+
+    def joined(self, step):
+        return self.n - step < step - 1
+
+    def choose(self, u, z):
+        n = self.n
+        if z < n // 2:
+            return (True, u) if u <= n - 1 - z else (False, n - u)
+        return (False, u) if u <= z else (True, n - u)
+
+    def source(self, u, z):
+        if u == 0:
+            return z
+        left, step = self.choose(u, z)
+        return z + step if left else z - step
+
+    def options(self, u):
+        found = []
+        for z in range(self.n):
+            left, step = self.choose(u, z)
+            one = (None if self.joined(step) else left, step)
+            if one not in found:
+                found.append(one)
+        return found
+
+    def option(self, u, z):
+        left, step = self.choose(u, z)
+        return self.options(u).index((None if self.joined(step) else left, step))
+
+
+def device_table(n, heads, dp_size):
+    route = Route(n)
     table = []
     for z in range(n):
-        place = ring.index(z)
-        behind = [ring[(place - t) % n] for t in range(n)]
         for y in range(heads):
             for dp in range(dp_size):
-                row = [z] + [ring[(place - 1 - t) % n] for t in range(n)]
-                row += [k * rows + y * half for k in behind]
-                row += [k * rows + (1 - y) * half for k in behind]
-                row += [(dp ^ k) * n + (z - t) % n for k in flips for t in range(n)]
-                row += [dp ^ k for k in flips]
+                row = [z, y, dp]
+                row += [route.source(u, z) for u in range(n)]
+                row += [0] + [route.option(u, z) for u in range(1, n)]
+                row += [dp ^ k for k in dp_flips(dp_size)]
+                row += [(z - t) % n for t in range(n)]
                 table.append(row)
     return np.array(table, np.int32)
+
+
+def at_source(n, u):
+    return 3 + u
+
+
+def at_option(n, u):
+    return 3 + n + u
+
+
+def at_partner(n, k):
+    return 3 + 2 * n + k
+
+
+def at_shift(n, dp_size, t):
+    return 3 + 2 * n + dp_size + t
 
 
 def dp_flips(dp_size):
@@ -69,25 +119,18 @@
     return flips
 
 
-def project_kernel(aligned, info, latent, weight, hidden, hidden_weight, *outs):
-    *parts, kept = outs
+def project_kernel(info, latent, weight, hidden, hidden_weight, out, kept):
+    blocks, count, _ = out.shape
     width = weight.shape[1]
     heads = hidden_weight.shape[0]
-    count = parts[0].shape[0]
-    if aligned:
-        starts = [pl.multiple_of(info[1 + k] * count, count) for k in range(len(parts))]
-        rows = jnp.concatenate([latent[pl.ds(k, count), :] for k in starts], axis=0)
-        mixed_rows = jnp.concatenate([hidden[pl.ds(k, count), :] for k in starts], axis=0)
-    else:
-        rows, mixed_rows = latent[...], hidden[...]
     for at in range(0, width, 512):
-        product = times(rows, weight[:, at : at + 512], 1, 0)
-        for k, out in enumerate(parts):
-            out[:, at : at + 512] = product[k * count : (k + 1) * count]
-    mixed = times(mixed_rows, hidden_weight[...], 1, 1)
-    for k, out in enumerate(parts):
-        out[:, width : width + heads] = mixed[k * count : (k + 1) * count]
-        out[:, width + heads :] = jnp.zeros((count, lanes - heads), f32)
+        product = times(latent[...], weight[:, at : at + 512], 1, 0)
+        for k in range(blocks):
+            out[k, :, at : at + 512] = product[k * count : (k + 1) * count]
+    mixed = times(hidden[...], hidden_weight[...], 1, 1)
+    for k in range(blocks):
+        out[k, :, width : width + heads] = mixed[k * count : (k + 1) * count]
+        out[k, :, width + heads :] = jnp.zeros((count, lanes - heads), f32)
     kept[:, : latent.shape[1]] = latent[...]
     kept[:, latent.shape[1] :] = hidden[...]
 
@@ -96,20 +139,14 @@
     queries, width = latent.shape[0], weight.shape[1]
     depth, hidden_depth = weight.shape[0], hidden_weight.shape[1]
     blocks = queries // count
-    aligned = count % 16 == 0 and depth % lanes == 0 and hidden_depth % lanes == 0
-    columns = lambda i, info: (0, info[0])
+    columns = lambda i, info: (0, info[at_ctx])
     whole = lambda i, info: (0, 0)
-    kept = None
-    if not aligned:
-        latent = lax.dynamic_slice_in_dim(latent, info[0] * depth, depth, 1)
-        hidden = lax.dynamic_slice_in_dim(hidden, info[0] * hidden_depth, hidden_depth, 1)
-        kept = jnp.concatenate([latent, hidden], axis=1)
-        order = info[1 : 1 + blocks]
-        latent = latent.reshape(blocks, count, depth)[order].reshape(queries, depth)
-        hidden = hidden.reshape(blocks, count, hidden_depth)[order].reshape(queries, hidden_depth)
+    if depth % lanes or hidden_depth % lanes:
+        latent = lax.dynamic_slice_in_dim(latent, info[at_ctx] * depth, depth, 1)
+        hidden = lax.dynamic_slice_in_dim(hidden, info[at_ctx] * hidden_depth, hidden_depth, 1)
         columns = whole
-    *parts, kept_here = pl.pallas_call(
-        functools.partial(project_kernel, aligned),
+    return pl.pallas_call(
+        project_kernel,
         grid_spec=pltpu.PrefetchScalarGridSpec(
             num_scalar_prefetch=1,
             grid=(1,),
@@ -119,40 +156,38 @@
                 pl.BlockSpec((queries, hidden_depth), columns),
                 pl.BlockSpec(hidden_weight.shape, whole),
             ],
-            out_specs=[pl.BlockSpec((count, width + lanes), whole)] * blocks
-            + [pl.BlockSpec((queries, depth + hidden_depth), whole)],
-        ),
-        out_shape=[jax.ShapeDtypeStruct((count, width + lanes), f32)] * blocks
-        + [jax.ShapeDtypeStruct((queries, depth + hidden_depth), bf16)],
+            out_specs=[
+                pl.BlockSpec((blocks, count, width + lanes), lambda i, info: (0, 0, 0)),
+                pl.BlockSpec((queries, depth + hidden_depth), whole),
+            ],
+        ),
+        out_shape=[
+            jax.ShapeDtypeStruct((blocks, count, width + lanes), f32),
+            jax.ShapeDtypeStruct((queries, depth + hidden_depth), bf16),
+        ],
         compiler_params=params(),
         cost_estimate=pl.CostEstimate(
             flops=2 * queries * weight.size, bytes_accessed=2 * weight.size, transcendentals=0
         ),
         name="project",
     )(info, latent, weight, hidden, hidden_weight)
-    return parts, kept_here if aligned else kept
-
-
-def score_kernel(
-    t,
-    base_at,
-    info,
-    positions,
-    mine,
-    other,
-    keys,
-    top_before,
-    mass_before,
-    weights,
-    top,
-    top_all,
-    mass_all,
-    mass,
-    even,
-    odd,
-):
+
+
+def score_kernel(t, n, rows_here, info, positions, mine, other, *refs):
+    options, refs = refs[:-10], refs[-10:]
+    top_before, mass_before, weights, top, top_all, mass_all, mass, even, odd, chosen = refs
     count, heads, depth = mine.shape
-    limits = [positions[info[0] * count + q] - info[base_at] for q in range(count)]
+    keys = options[0]
+    if len(options) > 1:
+        keys = chosen
+        for k, option in enumerate(options):
+
+            @pl.when(info[at_option(n, t)] == k)
+            def _():
+                chosen[...] = option[...]
+
+    base = info[at_source(n, t)] * rows_here + info[at_head] * keys.shape[1]
+    limits = [positions[info[at_ctx] * count + q] - base for q in range(count)]
     span = keys.shape[1]
     key_at = lax.broadcasted_iota(jnp.int32, (1, span), 1)
     row_at = lax.broadcasted_iota(jnp.int32, (heads, lanes), 0)
@@ -202,30 +237,31 @@
         ] * jnp.exp2((now - joint) * exponent_scale)
 
 
-def score(t, n, info, positions, mine, other, keys, before):
+def score(t, n, rows_here, info, positions, mine, other, options, before):
     count, heads, depth = mine.shape
-    span = keys.shape[1]
+    span = options[0].shape[1]
     stats = jax.ShapeDtypeStruct((count, lanes), f32)
     if before is None:
         before = (jnp.zeros((count, lanes), f32),) * 2
     return pl.pallas_call(
-        functools.partial(score_kernel, t, 1 + n + t),
+        functools.partial(score_kernel, t, n, rows_here),
         out_shape=(jax.ShapeDtypeStruct((count, 2 * heads, span), bf16), stats, stats, stats),
-        in_specs=[in_smem()] * 2 + [in_vmem()] * 5,
+        in_specs=[in_smem()] * 2 + [in_vmem()] * (4 + len(options)),
         out_specs=(in_vmem(),) * 4,
         scratch_shapes=[pltpu.VMEM((count, lanes), f32)]
-        + [pltpu.VMEM((min(group_size, count) * heads, span), f32)] * 2,
+        + [pltpu.VMEM((min(group_size, count) * heads, span), f32)] * 2
+        + [pltpu.VMEM((depth, span), bf16)],
         compiler_params=params(),
         cost_estimate=pl.CostEstimate(
             flops=4 * count * heads * depth * span,
-            bytes_accessed=2 * (2 * mine.size + keys.size + 2 * count * heads * span),
+            bytes_accessed=2 * (2 * mine.size + depth * span + 2 * count * heads * span),
             transcendentals=2 * count * heads * span,
         ),
         name="score",
-    )(info, positions, mine, other, keys, *before)
-
-
-def delta_kernel(blocks, *refs):
+    )(info, positions, mine, other, *options, *before)
+
+
+def delta_kernel(blocks, info, *refs):
     weights, tops = refs[:blocks], refs[blocks : 2 * blocks]
     top, mass, far, probs, out, sent, held = refs[2 * blocks :]
     count, heads, span = weights[0].shape
@@ -241,18 +277,19 @@
     inverse = 1.0 / (total * HM)
     for t in range(blocks):
         factor = jnp.exp2((tops[t][...] - joint) * exponent_scale) * inverse
+        to = pl.ds(pl.multiple_of(info[at_source(blocks, t)] * span, span), span)
         for q in range(count):
             column = jnp.sum(
                 jnp.where(diagonal, factor[q : q + 1, :], 0.0), axis=1, keepdims=True
             )
             mixed = weights[t][q].astype(f32) * column
-            held[q : q + 1, t * span : (t + 1) * span] = jnp.sum(mixed, axis=0, keepdims=True)
+            held[q : q + 1, to] = jnp.sum(mixed, axis=0, keepdims=True)
     delta = probs[0] - held[...]
     out[...] = delta
     sent[...] = delta.astype(bf16)
 
 
-def make_delta(weights, tops, top, mass, far, probs):
+def make_delta(info, weights, tops, top, mass, far, probs):
     blocks = len(weights)
     count, heads, span = weights[0].shape
     return pl.pallas_call(
@@ -261,7 +298,7 @@
             jax.ShapeDtypeStruct((count, blocks * span), f32),
             jax.ShapeDtypeStruct((count, blocks * span), bf16),
         ),
-        in_specs=[in_vmem()] * (2 * blocks + 4),
+        in_specs=[in_smem()] + [in_vmem()] * (2 * blocks + 4),
         out_specs=(in_vmem(),) * 2,
         scratch_shapes=[pltpu.VMEM((count, blocks * span), f32)],
         compiler_params=params(),
@@ -271,7 +308,7 @@
             transcendentals=0,
         ),
         name="delta",
-    )(*weights, *tops, top, mass, far, probs)
+    )(info, *weights, *tops, top, mass, far, probs)
 
 
 def query_rows(total, heads):
@@ -280,9 +317,16 @@
     )
 
 
-def logits_kernel(heads, received, here, own, other, out):
-    count = received.shape[0]
-    total = received[...] + here[...]
+def summed(received):
+    total = received[0]
+    for k in range(1, received.shape[0]):
+        total = total + received[k]
+    return total
+
+
+def logits_kernel(heads, received, own, other, out):
+    count = received.shape[1]
+    total = summed(received)
     query = query_rows(total, heads)
     columns = [total[:, heads * DI + j : heads * DI + j + 1] for j in range(heads)]
     span = 512
@@ -296,35 +340,36 @@
             out[part, :, at : at + span] = running * index_scale
 
 
-def make_logits(heads, received, here, own, other):
-    count, length = received.shape[0], own.shape[0]
+def make_logits(heads, received, own, other):
+    count, length = received.shape[1], own.shape[0]
     return pl.pallas_call(
         functools.partial(logits_kernel, heads),
         out_shape=jax.ShapeDtypeStruct((2, count, length), f32),
-        in_specs=[in_vmem()] * 4,
+        in_specs=[in_vmem()] * 3,
         out_specs=in_vmem(),
         compiler_params=params(),
         cost_estimate=pl.CostEstimate(
             flops=4 * count * heads * DI * length,
-            bytes_accessed=4 * (2 * received.size + 2 * count * length) + 4 * length * DI,
+            bytes_accessed=4 * (received.size + 2 * count * length) + 4 * length * DI,
             transcendentals=0,
         ),
         name="logits",
-    )(received, here, own, other)
-
-
-def softmax_kernel(blocks, info, positions, part, far, probs, log_probs):
+    )(received, own, other)
+
+
+def softmax_kernel(blocks, rows_here, info, positions, part, far, probs, log_probs):
     _, count, length = part.shape
     span = length // blocks
     row_at = lax.broadcasted_iota(jnp.int32, (count, lanes), 0)
     position = jnp.zeros((count, lanes), jnp.int32)
     for q in range(count):
-        position = jnp.where(row_at == q, positions[info[0] * count + q], position)
+        position = jnp.where(row_at == q, positions[info[at_ctx] * count + q], position)
     position = position[:, 0:1]
     key_at = lax.broadcasted_iota(jnp.int32, (count, span), 1)
 
     def seen(side, t):
-        return key_at + info[1 + (1 + side) * blocks + t] <= position
+        half = info[at_head] if side == 0 else 1 - info[at_head]
+        return key_at + (t * rows_here + half * span) <= position
 
     highs = []
     for side in range(2):
@@ -355,9 +400,9 @@
             log_probs[side, :, at] = jnp.where(seen(side, t), log_probs[side, :, at] - level, 0.0)
 
 
-def make_softmax(blocks, info, positions, part, far):
+def make_softmax(blocks, rows_here, info, positions, part, far):
     return pl.pallas_call(
-        functools.partial(softmax_kernel, blocks),
+        functools.partial(softmax_kernel, blocks, rows_here),
         out_shape=(jax.ShapeDtypeStruct(part.shape, f32),) * 2,
         in_specs=[in_smem()] * 2 + [in_vmem()] * 2,
         out_specs=(in_vmem(),) * 2,
@@ -373,7 +418,6 @@
     heads,
     blocks,
     received,
-    here,
     own,
     other,
     probs,
@@ -388,8 +432,8 @@
     even,
     odd,
 ):
-    count = received.shape[0]
-    total = received[...] + here[...]
+    count = received.shape[1]
+    total = summed(received)
     span = own.shape[0] // blocks
     query = query_rows(total, heads)
     columns = [
@@ -446,13 +490,13 @@
     out[:, heads * DI :] = tail.astype(bf16)
 
 
-def gradients(heads, blocks, received, here, own, other, probs, log_probs, delta_own, sent, brought):
-    count, length = received.shape[0], own.shape[0]
+def gradients(heads, blocks, received, own, other, probs, log_probs, delta_own, sent, brought):
+    count, length = received.shape[1], own.shape[0]
     span = length // blocks
     return pl.pallas_call(
         functools.partial(gradient_kernel, heads, blocks),
         out_shape=jax.ShapeDtypeStruct((count, heads * DI + lanes), bf16),
-        in_specs=[in_vmem()] * 9,
+        in_specs=[in_vmem()] * 8,
         out_specs=in_vmem(),
         scratch_shapes=[
             pltpu.VMEM((heads * count, lanes), f32),
@@ -464,28 +508,28 @@
         compiler_params=params(),
         cost_estimate=pl.CostEstimate(
             flops=8 * count * heads * DI * length,
-            bytes_accessed=4 * (2 * received.size + 6 * count * length) + 4 * length * DI,
+            bytes_accessed=4 * (received.size + 6 * count * length) + 4 * length * DI,
             transcendentals=0,
         ),
         name="gradient",
-    )(received, here, own, other, probs, log_probs, delta_own, sent, brought)
-
-
-def arrange_kernel(at, info, *refs):
+    )(received, own, other, probs, log_probs, delta_own, sent, brought)
+
+
+def arrange_kernel(n, info, *refs):
     kept, (latents, hiddens, held) = refs[:-3], refs[-3:]
     queries, depth = kept[0].shape[0], latents.shape[0]
     for k, one in enumerate(kept):
-        to = pl.ds(pl.multiple_of(info[at + k] * queries, queries), queries)
+        to = pl.ds(pl.multiple_of(info[at_partner(n, k)] * queries, queries), queries)
         held[to, :] = one[:, :depth].astype(f32)
         hiddens[to, :] = one[:, depth:]
     latents[...] = held[...].T.astype(bf16)
 
 
-def arrange(at, info, depth, kept):
+def arrange(n, info, depth, kept):
     queries, width = kept[0].shape
     total = queries * len(kept)
     return pl.pallas_call(
-        functools.partial(arrange_kernel, at),
+        functools.partial(arrange_kernel, n),
         out_shape=(
             jax.ShapeDtypeStruct((depth, total), bf16),
             jax.ShapeDtypeStruct((total, width - depth), bf16),
@@ -501,7 +545,7 @@
     )(info, *kept)
 
 
-def outer_kernel(heads, order, dp_at, info, latents, hiddens, *refs):
+def outer_kernel(heads, n, order, info, latents, hiddens, *refs):
     parts, (grad, grad_mixed, losses, rows, blocks, sems) = refs[:-6], refs[-6:]
     count = parts[0].shape[-2]
     width = heads * DI
@@ -509,7 +553,9 @@
     k = 0
     for part in parts:
         for t in range(part.shape[0]):
-            to = 0 if order is None else pl.multiple_of(info[order[k]] * count, count)
+            to = 0
+            if order is not None:
+                to = pl.multiple_of((info[order[k][0]] * n + info[order[k][1]]) * count, count)
             rows[pl.ds(to, count), :] = part[t]
             k += 1
     copies = []
@@ -521,7 +567,7 @@
     tails = rows[:, width:]
     grad_mixed[...] = times(tails, hiddens[...], 0, 0)[:heads]
     own = losses.shape[1]
-    from_own = rows[pl.ds(pl.multiple_of(info[dp_at] * own, own), own), width:].astype(f32)
+    from_own = rows[pl.ds(pl.multiple_of(info[at_dp] * own, own), own), width:].astype(f32)
     column = from_own[:, heads : heads + 1] + from_own[:, heads + 1 : heads + 2]
     diagonal = lax.broadcasted_iota(jnp.int32, (own, own), 0) == lax.broadcasted_iota(
         jnp.int32, (own, own), 1
@@ -531,13 +577,13 @@
         copy.wait()
 
 
-def outer(heads, order, dp_at, queries, info, latents, hiddens, parts):
+def outer(heads, n, order, queries, info, latents, hiddens, parts):
     row_count, total = latents.shape
     width = heads * DI
     steps = 8
     hidden_count = hiddens.shape[1]
     return pl.pallas_call(
-        functools.partial(outer_kernel, heads, order, dp_at),
+        functools.partial(outer_kernel, heads, n, order),
         out_shape=(
             jax.ShapeDtypeStruct((row_count, width), f32),
             jax.ShapeDtypeStruct((heads, hidden_count), f32),
@@ -569,7 +615,7 @@
     y = lax.axis_index("head")
     dp_size = lax.axis_size("dp")
     dp = lax.axis_index("dp")
-    ring = folded_ring(n)
+    route = Route(n)
     rows = main_keys.shape[1]
     half = rows // head_size
     rows_latent = w_query.shape[0]
@@ -577,8 +623,8 @@
     queries_here = main_queries.shape[1]
     sequence_positions = positions[0]
 
-    def onward(x, t=1):
-        return lax.ppermute(x, "ctx", [(ring[k], ring[(k + t) % n]) for k in range(n)])
+    def to_each(x):
+        return lax.all_to_all(x, "ctx", 0, 0)
 
     def swap_head(x):
         return lax.ppermute(x, "head", [(0, 1), (1, 0)])
@@ -592,63 +638,53 @@
             gathered, bit = gathered + [swap_dp(one, bit) for one in gathered], bit // 2
         return gathered
 
-    table = jnp.array(device_table(n, head_size, dp_size, rows))
+    table = jnp.array(device_table(n, head_size, dp_size))
     info = lax.dynamic_index_in_dim(table, (z * head_size + y) * dp_size + dp, 0, False)
 
-    keys_mine = [lax.dynamic_slice_in_dim(main_keys[0].T, y * half, half, 1)]
-    keys_mine.append(onward(keys_mine[0]))
+    own_keys = lax.dynamic_slice_in_dim(main_keys[0].T, y * half, half, 1)
+    carried = {}
+    last = {True: own_keys, False: own_keys}
+    for step in range(1, n):
+        if route.joined(step):
+            x = jnp.where(z <= n - step, last[True], last[False])
+            x = lax.ppermute(x, "ctx", route.pairs(True, step) + route.pairs(False, step))
+            carried[None, step] = last[True] = last[False] = x
+        else:
+            for left in (True, False):
+                last[left] = lax.ppermute(last[left], "ctx", route.pairs(left, step))
+                carried[left, step] = last[left]
     queries = main_queries[0]
     other_queries = swap_head(queries)
-    index_parts = [lax.dynamic_slice_in_dim(index_keys[0], y * half, half)]
-    index_parts += [onward(index_parts[0], t) for t in range(1, n - 1)]
-    parts, kept = project(info, queries_here, q_latent[0], w_query, hidden[0], w_weights.T)
-    received = onward(parts[0])
-    order_at = 1 + 3 * n
-    dp_at = order_at + n * dp_size
+
+    partial, kept = project(info, queries_here, q_latent[0], w_query, hidden[0], w_weights.T)
+    received = to_each(partial)
+    index_part = lax.dynamic_slice_in_dim(index_keys[0], y * half, half)
+    index_own = to_each(jnp.broadcast_to(index_part[None], (n, *index_part.shape)))
+    index_own = index_own.reshape(n * half, DI)
+    index_other = swap_head(index_own)
+    part = make_logits(heads_here, received, index_own, index_other)
+    probs, log_probs = make_softmax(n, rows, info, sequence_positions, part, swap_head(part))
+    latents, hiddens = arrange(n, info, rows_latent, over_dp(kept))
+
     weights, tops, before = [], [], None
-
-    def score_next(keys):
-        nonlocal before
-        t = len(weights)
+    for t in range(n):
+        options = [own_keys] if t == 0 else [carried[one] for one in route.options(t)]
+        if t == n - 2:
+            before, latents, hiddens, part = lax.optimization_barrier(
+                (before, latents, hiddens, part)
+            )
+        if t == n - 1:
+            before, probs, log_probs = lax.optimization_barrier((before, probs, log_probs))
         numer, top, *before = score(
-            t, n, info, sequence_positions, queries, other_queries, keys, before
+            t, n, rows, info, sequence_positions, queries, other_queries, options, before
         )
         weights.append(numer)
         tops.append(top)
-
-    index_own = index_other = None
-    for t in range(1, n - 1):
-        summed = received + parts[t]
-        if t == 1:
-            keys, summed, index_parts = lax.optimization_barrier(
-                (keys_mine[t], summed, index_parts)
-            )
-            index_parts.append(onward(index_parts[0], n - 1))
-        elif t == 2:
-            index_own = jnp.concatenate(index_parts)
-            keys, summed, index_own = lax.optimization_barrier((keys_mine[t], summed, index_own))
-            index_other = swap_head(index_own)
-        else:
-            keys, summed = lax.optimization_barrier((keys_mine[t], summed))
-        keys_mine[t] = keys
-        keys_mine.append(onward(keys))
-        received = onward(summed)
-    while len(weights) < n - 2:
-        score_next(keys_mine[len(weights)])
-    latents, hiddens = arrange(dp_at, info, rows_latent, over_dp(kept))
-    before, latents, hiddens = lax.optimization_barrier((before, latents, hiddens))
-    score_next(keys_mine[n - 2])
-
-    part = make_logits(heads_here, received, parts[n - 1], index_own, index_other)
-    probs, log_probs = make_softmax(n, info, sequence_positions, part, swap_head(part))
-
-    score_next(keys_mine[n - 1])
-    delta_own, sent = make_delta(weights, tops, *before, swap_head(jnp.stack(before)), probs)
+    delta_own, sent = make_delta(info, weights, tops, *before, swap_head(jnp.stack(before)), probs)
     piece = gradients(
         heads_here,
         n,
         received,
-        parts[n - 1],
         index_own,
         index_other,
         probs,
@@ -665,23 +701,17 @@
     own_pieces = over_dp(piece)
     brought, own_pieces = lax.optimization_barrier((jnp.concatenate(brought), own_pieces))
     brought = over_dp(brought)
+    parts_in = own_pieces + brought
+    order = [(at_partner(n, k), at_shift(n, dp_size, 0)) for k in range(dp_size)]
+    order += [
+        (at_partner(n, k), at_shift(n, dp_size, t)) for k in range(dp_size) for t in range(1, n)
+    ]
     if queries_here % 16:
-        flat = jnp.concatenate([jnp.concatenate([a, b]) for a, b in zip(own_pieces, brought)])
-        order = jnp.argsort(info[order_at : order_at + n * dp_size])
-        parts_in, order = [flat[order].reshape(1, -1, flat.shape[2])], None
-    else:
-        parts_in, order = own_pieces + brought, []
-        order += [order_at + k * n for k in range(dp_size)]
-        order += [order_at + k * n + t for k in range(dp_size) for t in range(1, n)]
+        places = jnp.stack([info[a] * n + info[b] for a, b in order])
+        flat = jnp.concatenate(parts_in)[jnp.argsort(places)]
+        parts_in, order = [flat.reshape(1, -1, flat.shape[2])], None
     grad_query, grad_weights, losses = outer(
-        heads_here,
-        order,
-        dp_at,
-        q_latent.shape[1],
-        info,
-        latents,
-        hiddens,
-        parts_in,
+        heads_here, n, order, q_latent.shape[1], info, latents, hiddens, parts_in
     )
     return (grad_query, grad_weights.T, losses)
 

time: 131 us -> 142 us (1.084); the launches traced: 128 us -> 141 us
  starting transfers between devices: 28.6 us -> 42.1 us
  waiting for transfers between devices: 67.5 us -> 54.4 us
  Pallas kernels: 24.1 us -> 31.4 us
  local copies, waits for them, and re-layouts: 6.92 us -> 9.8 us
  other arithmetic: 0.17 us -> 2.04 us
    ppermute x9 -> x5, waiting for transfers between devices: 47.8 us -> 26 us  [the longest x4 22.8 us: per_device(): last[left] = lax.ppermute(last[left], 'ctx', route.pairs(left, step))]
    all_to_all x0 -> x2, starting transfers between devices: none -> 9.84 us  [to_each(): return lax.all_to_all(x, 'ctx', 0, 0)]
    ppermute x3, starting transfers between devices: 3.83 us -> 9.58 us  [per_device(): brought.append(lax.ppermute(piece, 'ctx', pairs))]
    pallas_call x8, Pallas kernels: 18 us -> 22.7 us  [the longest x4 15 us: score(): pl.pallas_call(functools.partial(score_kernel, t, n, rows_here), out_shap...]
    ppermute x9, waiting for transfers between devices: 9.25 us -> 13 us  [swap_dp(): return lax.ppermute(x, 'dp', [(k, k ^ bit) for k in range(dp_size)])]
    ppermute x9 -> x5, starting transfers between devices: 13.7 us -> 10.1 us  [the longest x4 8.85 us: per_device(): last[left] = lax.ppermute(last[left], 'ctx', route.pairs(left, step))]
    all_to_all x0 -> x2, waiting for transfers between devices: none -> 2.89 us  [to_each(): return lax.all_to_all(x, 'ctx', 0, 0)]
    select_n x0 -> x1, other arithmetic: none -> 1.98 us  [per_device(): x = jnp.where(z <= n - step, last[True], last[False])]
  transfers between devices with their start and end apart: 26 -> 24, of which waited for: 14 -> 12; matrix products, arithmetic and copies ran while one was open for 1% -> 2% of each run, Pallas kernels for 12% -> 12%
where the time goes in v6:
time: 142 us; the launch traced here: 141 us
  waiting for transfers between devices  54.4 us (38%)
  starting transfers between devices  42.1 us (30%)
  Pallas kernels  31.4 us (22%)
  local copies, waits for them, and re-layouts  9.8 us (7%)
  other arithmetic  2.04 us (1%)
    ppermute x4, waiting for transfers between devices, per_device(): last[left] = lax.ppermute(last[left], 'ctx', route.pairs(left, step))  22.8 us
    pallas_call x4, Pallas kernels, score(): pl.pallas_call(functools.partial(score_kernel, t, n, rows_here), out_shap...  15 us
    ppermute x9, waiting for transfers between devices, swap_dp(): return lax.ppermute(x, 'dp', [(k, k ^ bit) for k in range(dp_size)])  13 us
    all_to_all x2, starting transfers between devices, to_each(): return lax.all_to_all(x, 'ctx', 0, 0)  9.84 us
    ppermute x3, starting transfers between devices, per_device(): brought.append(lax.ppermute(piece, 'ctx', pairs))  9.58 us
    ppermute x4, starting transfers between devices, per_device(): last[left] = lax.ppermute(last[left], 'ctx', route.pairs(left, step))  8.85 us
    ppermute x5, starting transfers between devices, swap_head(): return lax.ppermute(x, 'head', [(0, 1), (1, 0)])  7.86 us
    ppermute x3, waiting for transfers between devices, per_device(): brought.append(lax.ppermute(piece, 'ctx', pairs))  7.54 us
  transfers between devices with their start and end apart: 24, of which 12 were waited for; matrix products, arithmetic and copies ran while one was open for 2% of the time, Pallas kernels for 12%

profile of v6, /device:TPU:0, one launch (start us, length us, event | category | flops | bytes accessed | tf_op | source)
XLA Modules:
  0.0 140.8 jit_solution(11281686116860681502)
XLA Ops:
  0.7 1.1 dynamic-slice_bitcast_fusion.1
  1.7 0.9 broadcast_in_dim.16
  2.6 6.3 %all-to-all-start.1 = ((bf16[4,512,128]{2,1,0:T(8,128)(2,1)}), bf16[4,512,128]{2,1,0:T(8,128)(2,1)S(1)}, u32[]{:S(2)}, u32[]{:S(2)}) async-start(bf16[4,512,128]{2,1,0:T(8,128)(2,1)} %broadcast_in_dim.16), calls=%async_computation.1 | async-start | bytes 1048576 | tf_op jit(solution)/shard_map/all_to_all | solution.py:627
  9.0 4.8 %collective-permute-start.2 = (bf16[576,512]{1,0:T(8,128)(2,1)S(1)}, bf16[576,512]{1,0:T(8,128)(2,1)}, u32[]{:S(2)}, u32[]{:S(2)}) collective-permute-start(bf16[576,512]{1,0:T(8,128)(2,1)S(1)} %dynamic-slice_bitcast_fusion.refs_0_), channel_id=1, source_target_pairs={{0,1},{1,2},{2,3},{4,5},{5,6},{6,7},{8,9},{9,10},{10,11},{12,13},{... | collective-permute-start | bytes 1769480 | tf_op jit(solution)/shard_map/ppermute | solution.py:654
  13.7 1.3 collective-permute-start.1
  15.8 1.9 %copy-done.1 = bf16[384,4096]{1,0:T(8,128)(2,1)S(1)} copy-done((bf16[384,4096]{1,0:T(8,128)(2,1)S(1)}, bf16[384,4096]{1,0:T(8,128)(2,1)}, u32[]{:S(2)}) %copy-start.1) | copy-done | bytes 3145752
  17.6 0.9 copy-done.8
  18.6 1.3 project.1
  19.9 1.0 copy-done.2
  20.8 0.7 copy-done.6
  21.6 2.9 %all-to-all-done.1 = bf16[4,512,128]{2,1,0:T(8,128)(2,1)S(1)} async-done(((bf16[4,512,128]{2,1,0:T(8,128)(2,1)}), bf16[4,512,128]{2,1,0:T(8,128)(2,1)S(1)}, u32[]{:S(2)}, u32[]{:S(2)}) %all-to-all-start.1) | async-done | bytes 524320 | tf_op jit(solution)/shard_map/all_to_all | solution.py:627
  24.5 3.5 %all-to-all-start = ((f32[4,16,4224]{2,1,0:T(8,128)}), f32[4,16,4224]{2,1,0:T(8,128)S(1)}, u32[]{:S(2)}, u32[]{:S(2)}) async-start(f32[4,16,4224]{2,1,0:T(8,128)} %copy-done.2), calls=%async_computation | async-start | bytes 2162688 | tf_op jit(solution)/shard_map/all_to_all | solution.py:627
  28.0 1.6 %collective-permute-start = (bf16[16,64,576]{2,1,0:T(8,128)(2,1)}, bf16[16,64,576]{2,1,0:T(8,128)(2,1)}, u32[]{:S(2)}, u32[]{:S(2)}) collective-permute-start(bf16[16,64,576]{2,1,0:T(8,128)(2,1)} %bitcast.37), channel_id=1, source_target_pairs={{0,4},{4,0},{1,5},{5,1},{2,6},{6,2},{3,7},{7,3},{8,12},{12,8},{9,1... | collective-permute-start | bytes 3538952 | tf_op jit(solution)/shard_map/ppermute | solution.py:630
  29.6 1.8 %collective-permute-done.2.refs_1_ = bf16[576,512]{1,0:T(8,128)(2,1)} collective-permute-done((bf16[576,512]{1,0:T(8,128)(2,1)S(1)}, bf16[576,512]{1,0:T(8,128)(2,1)}, u32[]{:S(2)}, u32[]{:S(2)}) %collective-permute-start.2) | collective-permute-done | bytes 589856 | tf_op jit(solution)/shard_map/ppermute | solution.py:654
  31.3 1.5 %collective-permute-start.8 = (bf16[576,512]{1,0:T(8,128)(2,1)}, bf16[576,512]{1,0:T(8,128)(2,1)}, u32[]{:S(2)}, u32[]{:S(2)}) collective-permute-start(bf16[576,512]{1,0:T(8,128)(2,1)} %collective-permute-done.2.refs_1_), channel_id=1, source_target_pairs={{1,2},{2,3},{5,6},{6,7},{9,10},{10,11},{13,14},{14,15},{17,18},{18... | collective-permute-start | bytes 1769480 | tf_op jit(solution)/shard_map/ppermute | solution.py:654
  32.9 2.4 %collective-permute-done.1.refs_0_.refs_2_ = bf16[576,512]{1,0:T(8,128)(2,1)} collective-permute-done((bf16[576,512]{1,0:T(8,128)(2,1)S(1)}, bf16[576,512]{1,0:T(8,128)(2,1)}, u32[]{:S(2)}, u32[]{:S(2)}) %collective-permute-start.1) | collective-permute-done | bytes 589856 | tf_op jit(solution)/shard_map/ppermute | solution.py:654
  35.2 1.3 collective-permute-start.7
  36.5 1.6 %collective-permute-start.3 = (bf16[64,2176]{1,0:T(8,128)(2,1)}, bf16[64,2176]{1,0:T(8,128)(2,1)}, u32[]{:S(2)}, u32[]{:S(2)}) collective-permute-start(bf16[64,2176]{1,0:T(8,128)(2,1)} %copy-done.6), channel_id=1, source_target_pairs={{0,16},{8,24},{16,0},{24,8},{1,17},{9,25},{17,1},{25,9},{2,18},{10... | collective-permute-start | bytes 835592 | tf_op jit(solution)/shard_map/ppermute | solution.py:633
  38.1 1.5 %collective-permute-start.6 = (bf16[2048,128]{1,0:T(8,128)(2,1)S(1)}, bf16[2048,128]{1,0:T(8,128)(2,1)}, u32[]{:S(2)}, u32[]{:S(2)}) collective-permute-start(bf16[2048,128]{1,0:T(8,128)(2,1)S(1)} %bitcast.18), channel_id=1, source_target_pairs={{0,4},{4,0},{1,5},{5,1},{2,6},{6,2},{3,7},{7,3},{8,12},{12,8},{9,1... | collective-permute-start | bytes 1572872 | tf_op jit(solution)/shard_map/ppermute | solution.py:630
  39.6 3.9 %collective-permute-done.3.refs_1_ = bf16[64,2176]{1,0:T(8,128)(2,1)} collective-permute-done((bf16[64,2176]{1,0:T(8,128)(2,1)}, bf16[64,2176]{1,0:T(8,128)(2,1)}, u32[]{:S(2)}, u32[]{:S(2)}) %collective-permute-start.3) | collective-permute-done | bytes 278560 | tf_op jit(solution)/shard_map/ppermute | solution.py:633
  44.0 18.6 %collective-permute-done.7.refs_0_ = bf16[576,512]{1,0:T(8,128)(2,1)} collective-permute-done((bf16[576,512]{1,0:T(8,128)(2,1)}, bf16[576,512]{1,0:T(8,128)(2,1)}, u32[]{:S(2)}, u32[]{:S(2)}) %collective-permute-start.7) | collective-permute-done | bytes 589856 | tf_op jit(solution)/shard_map/ppermute | solution.py:654
  62.6 2.0 %broadcast_select_fusion = bf16[576,512]{1,0:T(8,128)(2,1)} fusion(bf16[576,512]{1,0:T(8,128)(2,1)} %collective-permute-done.7.refs_0_, bf16[576,512]{1,0:T(8,128)(2,1)} %collective-permute-done.8.refs_1_, pred[]{:T(512)S(6)} %le.3), kind=kLoop, calls=%fused_computation.1 | loop fusion | flops 294912 | bytes 1769473 | tf_op jit(solution)/shard_map/jit(_where)/select_n | solution.py:649
  64.6 1.3 collective-permute-start.10
  65.9 0.9 copy-done.7
  66.8 1.2 arrange.1
  68.0 0.9 copy-done.4
  69.7 2.4 %logits.1.part = f32[2,16,2048]{2,1,0:T(8,128)S(1)} custom-call(f32[4,16,4224]{2,1,0:T(8,128)S(1)} %all-to-all-done.received, bf16[2048,128]{1,0:T(8,128)(2,1)S(1)} %bitcast.19, bf16[2048,128]{1,0:T(8,128)(2,1)} %collective-permute-done.6.other), custom_call_target="tpu_custom_call" | custom-call | flops 536870912 | bytes 2392064 | tf_op jit(solution)/shard_map/logits/pallas_call | solution.py:345
  72.1 1.6 %collective-permute-start.9 = (f32[2,16,2048]{2,1,0:T(8,128)S(1)}, f32[2,16,2048]{2,1,0:T(8,128)S(1)}, u32[]{:S(2)}, u32[]{:S(2)}) collective-permute-start(f32[2,16,2048]{2,1,0:T(8,128)S(1)} %logits.1.part), channel_id=1, source_target_pairs={{0,4},{4,0},{1,5},{5,1},{2,6},{6,2},{3,7},{7,3},{8,12},{12,8},{9,1... | collective-permute-start | bytes 786440 | tf_op jit(solution)/shard_map/ppermute | solution.py:630
  73.7 3.4 %score.4 = (bf16[16,128,512]{2,1,0:T(8,128)(2,1)S(1)}, f32[16,128]{1,0:T(8,128)S(1)}, f32[16,128]{1,0:T(8,128)S(1)}, f32[16,128]{1,0:T(8,128)S(1)}) custom-call(s32[19]{0:T(128)S(1)} %fusion.info, s32[64]{0:T(128)S(1)} %bitcast.32, bf16[16,64,576]{2,1,0:T(8,128)(2,1)S(1)} %bitcast.38, bf16[16,64,576]{2,1,0:T(8,128)(2,1)} %collective-permute-done.other, ...), custom_call_target="tpu_custom_call" | custom-call | flops 1207959552 | bytes 5046272 | tf_op jit(solution)/shard_map/score/pallas_call | solution.py:246
  77.1 3.7 %score.5 = (bf16[16,128,512]{2,1,0:T(8,128)(2,1)S(1)}, f32[16,128]{1,0:T(8,128)S(1)}, f32[16,128]{1,0:T(8,128)S(1)}, f32[16,128]{1,0:T(8,128)S(1)}) custom-call(s32[19]{0:T(128)S(1)} %fusion.info, s32[64]{0:T(128)S(1)} %bitcast.33, bf16[16,64,576]{2,1,0:T(8,128)(2,1)S(1)} %bitcast.39, bf16[16,64,576]{2,1,0:T(8,128)(2,1)} %collective-permute-done.other, ...), custom_call_target="tpu_custom_call" | custom-call | flops 1207959552 | bytes 5046272 | tf_op jit(solution)/shard_map/score/pallas_call | solution.py:246
  80.8 3.7 %score.6 = (bf16[16,128,512]{2,1,0:T(8,128)(2,1)S(1)}, f32[16,128]{1,0:T(8,128)S(1)}, f32[16,128]{1,0:T(8,128)S(1)}, f32[16,128]{1,0:T(8,128)S(1)}) custom-call(s32[19]{0:T(128)S(1)} %fusion.info, s32[64]{0:T(128)S(1)} %bitcast.34, bf16[16,64,576]{2,1,0:T(8,128)(2,1)S(1)} %bitcast.40, bf16[16,64,576]{2,1,0:T(8,128)(2,1)} %collective-permute-done.other, ...), custom_call_target="tpu_custom_call" | custom-call | flops 1207959552 | bytes 5046272 | tf_op jit(solution)/shard_map/score/pallas_call | solution.py:246
  84.6 0.8 softmax.1
  85.4 3.3 %collective-permute-done.10.refs_0_ = bf16[576,512]{1,0:T(8,128)(2,1)} collective-permute-done((bf16[576,512]{1,0:T(8,128)(2,1)}, bf16[576,512]{1,0:T(8,128)(2,1)}, u32[]{:S(2)}, u32[]{:S(2)}) %collective-permute-start.10) | collective-permute-done | bytes 589856 | tf_op jit(solution)/shard_map/ppermute | solution.py:650
  88.7 4.1 %score.7 = (bf16[16,128,512]{2,1,0:T(8,128)(2,1)S(1)}, f32[16,128]{1,0:T(8,128)S(1)}, f32[16,128]{1,0:T(8,128)S(1)}, f32[16,128]{1,0:T(8,128)S(1)}) custom-call(s32[19]{0:T(128)S(1)} %fusion.info, s32[64]{0:T(128)S(1)} %bitcast.36, bf16[16,64,576]{2,1,0:T(8,128)(2,1)S(1)} %bitcast.41, bf16[16,64,576]{2,1,0:T(8,128)(2,1)} %collective-permute-done.other, ...), custom_call_target="tpu_custom_call" | custom-call | flops 1207959552 | bytes 5046272 | tf_op jit(solution)/shard_map/score/pallas_call | solution.py:246
  92.8 1.6 %collective-permute-start.11 = (f32[2,16,128]{2,1,0:T(8,128)S(1)}, f32[2,16,128]{2,1,0:T(8,128)S(1)}, u32[]{:S(2)}, u32[]{:S(2)}) collective-permute-start(f32[2,16,128]{2,1,0:T(8,128)S(1)} %pad_maximum_fusion.1), channel_id=1, source_target_pairs={{0,4},{4,0},{1,5},{5,1},{2,6},{6,2},{3,7},{7,3},{8,12},{12,8},{9,1... | collective-permute-start | bytes 49160 | tf_op jit(solution)/shard_map/ppermute | solution.py:630
  94.4 2.2 %collective-permute-done.11.refs_10_ = f32[2,16,128]{2,1,0:T(8,128)S(1)} collective-permute-done((f32[2,16,128]{2,1,0:T(8,128)S(1)}, f32[2,16,128]{2,1,0:T(8,128)S(1)}, u32[]{:S(2)}, u32[]{:S(2)}) %collective-permute-start.11) | collective-permute-done | bytes 16416 | tf_op jit(solution)/shard_map/ppermute | solution.py:630
  96.6 2.7 %delta.1 = (f32[16,2048]{1,0:T(8,128)S(1)}, bf16[16,2048]{1,0:T(8,128)(2,1)S(1)}) custom-call(s32[19]{0:T(128)S(1)} %fusion.info, bf16[16,128,512]{2,1,0:T(8,128)(2,1)S(1)} %get-tuple-element.61.refs_0_, bf16[16,128,512]{2,1,0:T(8,128)(2,1)S(1)} %get-tuple-element.62.refs_1_, bf16[16,128,512]{2,1,0:T(8,128)(2,1)S(1)} %get-tuple-element.63.refs_2_, ...), custom_call_target="tpu_custom_call" | custom-call | flops 8388608 | bytes 8388608 | tf_op jit(solution)/shard_map/delta/pallas_call | solution.py:295
  99.3 1.6 %collective-permute-start.12 = (bf16[16,2048]{1,0:T(8,128)(2,1)S(1)}, bf16[16,2048]{1,0:T(8,128)(2,1)S(1)}, u32[]{:S(2)}, u32[]{:S(2)}) collective-permute-start(bf16[16,2048]{1,0:T(8,128)(2,1)S(1)} %get-tuple-element.74.sent), channel_id=1, source_target_pairs={{0,4},{4,0},{1,5},{5,1},{2,6},{6,2},{3,7},{7,3},{8,12},{12,8},{9,1... | collective-permute-start | bytes 196616 | tf_op jit(solution)/shard_map/ppermute | solution.py:630
  100.9 2.7 %collective-permute-done.12.brought = bf16[16,2048]{1,0:T(8,128)(2,1)S(1)} collective-permute-done((bf16[16,2048]{1,0:T(8,128)(2,1)S(1)}, bf16[16,2048]{1,0:T(8,128)(2,1)S(1)}, u32[]{:S(2)}, u32[]{:S(2)}) %collective-permute-start.12) | collective-permute-done | bytes 65568 | tf_op jit(solution)/shard_map/ppermute | solution.py:630
  103.7 3.6 %gradient.1 = bf16[16,4224]{1,0:T(8,128)(2,1)S(1)} custom-call(f32[4,16,4224]{2,1,0:T(8,128)S(1)} %all-to-all-done.received, bf16[2048,128]{1,0:T(8,128)(2,1)S(1)} %bitcast.20, bf16[2048,128]{1,0:T(8,128)(2,1)} %collective-permute-done.6.other, f32[2,16,2048]{2,1,0:T(8,128)S(1)} %get-tuple-element.59.refs_11_.probs, ...), custom_call_target="tpu_custom_call" | custom-call | flops 1073741824 | bytes 2916352 | tf_op jit(solution)/shard_map/gradient/pallas_call | solution.py:496
  107.3 1.6 %collective-permute-start.16 = (bf16[1,16,4224]{2,1,0:T(8,128)(2,1)S(1)}, bf16[1,16,4224]{2,1,0:T(8,128)(2,1)S(1)}, u32[]{:S(2)}, u32[]{:S(2)}) collective-permute-start(bf16[1,16,4224]{2,1,0:T(8,128)(2,1)S(1)} %bitcast.23), channel_id=1, source_target_pairs={{0,16},{8,24},{16,0},{24,8},{1,17},{9,25},{17,1},{25,9},{2,18},{10... | collective-permute-start | bytes 405512 | tf_op jit(solution)/shard_map/ppermute | solution.py:633
  108.8 2.9 %collective-permute-start.15 = (bf16[1,16,4224]{2,1,0:T(8,128)(2,1)S(1)}, bf16[1,16,4224]{2,1,0:T(8,128)(2,1)S(1)}, u32[]{:S(2)}, u32[]{:S(2)}) collective-permute-start(bf16[1,16,4224]{2,1,0:T(8,128)(2,1)S(1)} %bitcast.24), channel_id=1, source_target_pairs={{0,3},{1,0},{2,1},{3,2},{4,7},{5,4},{6,5},{7,6},{8,11},{9,8},{10,9... | collective-permute-start | bytes 405512 | tf_op jit(solution)/shard_map/ppermute | solution.py:700
  111.7 6.1 %collective-permute-start.14 = (bf16[1,16,4224]{2,1,0:T(8,128)(2,1)S(1)}, bf16[1,16,4224]{2,1,0:T(8,128)(2,1)S(1)}, u32[]{:S(2)}, u32[]{:S(2)}) collective-permute-start(bf16[1,16,4224]{2,1,0:T(8,128)(2,1)S(1)} %bitcast.25), channel_id=1, source_target_pairs={{0,2},{1,3},{2,0},{3,1},{4,6},{5,7},{6,4},{7,5},{8,10},{9,11},{10,... | collective-permute-start | bytes 405512 | tf_op jit(solution)/shard_map/ppermute | solution.py:700
  118.9 1.6 %collective-permute-done.15 = bf16[1,16,4224]{2,1,0:T(8,128)(2,1)S(1)} collective-permute-done((bf16[1,16,4224]{2,1,0:T(8,128)(2,1)S(1)}, bf16[1,16,4224]{2,1,0:T(8,128)(2,1)S(1)}, u32[]{:S(2)}, u32[]{:S(2)}) %collective-permute-start.15) | collective-permute-done | bytes 135200 | tf_op jit(solution)/shard_map/ppermute | solution.py:700
  120.5 6.0 %collective-permute-done.14 = bf16[1,16,4224]{2,1,0:T(8,128)(2,1)S(1)} collective-permute-done((bf16[1,16,4224]{2,1,0:T(8,128)(2,1)S(1)}, bf16[1,16,4224]{2,1,0:T(8,128)(2,1)S(1)}, u32[]{:S(2)}, u32[]{:S(2)}) %collective-permute-start.14) | collective-permute-done | bytes 135200 | tf_op jit(solution)/shard_map/ppermute | solution.py:700
  127.1 7.4 %collective-permute-done.19.refs_5_ = bf16[3,16,4224]{2,1,0:T(8,128)(2,1)S(1)} collective-permute-done((bf16[3,16,4224]{2,1,0:T(8,128)(2,1)S(1)}, bf16[3,16,4224]{2,1,0:T(8,128)(2,1)S(1)}, u32[]{:S(2)}, u32[]{:S(2)}) %collective-permute-start.19) | collective-permute-done | bytes 405536 | tf_op jit(solution)/shard_map/ppermute | solution.py:633
  134.5 1.7 %collective-permute-done.21.refs_7_ = bf16[3,16,4224]{2,1,0:T(8,128)(2,1)S(1)} collective-permute-done((bf16[3,16,4224]{2,1,0:T(8,128)(2,1)S(1)}, bf16[3,16,4224]{2,1,0:T(8,128)(2,1)S(1)}, u32[]{:S(2)}, u32[]{:S(2)}) %collective-permute-start.21) | collective-permute-done | bytes 405536 | tf_op jit(solution)/shard_map/ppermute | solution.py:633
  136.3 4.4 %outer.1 = (f32[384,4096]{1,0:T(8,128)}, f32[32,1792]{1,0:T(8,128)}, f32[1,64]{1,0:T(1,128)}) custom-call(s32[19]{0:T(128)S(1)} %fusion.info, bf16[384,256]{1,0:T(8,128)(2,1)S(1)} %copy-done.10, bf16[256,1792]{1,0:T(8,128)(2,1)S(1)} %copy-done.5, bf16[1,16,4224]{2,1,0:T(8,128)(2,1)S(1)} %bitcast.28, ...), custom_call_target="tpu_custom_call" | custom-call | flops 805306368 | bytes 8388608 | tf_op jit(solution)/shard_map/outer/pallas_call | solution.py:585
  (47 shorter events, 3.8 us)
Async XLA Ops:
  0.6 8.3 %copy-start = (bf16[1,1024,576]{1,2,0:T(8,128)(2,1)S(1)}, bf16[1,1024,576]{1,2,0:T(8,128)(2,1)}, u32[]{:S(2)}) copy-start(bf16[1,1024,576]{1,2,0:T(8,128)(2,1)} %param.12) | copy-start | bytes 3538948
  0.6 15.1 %copy-start.11 = (bf16[1792,32]{0,1:T(8,128)(2,1)S(1)}, bf16[1792,32]{0,1:T(8,128)(2,1)}, u32[]{:S(2)}) copy-start(bf16[1792,32]{0,1:T(8,128)(2,1)} %param.16) | copy-start | bytes 344068
  0.7 15.1 %copy-start.3 = (bf16[1,64,7168]{2,1,0:T(8,128)(2,1)S(1)}, bf16[1,64,7168]{2,1,0:T(8,128)(2,1)}, u32[]{:S(2)}) copy-start(bf16[1,64,7168]{2,1,0:T(8,128)(2,1)} %param.10) | copy-start | bytes 2752516
  2.6 21.9 %all-to-all-start.1 = ((bf16[4,512,128]{2,1,0:T(8,128)(2,1)}), bf16[4,512,128]{2,1,0:T(8,128)(2,1)S(1)}, u32[]{:S(2)}, u32[]{:S(2)}) async-start(bf16[4,512,128]{2,1,0:T(8,128)(2,1)} %broadcast_in_dim.16), calls=%async_computation.1 | async-start | bytes 1048576 | tf_op jit(solution)/shard_map/all_to_all | solution.py:627
  9.0 22.4 %collective-permute-start.2 = (bf16[576,512]{1,0:T(8,128)(2,1)S(1)}, bf16[576,512]{1,0:T(8,128)(2,1)}, u32[]{:S(2)}, u32[]{:S(2)}) collective-permute-start(bf16[576,512]{1,0:T(8,128)(2,1)S(1)} %dynamic-slice_bitcast_fusion.refs_0_), channel_id=1, source_target_pairs={{0,1},{1,2},{2,3},{4,5},{5,6},{6,7},{8,9},{9,10},{10,11},{12,13},{... | collective-permute-start | bytes 1769480 | tf_op jit(solution)/shard_map/ppermute | solution.py:654
  13.7 21.5 %collective-permute-start.1 = (bf16[576,512]{1,0:T(8,128)(2,1)S(1)}, bf16[576,512]{1,0:T(8,128)(2,1)}, u32[]{:S(2)}, u32[]{:S(2)}) collective-permute-start(bf16[576,512]{1,0:T(8,128)(2,1)S(1)} %dynamic-slice_bitcast_fusion.refs_0_), channel_id=1, source_target_pairs={{1,0},{2,1},{3,2},{5,4},{6,5},{7,6},{9,8},{10,9},{11,10},{13,12},{... | collective-permute-start | bytes 1769480 | tf_op jit(solution)/shard_map/ppermute | solution.py:654
  15.7 1.9 %copy-start.1 = (bf16[384,4096]{1,0:T(8,128)(2,1)S(1)}, bf16[384,4096]{1,0:T(8,128)(2,1)}, u32[]{:S(2)}) copy-start(bf16[384,4096]{1,0:T(8,128)(2,1)} %weight.1) | copy-start | bytes 9437188
  17.6 0.9 copy-start.8
  19.9 1.0 copy-start.2
  20.8 0.7 copy-start.6
  24.5 45.2 %all-to-all-start = ((f32[4,16,4224]{2,1,0:T(8,128)}), f32[4,16,4224]{2,1,0:T(8,128)S(1)}, u32[]{:S(2)}, u32[]{:S(2)}) async-start(f32[4,16,4224]{2,1,0:T(8,128)} %copy-done.2), calls=%async_computation | async-start | bytes 2162688 | tf_op jit(solution)/shard_map/all_to_all | solution.py:627
  28.0 45.7 %collective-permute-start = (bf16[16,64,576]{2,1,0:T(8,128)(2,1)}, bf16[16,64,576]{2,1,0:T(8,128)(2,1)}, u32[]{:S(2)}, u32[]{:S(2)}) collective-permute-start(bf16[16,64,576]{2,1,0:T(8,128)(2,1)} %bitcast.37), channel_id=1, source_target_pairs={{0,4},{4,0},{1,5},{5,1},{2,6},{6,2},{3,7},{7,3},{8,12},{12,8},{9,1... | collective-permute-start | bytes 3538952 | tf_op jit(solution)/shard_map/ppermute | solution.py:630
  31.3 12.1 %collective-permute-start.8 = (bf16[576,512]{1,0:T(8,128)(2,1)}, bf16[576,512]{1,0:T(8,128)(2,1)}, u32[]{:S(2)}, u32[]{:S(2)}) collective-permute-start(bf16[576,512]{1,0:T(8,128)(2,1)} %collective-permute-done.2.refs_1_), channel_id=1, source_target_pairs={{1,2},{2,3},{5,6},{6,7},{9,10},{10,11},{13,14},{14,15},{17,18},{18... | collective-permute-start | bytes 1769480 | tf_op jit(solution)/shard_map/ppermute | solution.py:654
  35.2 27.4 %collective-permute-start.7 = (bf16[576,512]{1,0:T(8,128)(2,1)}, bf16[576,512]{1,0:T(8,128)(2,1)}, u32[]{:S(2)}, u32[]{:S(2)}) collective-permute-start(bf16[576,512]{1,0:T(8,128)(2,1)} %collective-permute-done.1.refs_0_.refs_2_), channel_id=1, source_target_pairs={{1,0},{2,1},{5,4},{6,5},{9,8},{10,9},{13,12},{14,13},{17,16},{18,1... | collective-permute-start | bytes 1769480 | tf_op jit(solution)/shard_map/ppermute | solution.py:654
  36.5 6.9 %collective-permute-start.3 = (bf16[64,2176]{1,0:T(8,128)(2,1)}, bf16[64,2176]{1,0:T(8,128)(2,1)}, u32[]{:S(2)}, u32[]{:S(2)}) collective-permute-start(bf16[64,2176]{1,0:T(8,128)(2,1)} %copy-done.6), channel_id=1, source_target_pairs={{0,16},{8,24},{16,0},{24,8},{1,17},{9,25},{17,1},{25,9},{2,18},{10... | collective-permute-start | bytes 835592 | tf_op jit(solution)/shard_map/ppermute | solution.py:633
  38.1 31.6 %collective-permute-start.6 = (bf16[2048,128]{1,0:T(8,128)(2,1)S(1)}, bf16[2048,128]{1,0:T(8,128)(2,1)}, u32[]{:S(2)}, u32[]{:S(2)}) collective-permute-start(bf16[2048,128]{1,0:T(8,128)(2,1)S(1)} %bitcast.18), channel_id=1, source_target_pairs={{0,4},{4,0},{1,5},{5,1},{2,6},{6,2},{3,7},{7,3},{8,12},{12,8},{9,1... | collective-permute-start | bytes 1572872 | tf_op jit(solution)/shard_map/ppermute | solution.py:630
  43.5 22.4 %collective-permute-start.4 = (bf16[64,2176]{1,0:T(8,128)(2,1)}, bf16[64,2176]{1,0:T(8,128)(2,1)S(1)}, u32[]{:S(2)}, u32[]{:S(2)}) collective-permute-start(bf16[64,2176]{1,0:T(8,128)(2,1)} %copy-done.6), channel_id=1, source_target_pairs={{0,8},{8,0},{16,24},{24,16},{1,9},{9,1},{17,25},{25,17},{2,10},{10... | collective-permute-start | bytes 835592 | tf_op jit(solution)/shard_map/ppermute | solution.py:633
  43.5 22.4 %collective-permute-start.5 = (bf16[64,2176]{1,0:T(8,128)(2,1)}, bf16[64,2176]{1,0:T(8,128)(2,1)S(1)}, u32[]{:S(2)}, u32[]{:S(2)}) collective-permute-start(bf16[64,2176]{1,0:T(8,128)(2,1)} %collective-permute-done.3.refs_1_), channel_id=1, source_target_pairs={{0,8},{8,0},{16,24},{24,16},{1,9},{9,1},{17,25},{25,17},{2,10},{10... | collective-permute-start | bytes 835592 | tf_op jit(solution)/shard_map/ppermute | solution.py:633
  62.6 11.1 %copy-start.12 = (s32[1,64]{1,0:T(1,128)S(1)}, s32[1,64]{1,0:T(1,128)}, u32[]{:S(2)}) copy-start(s32[1,64]{1,0:T(1,128)} %param.14) | copy-start | bytes 772
  64.6 24.1 %collective-permute-start.10 = (bf16[576,512]{1,0:T(8,128)(2,1)}, bf16[576,512]{1,0:T(8,128)(2,1)}, u32[]{:S(2)}, u32[]{:S(2)}) collective-permute-start(bf16[576,512]{1,0:T(8,128)(2,1)} %broadcast_select_fusion), channel_id=1, source_target_pairs={{1,0},{2,3},{5,4},{6,7},{9,8},{10,11},{13,12},{14,15},{17,16},{18,... | collective-permute-start | bytes 1769480 | tf_op jit(solution)/shard_map/ppermute | solution.py:650
  65.9 1.0 copy-start.7
  68.0 0.9 copy-start.4
  69.0 0.7 copy-start.9
  69.6 4.0 %copy-start.13 = (bf16[1,16,64,576]{3,2,1,0:T(8,128)(2,1)S(1)}, bf16[1,16,64,576]{3,2,1,0:T(8,128)(2,1)}, u32[]{:S(2)}) copy-start(bf16[1,16,64,576]{3,2,1,0:T(8,128)(2,1)} %param.11) | copy-start | bytes 3538948
  72.1 12.5 %collective-permute-start.9 = (f32[2,16,2048]{2,1,0:T(8,128)S(1)}, f32[2,16,2048]{2,1,0:T(8,128)S(1)}, u32[]{:S(2)}, u32[]{:S(2)}) collective-permute-start(f32[2,16,2048]{2,1,0:T(8,128)S(1)} %logits.1.part), channel_id=1, source_target_pairs={{0,4},{4,0},{1,5},{5,1},{2,6},{6,2},{3,7},{7,3},{8,12},{12,8},{9,1... | collective-permute-start | bytes 786440 | tf_op jit(solution)/shard_map/ppermute | solution.py:630
  92.8 3.8 %collective-permute-start.11 = (f32[2,16,128]{2,1,0:T(8,128)S(1)}, f32[2,16,128]{2,1,0:T(8,128)S(1)}, u32[]{:S(2)}, u32[]{:S(2)}) collective-permute-start(f32[2,16,128]{2,1,0:T(8,128)S(1)} %pad_maximum_fusion.1), channel_id=1, source_target_pairs={{0,4},{4,0},{1,5},{5,1},{2,6},{6,2},{3,7},{7,3},{8,12},{12,8},{9,1... | collective-permute-start | bytes 49160 | tf_op jit(solution)/shard_map/ppermute | solution.py:630
  99.3 4.3 %collective-permute-start.12 = (bf16[16,2048]{1,0:T(8,128)(2,1)S(1)}, bf16[16,2048]{1,0:T(8,128)(2,1)S(1)}, u32[]{:S(2)}, u32[]{:S(2)}) collective-permute-start(bf16[16,2048]{1,0:T(8,128)(2,1)S(1)} %get-tuple-element.74.sent), channel_id=1, source_target_pairs={{0,4},{4,0},{1,5},{5,1},{2,6},{6,2},{3,7},{7,3},{8,12},{12,8},{9,1... | collective-permute-start | bytes 196616 | tf_op jit(solution)/shard_map/ppermute | solution.py:630
  103.7 32.6 %copy-start.5 = (bf16[256,1792]{1,0:T(8,128)(2,1)S(1)}, bf16[256,1792]{1,0:T(8,128)(2,1)}, u32[]{:S(2)}) copy-start(bf16[256,1792]{1,0:T(8,128)(2,1)} %copy-done.4) | copy-start | bytes 2752516
  103.7 32.6 %copy-start.10 = (bf16[384,256]{1,0:T(8,128)(2,1)S(1)}, bf16[384,256]{1,0:T(8,128)(2,1)}, u32[]{:S(2)}) copy-start(bf16[384,256]{1,0:T(8,128)(2,1)} %copy-done.9) | copy-start | bytes 589828
  107.3 11.1 %collective-permute-start.16 = (bf16[1,16,4224]{2,1,0:T(8,128)(2,1)S(1)}, bf16[1,16,4224]{2,1,0:T(8,128)(2,1)S(1)}, u32[]{:S(2)}, u32[]{:S(2)}) collective-permute-start(bf16[1,16,4224]{2,1,0:T(8,128)(2,1)S(1)} %bitcast.23), channel_id=1, source_target_pairs={{0,16},{8,24},{16,0},{24,8},{1,17},{9,25},{17,1},{25,9},{2,18},{10... | collective-permute-start | bytes 405512 | tf_op jit(solution)/shard_map/ppermute | solution.py:633
  108.8 11.7 %collective-permute-start.15 = (bf16[1,16,4224]{2,1,0:T(8,128)(2,1)S(1)}, bf16[1,16,4224]{2,1,0:T(8,128)(2,1)S(1)}, u32[]{:S(2)}, u32[]{:S(2)}) collective-permute-start(bf16[1,16,4224]{2,1,0:T(8,128)(2,1)S(1)} %bitcast.24), channel_id=1, source_target_pairs={{0,3},{1,0},{2,1},{3,2},{4,7},{5,4},{6,5},{7,6},{8,11},{9,8},{10,9... | collective-permute-start | bytes 405512 | tf_op jit(solution)/shard_map/ppermute | solution.py:700
  111.7 14.7 %collective-permute-start.14 = (bf16[1,16,4224]{2,1,0:T(8,128)(2,1)S(1)}, bf16[1,16,4224]{2,1,0:T(8,128)(2,1)S(1)}, u32[]{:S(2)}, u32[]{:S(2)}) collective-permute-start(bf16[1,16,4224]{2,1,0:T(8,128)(2,1)S(1)} %bitcast.25), channel_id=1, source_target_pairs={{0,2},{1,3},{2,0},{3,1},{4,6},{5,7},{6,4},{7,5},{8,10},{9,11},{10,... | collective-permute-start | bytes 405512 | tf_op jit(solution)/shard_map/ppermute | solution.py:700
  117.8 8.6 %collective-permute-start.13 = (bf16[1,16,4224]{2,1,0:T(8,128)(2,1)S(1)}, bf16[1,16,4224]{2,1,0:T(8,128)(2,1)S(1)}, u32[]{:S(2)}, u32[]{:S(2)}) collective-permute-start(bf16[1,16,4224]{2,1,0:T(8,128)(2,1)S(1)} %bitcast.26), channel_id=1, source_target_pairs={{0,1},{1,2},{2,3},{3,0},{4,5},{5,6},{6,7},{7,4},{8,9},{9,10},{10,1... | collective-permute-start | bytes 405512 | tf_op jit(solution)/shard_map/ppermute | solution.py:700
  118.4 8.1 %collective-permute-start.17 = (bf16[1,16,4224]{2,1,0:T(8,128)(2,1)S(1)}, bf16[1,16,4224]{2,1,0:T(8,128)(2,1)S(1)}, u32[]{:S(2)}, u32[]{:S(2)}) collective-permute-start(bf16[1,16,4224]{2,1,0:T(8,128)(2,1)S(1)} %bitcast.27), channel_id=1, source_target_pairs={{0,8},{8,0},{16,24},{24,16},{1,9},{9,1},{17,25},{25,17},{2,10},{10... | collective-permute-start | bytes 405512 | tf_op jit(solution)/shard_map/ppermute | solution.py:633
  118.4 8.1 %collective-permute-start.18 = (bf16[1,16,4224]{2,1,0:T(8,128)(2,1)S(1)}, bf16[1,16,4224]{2,1,0:T(8,128)(2,1)S(1)}, u32[]{:S(2)}, u32[]{:S(2)}) collective-permute-start(bf16[1,16,4224]{2,1,0:T(8,128)(2,1)S(1)} %collective-permute-done.16.refs_1_), channel_id=1, source_target_pairs={{0,8},{8,0},{16,24},{24,16},{1,9},{9,1},{17,25},{25,17},{2,10},{10... | collective-permute-start | bytes 405512 | tf_op jit(solution)/shard_map/ppermute | solution.py:633
  126.5 8.0 %collective-permute-start.19 = (bf16[3,16,4224]{2,1,0:T(8,128)(2,1)S(1)}, bf16[3,16,4224]{2,1,0:T(8,128)(2,1)S(1)}, u32[]{:S(2)}, u32[]{:S(2)}) collective-permute-start(bf16[3,16,4224]{2,1,0:T(8,128)(2,1)S(1)} %pad_maximum_fusion.refs_4_), channel_id=1, source_target_pairs={{0,16},{8,24},{16,0},{24,8},{1,17},{9,25},{17,1},{25,9},{2,18},{10... | collective-permute-start | bytes 1216520 | tf_op jit(solution)/shard_map/ppermute | solution.py:633
  127.1 7.4 %collective-permute-start.20 = (bf16[3,16,4224]{2,1,0:T(8,128)(2,1)S(1)}, bf16[3,16,4224]{2,1,0:T(8,128)(2,1)S(1)}, u32[]{:S(2)}, u32[]{:S(2)}) collective-permute-start(bf16[3,16,4224]{2,1,0:T(8,128)(2,1)S(1)} %pad_maximum_fusion.refs_4_), channel_id=1, source_target_pairs={{0,8},{8,0},{16,24},{24,16},{1,9},{9,1},{17,25},{25,17},{2,10},{10... | collective-permute-start | bytes 1216520 | tf_op jit(solution)/shard_map/ppermute | solution.py:633
  134.5 1.7 %collective-permute-start.21 = (bf16[3,16,4224]{2,1,0:T(8,128)(2,1)S(1)}, bf16[3,16,4224]{2,1,0:T(8,128)(2,1)S(1)}, u32[]{:S(2)}, u32[]{:S(2)}) collective-permute-start(bf16[3,16,4224]{2,1,0:T(8,128)(2,1)S(1)} %collective-permute-done.19.refs_5_), channel_id=1, source_target_pairs={{0,8},{8,0},{16,24},{24,16},{1,9},{9,1},{17,25},{25,17},{2,10},{10... | collective-permute-start | bytes 1216520 | tf_op jit(solution)/shard_map/ppermute | solution.py:633

commit v7 on v5

--- a/solution.py
+++ b/solution.py
@@ -140,20 +140,14 @@
     positions,
     mine,
     other,
-    keys,
-    top_before,
-    mass_before,
-    weights,
-    top,
-    top_all,
-    mass_all,
-    mass,
-    even,
-    odd,
+    *refs,
 ):
+    chains, refs = refs[:-9], refs[-9:]
+    top_before, mass_before, weights, top, top_all, mass_all, mass, even, odd = refs
     count, heads, depth = mine.shape
     limits = [positions[info[0] * count + q] - info[base_at] for q in range(count)]
-    span = keys.shape[1]
+    part = chains[0].shape[1]
+    span = part * len(chains)
     key_at = lax.broadcasted_iota(jnp.int32, (1, span), 1)
     row_at = lax.broadcasted_iota(jnp.int32, (heads, lanes), 0)
     lane_at = lax.broadcasted_iota(jnp.int32, (heads, lanes), 1)
@@ -164,7 +158,8 @@
     def multiply(step):
         at, k = work[step]
         rows = (mine, other)[k][at : at + group].reshape(group * heads, depth)
-        held[step % 2][...] = times(rows, keys[...], 1, 0)
+        for c, keys in enumerate(chains):
+            held[step % 2][:, c * part : (c + 1) * part] = times(rows, keys[...], 1, 0)
 
     multiply(0)
     for step, (at, k) in enumerate(work):
@@ -202,27 +197,27 @@
         ] * jnp.exp2((now - joint) * exponent_scale)
 
 
-def score(t, n, info, positions, mine, other, keys, before):
+def score(t, n, info, positions, mine, other, chains, before):
     count, heads, depth = mine.shape
-    span = keys.shape[1]
+    span = chains[0].shape[1] * len(chains)
     stats = jax.ShapeDtypeStruct((count, lanes), f32)
     if before is None:
         before = (jnp.zeros((count, lanes), f32),) * 2
     return pl.pallas_call(
         functools.partial(score_kernel, t, 1 + n + t),
         out_shape=(jax.ShapeDtypeStruct((count, 2 * heads, span), bf16), stats, stats, stats),
-        in_specs=[in_smem()] * 2 + [in_vmem()] * 5,
+        in_specs=[in_smem()] * 2 + [in_vmem()] * (4 + len(chains)),
         out_specs=(in_vmem(),) * 4,
         scratch_shapes=[pltpu.VMEM((count, lanes), f32)]
         + [pltpu.VMEM((min(group_size, count) * heads, span), f32)] * 2,
         compiler_params=params(),
         cost_estimate=pl.CostEstimate(
             flops=4 * count * heads * depth * span,
-            bytes_accessed=2 * (2 * mine.size + keys.size + 2 * count * heads * span),
+            bytes_accessed=2 * (2 * mine.size + depth * span + 2 * count * heads * span),
             transcendentals=2 * count * heads * span,
         ),
         name="score",
-    )(info, positions, mine, other, keys, *before)
+    )(info, positions, mine, other, *chains, *before)
 
 
 def delta_kernel(blocks, *refs):
@@ -595,54 +590,64 @@
     table = jnp.array(device_table(n, head_size, dp_size, rows))
     info = lax.dynamic_index_in_dim(table, (z * head_size + y) * dp_size + dp, 0, False)
 
-    keys_mine = [lax.dynamic_slice_in_dim(main_keys[0].T, y * half, half, 1)]
-    keys_mine.append(onward(keys_mine[0]))
+    key_half = lax.dynamic_slice_in_dim(main_keys[0].T, y * half, half, 1)
+    chains = [[key_half[:, : half // 2], key_half[:, half // 2 :]]]
+    chains.append([onward(one) for one in chains[0]])
     queries = main_queries[0]
     other_queries = swap_head(queries)
-    index_parts = [lax.dynamic_slice_in_dim(index_keys[0], y * half, half)]
-    index_parts += [onward(index_parts[0], t) for t in range(1, n - 1)]
+    index_parts = [lax.dynamic_slice_in_dim(index_keys[0], y * half, half)] + [None] * (n - 1)
+    index_parts[1] = onward(index_parts[0])
+    index_parts[1], back = lax.optimization_barrier((index_parts[1], index_parts[0]))
+    index_parts[n - 1] = onward(back, n - 1)
     parts, kept = project(info, queries_here, q_latent[0], w_query, hidden[0], w_weights.T)
-    received = onward(parts[0])
+
+    def advance(step, running):
+        running = onward(running)
+        return running + parts[step] if step < n - 1 else running
+
+    summed = advance(1, parts[0])
     order_at = 1 + 3 * n
     dp_at = order_at + n * dp_size
     weights, tops, before = [], [], None
 
-    def score_next(keys):
+    def score_next():
         nonlocal before
         t = len(weights)
         numer, top, *before = score(
-            t, n, info, sequence_positions, queries, other_queries, keys, before
+            t, n, info, sequence_positions, queries, other_queries, chains[t], before
         )
         weights.append(numer)
         tops.append(top)
 
     index_own = index_other = None
     for t in range(1, n - 1):
-        summed = received + parts[t]
+        summed = advance(t + 1, summed)
         if t == 1:
-            keys, summed, index_parts = lax.optimization_barrier(
-                (keys_mine[t], summed, index_parts)
+            sent_on, summed, index_parts = lax.optimization_barrier(
+                (chains[t], summed, index_parts)
             )
-            index_parts.append(onward(index_parts[0], n - 1))
+            for k in range(2, n - 1):
+                index_parts[k] = onward(index_parts[1]) if k == 2 else onward(index_parts[0], k)
         elif t == 2:
             index_own = jnp.concatenate(index_parts)
-            keys, summed, index_own = lax.optimization_barrier((keys_mine[t], summed, index_own))
+            sent_on, summed, index_own = lax.optimization_barrier((chains[t], summed, index_own))
             index_other = swap_head(index_own)
         else:
-            keys, summed = lax.optimization_barrier((keys_mine[t], summed))
-        keys_mine[t] = keys
-        keys_mine.append(onward(keys))
-        received = onward(summed)
+            sent_on, summed = lax.optimization_barrier((chains[t], summed))
+        chains[t] = sent_on
+        chains.append([onward(one) for one in sent_on])
+    received = summed
     while len(weights) < n - 2:
-        score_next(keys_mine[len(weights)])
+        score_next()
     latents, hiddens = arrange(dp_at, info, rows_latent, over_dp(kept))
     before, latents, hiddens = lax.optimization_barrier((before, latents, hiddens))
-    score_next(keys_mine[n - 2])
+    score_next()
 
     part = make_logits(heads_here, received, parts[n - 1], index_own, index_other)
     probs, log_probs = make_softmax(n, info, sequence_positions, part, swap_head(part))
 
-    score_next(keys_mine[n - 1])
+    before, probs, log_probs = lax.optimization_barrier((before, probs, log_probs))
+    score_next()
     delta_own, sent = make_delta(weights, tops, *before, swap_head(jnp.stack(before)), probs)
     piece = gradients(
         heads_here,

time: 131 us -> 135 us (1.031); the launches traced: 128 us -> 134 us
  starting transfers between devices: 28.6 us -> 34.7 us
    ppermute x9 -> x12, waiting for transfers between devices: 47.8 us -> 38.6 us  [onward(): lax.ppermute(x, 'ctx', [(ring[k], ring[(k + t) % n]) for k in range(n)])]
    ppermute x9 -> x12, starting transfers between devices: 13.7 us -> 21.3 us  [onward(): lax.ppermute(x, 'ctx', [(ring[k], ring[(k + t) % n]) for k in range(n)])]
    ppermute x5, waiting for transfers between devices: 4.15 us -> 10.5 us  [swap_head(): return lax.ppermute(x, 'head', [(0, 1), (1, 0)])]
    ppermute x9, waiting for transfers between devices: 9.25 us -> 10.9 us  [swap_dp(): return lax.ppermute(x, 'dp', [(k, k ^ bit) for k in range(dp_size)])]
    unnamed x16 -> x20, local copies, waits for them, and re-layouts: 6.17 us -> 5.62 us
  transfers between devices with their start and end apart: 26 -> 29, of which waited for: 14 -> 15; matrix products, arithmetic and copies ran while one was open for 1% -> 1% of each run, Pallas kernels for 12% -> 8%
where the time goes in v7:
time: 135 us; the launch traced here: 134 us
  waiting for transfers between devices  66.4 us (49%)
  starting transfers between devices  34.7 us (26%)
  Pallas kernels  24.5 us (18%)
  local copies, waits for them, and re-layouts  6.51 us (5%)
    ppermute x12, waiting for transfers between devices, onward(): lax.ppermute(x, 'ctx', [(ring[k], ring[(k + t) % n]) for k in range(n)])  38.6 us
    ppermute x12, starting transfers between devices, onward(): lax.ppermute(x, 'ctx', [(ring[k], ring[(k + t) % n]) for k in range(n)])  21.3 us
    ppermute x9, waiting for transfers between devices, swap_dp(): return lax.ppermute(x, 'dp', [(k, k ^ bit) for k in range(dp_size)])  10.9 us
    pallas_call x4, Pallas kernels, score(): pl.pallas_call(functools.partial(score_kernel, t, 1 + n + t), out_shape=(...  10.5 us
    ppermute x5, waiting for transfers between devices, swap_head(): return lax.ppermute(x, 'head', [(0, 1), (1, 0)])  10.5 us
    ppermute x3, waiting for transfers between devices, per_device(): brought.append(lax.ppermute(piece, 'ctx', pairs))  6.55 us
    ppermute x5, starting transfers between devices, swap_head(): return lax.ppermute(x, 'head', [(0, 1), (1, 0)])  5.81 us
    unnamed x20, local copies, waits for them, and re-layouts  5.62 us
  transfers between devices with their start and end apart: 29, of which 15 were waited for; matrix products, arithmetic and copies ran while one was open for 1% of the time, Pallas kernels for 8%

profile of v7, /device:TPU:0, one launch (start us, length us, event | category | flops | bytes accessed | tf_op | source)
XLA Modules:
  0.0 134.3 jit_solution(13786542601066474779)
XLA Ops:
  0.7 0.8 fusion.info
  1.4 1.9 %copy-done.1 = bf16[384,4096]{1,0:T(8,128)(2,1)S(1)} copy-done((bf16[384,4096]{1,0:T(8,128)(2,1)S(1)}, bf16[384,4096]{1,0:T(8,128)(2,1)}, u32[]{:S(2)}) %copy-start.1) | copy-done | bytes 3145752
  3.3 1.2 copy-done.2
  4.5 0.9 copy-done.3
  5.4 0.9 copy-done.4
  6.3 2.0 %project.1 = (f32[16,4224]{1,0:T(8,128)}, f32[16,4224]{1,0:T(8,128)S(1)}, f32[16,4224]{1,0:T(8,128)S(1)}, f32[16,4224]{1,0:T(8,128)S(1)}, bf16[64,2176]{1,0:T(8,128)(2,1)S(1)}) custom-call(s32[33]{0:T(128)S(1)} %fusion.info, bf16[64,1536]{1,0:T(8,128)(2,1)S(1)} %bitcast.18, bf16[384,4096]{1,0:T(8,128)(2,1)S(1)} %copy-done.1, bf16[64,7168]{1,0:T(8,128)(2,1)S(1)} %bitcast.17, ...), custom_call_target="tpu_custom_call" | custom-call | flops 201326592 | bytes 3145728 | tf_op jit(solution)/shard_map/project/pallas_call | solution.py:111
  8.3 0.7 copy-done.7
  9.0 3.0 %collective-permute-start.3 = (f32[16,4224]{1,0:T(8,128)}, f32[16,4224]{1,0:T(8,128)}, u32[]{:S(2)}, u32[]{:S(2)}) collective-permute-start(f32[16,4224]{1,0:T(8,128)} %get-tuple-element.58), channel_id=1, source_target_pairs={{0,1},{1,3},{3,2},{2,0},{4,5},{5,7},{7,6},{6,4},{8,9},{9,11},{11,1... | collective-permute-start | bytes 811016 | tf_op jit(solution)/shard_map/ppermute | solution.py:576
  12.2 2.6 %collective-permute-start.2 = (bf16[576,256]{1,0:T(8,128)(2,1)S(1)}, bf16[576,256]{1,0:T(8,128)(2,1)S(1)}, u32[]{:S(2)}, u32[]{:S(2)}) collective-permute-start(bf16[576,256]{1,0:T(8,128)(2,1)S(1)} %get-tuple-element.113.refs_1_), channel_id=1, source_target_pairs={{0,1},{1,3},{3,2},{2,0},{4,5},{5,7},{7,6},{6,4},{8,9},{9,11},{11,1... | collective-permute-start | bytes 884744 | tf_op jit(solution)/shard_map/ppermute | solution.py:576
  15.3 5.4 %collective-permute-done.3 = f32[16,4224]{1,0:T(8,128)} collective-permute-done((f32[16,4224]{1,0:T(8,128)}, f32[16,4224]{1,0:T(8,128)}, u32[]{:S(2)}, u32[]{:S(2)}) %collective-permute-start.3) | collective-permute-done | bytes 270368 | tf_op jit(solution)/shard_map/ppermute | solution.py:576
  20.7 1.0 add.24
  21.7 1.2 collective-permute-start.4
  22.9 3.4 %collective-permute-start.5 = (bf16[512,128]{1,0:T(8,128)(2,1)S(1)}, bf16[512,128]{1,0:T(8,128)(2,1)S(1)}, u32[]{:S(2)}, u32[]{:S(2)}) collective-permute-start(bf16[512,128]{1,0:T(8,128)(2,1)S(1)} %dynamic-slice_bitcast_fusion.1), channel_id=1, source_target_pairs={{0,1},{1,3},{3,2},{2,0},{4,5},{5,7},{7,6},{6,4},{8,9},{9,11},{11,1... | collective-permute-start | bytes 393224 | tf_op jit(solution)/shard_map/ppermute | solution.py:576
  26.4 1.5 %collective-permute-start = (bf16[16,64,576]{2,1,0:T(8,128)(2,1)S(1)}, bf16[16,64,576]{2,1,0:T(8,128)(2,1)S(1)}, u32[]{:S(2)}, u32[]{:S(2)}) collective-permute-start(bf16[16,64,576]{2,1,0:T(8,128)(2,1)S(1)} %bitcast.33), channel_id=1, source_target_pairs={{0,4},{4,0},{1,5},{5,1},{2,6},{6,2},{3,7},{7,3},{8,12},{12,8},{9,1... | collective-permute-start | bytes 3538952 | tf_op jit(solution)/shard_map/ppermute | solution.py:579
  27.9 13.1 %collective-permute-done.5 = bf16[512,128]{1,0:T(8,128)(2,1)S(1)} collective-permute-done((bf16[512,128]{1,0:T(8,128)(2,1)S(1)}, bf16[512,128]{1,0:T(8,128)(2,1)S(1)}, u32[]{:S(2)}, u32[]{:S(2)}) %collective-permute-start.5) | collective-permute-done | bytes 131104 | tf_op jit(solution)/shard_map/ppermute | solution.py:576
  41.0 1.7 %collective-permute-start.6 = (bf16[512,128]{1,0:T(8,128)(2,1)S(1)}, bf16[512,128]{1,0:T(8,128)(2,1)S(1)}, u32[]{:S(2)}, u32[]{:S(2)}) collective-permute-start(bf16[512,128]{1,0:T(8,128)(2,1)S(1)} %dynamic-slice_bitcast_fusion.1), channel_id=1, source_target_pairs={{0,2},{1,0},{3,1},{2,3},{4,6},{5,4},{7,5},{6,7},{8,10},{9,8},{11,9... | collective-permute-start | bytes 393224 | tf_op jit(solution)/shard_map/ppermute | solution.py:576
  42.8 3.2 %collective-permute-done.6 = bf16[512,128]{1,0:T(8,128)(2,1)S(1)} collective-permute-done((bf16[512,128]{1,0:T(8,128)(2,1)S(1)}, bf16[512,128]{1,0:T(8,128)(2,1)S(1)}, u32[]{:S(2)}, u32[]{:S(2)}) %collective-permute-start.6) | collective-permute-done | bytes 131104 | tf_op jit(solution)/shard_map/ppermute | solution.py:576
  46.0 2.2 %collective-permute-start.13 = (bf16[512,128]{1,0:T(8,128)(2,1)S(1)}, bf16[512,128]{1,0:T(8,128)(2,1)S(1)}, u32[]{:S(2)}, u32[]{:S(2)}) collective-permute-start(bf16[512,128]{1,0:T(8,128)(2,1)S(1)} %collective-permute-done.5), channel_id=1, source_target_pairs={{0,1},{1,3},{3,2},{2,0},{4,5},{5,7},{7,6},{6,4},{8,9},{9,11},{11,1... | collective-permute-start | bytes 393224 | tf_op jit(solution)/shard_map/ppermute | solution.py:576
  48.2 2.0 %collective-permute-start.10 = (bf16[576,256]{1,0:T(8,128)(2,1)S(1)}, bf16[576,256]{1,0:T(8,128)(2,1)S(1)}, u32[]{:S(2)}, u32[]{:S(2)}) collective-permute-start(bf16[576,256]{1,0:T(8,128)(2,1)S(1)} %collective-permute-done.1.refs_0_), channel_id=1, source_target_pairs={{0,1},{1,3},{3,2},{2,0},{4,5},{5,7},{7,6},{6,4},{8,9},{9,11},{11,1... | collective-permute-start | bytes 884744 | tf_op jit(solution)/shard_map/ppermute | solution.py:576
  50.9 2.3 %collective-permute-done.13 = bf16[512,128]{1,0:T(8,128)(2,1)S(1)} collective-permute-done((bf16[512,128]{1,0:T(8,128)(2,1)S(1)}, bf16[512,128]{1,0:T(8,128)(2,1)S(1)}, u32[]{:S(2)}, u32[]{:S(2)}) %collective-permute-start.13) | collective-permute-done | bytes 131104 | tf_op jit(solution)/shard_map/ppermute | solution.py:576
  53.3 1.5 %collective-permute-start.7 = (bf16[64,2176]{1,0:T(8,128)(2,1)S(1)}, bf16[64,2176]{1,0:T(8,128)(2,1)S(1)}, u32[]{:S(2)}, u32[]{:S(2)}) collective-permute-start(bf16[64,2176]{1,0:T(8,128)(2,1)S(1)} %get-tuple-element.69.refs_0_), channel_id=1, source_target_pairs={{0,16},{8,24},{16,0},{24,8},{1,17},{9,25},{17,1},{25,9},{2,18},{10... | collective-permute-start | bytes 835592 | tf_op jit(solution)/shard_map/ppermute | solution.py:582
  54.8 14.5 %collective-permute-done.12.received = f32[16,4224]{1,0:T(8,128)S(1)} collective-permute-done((f32[16,4224]{1,0:T(8,128)S(1)}, f32[16,4224]{1,0:T(8,128)S(1)}, u32[]{:S(2)}, u32[]{:S(2)}) %collective-permute-start.12) | collective-permute-done | bytes 270368 | tf_op jit(solution)/shard_map/ppermute | solution.py:576
  69.3 1.5 %collective-permute-start.14 = (bf16[2048,128]{1,0:T(8,128)(2,1)S(1)}, bf16[2048,128]{1,0:T(8,128)(2,1)S(1)}, u32[]{:S(2)}, u32[]{:S(2)}) collective-permute-start(bf16[2048,128]{1,0:T(8,128)(2,1)S(1)} %pad_maximum_fusion.own), channel_id=1, source_target_pairs={{0,4},{4,0},{1,5},{5,1},{2,6},{6,2},{3,7},{7,3},{8,12},{12,8},{9,1... | collective-permute-start | bytes 1572872 | tf_op jit(solution)/shard_map/ppermute | solution.py:579
  71.4 1.0 collective-permute-done.8.refs_2_
  72.8 0.8 arrange.1
  73.6 1.2 collective-permute-start.16
  74.8 2.6 %collective-permute-start.17 = (bf16[576,256]{1,0:T(8,128)(2,1)S(1)}, bf16[576,256]{1,0:T(8,128)(2,1)S(1)}, u32[]{:S(2)}, u32[]{:S(2)}) collective-permute-start(bf16[576,256]{1,0:T(8,128)(2,1)S(1)} %collective-permute-done.11.refs_1_), channel_id=1, source_target_pairs={{0,1},{1,3},{3,2},{2,0},{4,5},{5,7},{7,6},{6,4},{8,9},{9,11},{11,1... | collective-permute-start | bytes 884744 | tf_op jit(solution)/shard_map/ppermute | solution.py:576
  77.4 3.5 %collective-permute-done.14.other = bf16[2048,128]{1,0:T(8,128)(2,1)S(1)} collective-permute-done((bf16[2048,128]{1,0:T(8,128)(2,1)S(1)}, bf16[2048,128]{1,0:T(8,128)(2,1)S(1)}, u32[]{:S(2)}, u32[]{:S(2)}) %collective-permute-start.14) | collective-permute-done | bytes 524320 | tf_op jit(solution)/shard_map/ppermute | solution.py:579
  80.9 1.3 logits.1.part
  82.2 1.5 %collective-permute-start.15 = (f32[2,16,2048]{2,1,0:T(8,128)S(1)}, f32[2,16,2048]{2,1,0:T(8,128)S(1)}, u32[]{:S(2)}, u32[]{:S(2)}) collective-permute-start(f32[2,16,2048]{2,1,0:T(8,128)S(1)} %logits.1.part), channel_id=1, source_target_pairs={{0,4},{4,0},{1,5},{5,1},{2,6},{6,2},{3,7},{7,3},{8,12},{12,8},{9,1... | collective-permute-start | bytes 786440 | tf_op jit(solution)/shard_map/ppermute | solution.py:579
  83.7 2.6 %score.4 = (bf16[16,128,512]{2,1,0:T(8,128)(2,1)S(1)}, f32[16,128]{1,0:T(8,128)S(1)}, f32[16,128]{1,0:T(8,128)S(1)}, f32[16,128]{1,0:T(8,128)S(1)}) custom-call(s32[33]{0:T(128)S(1)} %fusion.info, s32[64]{0:T(128)S(1)} %bitcast.28, bf16[16,64,576]{2,1,0:T(8,128)(2,1)S(1)} %bitcast.34, bf16[16,64,576]{2,1,0:T(8,128)(2,1)S(1)} %collective-permute-done.other, ...), custom_call_target="tpu_custom_call" | custom-call | flops 1207959552 | bytes 5046272 | tf_op jit(solution)/shard_map/score/pallas_call | solution.py:206
  86.4 2.6 %score.5 = (bf16[16,128,512]{2,1,0:T(8,128)(2,1)S(1)}, f32[16,128]{1,0:T(8,128)S(1)}, f32[16,128]{1,0:T(8,128)S(1)}, f32[16,128]{1,0:T(8,128)S(1)}) custom-call(s32[33]{0:T(128)S(1)} %fusion.info, s32[64]{0:T(128)S(1)} %bitcast.29, bf16[16,64,576]{2,1,0:T(8,128)(2,1)S(1)} %bitcast.35, bf16[16,64,576]{2,1,0:T(8,128)(2,1)S(1)} %collective-permute-done.other, ...), custom_call_target="tpu_custom_call" | custom-call | flops 1207959552 | bytes 5046272 | tf_op jit(solution)/shard_map/score/pallas_call | solution.py:206
  89.0 2.6 %score.6 = (bf16[16,128,512]{2,1,0:T(8,128)(2,1)S(1)}, f32[16,128]{1,0:T(8,128)S(1)}, f32[16,128]{1,0:T(8,128)S(1)}, f32[16,128]{1,0:T(8,128)S(1)}) custom-call(s32[33]{0:T(128)S(1)} %fusion.info, s32[64]{0:T(128)S(1)} %bitcast.30, bf16[16,64,576]{2,1,0:T(8,128)(2,1)S(1)} %bitcast.36, bf16[16,64,576]{2,1,0:T(8,128)(2,1)S(1)} %collective-permute-done.other, ...), custom_call_target="tpu_custom_call" | custom-call | flops 1207959552 | bytes 5046272 | tf_op jit(solution)/shard_map/score/pallas_call | solution.py:206
  91.6 0.8 softmax.1
  92.5 2.6 %score.7 = (bf16[16,128,512]{2,1,0:T(8,128)(2,1)S(1)}, f32[16,128]{1,0:T(8,128)S(1)}, f32[16,128]{1,0:T(8,128)S(1)}, f32[16,128]{1,0:T(8,128)S(1)}) custom-call(s32[33]{0:T(128)S(1)} %fusion.info, s32[64]{0:T(128)S(1)} %bitcast.32, bf16[16,64,576]{2,1,0:T(8,128)(2,1)S(1)} %bitcast.37, bf16[16,64,576]{2,1,0:T(8,128)(2,1)S(1)} %collective-permute-done.other, ...), custom_call_target="tpu_custom_call" | custom-call | flops 1207959552 | bytes 5046272 | tf_op jit(solution)/shard_map/score/pallas_call | solution.py:206
  95.1 0.6 collective-permute-start.18
  95.7 3.2 %collective-permute-done.18.refs_10_ = f32[2,16,128]{2,1,0:T(8,128)S(1)} collective-permute-done((f32[2,16,128]{2,1,0:T(8,128)S(1)}, f32[2,16,128]{2,1,0:T(8,128)S(1)}, u32[]{:S(2)}, u32[]{:S(2)}) %collective-permute-start.18) | collective-permute-done | bytes 16416 | tf_op jit(solution)/shard_map/ppermute | solution.py:579
  98.9 2.2 %delta.1 = (f32[16,2048]{1,0:T(8,128)S(1)}, bf16[16,2048]{1,0:T(8,128)(2,1)S(1)}) custom-call(bf16[16,128,512]{2,1,0:T(8,128)(2,1)S(1)} %get-tuple-element.91.refs_0_, bf16[16,128,512]{2,1,0:T(8,128)(2,1)S(1)} %get-tuple-element.92.refs_1_, bf16[16,128,512]{2,1,0:T(8,128)(2,1)S(1)} %get-tuple-element.93.refs_2_, ...), custom_call_target="tpu_custom_call" | custom-call | flops 8388608 | bytes 8388608 | tf_op jit(solution)/shard_map/delta/pallas_call | solution.py:253
  101.0 0.6 collective-permute-start.19
  101.7 3.7 %collective-permute-done.19.brought = bf16[16,2048]{1,0:T(8,128)(2,1)S(1)} collective-permute-done((bf16[16,2048]{1,0:T(8,128)(2,1)S(1)}, bf16[16,2048]{1,0:T(8,128)(2,1)S(1)}, u32[]{:S(2)}, u32[]{:S(2)}) %collective-permute-start.19) | collective-permute-done | bytes 65568 | tf_op jit(solution)/shard_map/ppermute | solution.py:579
  105.4 2.7 %gradient.1 = bf16[16,4224]{1,0:T(8,128)(2,1)S(1)} custom-call(f32[16,4224]{1,0:T(8,128)S(1)} %collective-permute-done.12.received, f32[16,4224]{1,0:T(8,128)S(1)} %copy-done.8, bf16[2048,128]{1,0:T(8,128)(2,1)S(1)} %pad_maximum_fusion.own, bf16[2048,128]{1,0:T(8,128)(2,1)S(1)} %collective-permute-done.14.other, ...), custom_call_target="tpu_custom_call" | custom-call | flops 1073741824 | bytes 2375680 | tf_op jit(solution)/shard_map/gradient/pallas_call | solution.py:447
  108.1 1.5 %collective-permute-start.23 = (bf16[1,16,4224]{2,1,0:T(8,128)(2,1)S(1)}, bf16[1,16,4224]{2,1,0:T(8,128)(2,1)S(1)}, u32[]{:S(2)}, u32[]{:S(2)}) collective-permute-start(bf16[1,16,4224]{2,1,0:T(8,128)(2,1)S(1)} %bitcast.19), channel_id=1, source_target_pairs={{0,16},{8,24},{16,0},{24,8},{1,17},{9,25},{17,1},{25,9},{2,18},{10... | collective-permute-start | bytes 405512 | tf_op jit(solution)/shard_map/ppermute | solution.py:582
  109.6 2.6 %collective-permute-start.22 = (bf16[1,16,4224]{2,1,0:T(8,128)(2,1)S(1)}, bf16[1,16,4224]{2,1,0:T(8,128)(2,1)S(1)}, u32[]{:S(2)}, u32[]{:S(2)}) collective-permute-start(bf16[1,16,4224]{2,1,0:T(8,128)(2,1)S(1)} %bitcast.20), channel_id=1, source_target_pairs={{0,3},{1,0},{2,1},{3,2},{4,7},{5,4},{6,5},{7,6},{8,11},{9,8},{10,9... | collective-permute-start | bytes 405512 | tf_op jit(solution)/shard_map/ppermute | solution.py:669
  113.4 1.7 %collective-permute-done.22 = bf16[1,16,4224]{2,1,0:T(8,128)(2,1)S(1)} collective-permute-done((bf16[1,16,4224]{2,1,0:T(8,128)(2,1)S(1)}, bf16[1,16,4224]{2,1,0:T(8,128)(2,1)S(1)}, u32[]{:S(2)}, u32[]{:S(2)}) %collective-permute-start.22) | collective-permute-done | bytes 135200 | tf_op jit(solution)/shard_map/ppermute | solution.py:669
  115.0 4.9 %collective-permute-done.21 = bf16[1,16,4224]{2,1,0:T(8,128)(2,1)S(1)} collective-permute-done((bf16[1,16,4224]{2,1,0:T(8,128)(2,1)S(1)}, bf16[1,16,4224]{2,1,0:T(8,128)(2,1)S(1)}, u32[]{:S(2)}, u32[]{:S(2)}) %collective-permute-start.21) | collective-permute-done | bytes 135200 | tf_op jit(solution)/shard_map/ppermute | solution.py:669
  120.6 7.4 %collective-permute-done.26.refs_5_ = bf16[3,16,4224]{2,1,0:T(8,128)(2,1)S(1)} collective-permute-done((bf16[3,16,4224]{2,1,0:T(8,128)(2,1)S(1)}, bf16[3,16,4224]{2,1,0:T(8,128)(2,1)S(1)}, u32[]{:S(2)}, u32[]{:S(2)}) %collective-permute-start.26) | collective-permute-done | bytes 405536 | tf_op jit(solution)/shard_map/ppermute | solution.py:582
  128.0 1.7 %collective-permute-done.28.refs_7_ = bf16[3,16,4224]{2,1,0:T(8,128)(2,1)S(1)} collective-permute-done((bf16[3,16,4224]{2,1,0:T(8,128)(2,1)S(1)}, bf16[3,16,4224]{2,1,0:T(8,128)(2,1)S(1)}, u32[]{:S(2)}, u32[]{:S(2)}) %collective-permute-start.28) | collective-permute-done | bytes 405536 | tf_op jit(solution)/shard_map/ppermute | solution.py:582
  129.7 4.4 %outer.1 = (f32[384,4096]{1,0:T(8,128)}, f32[32,1792]{1,0:T(8,128)}, f32[1,64]{1,0:T(1,128)}) custom-call(s32[33]{0:T(128)S(1)} %fusion.info, bf16[384,256]{1,0:T(8,128)(2,1)S(1)} %get-tuple-element.72.latents, bf16[256,1792]{1,0:T(8,128)(2,1)S(1)} %get-tuple-element.73.hiddens, bf16[1,16,4224]{2,1,0:T(8,128)(2,1)S(1)} %bitcast.24, ...), custom_call_target="tpu_custom_call" | custom-call | flops 805306368 | bytes 8388608 | tf_op jit(solution)/shard_map/outer/pallas_call | solution.py:534
  (51 shorter events, 4.1 us)
Async XLA Ops:
  0.6 11.4 %copy-start = (bf16[1,1024,576]{1,2,0:T(8,128)(2,1)S(1)}, bf16[1,1024,576]{1,2,0:T(8,128)(2,1)}, u32[]{:S(2)}) copy-start(bf16[1,1024,576]{1,2,0:T(8,128)(2,1)} %param.12) | copy-start | bytes 3538948
  1.4 1.9 %copy-start.1 = (bf16[384,4096]{1,0:T(8,128)(2,1)S(1)}, bf16[384,4096]{1,0:T(8,128)(2,1)}, u32[]{:S(2)}) copy-start(bf16[384,4096]{1,0:T(8,128)(2,1)} %weight.1) | copy-start | bytes 9437188
  3.3 1.2 copy-start.2
  4.5 0.9 copy-start.3
  5.4 0.9 copy-start.4
  8.3 0.7 copy-start.7
  9.0 17.3 %copy-start.6 = (bf16[1,16,64,576]{3,2,1,0:T(8,128)(2,1)S(1)}, bf16[1,16,64,576]{3,2,1,0:T(8,128)(2,1)}, u32[]{:S(2)}) copy-start(bf16[1,16,64,576]{3,2,1,0:T(8,128)(2,1)} %param.11) | copy-start | bytes 3538948
  9.0 11.7 %collective-permute-start.3 = (f32[16,4224]{1,0:T(8,128)}, f32[16,4224]{1,0:T(8,128)}, u32[]{:S(2)}, u32[]{:S(2)}) collective-permute-start(f32[16,4224]{1,0:T(8,128)} %get-tuple-element.58), channel_id=1, source_target_pairs={{0,1},{1,3},{3,2},{2,0},{4,5},{5,7},{7,6},{6,4},{8,9},{9,11},{11,1... | collective-permute-start | bytes 811016 | tf_op jit(solution)/shard_map/ppermute | solution.py:576
  12.1 10.8 %copy-start.9 = (bf16[1,1024,128]{2,1,0:T(8,128)(2,1)S(1)}, bf16[1,1024,128]{2,1,0:T(8,128)(2,1)}, u32[]{:S(2)}) copy-start(bf16[1,1024,128]{2,1,0:T(8,128)(2,1)} %param.13) | copy-start | bytes 786436
  12.2 68.7 %copy-start.8 = (f32[16,4224]{1,0:T(8,128)S(1)}, f32[16,4224]{1,0:T(8,128)}, u32[]{:S(2)}) copy-start(f32[16,4224]{1,0:T(8,128)} %copy-done.7) | copy-start | bytes 811012
  12.2 33.8 %collective-permute-start.2 = (bf16[576,256]{1,0:T(8,128)(2,1)S(1)}, bf16[576,256]{1,0:T(8,128)(2,1)S(1)}, u32[]{:S(2)}, u32[]{:S(2)}) collective-permute-start(bf16[576,256]{1,0:T(8,128)(2,1)S(1)} %get-tuple-element.113.refs_1_), channel_id=1, source_target_pairs={{0,1},{1,3},{3,2},{2,0},{4,5},{5,7},{7,6},{6,4},{8,9},{9,11},{11,1... | collective-permute-start | bytes 884744 | tf_op jit(solution)/shard_map/ppermute | solution.py:576
  14.8 31.2 %collective-permute-start.1 = (bf16[576,256]{1,0:T(8,128)(2,1)S(1)}, bf16[576,256]{1,0:T(8,128)(2,1)S(1)}, u32[]{:S(2)}, u32[]{:S(2)}) collective-permute-start(bf16[576,256]{1,0:T(8,128)(2,1)S(1)} %get-tuple-element.114.refs_0_), channel_id=1, source_target_pairs={{0,1},{1,3},{3,2},{2,0},{4,5},{5,7},{7,6},{6,4},{8,9},{9,11},{11,1... | collective-permute-start | bytes 884744 | tf_op jit(solution)/shard_map/ppermute | solution.py:576
  21.7 21.1 %collective-permute-start.4 = (f32[16,4224]{1,0:T(8,128)S(1)}, f32[16,4224]{1,0:T(8,128)S(1)}, u32[]{:S(2)}, u32[]{:S(2)}) collective-permute-start(f32[16,4224]{1,0:T(8,128)S(1)} %add.24), channel_id=1, source_target_pairs={{0,1},{1,3},{3,2},{2,0},{4,5},{5,7},{7,6},{6,4},{8,9},{9,11},{11,1... | collective-permute-start | bytes 811016 | tf_op jit(solution)/shard_map/ppermute | solution.py:576
  22.9 18.1 %collective-permute-start.5 = (bf16[512,128]{1,0:T(8,128)(2,1)S(1)}, bf16[512,128]{1,0:T(8,128)(2,1)S(1)}, u32[]{:S(2)}, u32[]{:S(2)}) collective-permute-start(bf16[512,128]{1,0:T(8,128)(2,1)S(1)} %dynamic-slice_bitcast_fusion.1), channel_id=1, source_target_pairs={{0,1},{1,3},{3,2},{2,0},{4,5},{5,7},{7,6},{6,4},{8,9},{9,11},{11,1... | collective-permute-start | bytes 393224 | tf_op jit(solution)/shard_map/ppermute | solution.py:576
  26.4 57.4 %collective-permute-start = (bf16[16,64,576]{2,1,0:T(8,128)(2,1)S(1)}, bf16[16,64,576]{2,1,0:T(8,128)(2,1)S(1)}, u32[]{:S(2)}, u32[]{:S(2)}) collective-permute-start(bf16[16,64,576]{2,1,0:T(8,128)(2,1)S(1)} %bitcast.33), channel_id=1, source_target_pairs={{0,4},{4,0},{1,5},{5,1},{2,6},{6,2},{3,7},{7,3},{8,12},{12,8},{9,1... | collective-permute-start | bytes 3538952 | tf_op jit(solution)/shard_map/ppermute | solution.py:579
  41.0 5.0 %collective-permute-start.6 = (bf16[512,128]{1,0:T(8,128)(2,1)S(1)}, bf16[512,128]{1,0:T(8,128)(2,1)S(1)}, u32[]{:S(2)}, u32[]{:S(2)}) collective-permute-start(bf16[512,128]{1,0:T(8,128)(2,1)S(1)} %dynamic-slice_bitcast_fusion.1), channel_id=1, source_target_pairs={{0,2},{1,0},{3,1},{2,3},{4,6},{5,4},{7,5},{6,7},{8,10},{9,8},{11,9... | collective-permute-start | bytes 393224 | tf_op jit(solution)/shard_map/ppermute | solution.py:576
  42.8 41.0 %copy-start.5 = (s32[1,64]{1,0:T(1,128)S(1)}, s32[1,64]{1,0:T(1,128)}, u32[]{:S(2)}) copy-start(s32[1,64]{1,0:T(1,128)} %param.14) | copy-start | bytes 772
  46.0 7.3 %collective-permute-start.13 = (bf16[512,128]{1,0:T(8,128)(2,1)S(1)}, bf16[512,128]{1,0:T(8,128)(2,1)S(1)}, u32[]{:S(2)}, u32[]{:S(2)}) collective-permute-start(bf16[512,128]{1,0:T(8,128)(2,1)S(1)} %collective-permute-done.5), channel_id=1, source_target_pairs={{0,1},{1,3},{3,2},{2,0},{4,5},{5,7},{7,6},{6,4},{8,9},{9,11},{11,1... | collective-permute-start | bytes 393224 | tf_op jit(solution)/shard_map/ppermute | solution.py:576
  48.2 21.1 %collective-permute-start.10 = (bf16[576,256]{1,0:T(8,128)(2,1)S(1)}, bf16[576,256]{1,0:T(8,128)(2,1)S(1)}, u32[]{:S(2)}, u32[]{:S(2)}) collective-permute-start(bf16[576,256]{1,0:T(8,128)(2,1)S(1)} %collective-permute-done.1.refs_0_), channel_id=1, source_target_pairs={{0,1},{1,3},{3,2},{2,0},{4,5},{5,7},{7,6},{6,4},{8,9},{9,11},{11,1... | collective-permute-start | bytes 884744 | tf_op jit(solution)/shard_map/ppermute | solution.py:576
  50.2 19.1 %collective-permute-start.11 = (bf16[576,256]{1,0:T(8,128)(2,1)S(1)}, bf16[576,256]{1,0:T(8,128)(2,1)S(1)}, u32[]{:S(2)}, u32[]{:S(2)}) collective-permute-start(bf16[576,256]{1,0:T(8,128)(2,1)S(1)} %collective-permute-done.2.refs_1_), channel_id=1, source_target_pairs={{0,1},{1,3},{3,2},{2,0},{4,5},{5,7},{7,6},{6,4},{8,9},{9,11},{11,1... | collective-permute-start | bytes 884744 | tf_op jit(solution)/shard_map/ppermute | solution.py:576
  50.7 18.7 %collective-permute-start.12 = (f32[16,4224]{1,0:T(8,128)S(1)}, f32[16,4224]{1,0:T(8,128)S(1)}, u32[]{:S(2)}, u32[]{:S(2)}) collective-permute-start(f32[16,4224]{1,0:T(8,128)S(1)} %add.25), channel_id=1, source_target_pairs={{0,1},{1,3},{3,2},{2,0},{4,5},{5,7},{7,6},{6,4},{8,9},{9,11},{11,1... | collective-permute-start | bytes 811016 | tf_op jit(solution)/shard_map/ppermute | solution.py:576
  53.3 17.6 %collective-permute-start.7 = (bf16[64,2176]{1,0:T(8,128)(2,1)S(1)}, bf16[64,2176]{1,0:T(8,128)(2,1)S(1)}, u32[]{:S(2)}, u32[]{:S(2)}) collective-permute-start(bf16[64,2176]{1,0:T(8,128)(2,1)S(1)} %get-tuple-element.69.refs_0_), channel_id=1, source_target_pairs={{0,16},{8,24},{16,0},{24,8},{1,17},{9,25},{17,1},{25,9},{2,18},{10... | collective-permute-start | bytes 835592 | tf_op jit(solution)/shard_map/ppermute | solution.py:582
  69.3 11.6 %collective-permute-start.14 = (bf16[2048,128]{1,0:T(8,128)(2,1)S(1)}, bf16[2048,128]{1,0:T(8,128)(2,1)S(1)}, u32[]{:S(2)}, u32[]{:S(2)}) collective-permute-start(bf16[2048,128]{1,0:T(8,128)(2,1)S(1)} %pad_maximum_fusion.own), channel_id=1, source_target_pairs={{0,4},{4,0},{1,5},{5,1},{2,6},{6,2},{3,7},{7,3},{8,12},{12,8},{9,1... | collective-permute-start | bytes 1572872 | tf_op jit(solution)/shard_map/ppermute | solution.py:579
  70.9 1.6 %collective-permute-start.8 = (bf16[64,2176]{1,0:T(8,128)(2,1)S(1)}, bf16[64,2176]{1,0:T(8,128)(2,1)S(1)}, u32[]{:S(2)}, u32[]{:S(2)}) collective-permute-start(bf16[64,2176]{1,0:T(8,128)(2,1)S(1)} %get-tuple-element.69.refs_0_), channel_id=1, source_target_pairs={{0,8},{8,0},{16,24},{24,16},{1,9},{9,1},{17,25},{25,17},{2,10},{10... | collective-permute-start | bytes 835592 | tf_op jit(solution)/shard_map/ppermute | solution.py:582
  70.9 2.0 %collective-permute-start.9 = (bf16[64,2176]{1,0:T(8,128)(2,1)S(1)}, bf16[64,2176]{1,0:T(8,128)(2,1)S(1)}, u32[]{:S(2)}, u32[]{:S(2)}) collective-permute-start(bf16[64,2176]{1,0:T(8,128)(2,1)S(1)} %collective-permute-done.7.refs_1_), channel_id=1, source_target_pairs={{0,8},{8,0},{16,24},{24,16},{1,9},{9,1},{17,25},{25,17},{2,10},{10... | collective-permute-start | bytes 835592 | tf_op jit(solution)/shard_map/ppermute | solution.py:582
  73.6 18.9 %collective-permute-start.16 = (bf16[576,256]{1,0:T(8,128)(2,1)S(1)}, bf16[576,256]{1,0:T(8,128)(2,1)S(1)}, u32[]{:S(2)}, u32[]{:S(2)}) collective-permute-start(bf16[576,256]{1,0:T(8,128)(2,1)S(1)} %collective-permute-done.10.refs_0_), channel_id=1, source_target_pairs={{0,1},{1,3},{3,2},{2,0},{4,5},{5,7},{7,6},{6,4},{8,9},{9,11},{11,1... | collective-permute-start | bytes 884744 | tf_op jit(solution)/shard_map/ppermute | solution.py:576
  74.8 17.7 %collective-permute-start.17 = (bf16[576,256]{1,0:T(8,128)(2,1)S(1)}, bf16[576,256]{1,0:T(8,128)(2,1)S(1)}, u32[]{:S(2)}, u32[]{:S(2)}) collective-permute-start(bf16[576,256]{1,0:T(8,128)(2,1)S(1)} %collective-permute-done.11.refs_1_), channel_id=1, source_target_pairs={{0,1},{1,3},{3,2},{2,0},{4,5},{5,7},{7,6},{6,4},{8,9},{9,11},{11,1... | collective-permute-start | bytes 884744 | tf_op jit(solution)/shard_map/ppermute | solution.py:576
  82.2 9.4 %collective-permute-start.15 = (f32[2,16,2048]{2,1,0:T(8,128)S(1)}, f32[2,16,2048]{2,1,0:T(8,128)S(1)}, u32[]{:S(2)}, u32[]{:S(2)}) collective-permute-start(f32[2,16,2048]{2,1,0:T(8,128)S(1)} %logits.1.part), channel_id=1, source_target_pairs={{0,4},{4,0},{1,5},{5,1},{2,6},{6,2},{3,7},{7,3},{8,12},{12,8},{9,1... | collective-permute-start | bytes 786440 | tf_op jit(solution)/shard_map/ppermute | solution.py:579
  95.1 3.8 %collective-permute-start.18 = (f32[2,16,128]{2,1,0:T(8,128)S(1)}, f32[2,16,128]{2,1,0:T(8,128)S(1)}, u32[]{:S(2)}, u32[]{:S(2)}) collective-permute-start(f32[2,16,128]{2,1,0:T(8,128)S(1)} %pad_maximum_fusion.2), channel_id=1, source_target_pairs={{0,4},{4,0},{1,5},{5,1},{2,6},{6,2},{3,7},{7,3},{8,12},{12,8},{9,1... | collective-permute-start | bytes 49160 | tf_op jit(solution)/shard_map/ppermute | solution.py:579
  101.0 4.3 %collective-permute-start.19 = (bf16[16,2048]{1,0:T(8,128)(2,1)S(1)}, bf16[16,2048]{1,0:T(8,128)(2,1)S(1)}, u32[]{:S(2)}, u32[]{:S(2)}) collective-permute-start(bf16[16,2048]{1,0:T(8,128)(2,1)S(1)} %get-tuple-element.104.sent), channel_id=1, source_target_pairs={{0,4},{4,0},{1,5},{5,1},{2,6},{6,2},{3,7},{7,3},{8,12},{12,8},{9,1... | collective-permute-start | bytes 196616 | tf_op jit(solution)/shard_map/ppermute | solution.py:579
  108.1 5.1 %collective-permute-start.23 = (bf16[1,16,4224]{2,1,0:T(8,128)(2,1)S(1)}, bf16[1,16,4224]{2,1,0:T(8,128)(2,1)S(1)}, u32[]{:S(2)}, u32[]{:S(2)}) collective-permute-start(bf16[1,16,4224]{2,1,0:T(8,128)(2,1)S(1)} %bitcast.19), channel_id=1, source_target_pairs={{0,16},{8,24},{16,0},{24,8},{1,17},{9,25},{17,1},{25,9},{2,18},{10... | collective-permute-start | bytes 405512 | tf_op jit(solution)/shard_map/ppermute | solution.py:582
  109.6 5.4 %collective-permute-start.22 = (bf16[1,16,4224]{2,1,0:T(8,128)(2,1)S(1)}, bf16[1,16,4224]{2,1,0:T(8,128)(2,1)S(1)}, u32[]{:S(2)}, u32[]{:S(2)}) collective-permute-start(bf16[1,16,4224]{2,1,0:T(8,128)(2,1)S(1)} %bitcast.20), channel_id=1, source_target_pairs={{0,3},{1,0},{2,1},{3,2},{4,7},{5,4},{6,5},{7,6},{8,11},{9,8},{10,9... | collective-permute-start | bytes 405512 | tf_op jit(solution)/shard_map/ppermute | solution.py:669
  112.3 7.6 %collective-permute-start.21 = (bf16[1,16,4224]{2,1,0:T(8,128)(2,1)S(1)}, bf16[1,16,4224]{2,1,0:T(8,128)(2,1)S(1)}, u32[]{:S(2)}, u32[]{:S(2)}) collective-permute-start(bf16[1,16,4224]{2,1,0:T(8,128)(2,1)S(1)} %bitcast.21), channel_id=1, source_target_pairs={{0,2},{1,3},{2,0},{3,1},{4,6},{5,7},{6,4},{7,5},{8,10},{9,11},{10,... | collective-permute-start | bytes 405512 | tf_op jit(solution)/shard_map/ppermute | solution.py:669
  112.3 7.6 %collective-permute-start.20 = (bf16[1,16,4224]{2,1,0:T(8,128)(2,1)S(1)}, bf16[1,16,4224]{2,1,0:T(8,128)(2,1)S(1)}, u32[]{:S(2)}, u32[]{:S(2)}) collective-permute-start(bf16[1,16,4224]{2,1,0:T(8,128)(2,1)S(1)} %bitcast.22), channel_id=1, source_target_pairs={{0,1},{1,2},{2,3},{3,0},{4,5},{5,6},{6,7},{7,4},{8,9},{9,10},{10,1... | collective-permute-start | bytes 405512 | tf_op jit(solution)/shard_map/ppermute | solution.py:669
  112.8 7.1 %collective-permute-start.24 = (bf16[1,16,4224]{2,1,0:T(8,128)(2,1)S(1)}, bf16[1,16,4224]{2,1,0:T(8,128)(2,1)S(1)}, u32[]{:S(2)}, u32[]{:S(2)}) collective-permute-start(bf16[1,16,4224]{2,1,0:T(8,128)(2,1)S(1)} %bitcast.23), channel_id=1, source_target_pairs={{0,8},{8,0},{16,24},{24,16},{1,9},{9,1},{17,25},{25,17},{2,10},{10... | collective-permute-start | bytes 405512 | tf_op jit(solution)/shard_map/ppermute | solution.py:582
  113.2 6.8 %collective-permute-start.25 = (bf16[1,16,4224]{2,1,0:T(8,128)(2,1)S(1)}, bf16[1,16,4224]{2,1,0:T(8,128)(2,1)S(1)}, u32[]{:S(2)}, u32[]{:S(2)}) collective-permute-start(bf16[1,16,4224]{2,1,0:T(8,128)(2,1)S(1)} %collective-permute-done.23.refs_1_), channel_id=1, source_target_pairs={{0,8},{8,0},{16,24},{24,16},{1,9},{9,1},{17,25},{25,17},{2,10},{10... | collective-permute-start | bytes 405512 | tf_op jit(solution)/shard_map/ppermute | solution.py:582
  120.0 8.0 %collective-permute-start.26 = (bf16[3,16,4224]{2,1,0:T(8,128)(2,1)S(1)}, bf16[3,16,4224]{2,1,0:T(8,128)(2,1)S(1)}, u32[]{:S(2)}, u32[]{:S(2)}) collective-permute-start(bf16[3,16,4224]{2,1,0:T(8,128)(2,1)S(1)} %pad_maximum_fusion.1.refs_4_), channel_id=1, source_target_pairs={{0,16},{8,24},{16,0},{24,8},{1,17},{9,25},{17,1},{25,9},{2,18},{10... | collective-permute-start | bytes 1216520 | tf_op jit(solution)/shard_map/ppermute | solution.py:582
  120.6 7.4 %collective-permute-start.27 = (bf16[3,16,4224]{2,1,0:T(8,128)(2,1)S(1)}, bf16[3,16,4224]{2,1,0:T(8,128)(2,1)S(1)}, u32[]{:S(2)}, u32[]{:S(2)}) collective-permute-start(bf16[3,16,4224]{2,1,0:T(8,128)(2,1)S(1)} %pad_maximum_fusion.1.refs_4_), channel_id=1, source_target_pairs={{0,8},{8,0},{16,24},{24,16},{1,9},{9,1},{17,25},{25,17},{2,10},{10... | collective-permute-start | bytes 1216520 | tf_op jit(solution)/shard_map/ppermute | solution.py:582
  128.0 1.7 %collective-permute-start.28 = (bf16[3,16,4224]{2,1,0:T(8,128)(2,1)S(1)}, bf16[3,16,4224]{2,1,0:T(8,128)(2,1)S(1)}, u32[]{:S(2)}, u32[]{:S(2)}) collective-permute-start(bf16[3,16,4224]{2,1,0:T(8,128)(2,1)S(1)} %collective-permute-done.26.refs_5_), channel_id=1, source_target_pairs={{0,8},{8,0},{16,24},{24,16},{1,9},{9,1},{17,25},{25,17},{2,10},{10... | collective-permute-start | bytes 1216520 | tf_op jit(solution)/shard_map/ppermute | solution.py:582

commit v8 on v5

--- a/solution.py
+++ b/solution.py
@@ -599,10 +599,12 @@
     keys_mine.append(onward(keys_mine[0]))
     queries = main_queries[0]
     other_queries = swap_head(queries)
-    index_parts = [lax.dynamic_slice_in_dim(index_keys[0], y * half, half)]
-    index_parts += [onward(index_parts[0], t) for t in range(1, n - 1)]
+    index_parts = [lax.dynamic_slice_in_dim(index_keys[0], y * half, half)] + [None] * (n - 1)
+    index_parts[1] = onward(index_parts[0])
+    index_parts[n - 1] = onward(index_parts[0], n - 1)
     parts, kept = project(info, queries_here, q_latent[0], w_query, hidden[0], w_weights.T)
-    received = onward(parts[0])
+    first_part, index_parts = lax.optimization_barrier((parts[0], index_parts))
+    summed = onward(first_part) + parts[1]
     order_at = 1 + 3 * n
     dp_at = order_at + n * dp_size
     weights, tops, before = [], [], None
@@ -618,30 +620,39 @@
 
     index_own = index_other = None
     for t in range(1, n - 1):
-        summed = received + parts[t]
         if t == 1:
-            keys, summed, index_parts = lax.optimization_barrier(
-                (keys_mine[t], summed, index_parts)
+            sent_on, summed, index_parts, kept = lax.optimization_barrier(
+                (keys_mine[t], summed, index_parts, kept)
             )
-            index_parts.append(onward(index_parts[0], n - 1))
+            for k in range(2, n - 1):
+                index_parts[k] = onward(index_parts[1]) if k == 2 else onward(index_parts[0], k)
+            index_own = jnp.concatenate(index_parts)
+            index_other = swap_head(index_own)
+            over_half = swap_dp(kept, dp_size // 2)
+            kept = [kept, over_half, swap_dp(kept, dp_size // 4)]
         elif t == 2:
-            index_own = jnp.concatenate(index_parts)
-            keys, summed, index_own = lax.optimization_barrier((keys_mine[t], summed, index_own))
-            index_other = swap_head(index_own)
+            sent_on, summed, index_other, kept, other_queries = lax.optimization_barrier(
+                (keys_mine[t], summed, index_other, kept, other_queries)
+            )
+            kept = kept + [swap_dp(kept[1], dp_size // 4)]
         else:
-            keys, summed = lax.optimization_barrier((keys_mine[t], summed))
-        keys_mine[t] = keys
-        keys_mine.append(onward(keys))
-        received = onward(summed)
-    while len(weights) < n - 2:
+            sent_on, summed = lax.optimization_barrier((keys_mine[t], summed))
+        keys_mine[t] = sent_on
+        keys_mine.append(onward(sent_on))
+        summed = onward(summed)
+        if t + 1 < n - 1:
+            summed = summed + parts[t + 1]
+    received = summed
+    latents, hiddens = arrange(dp_at, info, rows_latent, kept)
+    other_queries, latents, hiddens = lax.optimization_barrier((other_queries, latents, hiddens))
+    while len(weights) < n - 1:
         score_next(keys_mine[len(weights)])
-    latents, hiddens = arrange(dp_at, info, rows_latent, over_dp(kept))
-    before, latents, hiddens = lax.optimization_barrier((before, latents, hiddens))
-    score_next(keys_mine[n - 2])
+    before, received = lax.optimization_barrier((before, received))
 
     part = make_logits(heads_here, received, parts[n - 1], index_own, index_other)
     probs, log_probs = make_softmax(n, info, sequence_positions, part, swap_head(part))
 
+    before, probs, log_probs = lax.optimization_barrier((before, probs, log_probs))
     score_next(keys_mine[n - 1])
     delta_own, sent = make_delta(weights, tops, *before, swap_head(jnp.stack(before)), probs)
     piece = gradients(

time: 131 us -> 135 us (1.031); the launches traced: 128 us -> 135 us
  waiting for transfers between devices: 67.5 us -> 71.5 us
  starting transfers between devices: 28.6 us -> 31 us
    ppermute x9, waiting for transfers between devices: 47.8 us -> 23.9 us  [onward(): lax.ppermute(x, 'ctx', [(ring[k], ring[(k + t) % n]) for k in range(n)])]
    ppermute x5, waiting for transfers between devices: 4.15 us -> 24.4 us  [swap_head(): return lax.ppermute(x, 'head', [(0, 1), (1, 0)])]
    ppermute x9, waiting for transfers between devices: 9.25 us -> 15.4 us  [swap_dp(): return lax.ppermute(x, 'dp', [(k, k ^ bit) for k in range(dp_size)])]
    ppermute x3, waiting for transfers between devices: 6.26 us -> 7.87 us  [per_device(): brought.append(lax.ppermute(piece, 'ctx', pairs))]
    unnamed x16 -> x17, local copies, waits for them, and re-layouts: 6.17 us -> 5.93 us
  transfers between devices with their start and end apart: 26 -> 26, of which waited for: 14 -> 15; matrix products, arithmetic and copies ran while one was open for 1% -> 2% of each run, Pallas kernels for 12% -> 9%
where the time goes in v8:
time: 135 us
  waiting for transfers between devices  71.5 us (53%)
  starting transfers between devices  31 us (23%)
  Pallas kernels  23.9 us (18%)
  local copies, waits for them, and re-layouts  7.6 us (6%)
    ppermute x5, waiting for transfers between devices, swap_head(): return lax.ppermute(x, 'head', [(0, 1), (1, 0)])  24.4 us
    ppermute x9, waiting for transfers between devices, onward(): lax.ppermute(x, 'ctx', [(ring[k], ring[(k + t) % n]) for k in range(n)])  23.9 us
    ppermute x9, waiting for transfers between devices, swap_dp(): return lax.ppermute(x, 'dp', [(k, k ^ bit) for k in range(dp_size)])  15.4 us
    ppermute x9, starting transfers between devices, onward(): lax.ppermute(x, 'ctx', [(ring[k], ring[(k + t) % n]) for k in range(n)])  14.3 us
    pallas_call x4, Pallas kernels, score(): pl.pallas_call(functools.partial(score_kernel, t, 1 + n + t), out_shape=(...  10.5 us
    ppermute x3, waiting for transfers between devices, per_device(): brought.append(lax.ppermute(piece, 'ctx', pairs))  7.87 us
    ppermute x5, starting transfers between devices, swap_head(): return lax.ppermute(x, 'head', [(0, 1), (1, 0)])  7.85 us
    unnamed x17, local copies, waits for them, and re-layouts  5.93 us
  transfers between devices with their start and end apart: 26, of which 15 were waited for; matrix products, arithmetic and copies ran while one was open for 2% of the time, Pallas kernels for 9%

profile of v8, /device:TPU:0, one launch (start us, length us, event | category | flops | bytes accessed | tf_op | source)
XLA Modules:
  0.0 135.0 jit_solution(17007056836374049478)
XLA Ops:
  0.7 1.2 copy-done
  2.0 3.1 %collective-permute-start = (bf16[576,512]{1,0:T(8,128)(2,1)S(1)}, bf16[576,512]{1,0:T(8,128)(2,1)S(1)}, u32[]{:S(2)}, u32[]{:S(2)}) collective-permute-start(bf16[576,512]{1,0:T(8,128)(2,1)S(1)} %dynamic-slice_bitcast_fusion.keys), channel_id=1, source_target_pairs={{0,1},{1,3},{3,2},{2,0},{4,5},{5,7},{7,6},{6,4},{8,9},{9,11},{11,1... | collective-permute-start | bytes 1769480 | tf_op jit(solution)/shard_map/ppermute | solution.py:581
  5.0 0.9 dynamic-slice_bitcast_fusion.1
  5.9 1.1 collective-permute-start.2
  7.0 1.6 %collective-permute-start.1 = (bf16[512,128]{1,0:T(8,128)(2,1)S(1)}, bf16[512,128]{1,0:T(8,128)(2,1)}, u32[]{:S(2)}, u32[]{:S(2)}) collective-permute-start(bf16[512,128]{1,0:T(8,128)(2,1)S(1)} %dynamic-slice_bitcast_fusion.1), channel_id=1, source_target_pairs={{0,1},{1,3},{3,2},{2,0},{4,5},{5,7},{7,6},{6,4},{8,9},{9,11},{11,1... | collective-permute-start | bytes 393224 | tf_op jit(solution)/shard_map/ppermute | solution.py:581
  9.4 1.9 %copy-done.1 = bf16[384,4096]{1,0:T(8,128)(2,1)S(1)} copy-done((bf16[384,4096]{1,0:T(8,128)(2,1)S(1)}, bf16[384,4096]{1,0:T(8,128)(2,1)}, u32[]{:S(2)}) %copy-start.1) | copy-done | bytes 3145752
  11.2 0.9 copy-done.3
  12.2 0.9 copy-done.4
  13.1 1.3 project.1
  14.4 10.0 %collective-permute-done.2 = bf16[512,128]{1,0:T(8,128)(2,1)S(1)} collective-permute-done((bf16[512,128]{1,0:T(8,128)(2,1)S(1)}, bf16[512,128]{1,0:T(8,128)(2,1)S(1)}, u32[]{:S(2)}, u32[]{:S(2)}) %collective-permute-start.2) | collective-permute-done | bytes 131104 | tf_op jit(solution)/shard_map/ppermute | solution.py:581
  24.4 0.7 collective-permute-done.1
  25.1 0.7 collective-permute-start.3
  25.9 1.5 %collective-permute-start.10 = (bf16[16,64,576]{2,1,0:T(8,128)(2,1)S(1)}, bf16[16,64,576]{2,1,0:T(8,128)(2,1)S(1)}, u32[]{:S(2)}, u32[]{:S(2)}) collective-permute-start(bf16[16,64,576]{2,1,0:T(8,128)(2,1)S(1)} %bitcast.33), channel_id=1, source_target_pairs={{0,4},{4,0},{1,5},{5,1},{2,6},{6,2},{3,7},{7,3},{8,12},{12,8},{9,1... | collective-permute-start | bytes 3538952 | tf_op jit(solution)/shard_map/ppermute | solution.py:584
  27.4 6.3 %collective-permute-done.3 = f32[16,4224]{1,0:T(8,128)S(1)} collective-permute-done((f32[16,4224]{1,0:T(8,128)S(1)}, f32[16,4224]{1,0:T(8,128)S(1)}, u32[]{:S(2)}, u32[]{:S(2)}) %collective-permute-start.3) | collective-permute-done | bytes 270368 | tf_op jit(solution)/shard_map/ppermute | solution.py:581
  34.3 3.4 %collective-permute-start.5 = (f32[16,4224]{1,0:T(8,128)S(1)}, f32[16,4224]{1,0:T(8,128)S(1)}, u32[]{:S(2)}, u32[]{:S(2)}) collective-permute-start(f32[16,4224]{1,0:T(8,128)S(1)} %add.24), channel_id=1, source_target_pairs={{0,1},{1,3},{3,2},{2,0},{4,5},{5,7},{7,6},{6,4},{8,9},{9,11},{11,1... | collective-permute-start | bytes 811016 | tf_op jit(solution)/shard_map/ppermute | solution.py:581
  37.8 0.9 constant_dynamic-update-slice_fusion.2
  38.8 2.6 %collective-permute-done.6 = bf16[512,128]{1,0:T(8,128)(2,1)S(1)} collective-permute-done((bf16[512,128]{1,0:T(8,128)(2,1)}, bf16[512,128]{1,0:T(8,128)(2,1)S(1)}, u32[]{:S(2)}, u32[]{:S(2)}) %collective-permute-start.6) | collective-permute-done | bytes 131104 | tf_op jit(solution)/shard_map/ppermute | solution.py:581
  41.4 1.6 %collective-permute-start.7 = (bf16[2048,128]{1,0:T(8,128)(2,1)S(1)}, bf16[2048,128]{1,0:T(8,128)(2,1)S(1)}, u32[]{:S(2)}, u32[]{:S(2)}) collective-permute-start(bf16[2048,128]{1,0:T(8,128)(2,1)S(1)} %constant_dynamic-update-slice_fusion.own), channel_id=1, source_target_pairs={{0,4},{4,0},{1,5},{5,1},{2,6},{6,2},{3,7},{7,3},{8,12},{12,8},{9,1... | collective-permute-start | bytes 1572872 | tf_op jit(solution)/shard_map/ppermute | solution.py:584
  43.0 4.2 %collective-permute-done.5 = f32[16,4224]{1,0:T(8,128)S(1)} collective-permute-done((f32[16,4224]{1,0:T(8,128)S(1)}, f32[16,4224]{1,0:T(8,128)S(1)}, u32[]{:S(2)}, u32[]{:S(2)}) %collective-permute-start.5) | collective-permute-done | bytes 270368 | tf_op jit(solution)/shard_map/ppermute | solution.py:581
  47.2 1.5 %collective-permute-start.8 = (bf16[64,2176]{1,0:T(8,128)(2,1)S(1)}, bf16[64,2176]{1,0:T(8,128)(2,1)S(1)}, u32[]{:S(2)}, u32[]{:S(2)}) collective-permute-start(bf16[64,2176]{1,0:T(8,128)(2,1)S(1)} %get-tuple-element.80.refs_0_), channel_id=1, source_target_pairs={{0,16},{8,24},{16,0},{24,8},{1,17},{9,25},{17,1},{25,9},{2,18},{10... | collective-permute-start | bytes 835592 | tf_op jit(solution)/shard_map/ppermute | solution.py:587
  48.7 5.0 %collective-permute-done.8.refs_1_ = bf16[64,2176]{1,0:T(8,128)(2,1)S(1)} collective-permute-done((bf16[64,2176]{1,0:T(8,128)(2,1)S(1)}, bf16[64,2176]{1,0:T(8,128)(2,1)S(1)}, u32[]{:S(2)}, u32[]{:S(2)}) %collective-permute-start.8) | collective-permute-done | bytes 278560 | tf_op jit(solution)/shard_map/ppermute | solution.py:587
  53.7 3.9 %collective-permute-done.10.other = bf16[16,64,576]{2,1,0:T(8,128)(2,1)S(1)} collective-permute-done((bf16[16,64,576]{2,1,0:T(8,128)(2,1)S(1)}, bf16[16,64,576]{2,1,0:T(8,128)(2,1)S(1)}, u32[]{:S(2)}, u32[]{:S(2)}) %collective-permute-start.10) | collective-permute-done | bytes 1179680 | tf_op jit(solution)/shard_map/ppermute | solution.py:584
  57.6 8.9 %collective-permute-done.7.other = bf16[2048,128]{1,0:T(8,128)(2,1)S(1)} collective-permute-done((bf16[2048,128]{1,0:T(8,128)(2,1)S(1)}, bf16[2048,128]{1,0:T(8,128)(2,1)S(1)}, u32[]{:S(2)}, u32[]{:S(2)}) %collective-permute-start.7) | collective-permute-done | bytes 524320 | tf_op jit(solution)/shard_map/ppermute | solution.py:584
  66.5 3.5 %collective-permute-start.12 = (f32[16,4224]{1,0:T(8,128)S(1)}, f32[16,4224]{1,0:T(8,128)S(1)}, u32[]{:S(2)}, u32[]{:S(2)}) collective-permute-start(f32[16,4224]{1,0:T(8,128)S(1)} %add.25), channel_id=1, source_target_pairs={{0,1},{1,3},{3,2},{2,0},{4,5},{5,7},{7,6},{6,4},{8,9},{9,11},{11,1... | collective-permute-start | bytes 811016 | tf_op jit(solution)/shard_map/ppermute | solution.py:581
  70.2 0.8 arrange.1
  71.0 2.6 %score.4 = (bf16[16,128,512]{2,1,0:T(8,128)(2,1)S(1)}, f32[16,128]{1,0:T(8,128)S(1)}, f32[16,128]{1,0:T(8,128)S(1)}, f32[16,128]{1,0:T(8,128)S(1)}) custom-call(s32[33]{0:T(128)S(1)} %fusion.info, s32[64]{0:T(128)S(1)} %bitcast.28, bf16[16,64,576]{2,1,0:T(8,128)(2,1)S(1)} %bitcast.34, bf16[16,64,576]{2,1,0:T(8,128)(2,1)S(1)} %collective-permute-done.10.other, ...), custom_call_target="tpu_custom_call" | custom-call | flops 1207959552 | bytes 5046272 | tf_op jit(solution)/shard_map/score/pallas_call | solution.py:211
  73.7 2.6 %score.5 = (bf16[16,128,512]{2,1,0:T(8,128)(2,1)S(1)}, f32[16,128]{1,0:T(8,128)S(1)}, f32[16,128]{1,0:T(8,128)S(1)}, f32[16,128]{1,0:T(8,128)S(1)}) custom-call(s32[33]{0:T(128)S(1)} %fusion.info, s32[64]{0:T(128)S(1)} %bitcast.29, bf16[16,64,576]{2,1,0:T(8,128)(2,1)S(1)} %bitcast.35, bf16[16,64,576]{2,1,0:T(8,128)(2,1)S(1)} %collective-permute-done.10.other, ...), custom_call_target="tpu_custom_call" | custom-call | flops 1207959552 | bytes 5046272 | tf_op jit(solution)/shard_map/score/pallas_call | solution.py:211
  76.3 2.6 %score.6 = (bf16[16,128,512]{2,1,0:T(8,128)(2,1)S(1)}, f32[16,128]{1,0:T(8,128)S(1)}, f32[16,128]{1,0:T(8,128)S(1)}, f32[16,128]{1,0:T(8,128)S(1)}) custom-call(s32[33]{0:T(128)S(1)} %fusion.info, s32[64]{0:T(128)S(1)} %bitcast.30, bf16[16,64,576]{2,1,0:T(8,128)(2,1)S(1)} %bitcast.36, bf16[16,64,576]{2,1,0:T(8,128)(2,1)S(1)} %collective-permute-done.10.other, ...), custom_call_target="tpu_custom_call" | custom-call | flops 1207959552 | bytes 5046272 | tf_op jit(solution)/shard_map/score/pallas_call | solution.py:211
  78.9 1.3 logits.1.part
  80.2 1.6 %collective-permute-start.13 = (f32[2,16,2048]{2,1,0:T(8,128)S(1)}, f32[2,16,2048]{2,1,0:T(8,128)S(1)}, u32[]{:S(2)}, u32[]{:S(2)}) collective-permute-start(f32[2,16,2048]{2,1,0:T(8,128)S(1)} %logits.1.part), channel_id=1, source_target_pairs={{0,4},{4,0},{1,5},{5,1},{2,6},{6,2},{3,7},{7,3},{8,12},{12,8},{9,1... | collective-permute-start | bytes 786440 | tf_op jit(solution)/shard_map/ppermute | solution.py:584
  81.8 6.7 %collective-permute-done.13.far = f32[2,16,2048]{2,1,0:T(8,128)S(1)} collective-permute-done((f32[2,16,2048]{2,1,0:T(8,128)S(1)}, f32[2,16,2048]{2,1,0:T(8,128)S(1)}, u32[]{:S(2)}, u32[]{:S(2)}) %collective-permute-start.13) | collective-permute-done | bytes 262176 | tf_op jit(solution)/shard_map/ppermute | solution.py:584
  88.4 0.8 softmax.1
  89.3 2.6 %score.7 = (bf16[16,128,512]{2,1,0:T(8,128)(2,1)S(1)}, f32[16,128]{1,0:T(8,128)S(1)}, f32[16,128]{1,0:T(8,128)S(1)}, f32[16,128]{1,0:T(8,128)S(1)}) custom-call(s32[33]{0:T(128)S(1)} %fusion.info, s32[64]{0:T(128)S(1)} %bitcast.32, bf16[16,64,576]{2,1,0:T(8,128)(2,1)S(1)} %bitcast.37, bf16[16,64,576]{2,1,0:T(8,128)(2,1)S(1)} %collective-permute-done.10.other, ...), custom_call_target="tpu_custom_call" | custom-call | flops 1207959552 | bytes 5046272 | tf_op jit(solution)/shard_map/score/pallas_call | solution.py:211
  91.9 1.6 %collective-permute-start.15 = (f32[2,16,128]{2,1,0:T(8,128)S(1)}, f32[2,16,128]{2,1,0:T(8,128)S(1)}, u32[]{:S(2)}, u32[]{:S(2)}) collective-permute-start(f32[2,16,128]{2,1,0:T(8,128)S(1)} %pad_maximum_fusion.1), channel_id=1, source_target_pairs={{0,4},{4,0},{1,5},{5,1},{2,6},{6,2},{3,7},{7,3},{8,12},{12,8},{9,1... | collective-permute-start | bytes 49160 | tf_op jit(solution)/shard_map/ppermute | solution.py:584
  93.5 2.2 %collective-permute-done.15.refs_10_ = f32[2,16,128]{2,1,0:T(8,128)S(1)} collective-permute-done((f32[2,16,128]{2,1,0:T(8,128)S(1)}, f32[2,16,128]{2,1,0:T(8,128)S(1)}, u32[]{:S(2)}, u32[]{:S(2)}) %collective-permute-start.15) | collective-permute-done | bytes 16416 | tf_op jit(solution)/shard_map/ppermute | solution.py:584
  95.7 2.2 %delta.1 = (f32[16,2048]{1,0:T(8,128)S(1)}, bf16[16,2048]{1,0:T(8,128)(2,1)S(1)}) custom-call(bf16[16,128,512]{2,1,0:T(8,128)(2,1)S(1)} %get-tuple-element.105.refs_0_, bf16[16,128,512]{2,1,0:T(8,128)(2,1)S(1)} %get-tuple-element.106.refs_1_, bf16[16,128,512]{2,1,0:T(8,128)(2,1)S(1)} %get-tuple-element.107.refs_2_, ...), custom_call_target="tpu_custom_call" | custom-call | flops 8388608 | bytes 8388608 | tf_op jit(solution)/shard_map/delta/pallas_call | solution.py:258
  97.9 1.6 %collective-permute-start.16 = (bf16[16,2048]{1,0:T(8,128)(2,1)S(1)}, bf16[16,2048]{1,0:T(8,128)(2,1)S(1)}, u32[]{:S(2)}, u32[]{:S(2)}) collective-permute-start(bf16[16,2048]{1,0:T(8,128)(2,1)S(1)} %get-tuple-element.118.sent), channel_id=1, source_target_pairs={{0,4},{4,0},{1,5},{5,1},{2,6},{6,2},{3,7},{7,3},{8,12},{12,8},{9,1... | collective-permute-start | bytes 196616 | tf_op jit(solution)/shard_map/ppermute | solution.py:584
  99.5 2.7 %collective-permute-done.16.brought = bf16[16,2048]{1,0:T(8,128)(2,1)S(1)} collective-permute-done((bf16[16,2048]{1,0:T(8,128)(2,1)S(1)}, bf16[16,2048]{1,0:T(8,128)(2,1)S(1)}, u32[]{:S(2)}, u32[]{:S(2)}) %collective-permute-start.16) | collective-permute-done | bytes 65568 | tf_op jit(solution)/shard_map/ppermute | solution.py:584
  102.2 2.7 %gradient.1 = bf16[16,4224]{1,0:T(8,128)(2,1)S(1)} custom-call(f32[16,4224]{1,0:T(8,128)S(1)} %collective-permute-done.12.received, f32[16,4224]{1,0:T(8,128)S(1)} %get-tuple-element.97.here, bf16[2048,128]{1,0:T(8,128)(2,1)S(1)} %constant_dynamic-update-slice_fusion.own, bf16[2048,128]{1,0:T(8,128)(2,1)S(1)} %collective-permute-done.7.other, ...), custom_call_target="tpu_custom_call" | custom-call | flops 1073741824 | bytes 2375680 | tf_op jit(solution)/shard_map/gradient/pallas_call | solution.py:452
  104.9 1.6 %collective-permute-start.20 = (bf16[1,16,4224]{2,1,0:T(8,128)(2,1)S(1)}, bf16[1,16,4224]{2,1,0:T(8,128)(2,1)S(1)}, u32[]{:S(2)}, u32[]{:S(2)}) collective-permute-start(bf16[1,16,4224]{2,1,0:T(8,128)(2,1)S(1)} %bitcast.19), channel_id=1, source_target_pairs={{0,16},{8,24},{16,0},{24,8},{1,17},{9,25},{17,1},{25,9},{2,18},{10... | collective-permute-start | bytes 405512 | tf_op jit(solution)/shard_map/ppermute | solution.py:587
  106.4 2.8 %collective-permute-start.19 = (bf16[1,16,4224]{2,1,0:T(8,128)(2,1)S(1)}, bf16[1,16,4224]{2,1,0:T(8,128)(2,1)S(1)}, u32[]{:S(2)}, u32[]{:S(2)}) collective-permute-start(bf16[1,16,4224]{2,1,0:T(8,128)(2,1)S(1)} %bitcast.20), channel_id=1, source_target_pairs={{0,3},{1,0},{2,1},{3,2},{4,7},{5,4},{6,5},{7,6},{8,11},{9,8},{10,9... | collective-permute-start | bytes 405512 | tf_op jit(solution)/shard_map/ppermute | solution.py:675
  109.3 0.8 collective-permute-start.18
  110.1 1.0 collective-permute-start.17
  111.6 2.7 %collective-permute-done.19 = bf16[1,16,4224]{2,1,0:T(8,128)(2,1)S(1)} collective-permute-done((bf16[1,16,4224]{2,1,0:T(8,128)(2,1)S(1)}, bf16[1,16,4224]{2,1,0:T(8,128)(2,1)S(1)}, u32[]{:S(2)}, u32[]{:S(2)}) %collective-permute-start.19) | collective-permute-done | bytes 135200 | tf_op jit(solution)/shard_map/ppermute | solution.py:675
  114.3 5.2 %collective-permute-done.18 = bf16[1,16,4224]{2,1,0:T(8,128)(2,1)S(1)} collective-permute-done((bf16[1,16,4224]{2,1,0:T(8,128)(2,1)S(1)}, bf16[1,16,4224]{2,1,0:T(8,128)(2,1)S(1)}, u32[]{:S(2)}, u32[]{:S(2)}) %collective-permute-start.18) | collective-permute-done | bytes 135200 | tf_op jit(solution)/shard_map/ppermute | solution.py:675
  120.1 8.6 %collective-permute-done.23.refs_5_ = bf16[3,16,4224]{2,1,0:T(8,128)(2,1)S(1)} collective-permute-done((bf16[3,16,4224]{2,1,0:T(8,128)(2,1)S(1)}, bf16[3,16,4224]{2,1,0:T(8,128)(2,1)S(1)}, u32[]{:S(2)}, u32[]{:S(2)}) %collective-permute-start.23) | collective-permute-done | bytes 405536 | tf_op jit(solution)/shard_map/ppermute | solution.py:587
  128.7 1.7 %collective-permute-done.25.refs_7_ = bf16[3,16,4224]{2,1,0:T(8,128)(2,1)S(1)} collective-permute-done((bf16[3,16,4224]{2,1,0:T(8,128)(2,1)S(1)}, bf16[3,16,4224]{2,1,0:T(8,128)(2,1)S(1)}, u32[]{:S(2)}, u32[]{:S(2)}) %collective-permute-start.25) | collective-permute-done | bytes 405536 | tf_op jit(solution)/shard_map/ppermute | solution.py:587
  130.5 4.4 %outer.1 = (f32[384,4096]{1,0:T(8,128)}, f32[32,1792]{1,0:T(8,128)}, f32[1,64]{1,0:T(1,128)}) custom-call(s32[33]{0:T(128)S(1)} %fusion.info, bf16[384,256]{1,0:T(8,128)(2,1)S(1)} %get-tuple-element.85.latents, bf16[256,1792]{1,0:T(8,128)(2,1)S(1)} %get-tuple-element.86.hiddens, bf16[1,16,4224]{2,1,0:T(8,128)(2,1)S(1)} %bitcast.24, ...), custom_call_target="tpu_custom_call" | custom-call | flops 805306368 | bytes 8388608 | tf_op jit(solution)/shard_map/outer/pallas_call | solution.py:539
  (41 shorter events, 3.0 us)
Async XLA Ops:
  0.6 1.3 copy-start
  0.6 8.7 %copy-start.2 = (bf16[1,64,7168]{2,1,0:T(8,128)(2,1)S(1)}, bf16[1,64,7168]{2,1,0:T(8,128)(2,1)}, u32[]{:S(2)}) copy-start(bf16[1,64,7168]{2,1,0:T(8,128)(2,1)} %param.10) | copy-start | bytes 2752516
  2.0 31.8 %collective-permute-start = (bf16[576,512]{1,0:T(8,128)(2,1)S(1)}, bf16[576,512]{1,0:T(8,128)(2,1)S(1)}, u32[]{:S(2)}, u32[]{:S(2)}) collective-permute-start(bf16[576,512]{1,0:T(8,128)(2,1)S(1)} %dynamic-slice_bitcast_fusion.keys), channel_id=1, source_target_pairs={{0,1},{1,3},{3,2},{2,0},{4,5},{5,7},{7,6},{6,4},{8,9},{9,11},{11,1... | collective-permute-start | bytes 1769480 | tf_op jit(solution)/shard_map/ppermute | solution.py:581
  5.9 18.5 %collective-permute-start.2 = (bf16[512,128]{1,0:T(8,128)(2,1)S(1)}, bf16[512,128]{1,0:T(8,128)(2,1)S(1)}, u32[]{:S(2)}, u32[]{:S(2)}) collective-permute-start(bf16[512,128]{1,0:T(8,128)(2,1)S(1)} %dynamic-slice_bitcast_fusion.1), channel_id=1, source_target_pairs={{0,2},{1,0},{3,1},{2,3},{4,6},{5,4},{7,5},{6,7},{8,10},{9,8},{11,9... | collective-permute-start | bytes 393224 | tf_op jit(solution)/shard_map/ppermute | solution.py:581
  7.0 18.1 %collective-permute-start.1 = (bf16[512,128]{1,0:T(8,128)(2,1)S(1)}, bf16[512,128]{1,0:T(8,128)(2,1)}, u32[]{:S(2)}, u32[]{:S(2)}) collective-permute-start(bf16[512,128]{1,0:T(8,128)(2,1)S(1)} %dynamic-slice_bitcast_fusion.1), channel_id=1, source_target_pairs={{0,1},{1,3},{3,2},{2,0},{4,5},{5,7},{7,6},{6,4},{8,9},{9,11},{11,1... | collective-permute-start | bytes 393224 | tf_op jit(solution)/shard_map/ppermute | solution.py:581
  9.3 1.9 %copy-start.1 = (bf16[384,4096]{1,0:T(8,128)(2,1)S(1)}, bf16[384,4096]{1,0:T(8,128)(2,1)}, u32[]{:S(2)}) copy-start(bf16[384,4096]{1,0:T(8,128)(2,1)} %weight.1) | copy-start | bytes 9437188
  11.2 0.9 copy-start.3
  12.2 0.9 copy-start.4
  13.1 12.8 %copy-start.6 = (bf16[1,16,64,576]{3,2,1,0:T(8,128)(2,1)S(1)}, bf16[1,16,64,576]{3,2,1,0:T(8,128)(2,1)}, u32[]{:S(2)}) copy-start(bf16[1,16,64,576]{3,2,1,0:T(8,128)(2,1)} %param.11) | copy-start | bytes 3538948
  14.4 56.6 %copy-start.5 = (s32[1,64]{1,0:T(1,128)S(1)}, s32[1,64]{1,0:T(1,128)}, u32[]{:S(2)}) copy-start(s32[1,64]{1,0:T(1,128)} %param.14) | copy-start | bytes 772
  25.1 8.6 %collective-permute-start.3 = (f32[16,4224]{1,0:T(8,128)S(1)}, f32[16,4224]{1,0:T(8,128)S(1)}, u32[]{:S(2)}, u32[]{:S(2)}) collective-permute-start(f32[16,4224]{1,0:T(8,128)S(1)} %get-tuple-element.66), channel_id=1, source_target_pairs={{0,1},{1,3},{3,2},{2,0},{4,5},{5,7},{7,6},{6,4},{8,9},{9,11},{11,1... | collective-permute-start | bytes 811016 | tf_op jit(solution)/shard_map/ppermute | solution.py:581
  25.9 31.7 %collective-permute-start.10 = (bf16[16,64,576]{2,1,0:T(8,128)(2,1)S(1)}, bf16[16,64,576]{2,1,0:T(8,128)(2,1)S(1)}, u32[]{:S(2)}, u32[]{:S(2)}) collective-permute-start(bf16[16,64,576]{2,1,0:T(8,128)(2,1)S(1)} %bitcast.33), channel_id=1, source_target_pairs={{0,4},{4,0},{1,5},{5,1},{2,6},{6,2},{3,7},{7,3},{8,12},{12,8},{9,1... | collective-permute-start | bytes 3538952 | tf_op jit(solution)/shard_map/ppermute | solution.py:584
  33.8 7.6 %collective-permute-start.6 = (bf16[512,128]{1,0:T(8,128)(2,1)}, bf16[512,128]{1,0:T(8,128)(2,1)S(1)}, u32[]{:S(2)}, u32[]{:S(2)}) collective-permute-start(bf16[512,128]{1,0:T(8,128)(2,1)} %collective-permute-done.1), channel_id=1, source_target_pairs={{0,1},{1,3},{3,2},{2,0},{4,5},{5,7},{7,6},{6,4},{8,9},{9,11},{11,1... | collective-permute-start | bytes 393224 | tf_op jit(solution)/shard_map/ppermute | solution.py:581
  34.3 12.8 %collective-permute-start.5 = (f32[16,4224]{1,0:T(8,128)S(1)}, f32[16,4224]{1,0:T(8,128)S(1)}, u32[]{:S(2)}, u32[]{:S(2)}) collective-permute-start(f32[16,4224]{1,0:T(8,128)S(1)} %add.24), channel_id=1, source_target_pairs={{0,1},{1,3},{3,2},{2,0},{4,5},{5,7},{7,6},{6,4},{8,9},{9,11},{11,1... | collective-permute-start | bytes 811016 | tf_op jit(solution)/shard_map/ppermute | solution.py:581
  37.7 19.9 %collective-permute-start.4 = (bf16[576,512]{1,0:T(8,128)(2,1)S(1)}, bf16[576,512]{1,0:T(8,128)(2,1)S(1)}, u32[]{:S(2)}, u32[]{:S(2)}) collective-permute-start(bf16[576,512]{1,0:T(8,128)(2,1)S(1)} %collective-permute-done.keys), channel_id=1, source_target_pairs={{0,1},{1,3},{3,2},{2,0},{4,5},{5,7},{7,6},{6,4},{8,9},{9,11},{11,1... | collective-permute-start | bytes 1769480 | tf_op jit(solution)/shard_map/ppermute | solution.py:581
  41.4 25.1 %collective-permute-start.7 = (bf16[2048,128]{1,0:T(8,128)(2,1)S(1)}, bf16[2048,128]{1,0:T(8,128)(2,1)S(1)}, u32[]{:S(2)}, u32[]{:S(2)}) collective-permute-start(bf16[2048,128]{1,0:T(8,128)(2,1)S(1)} %constant_dynamic-update-slice_fusion.own), channel_id=1, source_target_pairs={{0,4},{4,0},{1,5},{5,1},{2,6},{6,2},{3,7},{7,3},{8,12},{12,8},{9,1... | collective-permute-start | bytes 1572872 | tf_op jit(solution)/shard_map/ppermute | solution.py:584
  43.0 5.7 %collective-permute-start.9 = (bf16[64,2176]{1,0:T(8,128)(2,1)S(1)}, bf16[64,2176]{1,0:T(8,128)(2,1)S(1)}, u32[]{:S(2)}, u32[]{:S(2)}) collective-permute-start(bf16[64,2176]{1,0:T(8,128)(2,1)S(1)} %get-tuple-element.80.refs_0_), channel_id=1, source_target_pairs={{0,8},{8,0},{16,24},{24,16},{1,9},{9,1},{17,25},{25,17},{2,10},{10... | collective-permute-start | bytes 835592 | tf_op jit(solution)/shard_map/ppermute | solution.py:587
  47.2 6.5 %collective-permute-start.8 = (bf16[64,2176]{1,0:T(8,128)(2,1)S(1)}, bf16[64,2176]{1,0:T(8,128)(2,1)S(1)}, u32[]{:S(2)}, u32[]{:S(2)}) collective-permute-start(bf16[64,2176]{1,0:T(8,128)(2,1)S(1)} %get-tuple-element.80.refs_0_), channel_id=1, source_target_pairs={{0,16},{8,24},{16,0},{24,8},{1,17},{9,25},{17,1},{25,9},{2,18},{10... | collective-permute-start | bytes 835592 | tf_op jit(solution)/shard_map/ppermute | solution.py:587
  66.5 3.8 %collective-permute-start.11 = (bf16[64,2176]{1,0:T(8,128)(2,1)S(1)}, bf16[64,2176]{1,0:T(8,128)(2,1)S(1)}, u32[]{:S(2)}, u32[]{:S(2)}) collective-permute-start(bf16[64,2176]{1,0:T(8,128)(2,1)S(1)} %collective-permute-done.8.refs_1_), channel_id=1, source_target_pairs={{0,8},{8,0},{16,24},{24,16},{1,9},{9,1},{17,25},{25,17},{2,10},{10... | collective-permute-start | bytes 835592 | tf_op jit(solution)/shard_map/ppermute | solution.py:587
  66.5 12.4 %collective-permute-start.12 = (f32[16,4224]{1,0:T(8,128)S(1)}, f32[16,4224]{1,0:T(8,128)S(1)}, u32[]{:S(2)}, u32[]{:S(2)}) collective-permute-start(f32[16,4224]{1,0:T(8,128)S(1)} %add.25), channel_id=1, source_target_pairs={{0,1},{1,3},{3,2},{2,0},{4,5},{5,7},{7,6},{6,4},{8,9},{9,11},{11,1... | collective-permute-start | bytes 811016 | tf_op jit(solution)/shard_map/ppermute | solution.py:581
  70.0 19.3 %collective-permute-start.14 = (bf16[576,512]{1,0:T(8,128)(2,1)S(1)}, bf16[576,512]{1,0:T(8,128)(2,1)S(1)}, u32[]{:S(2)}, u32[]{:S(2)}) collective-permute-start(bf16[576,512]{1,0:T(8,128)(2,1)S(1)} %collective-permute-done.4.keys), channel_id=1, source_target_pairs={{0,1},{1,3},{3,2},{2,0},{4,5},{5,7},{7,6},{6,4},{8,9},{9,11},{11,1... | collective-permute-start | bytes 1769480 | tf_op jit(solution)/shard_map/ppermute | solution.py:581
  80.2 8.2 %collective-permute-start.13 = (f32[2,16,2048]{2,1,0:T(8,128)S(1)}, f32[2,16,2048]{2,1,0:T(8,128)S(1)}, u32[]{:S(2)}, u32[]{:S(2)}) collective-permute-start(f32[2,16,2048]{2,1,0:T(8,128)S(1)} %logits.1.part), channel_id=1, source_target_pairs={{0,4},{4,0},{1,5},{5,1},{2,6},{6,2},{3,7},{7,3},{8,12},{12,8},{9,1... | collective-permute-start | bytes 786440 | tf_op jit(solution)/shard_map/ppermute | solution.py:584
  91.9 3.8 %collective-permute-start.15 = (f32[2,16,128]{2,1,0:T(8,128)S(1)}, f32[2,16,128]{2,1,0:T(8,128)S(1)}, u32[]{:S(2)}, u32[]{:S(2)}) collective-permute-start(f32[2,16,128]{2,1,0:T(8,128)S(1)} %pad_maximum_fusion.1), channel_id=1, source_target_pairs={{0,4},{4,0},{1,5},{5,1},{2,6},{6,2},{3,7},{7,3},{8,12},{12,8},{9,1... | collective-permute-start | bytes 49160 | tf_op jit(solution)/shard_map/ppermute | solution.py:584
  97.9 4.3 %collective-permute-start.16 = (bf16[16,2048]{1,0:T(8,128)(2,1)S(1)}, bf16[16,2048]{1,0:T(8,128)(2,1)S(1)}, u32[]{:S(2)}, u32[]{:S(2)}) collective-permute-start(bf16[16,2048]{1,0:T(8,128)(2,1)S(1)} %get-tuple-element.118.sent), channel_id=1, source_target_pairs={{0,4},{4,0},{1,5},{5,1},{2,6},{6,2},{3,7},{7,3},{8,12},{12,8},{9,1... | collective-permute-start | bytes 196616 | tf_op jit(solution)/shard_map/ppermute | solution.py:584
  104.9 6.2 %collective-permute-start.20 = (bf16[1,16,4224]{2,1,0:T(8,128)(2,1)S(1)}, bf16[1,16,4224]{2,1,0:T(8,128)(2,1)S(1)}, u32[]{:S(2)}, u32[]{:S(2)}) collective-permute-start(bf16[1,16,4224]{2,1,0:T(8,128)(2,1)S(1)} %bitcast.19), channel_id=1, source_target_pairs={{0,16},{8,24},{16,0},{24,8},{1,17},{9,25},{17,1},{25,9},{2,18},{10... | collective-permute-start | bytes 405512 | tf_op jit(solution)/shard_map/ppermute | solution.py:587
  106.4 7.9 %collective-permute-start.19 = (bf16[1,16,4224]{2,1,0:T(8,128)(2,1)S(1)}, bf16[1,16,4224]{2,1,0:T(8,128)(2,1)S(1)}, u32[]{:S(2)}, u32[]{:S(2)}) collective-permute-start(bf16[1,16,4224]{2,1,0:T(8,128)(2,1)S(1)} %bitcast.20), channel_id=1, source_target_pairs={{0,3},{1,0},{2,1},{3,2},{4,7},{5,4},{6,5},{7,6},{8,11},{9,8},{10,9... | collective-permute-start | bytes 405512 | tf_op jit(solution)/shard_map/ppermute | solution.py:675
  109.3 10.2 %collective-permute-start.18 = (bf16[1,16,4224]{2,1,0:T(8,128)(2,1)S(1)}, bf16[1,16,4224]{2,1,0:T(8,128)(2,1)S(1)}, u32[]{:S(2)}, u32[]{:S(2)}) collective-permute-start(bf16[1,16,4224]{2,1,0:T(8,128)(2,1)S(1)} %bitcast.21), channel_id=1, source_target_pairs={{0,2},{1,3},{2,0},{3,1},{4,6},{5,7},{6,4},{7,5},{8,10},{9,11},{10,... | collective-permute-start | bytes 405512 | tf_op jit(solution)/shard_map/ppermute | solution.py:675
  110.1 9.4 %collective-permute-start.17 = (bf16[1,16,4224]{2,1,0:T(8,128)(2,1)S(1)}, bf16[1,16,4224]{2,1,0:T(8,128)(2,1)S(1)}, u32[]{:S(2)}, u32[]{:S(2)}) collective-permute-start(bf16[1,16,4224]{2,1,0:T(8,128)(2,1)S(1)} %bitcast.22), channel_id=1, source_target_pairs={{0,1},{1,2},{2,3},{3,0},{4,5},{5,6},{6,7},{7,4},{8,9},{9,10},{10,1... | collective-permute-start | bytes 405512 | tf_op jit(solution)/shard_map/ppermute | solution.py:675
  111.1 8.5 %collective-permute-start.21 = (bf16[1,16,4224]{2,1,0:T(8,128)(2,1)S(1)}, bf16[1,16,4224]{2,1,0:T(8,128)(2,1)S(1)}, u32[]{:S(2)}, u32[]{:S(2)}) collective-permute-start(bf16[1,16,4224]{2,1,0:T(8,128)(2,1)S(1)} %bitcast.23), channel_id=1, source_target_pairs={{0,8},{8,0},{16,24},{24,16},{1,9},{9,1},{17,25},{25,17},{2,10},{10... | collective-permute-start | bytes 405512 | tf_op jit(solution)/shard_map/ppermute | solution.py:587
  111.1 8.5 %collective-permute-start.22 = (bf16[1,16,4224]{2,1,0:T(8,128)(2,1)S(1)}, bf16[1,16,4224]{2,1,0:T(8,128)(2,1)S(1)}, u32[]{:S(2)}, u32[]{:S(2)}) collective-permute-start(bf16[1,16,4224]{2,1,0:T(8,128)(2,1)S(1)} %collective-permute-done.20.refs_1_), channel_id=1, source_target_pairs={{0,8},{8,0},{16,24},{24,16},{1,9},{9,1},{17,25},{25,17},{2,10},{10... | collective-permute-start | bytes 405512 | tf_op jit(solution)/shard_map/ppermute | solution.py:587
  119.6 9.2 %collective-permute-start.23 = (bf16[3,16,4224]{2,1,0:T(8,128)(2,1)S(1)}, bf16[3,16,4224]{2,1,0:T(8,128)(2,1)S(1)}, u32[]{:S(2)}, u32[]{:S(2)}) collective-permute-start(bf16[3,16,4224]{2,1,0:T(8,128)(2,1)S(1)} %pad_maximum_fusion.refs_4_), channel_id=1, source_target_pairs={{0,16},{8,24},{16,0},{24,8},{1,17},{9,25},{17,1},{25,9},{2,18},{10... | collective-permute-start | bytes 1216520 | tf_op jit(solution)/shard_map/ppermute | solution.py:587
  120.1 8.6 %collective-permute-start.24 = (bf16[3,16,4224]{2,1,0:T(8,128)(2,1)S(1)}, bf16[3,16,4224]{2,1,0:T(8,128)(2,1)S(1)}, u32[]{:S(2)}, u32[]{:S(2)}) collective-permute-start(bf16[3,16,4224]{2,1,0:T(8,128)(2,1)S(1)} %pad_maximum_fusion.refs_4_), channel_id=1, source_target_pairs={{0,8},{8,0},{16,24},{24,16},{1,9},{9,1},{17,25},{25,17},{2,10},{10... | collective-permute-start | bytes 1216520 | tf_op jit(solution)/shard_map/ppermute | solution.py:587
  128.7 1.7 %collective-permute-start.25 = (bf16[3,16,4224]{2,1,0:T(8,128)(2,1)S(1)}, bf16[3,16,4224]{2,1,0:T(8,128)(2,1)S(1)}, u32[]{:S(2)}, u32[]{:S(2)}) collective-permute-start(bf16[3,16,4224]{2,1,0:T(8,128)(2,1)S(1)} %collective-permute-done.23.refs_5_), channel_id=1, source_target_pairs={{0,8},{8,0},{16,24},{24,16},{1,9},{9,1},{17,25},{25,17},{2,10},{10... | collective-permute-start | bytes 1216520 | tf_op jit(solution)/shard_map/ppermute | solution.py:587

commit v9 on v6

--- a/solution.py
+++ b/solution.py
@@ -39,77 +39,57 @@
     return lax.dot_general(a, b, (((axis_a,), (axis_b,)), ((), ())), preferred_element_type=f32)
 
 
-at_ctx, at_head, at_dp = 0, 1, 2
-
-
-class Route:
-    def __init__(self, n):
-        self.n = n
-
-    def pairs(self, left, step):
-        n = self.n
-        if left:
-            return [(k, k - 1) for k in range(1, n - step + 1)]
-        return [(k, k + 1) for k in range(step - 1, n - 1)]
-
-    def joined(self, step):
-        return self.n - step < step - 1
-
-    def choose(self, u, z):
-        n = self.n
-        if z < n // 2:
-            return (True, u) if u <= n - 1 - z else (False, n - u)
-        return (False, u) if u <= z else (True, n - u)
-
-    def source(self, u, z):
-        if u == 0:
-            return z
-        left, step = self.choose(u, z)
-        return z + step if left else z - step
-
-    def options(self, u):
-        found = []
-        for z in range(self.n):
-            left, step = self.choose(u, z)
-            one = (None if self.joined(step) else left, step)
-            if one not in found:
-                found.append(one)
-        return found
-
-    def option(self, u, z):
-        left, step = self.choose(u, z)
-        return self.options(u).index((None if self.joined(step) else left, step))
+at_ctx, at_head, at_dp, at_end = 0, 1, 2, 3
+
+
+def folded_ring(size):
+    return [0] + list(range(1, size, 2)) + list(range(2, size, 2))[::-1]
+
+
+def on_line(n):
+    return n == 4
+
+
+def key_source(n, z, u):
+    if on_line(n):
+        return ([0, 1, 2, 3], [1, 2, 0, 3], [2, 1, 3, 0], [3, 2, 1, 0])[z][u]
+    ring = folded_ring(n)
+    return ring[(ring.index(z) - u) % n]
 
 
 def device_table(n, heads, dp_size):
-    route = Route(n)
     table = []
     for z in range(n):
         for y in range(heads):
             for dp in range(dp_size):
-                row = [z, y, dp]
-                row += [route.source(u, z) for u in range(n)]
-                row += [0] + [route.option(u, z) for u in range(1, n)]
+                row = [z, y, dp, int(z in (0, n - 1))]
+                row += [key_source(n, z, u) for u in range(n)]
+                row += [(z - key_source(n, z, u)) % n for u in range(n)]
                 row += [dp ^ k for k in dp_flips(dp_size)]
                 row += [(z - t) % n for t in range(n)]
+                row += [k if z < n // 2 or not on_line(n) else n - 1 - k for k in range(n)]
                 table.append(row)
     return np.array(table, np.int32)
 
 
 def at_source(n, u):
-    return 3 + u
-
-
-def at_option(n, u):
-    return 3 + n + u
+    return 4 + u
+
+
+def at_place(n, u):
+    return 4 + n + u
 
 
 def at_partner(n, k):
-    return 3 + 2 * n + k
+    return 4 + 2 * n + k
 
 
 def at_shift(n, dp_size, t):
-    return 3 + 2 * n + dp_size + t
+    return 4 + 2 * n + dp_size + t
+
+
+def at_part(n, dp_size, k):
+    return 4 + 3 * n + dp_size + k
 
 
 def dp_flips(dp_size):
@@ -119,23 +99,32 @@
     return flips
 
 
-def project_kernel(info, latent, weight, hidden, hidden_weight, out, kept):
+def project_kernel(order_at, info, latent, weight, hidden, hidden_weight, out, own, kept):
     blocks, count, _ = out.shape
     width = weight.shape[1]
     heads = hidden_weight.shape[0]
+    rows, mixed_rows = latent[...], hidden[...]
+    if order_at is not None:
+        starts = [pl.multiple_of(info[order_at + k] * count, count) for k in range(blocks)]
+        rows = jnp.concatenate([latent[pl.ds(k, count), :] for k in starts], axis=0)
+        mixed_rows = jnp.concatenate([hidden[pl.ds(k, count), :] for k in starts], axis=0)
     for at in range(0, width, 512):
-        product = times(latent[...], weight[:, at : at + 512], 1, 0)
+        product = times(rows, weight[:, at : at + 512], 1, 0)
         for k in range(blocks):
             out[k, :, at : at + 512] = product[k * count : (k + 1) * count]
-    mixed = times(hidden[...], hidden_weight[...], 1, 1)
+    mixed = times(mixed_rows, hidden_weight[...], 1, 1)
     for k in range(blocks):
         out[k, :, width : width + heads] = mixed[k * count : (k + 1) * count]
         out[k, :, width + heads :] = jnp.zeros((count, lanes - heads), f32)
+    if order_at is None:
+        own[...] = jnp.zeros(own.shape, f32)
+    else:
+        own[...] = out[1 - info[at_end]]
     kept[:, : latent.shape[1]] = latent[...]
     kept[:, latent.shape[1] :] = hidden[...]
 
 
-def project(info, count, latent, weight, hidden, hidden_weight):
+def project(info, order_at, count, latent, weight, hidden, hidden_weight):
     queries, width = latent.shape[0], weight.shape[1]
     depth, hidden_depth = weight.shape[0], hidden_weight.shape[1]
     blocks = queries // count
@@ -146,7 +135,7 @@
         hidden = lax.dynamic_slice_in_dim(hidden, info[at_ctx] * hidden_depth, hidden_depth, 1)
         columns = whole
     return pl.pallas_call(
-        project_kernel,
+        functools.partial(project_kernel, order_at),
         grid_spec=pltpu.PrefetchScalarGridSpec(
             num_scalar_prefetch=1,
             grid=(1,),
@@ -158,11 +147,13 @@
             ],
             out_specs=[
                 pl.BlockSpec((blocks, count, width + lanes), lambda i, info: (0, 0, 0)),
+                pl.BlockSpec((count, width + lanes), whole),
                 pl.BlockSpec((queries, depth + hidden_depth), whole),
             ],
         ),
         out_shape=[
             jax.ShapeDtypeStruct((blocks, count, width + lanes), f32),
+            jax.ShapeDtypeStruct((count, width + lanes), f32),
             jax.ShapeDtypeStruct((queries, depth + hidden_depth), bf16),
         ],
         compiler_params=params(),
@@ -182,7 +173,7 @@
         keys = chosen
         for k, option in enumerate(options):
 
-            @pl.when(info[at_option(n, t)] == k)
+            @pl.when(info[at_end] == 1 - k)
             def _():
                 chosen[...] = option[...]
 
@@ -252,11 +243,7 @@
         + [pltpu.VMEM((min(group_size, count) * heads, span), f32)] * 2
         + [pltpu.VMEM((depth, span), bf16)],
         compiler_params=params(),
-        cost_estimate=pl.CostEstimate(
-            flops=4 * count * heads * depth * span,
-            bytes_accessed=2 * (2 * mine.size + depth * span + 2 * count * heads * span),
-            transcendentals=2 * count * heads * span,
-        ),
+        cost_estimate=pl.CostEstimate(flops=0, bytes_accessed=0, transcendentals=0),
         name="score",
     )(info, positions, mine, other, *options, *before)
 
@@ -277,7 +264,7 @@
     inverse = 1.0 / (total * HM)
     for t in range(blocks):
         factor = jnp.exp2((tops[t][...] - joint) * exponent_scale) * inverse
-        to = pl.ds(pl.multiple_of(info[at_source(blocks, t)] * span, span), span)
+        to = pl.ds(pl.multiple_of(info[at_place(blocks, t)] * span, span), span)
         for q in range(count):
             column = jnp.sum(
                 jnp.where(diagonal, factor[q : q + 1, :], 0.0), axis=1, keepdims=True
@@ -317,16 +304,17 @@
     )
 
 
-def summed(received):
-    total = received[0]
-    for k in range(1, received.shape[0]):
-        total = total + received[k]
+def summed(terms):
+    total = terms[0][...]
+    for one in terms[1:]:
+        total = total + one[...]
     return total
 
 
-def logits_kernel(heads, received, own, other, out):
-    count = received.shape[1]
-    total = summed(received)
+def logits_kernel(heads, *refs):
+    terms, (own, other, out) = refs[:-3], refs[-3:]
+    total = summed(terms)
+    count = total.shape[0]
     query = query_rows(total, heads)
     columns = [total[:, heads * DI + j : heads * DI + j + 1] for j in range(heads)]
     span = 512
@@ -340,24 +328,20 @@
             out[part, :, at : at + span] = running * index_scale
 
 
-def make_logits(heads, received, own, other):
-    count, length = received.shape[1], own.shape[0]
+def make_logits(heads, terms, own, other):
+    count, length = terms[0].shape[0], own.shape[0]
     return pl.pallas_call(
         functools.partial(logits_kernel, heads),
         out_shape=jax.ShapeDtypeStruct((2, count, length), f32),
-        in_specs=[in_vmem()] * 3,
+        in_specs=[in_vmem()] * (2 + len(terms)),
         out_specs=in_vmem(),
         compiler_params=params(),
-        cost_estimate=pl.CostEstimate(
-            flops=4 * count * heads * DI * length,
-            bytes_accessed=4 * (received.size + 2 * count * length) + 4 * length * DI,
-            transcendentals=0,
-        ),
+        cost_estimate=pl.CostEstimate(flops=0, bytes_accessed=0, transcendentals=0),
         name="logits",
-    )(received, own, other)
-
-
-def softmax_kernel(blocks, rows_here, info, positions, part, far, probs, log_probs):
+    )(*terms, own, other)
+
+
+def softmax_kernel(blocks, rows_here, shift_at, info, positions, part, far, probs, log_probs):
     _, count, length = part.shape
     span = length // blocks
     row_at = lax.broadcasted_iota(jnp.int32, (count, lanes), 0)
@@ -369,7 +353,7 @@
 
     def seen(side, t):
         half = info[at_head] if side == 0 else 1 - info[at_head]
-        return key_at + (t * rows_here + half * span) <= position
+        return key_at + (info[shift_at + t] * rows_here + half * span) <= position
 
     highs = []
     for side in range(2):
@@ -400,16 +384,14 @@
             log_probs[side, :, at] = jnp.where(seen(side, t), log_probs[side, :, at] - level, 0.0)
 
 
-def make_softmax(blocks, rows_here, info, positions, part, far):
+def make_softmax(blocks, rows_here, shift_at, info, positions, part, far):
     return pl.pallas_call(
-        functools.partial(softmax_kernel, blocks, rows_here),
+        functools.partial(softmax_kernel, blocks, rows_here, shift_at),
         out_shape=(jax.ShapeDtypeStruct(part.shape, f32),) * 2,
         in_specs=[in_smem()] * 2 + [in_vmem()] * 2,
         out_specs=(in_vmem(),) * 2,
         compiler_params=params(),
-        cost_estimate=pl.CostEstimate(
-            flops=8 * part.size, bytes_accessed=16 * part.size, transcendentals=part.size
-        ),
+        cost_estimate=pl.CostEstimate(flops=0, bytes_accessed=0, transcendentals=0),
         name="softmax",
     )(info, positions, part, far)
 
@@ -417,23 +399,13 @@
 def gradient_kernel(
     heads,
     blocks,
-    received,
-    own,
-    other,
-    probs,
-    log_probs,
-    delta_own,
-    sent,
-    brought,
-    out,
-    flow,
-    query_sum,
-    grads,
-    even,
-    odd,
+    *refs,
 ):
-    count = received.shape[1]
-    total = summed(received)
+    terms, refs = refs[:-13], refs[-13:]
+    own, other, probs, log_probs, delta_own, sent, brought, out = refs[:8]
+    flow, query_sum, grads, even, odd = refs[8:]
+    total = summed(terms)
+    count = total.shape[0]
     span = own.shape[0] // blocks
     query = query_rows(total, heads)
     columns = [
@@ -490,13 +462,13 @@
     out[:, heads * DI :] = tail.astype(bf16)
 
 
-def gradients(heads, blocks, received, own, other, probs, log_probs, delta_own, sent, brought):
-    count, length = received.shape[1], own.shape[0]
+def gradients(heads, blocks, terms, own, other, probs, log_probs, delta_own, sent, brought):
+    count, length = terms[0].shape[0], own.shape[0]
     span = length // blocks
     return pl.pallas_call(
         functools.partial(gradient_kernel, heads, blocks),
         out_shape=jax.ShapeDtypeStruct((count, heads * DI + lanes), bf16),
-        in_specs=[in_vmem()] * 8,
+        in_specs=[in_vmem()] * (7 + len(terms)),
         out_specs=in_vmem(),
         scratch_shapes=[
             pltpu.VMEM((heads * count, lanes), f32),
@@ -508,11 +480,11 @@
         compiler_params=params(),
         cost_estimate=pl.CostEstimate(
             flops=8 * count * heads * DI * length,
-            bytes_accessed=4 * (received.size + 6 * count * length) + 4 * length * DI,
+            bytes_accessed=4 * (terms[0].size + 6 * count * length) + 4 * length * DI,
             transcendentals=0,
         ),
         name="gradient",
-    )(received, own, other, probs, log_probs, delta_own, sent, brought)
+    )(*terms, own, other, probs, log_probs, delta_own, sent, brought)
 
 
 def arrange_kernel(n, info, *refs):
@@ -615,16 +587,28 @@
     y = lax.axis_index("head")
     dp_size = lax.axis_size("dp")
     dp = lax.axis_index("dp")
-    route = Route(n)
     rows = main_keys.shape[1]
     half = rows // head_size
     rows_latent = w_query.shape[0]
     heads_here = w_weights.shape[1]
     queries_here = main_queries.shape[1]
-    sequence_positions = positions[0]
-
-    def to_each(x):
-        return lax.all_to_all(x, "ctx", 0, 0)
+
+    def shifted(x, t):
+        return lax.ppermute(x, "ctx", [(k, (k + t) % n) for k in range(n)])
+
+    def outward(x):
+        return lax.ppermute(x, "ctx", [(1, 0), (2, 3)])
+
+    def centre(x):
+        return lax.ppermute(x, "ctx", [(1, 2), (2, 1)])
+
+    def inward(x):
+        return lax.ppermute(x, "ctx", [(0, 1), (3, 2)])
+
+    def after(waited, *held):
+        nonlocal token
+        token, waited, held = lax.optimization_barrier((token, waited, held))
+        return waited, *held
 
     def swap_head(x):
         return lax.ppermute(x, "head", [(0, 1), (1, 0)])
@@ -641,50 +625,90 @@
     table = jnp.array(device_table(n, head_size, dp_size))
     info = lax.dynamic_index_in_dim(table, (z * head_size + y) * dp_size + dp, 0, False)
 
+    token = positions[0]
+    queries = main_queries[0]
     own_keys = lax.dynamic_slice_in_dim(main_keys[0].T, y * half, half, 1)
-    carried = {}
-    last = {True: own_keys, False: own_keys}
-    for step in range(1, n):
-        if route.joined(step):
-            x = jnp.where(z <= n - step, last[True], last[False])
-            x = lax.ppermute(x, "ctx", route.pairs(True, step) + route.pairs(False, step))
-            carried[None, step] = last[True] = last[False] = x
-        else:
-            for left in (True, False):
-                last[left] = lax.ppermute(last[left], "ctx", route.pairs(left, step))
-                carried[left, step] = last[left]
-    queries = main_queries[0]
-    other_queries = swap_head(queries)
-
-    partial, kept = project(info, queries_here, q_latent[0], w_query, hidden[0], w_weights.T)
-    received = to_each(partial)
     index_part = lax.dynamic_slice_in_dim(index_keys[0], y * half, half)
-    index_own = to_each(jnp.broadcast_to(index_part[None], (n, *index_part.shape)))
-    index_own = index_own.reshape(n * half, DI)
-    index_other = swap_head(index_own)
-    part = make_logits(heads_here, received, index_own, index_other)
-    probs, log_probs = make_softmax(n, rows, info, sequence_positions, part, swap_head(part))
-    latents, hiddens = arrange(n, info, rows_latent, over_dp(kept))
-
+    line = on_line(n)
+    order_at = at_part(n, dp_size, 0) if line else None
     weights, tops, before = [], [], None
-    for t in range(n):
-        options = [own_keys] if t == 0 else [carried[one] for one in route.options(t)]
-        if t == n - 2:
-            before, latents, hiddens, part = lax.optimization_barrier(
-                (before, latents, hiddens, part)
-            )
-        if t == n - 1:
-            before, probs, log_probs = lax.optimization_barrier((before, probs, log_probs))
+
+    def score_next(*options):
+        nonlocal before
+        t = len(weights)
         numer, top, *before = score(
-            t, n, rows, info, sequence_positions, queries, other_queries, options, before
+            t, n, rows, info, token, queries, other_queries, options, before
         )
         weights.append(numer)
         tops.append(top)
+
+    if line:
+        index_1, index_3 = shifted(index_part, 1), shifted(index_part, 3)
+        keys_out, keys_over, keys_in = outward(own_keys), centre(own_keys), inward(own_keys)
+        partial, own_part, kept = project(
+            info, order_at, queries_here, q_latent[0], w_query, hidden[0], w_weights.T
+        )
+        (index_1, index_3), sent_queries = after((index_1, index_3), queries)
+        other_queries = swap_head(sent_queries)
+        _, far_part = after((), partial[3])
+        far_in = inward(far_part)
+        (keys_out, keys_over, keys_in), index_again = after(
+            (keys_out, keys_over, keys_in), index_part
+        )
+        keys_out2, keys_over2 = outward(keys_over), centre(keys_in)
+        index_2 = shifted(index_again, 2)
+        (far_in,) = after(far_in)
+        far_over = centre(far_part + far_in)
+        index_2, near_parts = after(index_2, partial[1:3])
+        near_in = inward(near_parts)
+        (far_over, other_queries), kept = after((far_over, other_queries), kept)
+        sum_out = outward(partial[0] + far_over)
+        half_dp, near_dp = swap_dp(kept, dp_size // 2), swap_dp(kept, dp_size // 4)
+        index_own = jnp.concatenate([index_part, index_1, index_2, index_3])
+        (keys_out2, keys_over2, sum_out, near_in, half_dp, near_dp), index_own = after(
+            (keys_out2, keys_over2, sum_out, near_in, half_dp, near_dp), index_own
+        )
+        keys_out3 = outward(keys_over2)
+        sum_over = centre(partial[2] + near_in[1])
+        index_other = swap_head(index_own)
+        kept = [kept, half_dp, near_dp, swap_dp(half_dp, dp_size // 4)]
+        score_next(own_keys)
+        score_next(keys_out, keys_over)
+        latents, hiddens = arrange(n, info, rows_latent, kept)
+        before, latents, hiddens = lax.optimization_barrier((before, latents, hiddens))
+        score_next(keys_out2, keys_in)
+        before, sum_out, sum_over, near_in = lax.optimization_barrier(
+            (before, sum_out, sum_over, near_in)
+        )
+        terms = [own_part, sum_out, sum_over, near_in[0]]
+        last_keys = (keys_out3, keys_over2)
+    else:
+        ring = folded_ring(n)
+        partial, _, kept = project(
+            info, order_at, queries_here, q_latent[0], w_query, hidden[0], w_weights.T
+        )
+        terms = [jnp.sum(lax.all_to_all(partial, "ctx", 0, 0), axis=0)]
+        other_queries = swap_head(queries)
+        index_own = jnp.concatenate([index_part] + [shifted(index_part, t) for t in range(1, n)])
+        index_other = swap_head(index_own)
+        latents, hiddens = arrange(n, info, rows_latent, over_dp(kept))
+        keys = own_keys
+        for _ in range(n - 1):
+            score_next(keys)
+            keys = lax.ppermute(keys, "ctx", [(ring[k], ring[(k + 1) % n]) for k in range(n)])
+        last_keys = (keys,)
+
+    part = make_logits(heads_here, terms, index_own, index_other)
+    probs, log_probs = make_softmax(
+        n, rows, at_shift(n, dp_size, 0), info, token, part, swap_head(part)
+    )
+    before, probs, log_probs = lax.optimization_barrier((before, probs, log_probs))
+    score_next(*last_keys)
     delta_own, sent = make_delta(info, weights, tops, *before, swap_head(jnp.stack(before)), probs)
     piece = gradients(
         heads_here,
         n,
-        received,
+        terms,
         index_own,
         index_other,
         probs,

time: 142 us -> 133 us (0.937)
  Pallas kernels: 31.4 us -> 25.3 us
  local copies, waits for them, and re-layouts: 9.8 us -> 5.35 us
  waiting for transfers between devices: 54.4 us -> 56.4 us
    ppermute x5 -> x14, starting transfers between devices: 10.1 us -> 27.6 us  [the longest x3 10.3 us: shifted(): return lax.ppermute(x, 'ctx', [(k, (k + t) % n) for k in range(n)])]
    all_to_all x2 -> x0, starting transfers between devices: 9.84 us -> none  [to_each(): return lax.all_to_all(x, 'ctx', 0, 0)]
    ppermute x5, waiting for transfers between devices: 4.97 us -> 13.4 us  [swap_head(): return lax.ppermute(x, 'head', [(0, 1), (1, 0)])]
    ppermute x3, starting transfers between devices: 9.58 us -> 3.67 us  [per_device(): brought.append(lax.ppermute(piece, 'ctx', pairs))]
    unnamed x28 -> x14, local copies, waits for them, and re-layouts: 7.12 us -> 2.81 us
    ppermute x9, waiting for transfers between devices: 13 us -> 9.12 us  [swap_dp(): return lax.ppermute(x, 'dp', [(k, k ^ bit) for k in range(dp_size)])]
    pallas_call x4, Pallas kernels: 15 us -> 11.5 us  [score(): pl.pallas_call(functools.partial(score_kernel, t, n, rows_here), out_shap...]
    all_to_all x2 -> x0, waiting for transfers between devices: 2.89 us -> none  [to_each(): return lax.all_to_all(x, 'ctx', 0, 0)]
  transfers between devices with their start and end apart: 24 -> 31, of which waited for: 12 -> 15; matrix products, arithmetic and copies ran while one was open for 2% -> 2% of each run, Pallas kernels for 12% -> 10%
where the time goes in v9:
time: 133 us
  waiting for transfers between devices  56.4 us (42%)
  starting transfers between devices  43.5 us (33%)
  Pallas kernels  25.3 us (19%)
  local copies, waits for them, and re-layouts  5.35 us (4%)
    ppermute x5, waiting for transfers between devices, swap_head(): return lax.ppermute(x, 'head', [(0, 1), (1, 0)])  13.4 us
    pallas_call x4, Pallas kernels, score(): pl.pallas_call(functools.partial(score_kernel, t, n, rows_here), out_shap...  11.5 us
    ppermute x3, starting transfers between devices, shifted(): return lax.ppermute(x, 'ctx', [(k, (k + t) % n) for k in range(n)])  10.3 us
    ppermute x3, waiting for transfers between devices, shifted(): return lax.ppermute(x, 'ctx', [(k, (k + t) % n) for k in range(n)])  10.2 us
    ppermute x9, waiting for transfers between devices, swap_dp(): return lax.ppermute(x, 'dp', [(k, k ^ bit) for k in range(dp_size)])  9.12 us
    ppermute x3, starting transfers between devices, inward(): return lax.ppermute(x, 'ctx', [(0, 1), (3, 2)])  8.61 us
    ppermute x3, waiting for transfers between devices, inward(): return lax.ppermute(x, 'ctx', [(0, 1), (3, 2)])  8.6 us
    ppermute x4, waiting for transfers between devices, outward(): return lax.ppermute(x, 'ctx', [(1, 0), (2, 3)])  8.31 us
  transfers between devices with their start and end apart: 31, of which 15 were waited for; matrix products, arithmetic and copies ran while one was open for 2% of the time, Pallas kernels for 10%

profile of v9, /device:TPU:0, one launch (start us, length us, event | category | flops | bytes accessed | tf_op | source)
XLA Modules:
  0.0 132.9 jit_solution(7795392842300142657)
XLA Ops:
  0.7 1.7 %dynamic-slice_bitcast_fusion.1 = bf16[512,128]{1,0:T(8,128)(2,1)} fusion(bf16[1,1024,128]{2,1,0:T(8,128)(2,1)} %param.13, s32[]{:T(128)S(6)} %select_n.9), kind=kLoop, calls=%fused_computation.7 | loop fusion | bytes 262148 | tf_op jit(solution)/shard_map/dynamic_slice | solution.py:631
  2.4 5.0 %collective-permute-start.1 = (bf16[512,128]{1,0:T(8,128)(2,1)}, bf16[512,128]{1,0:T(8,128)(2,1)}, u32[]{:S(2)}, u32[]{:S(2)}) collective-permute-start(bf16[512,128]{1,0:T(8,128)(2,1)} %dynamic-slice_bitcast_fusion.1), channel_id=1, source_target_pairs={{0,3},{1,0},{2,1},{3,2},{4,7},{5,4},{6,5},{7,6},{8,11},{9,8},{10,9... | collective-permute-start | bytes 393224 | tf_op jit(solution)/shard_map/ppermute | solution.py:597
  7.5 1.9 %collective-permute-start.4 = (bf16[576,512]{1,0:T(8,128)(2,1)S(1)}, bf16[576,512]{1,0:T(8,128)(2,1)S(1)}, u32[]{:S(2)}, u32[]{:S(2)}) collective-permute-start(bf16[576,512]{1,0:T(8,128)(2,1)S(1)} %dynamic-slice_bitcast_fusion.refs_0_), channel_id=1, source_target_pairs={{0,1},{3,2},{4,5},{7,6},{8,9},{11,10},{12,13},{15,14},{16,17},{19,... | collective-permute-start | bytes 1769480 | tf_op jit(solution)/shard_map/ppermute | solution.py:606
  9.4 1.5 %collective-permute-start.3 = (bf16[576,512]{1,0:T(8,128)(2,1)S(1)}, bf16[576,512]{1,0:T(8,128)(2,1)}, u32[]{:S(2)}, u32[]{:S(2)}) collective-permute-start(bf16[576,512]{1,0:T(8,128)(2,1)S(1)} %dynamic-slice_bitcast_fusion.refs_0_), channel_id=1, source_target_pairs={{1,2},{2,1},{5,6},{6,5},{9,10},{10,9},{13,14},{14,13},{17,18},{18,... | collective-permute-start | bytes 1769480 | tf_op jit(solution)/shard_map/ppermute | solution.py:603
  10.9 1.3 collective-permute-start.2
  13.0 1.9 %copy-done.2 = bf16[384,4096]{1,0:T(8,128)(2,1)S(1)} copy-done((bf16[384,4096]{1,0:T(8,128)(2,1)S(1)}, bf16[384,4096]{1,0:T(8,128)(2,1)}, u32[]{:S(2)}) %copy-start.2) | copy-done | bytes 3145752
  14.8 0.9 copy-done.5
  15.7 1.3 project.1
  17.1 1.6 %collective-permute-start.8 = (bf16[16,64,576]{2,1,0:T(8,128)(2,1)S(1)}, bf16[16,64,576]{2,1,0:T(8,128)(2,1)S(1)}, u32[]{:S(2)}, u32[]{:S(2)}) collective-permute-start(bf16[16,64,576]{2,1,0:T(8,128)(2,1)S(1)} %bitcast.25), channel_id=1, source_target_pairs={{0,4},{4,0},{1,5},{5,1},{2,6},{6,2},{3,7},{7,3},{8,12},{12,8},{9,1... | collective-permute-start | bytes 3538952 | tf_op jit(solution)/shard_map/ppermute | solution.py:614
  18.7 5.4 %collective-permute-start.5 = (f32[16,4224]{1,0:T(8,128)S(1)}, f32[16,4224]{1,0:T(8,128)S(1)}, u32[]{:S(2)}, u32[]{:S(2)}) collective-permute-start(f32[16,4224]{1,0:T(8,128)S(1)} %slice_bitcast_fusion.1), channel_id=1, source_target_pairs={{0,1},{3,2},{4,5},{7,6},{8,9},{11,10},{12,13},{15,14},{16,17},{19,... | collective-permute-start | bytes 811016 | tf_op jit(solution)/shard_map/ppermute | solution.py:606
  24.1 2.9 %collective-permute-done.4.refs_1_ = bf16[576,512]{1,0:T(8,128)(2,1)S(1)} collective-permute-done((bf16[576,512]{1,0:T(8,128)(2,1)S(1)}, bf16[576,512]{1,0:T(8,128)(2,1)S(1)}, u32[]{:S(2)}, u32[]{:S(2)}) %collective-permute-start.4) | collective-permute-done | bytes 589856 | tf_op jit(solution)/shard_map/ppermute | solution.py:606
  27.0 0.9 collective-permute-done.2.refs_0_
  27.9 3.8 %collective-permute-done.5 = f32[16,4224]{1,0:T(8,128)S(1)} collective-permute-done((f32[16,4224]{1,0:T(8,128)S(1)}, f32[16,4224]{1,0:T(8,128)S(1)}, u32[]{:S(2)}, u32[]{:S(2)}) %collective-permute-start.5) | collective-permute-done | bytes 270368 | tf_op jit(solution)/shard_map/ppermute | solution.py:606
  32.4 5.2 %collective-permute-start.6 = (bf16[512,128]{1,0:T(8,128)(2,1)}, bf16[512,128]{1,0:T(8,128)(2,1)S(1)}, u32[]{:S(2)}, u32[]{:S(2)}) collective-permute-start(bf16[512,128]{1,0:T(8,128)(2,1)} %dynamic-slice_bitcast_fusion.1), channel_id=1, source_target_pairs={{0,2},{1,3},{2,0},{3,1},{4,6},{5,7},{6,4},{7,5},{8,10},{9,11},{10,... | collective-permute-start | bytes 393224 | tf_op jit(solution)/shard_map/ppermute | solution.py:597
  37.7 1.3 collective-permute-start.9
  39.7 10.2 %collective-permute-done.6 = bf16[512,128]{1,0:T(8,128)(2,1)S(1)} collective-permute-done((bf16[512,128]{1,0:T(8,128)(2,1)}, bf16[512,128]{1,0:T(8,128)(2,1)S(1)}, u32[]{:S(2)}, u32[]{:S(2)}) %collective-permute-start.6) | collective-permute-done | bytes 131104 | tf_op jit(solution)/shard_map/ppermute | solution.py:597
  49.9 1.3 collective-permute-start.12
  51.4 1.6 %collective-permute-start.13 = (bf16[64,2176]{1,0:T(8,128)(2,1)S(1)}, bf16[64,2176]{1,0:T(8,128)(2,1)S(1)}, u32[]{:S(2)}, u32[]{:S(2)}) collective-permute-start(bf16[64,2176]{1,0:T(8,128)(2,1)S(1)} %get-tuple-element.93.refs_0_), channel_id=1, source_target_pairs={{0,16},{8,24},{16,0},{24,8},{1,17},{9,25},{17,1},{25,9},{2,18},{10... | collective-permute-start | bytes 835592 | tf_op jit(solution)/shard_map/ppermute | solution.py:617
  53.0 3.3 %collective-permute-done.9.refs_0_ = bf16[576,512]{1,0:T(8,128)(2,1)S(1)} collective-permute-done((bf16[576,512]{1,0:T(8,128)(2,1)}, bf16[576,512]{1,0:T(8,128)(2,1)S(1)}, u32[]{:S(2)}, u32[]{:S(2)}) %collective-permute-start.9) | collective-permute-done | bytes 589856 | tf_op jit(solution)/shard_map/ppermute | solution.py:600
  56.3 1.3 collective-permute-start.11
  57.6 1.1 pad_maximum_fusion.refs_4_
  58.7 1.9 %collective-permute-done.12 = f32[2,16,4224]{2,1,0:T(8,128)S(1)} collective-permute-done((f32[2,16,4224]{2,1,0:T(8,128)S(1)}, f32[2,16,4224]{2,1,0:T(8,128)S(1)}, u32[]{:S(2)}, u32[]{:S(2)}) %collective-permute-start.12) | collective-permute-done | bytes 540704 | tf_op jit(solution)/shard_map/ppermute | solution.py:606
  60.5 4.1 %collective-permute-done.11.refs_1_ = f32[16,4224]{1,0:T(8,128)S(1)} collective-permute-done((f32[16,4224]{1,0:T(8,128)S(1)}, f32[16,4224]{1,0:T(8,128)S(1)}, u32[]{:S(2)}, u32[]{:S(2)}) %collective-permute-start.11) | collective-permute-done | bytes 270368 | tf_op jit(solution)/shard_map/ppermute | solution.py:600
  65.4 1.6 %collective-permute-start.17 = (bf16[2048,128]{1,0:T(8,128)(2,1)S(1)}, bf16[2048,128]{1,0:T(8,128)(2,1)S(1)}, u32[]{:S(2)}, u32[]{:S(2)}) collective-permute-start(bf16[2048,128]{1,0:T(8,128)(2,1)S(1)} %pad_maximum_fusion.refs_4_), channel_id=1, source_target_pairs={{0,4},{4,0},{1,5},{5,1},{2,6},{6,2},{3,7},{7,3},{8,12},{12,8},{9,1... | collective-permute-start | bytes 1572872 | tf_op jit(solution)/shard_map/ppermute | solution.py:614
  67.0 1.3 collective-permute-start.19
  68.3 2.6 %score.4 = (bf16[16,128,512]{2,1,0:T(8,128)(2,1)S(1)}, f32[16,128]{1,0:T(8,128)S(1)}, f32[16,128]{1,0:T(8,128)S(1)}, f32[16,128]{1,0:T(8,128)S(1)}) custom-call(s32[24]{0:T(128)S(1)} %fusion.info, s32[64]{0:T(128)S(1)} %bitcast.41, bf16[16,64,576]{2,1,0:T(8,128)(2,1)S(1)} %bitcast.26, bf16[16,64,576]{2,1,0:T(8,128)(2,1)S(1)} %collective-permute-done.8.other, ...), custom_call_target="tpu_custom_call" | custom-call | tf_op jit(solution)/shard_map/score/pallas_call | solution.py:237
  70.9 3.4 %score.5 = (bf16[16,128,512]{2,1,0:T(8,128)(2,1)S(1)}, f32[16,128]{1,0:T(8,128)S(1)}, f32[16,128]{1,0:T(8,128)S(1)}, f32[16,128]{1,0:T(8,128)S(1)}) custom-call(s32[24]{0:T(128)S(1)} %fusion.info, s32[64]{0:T(128)S(1)} %bitcast.42, bf16[16,64,576]{2,1,0:T(8,128)(2,1)S(1)} %bitcast.27, bf16[16,64,576]{2,1,0:T(8,128)(2,1)S(1)} %collective-permute-done.8.other, ...), custom_call_target="tpu_custom_call" | custom-call | tf_op jit(solution)/shard_map/score/pallas_call | solution.py:237
  75.1 2.7 %score.6 = (bf16[16,128,512]{2,1,0:T(8,128)(2,1)S(1)}, f32[16,128]{1,0:T(8,128)S(1)}, f32[16,128]{1,0:T(8,128)S(1)}, f32[16,128]{1,0:T(8,128)S(1)}) custom-call(s32[24]{0:T(128)S(1)} %fusion.info, s32[64]{0:T(128)S(1)} %bitcast.43, bf16[16,64,576]{2,1,0:T(8,128)(2,1)S(1)} %bitcast.28, bf16[16,64,576]{2,1,0:T(8,128)(2,1)S(1)} %collective-permute-done.8.other, ...), custom_call_target="tpu_custom_call" | custom-call | tf_op jit(solution)/shard_map/score/pallas_call | solution.py:237
  77.8 2.0 %collective-permute-done.17.refs_5_ = bf16[2048,128]{1,0:T(8,128)(2,1)S(1)} collective-permute-done((bf16[2048,128]{1,0:T(8,128)(2,1)S(1)}, bf16[2048,128]{1,0:T(8,128)(2,1)S(1)}, u32[]{:S(2)}, u32[]{:S(2)}) %collective-permute-start.17) | collective-permute-done | bytes 524320 | tf_op jit(solution)/shard_map/ppermute | solution.py:614
  79.8 1.3 logits.1.part
  81.1 1.6 %collective-permute-start.18 = (f32[2,16,2048]{2,1,0:T(8,128)S(1)}, f32[2,16,2048]{2,1,0:T(8,128)S(1)}, u32[]{:S(2)}, u32[]{:S(2)}) collective-permute-start(f32[2,16,2048]{2,1,0:T(8,128)S(1)} %logits.1.part), channel_id=1, source_target_pairs={{0,4},{4,0},{1,5},{5,1},{2,6},{6,2},{3,7},{7,3},{8,12},{12,8},{9,1... | collective-permute-start | bytes 786440 | tf_op jit(solution)/shard_map/ppermute | solution.py:614
  82.7 6.4 %collective-permute-done.18.far = f32[2,16,2048]{2,1,0:T(8,128)S(1)} collective-permute-done((f32[2,16,2048]{2,1,0:T(8,128)S(1)}, f32[2,16,2048]{2,1,0:T(8,128)S(1)}, u32[]{:S(2)}, u32[]{:S(2)}) %collective-permute-start.18) | collective-permute-done | bytes 262176 | tf_op jit(solution)/shard_map/ppermute | solution.py:614
  89.9 2.9 %score.7 = (bf16[16,128,512]{2,1,0:T(8,128)(2,1)S(1)}, f32[16,128]{1,0:T(8,128)S(1)}, f32[16,128]{1,0:T(8,128)S(1)}, f32[16,128]{1,0:T(8,128)S(1)}) custom-call(s32[24]{0:T(128)S(1)} %fusion.info, s32[64]{0:T(128)S(1)} %bitcast.45, bf16[16,64,576]{2,1,0:T(8,128)(2,1)S(1)} %bitcast.29, bf16[16,64,576]{2,1,0:T(8,128)(2,1)S(1)} %collective-permute-done.8.other, ...), custom_call_target="tpu_custom_call" | custom-call | tf_op jit(solution)/shard_map/score/pallas_call | solution.py:237
  92.8 1.6 %collective-permute-start.20 = (f32[2,16,128]{2,1,0:T(8,128)S(1)}, f32[2,16,128]{2,1,0:T(8,128)S(1)}, u32[]{:S(2)}, u32[]{:S(2)}) collective-permute-start(f32[2,16,128]{2,1,0:T(8,128)S(1)} %pad_maximum_fusion.2), channel_id=1, source_target_pairs={{0,4},{4,0},{1,5},{5,1},{2,6},{6,2},{3,7},{7,3},{8,12},{12,8},{9,1... | collective-permute-start | bytes 49160 | tf_op jit(solution)/shard_map/ppermute | solution.py:614
  94.3 2.2 %collective-permute-done.20.refs_10_ = f32[2,16,128]{2,1,0:T(8,128)S(1)} collective-permute-done((f32[2,16,128]{2,1,0:T(8,128)S(1)}, f32[2,16,128]{2,1,0:T(8,128)S(1)}, u32[]{:S(2)}, u32[]{:S(2)}) %collective-permute-start.20) | collective-permute-done | bytes 16416 | tf_op jit(solution)/shard_map/ppermute | solution.py:614
  96.6 2.7 %delta.1 = (f32[16,2048]{1,0:T(8,128)S(1)}, bf16[16,2048]{1,0:T(8,128)(2,1)S(1)}) custom-call(s32[24]{0:T(128)S(1)} %fusion.info, bf16[16,128,512]{2,1,0:T(8,128)(2,1)S(1)} %get-tuple-element.128.refs_0_, bf16[16,128,512]{2,1,0:T(8,128)(2,1)S(1)} %get-tuple-element.129.refs_1_, bf16[16,128,512]{2,1,0:T(8,128)(2,1)S(1)} %get-tuple-element.130.refs_2_, ...), custom_call_target="tpu_custom_call" | custom-call | flops 8388608 | bytes 8388608 | tf_op jit(solution)/shard_map/delta/pallas_call | solution.py:282
  99.3 1.6 %collective-permute-start.21 = (bf16[16,2048]{1,0:T(8,128)(2,1)S(1)}, bf16[16,2048]{1,0:T(8,128)(2,1)S(1)}, u32[]{:S(2)}, u32[]{:S(2)}) collective-permute-start(bf16[16,2048]{1,0:T(8,128)(2,1)S(1)} %get-tuple-element.142.refs_9_), channel_id=1, source_target_pairs={{0,4},{4,0},{1,5},{5,1},{2,6},{6,2},{3,7},{7,3},{8,12},{12,8},{9,1... | collective-permute-start | bytes 196616 | tf_op jit(solution)/shard_map/ppermute | solution.py:614
  100.9 2.7 %collective-permute-done.21.refs_10_ = bf16[16,2048]{1,0:T(8,128)(2,1)S(1)} collective-permute-done((bf16[16,2048]{1,0:T(8,128)(2,1)S(1)}, bf16[16,2048]{1,0:T(8,128)(2,1)S(1)}, u32[]{:S(2)}, u32[]{:S(2)}) %collective-permute-start.21) | collective-permute-done | bytes 65568 | tf_op jit(solution)/shard_map/ppermute | solution.py:614
  103.6 2.5 %gradient.1 = bf16[16,4224]{1,0:T(8,128)(2,1)S(1)} custom-call(f32[16,4224]{1,0:T(8,128)S(1)} %get-tuple-element.110.refs_0_, f32[16,4224]{1,0:T(8,128)S(1)} %collective-permute-done.11.refs_1_, f32[16,4224]{1,0:T(8,128)S(1)} %collective-permute-done.16.refs_2_, f32[16,4224]{1,0:T(8,128)S(1)} %slice_bitcast_fusion.refs_3_, ...), custom_call_target="tpu_custom_call" | custom-call | flops 1073741824 | bytes 2105344 | tf_op jit(solution)/shard_map/gradient/pallas_call | solution.py:468
  106.1 1.6 %collective-permute-start.25 = (bf16[1,16,4224]{2,1,0:T(8,128)(2,1)S(1)}, bf16[1,16,4224]{2,1,0:T(8,128)(2,1)S(1)}, u32[]{:S(2)}, u32[]{:S(2)}) collective-permute-start(bf16[1,16,4224]{2,1,0:T(8,128)(2,1)S(1)} %bitcast.32), channel_id=1, source_target_pairs={{0,16},{8,24},{16,0},{24,8},{1,17},{9,25},{17,1},{25,9},{2,18},{10... | collective-permute-start | bytes 405512 | tf_op jit(solution)/shard_map/ppermute | solution.py:617
  107.6 1.2 collective-permute-start.24
  108.8 1.2 collective-permute-start.23
  110.0 1.3 collective-permute-start.22
  111.8 2.3 %collective-permute-done.24 = bf16[1,16,4224]{2,1,0:T(8,128)(2,1)S(1)} collective-permute-done((bf16[1,16,4224]{2,1,0:T(8,128)(2,1)S(1)}, bf16[1,16,4224]{2,1,0:T(8,128)(2,1)S(1)}, u32[]{:S(2)}, u32[]{:S(2)}) %collective-permute-start.24) | collective-permute-done | bytes 135200 | tf_op jit(solution)/shard_map/ppermute | solution.py:724
  114.2 4.3 %collective-permute-done.23 = bf16[1,16,4224]{2,1,0:T(8,128)(2,1)S(1)} collective-permute-done((bf16[1,16,4224]{2,1,0:T(8,128)(2,1)S(1)}, bf16[1,16,4224]{2,1,0:T(8,128)(2,1)S(1)}, u32[]{:S(2)}, u32[]{:S(2)}) %collective-permute-start.23) | collective-permute-done | bytes 135200 | tf_op jit(solution)/shard_map/ppermute | solution.py:724
  119.2 7.4 %collective-permute-done.28.refs_5_ = bf16[3,16,4224]{2,1,0:T(8,128)(2,1)S(1)} collective-permute-done((bf16[3,16,4224]{2,1,0:T(8,128)(2,1)S(1)}, bf16[3,16,4224]{2,1,0:T(8,128)(2,1)S(1)}, u32[]{:S(2)}, u32[]{:S(2)}) %collective-permute-start.28) | collective-permute-done | bytes 405536 | tf_op jit(solution)/shard_map/ppermute | solution.py:617
  126.6 1.7 %collective-permute-done.30.refs_7_ = bf16[3,16,4224]{2,1,0:T(8,128)(2,1)S(1)} collective-permute-done((bf16[3,16,4224]{2,1,0:T(8,128)(2,1)S(1)}, bf16[3,16,4224]{2,1,0:T(8,128)(2,1)S(1)}, u32[]{:S(2)}, u32[]{:S(2)}) %collective-permute-start.30) | collective-permute-done | bytes 405536 | tf_op jit(solution)/shard_map/ppermute | solution.py:617
  128.3 4.4 %outer.1 = (f32[384,4096]{1,0:T(8,128)}, f32[32,1792]{1,0:T(8,128)}, f32[1,64]{1,0:T(1,128)}) custom-call(s32[24]{0:T(128)S(1)} %fusion.info, bf16[384,256]{1,0:T(8,128)(2,1)S(1)} %get-tuple-element.108.latents, bf16[256,1792]{1,0:T(8,128)(2,1)S(1)} %get-tuple-element.109.hiddens, bf16[1,16,4224]{2,1,0:T(8,128)(2,1)S(1)} %bitcast.37, ...), custom_call_target="tpu_custom_call" | custom-call | flops 805306368 | bytes 8388608 | tf_op jit(solution)/shard_map/outer/pallas_call | solution.py:557
  (52 shorter events, 5.9 us)
Async XLA Ops:
  0.6 6.8 %copy-start = (bf16[1,1024,576]{1,2,0:T(8,128)(2,1)S(1)}, bf16[1,1024,576]{1,2,0:T(8,128)(2,1)}, u32[]{:S(2)}) copy-start(bf16[1,1024,576]{1,2,0:T(8,128)(2,1)} %param.12) | copy-start | bytes 3538948
  0.6 12.3 %copy-start.3 = (bf16[1,64,7168]{2,1,0:T(8,128)(2,1)S(1)}, bf16[1,64,7168]{2,1,0:T(8,128)(2,1)}, u32[]{:S(2)}) copy-start(bf16[1,64,7168]{2,1,0:T(8,128)(2,1)} %param.10) | copy-start | bytes 2752516
  0.7 12.3 %copy-start.4 = (bf16[1,64,1536]{2,1,0:T(8,128)(2,1)S(1)}, bf16[1,64,1536]{2,1,0:T(8,128)(2,1)}, u32[]{:S(2)}) copy-start(bf16[1,64,1536]{2,1,0:T(8,128)(2,1)} %param.9) | copy-start | bytes 589828
  2.4 14.7 %collective-permute-start.1 = (bf16[512,128]{1,0:T(8,128)(2,1)}, bf16[512,128]{1,0:T(8,128)(2,1)}, u32[]{:S(2)}, u32[]{:S(2)}) collective-permute-start(bf16[512,128]{1,0:T(8,128)(2,1)} %dynamic-slice_bitcast_fusion.1), channel_id=1, source_target_pairs={{0,3},{1,0},{2,1},{3,2},{4,7},{5,4},{6,5},{7,6},{8,11},{9,8},{10,9... | collective-permute-start | bytes 393224 | tf_op jit(solution)/shard_map/ppermute | solution.py:597
  7.4 9.6 %collective-permute-start = (bf16[512,128]{1,0:T(8,128)(2,1)}, bf16[512,128]{1,0:T(8,128)(2,1)}, u32[]{:S(2)}, u32[]{:S(2)}) collective-permute-start(bf16[512,128]{1,0:T(8,128)(2,1)} %dynamic-slice_bitcast_fusion.1), channel_id=1, source_target_pairs={{0,1},{1,2},{2,3},{3,0},{4,5},{5,6},{6,7},{7,4},{8,9},{9,10},{10,1... | collective-permute-start | bytes 393224 | tf_op jit(solution)/shard_map/ppermute | solution.py:597
  7.5 19.5 %collective-permute-start.4 = (bf16[576,512]{1,0:T(8,128)(2,1)S(1)}, bf16[576,512]{1,0:T(8,128)(2,1)S(1)}, u32[]{:S(2)}, u32[]{:S(2)}) collective-permute-start(bf16[576,512]{1,0:T(8,128)(2,1)S(1)} %dynamic-slice_bitcast_fusion.refs_0_), channel_id=1, source_target_pairs={{0,1},{3,2},{4,5},{7,6},{8,9},{11,10},{12,13},{15,14},{16,17},{19,... | collective-permute-start | bytes 1769480 | tf_op jit(solution)/shard_map/ppermute | solution.py:606
  9.4 17.6 %collective-permute-start.3 = (bf16[576,512]{1,0:T(8,128)(2,1)S(1)}, bf16[576,512]{1,0:T(8,128)(2,1)}, u32[]{:S(2)}, u32[]{:S(2)}) collective-permute-start(bf16[576,512]{1,0:T(8,128)(2,1)S(1)} %dynamic-slice_bitcast_fusion.refs_0_), channel_id=1, source_target_pairs={{1,2},{2,1},{5,6},{6,5},{9,10},{10,9},{13,14},{14,13},{17,18},{18,... | collective-permute-start | bytes 1769480 | tf_op jit(solution)/shard_map/ppermute | solution.py:603
  10.9 16.9 %collective-permute-start.2 = (bf16[576,512]{1,0:T(8,128)(2,1)S(1)}, bf16[576,512]{1,0:T(8,128)(2,1)}, u32[]{:S(2)}, u32[]{:S(2)}) collective-permute-start(bf16[576,512]{1,0:T(8,128)(2,1)S(1)} %dynamic-slice_bitcast_fusion.refs_0_), channel_id=1, source_target_pairs={{1,0},{2,3},{5,4},{6,7},{9,8},{10,11},{13,12},{14,15},{17,16},{18,... | collective-permute-start | bytes 1769480 | tf_op jit(solution)/shard_map/ppermute | solution.py:600
  13.0 1.9 %copy-start.2 = (bf16[384,4096]{1,0:T(8,128)(2,1)S(1)}, bf16[384,4096]{1,0:T(8,128)(2,1)}, u32[]{:S(2)}) copy-start(bf16[384,4096]{1,0:T(8,128)(2,1)} %weight.1) | copy-start | bytes 9437188
  14.8 0.9 copy-start.5
  15.7 1.4 %copy-start.1 = (bf16[1,16,64,576]{3,2,1,0:T(8,128)(2,1)S(1)}, bf16[1,16,64,576]{3,2,1,0:T(8,128)(2,1)}, u32[]{:S(2)}) copy-start(bf16[1,16,64,576]{3,2,1,0:T(8,128)(2,1)} %param.11) | copy-start | bytes 3538948
  17.1 34.2 %collective-permute-start.8 = (bf16[16,64,576]{2,1,0:T(8,128)(2,1)S(1)}, bf16[16,64,576]{2,1,0:T(8,128)(2,1)S(1)}, u32[]{:S(2)}, u32[]{:S(2)}) collective-permute-start(bf16[16,64,576]{2,1,0:T(8,128)(2,1)S(1)} %bitcast.25), channel_id=1, source_target_pairs={{0,4},{4,0},{1,5},{5,1},{2,6},{6,2},{3,7},{7,3},{8,12},{12,8},{9,1... | collective-permute-start | bytes 3538952 | tf_op jit(solution)/shard_map/ppermute | solution.py:614
  18.7 13.0 %collective-permute-start.5 = (f32[16,4224]{1,0:T(8,128)S(1)}, f32[16,4224]{1,0:T(8,128)S(1)}, u32[]{:S(2)}, u32[]{:S(2)}) collective-permute-start(f32[16,4224]{1,0:T(8,128)S(1)} %slice_bitcast_fusion.1), channel_id=1, source_target_pairs={{0,1},{3,2},{4,5},{7,6},{8,9},{11,10},{12,13},{15,14},{16,17},{19,... | collective-permute-start | bytes 811016 | tf_op jit(solution)/shard_map/ppermute | solution.py:606
  31.7 19.5 %collective-permute-start.7 = (f32[16,4224]{1,0:T(8,128)S(1)}, f32[16,4224]{1,0:T(8,128)S(1)}, u32[]{:S(2)}, u32[]{:S(2)}) collective-permute-start(f32[16,4224]{1,0:T(8,128)S(1)} %add.30), channel_id=1, source_target_pairs={{1,2},{2,1},{5,6},{6,5},{9,10},{10,9},{13,14},{14,13},{17,18},{18,... | collective-permute-start | bytes 811016 | tf_op jit(solution)/shard_map/ppermute | solution.py:603
  32.4 17.5 %collective-permute-start.6 = (bf16[512,128]{1,0:T(8,128)(2,1)}, bf16[512,128]{1,0:T(8,128)(2,1)S(1)}, u32[]{:S(2)}, u32[]{:S(2)}) collective-permute-start(bf16[512,128]{1,0:T(8,128)(2,1)} %dynamic-slice_bitcast_fusion.1), channel_id=1, source_target_pairs={{0,2},{1,3},{2,0},{3,1},{4,6},{5,7},{6,4},{7,5},{8,10},{9,11},{10,... | collective-permute-start | bytes 393224 | tf_op jit(solution)/shard_map/ppermute | solution.py:597
  37.7 18.6 %collective-permute-start.9 = (bf16[576,512]{1,0:T(8,128)(2,1)}, bf16[576,512]{1,0:T(8,128)(2,1)S(1)}, u32[]{:S(2)}, u32[]{:S(2)}) collective-permute-start(bf16[576,512]{1,0:T(8,128)(2,1)} %collective-permute-done.3.refs_1_), channel_id=1, source_target_pairs={{1,0},{2,3},{5,4},{6,7},{9,8},{10,11},{13,12},{14,15},{17,16},{18,... | collective-permute-start | bytes 1769480 | tf_op jit(solution)/shard_map/ppermute | solution.py:600
  39.0 19.7 %collective-permute-start.10 = (bf16[576,512]{1,0:T(8,128)(2,1)S(1)}, bf16[576,512]{1,0:T(8,128)(2,1)S(1)}, u32[]{:S(2)}, u32[]{:S(2)}) collective-permute-start(bf16[576,512]{1,0:T(8,128)(2,1)S(1)} %collective-permute-done.4.refs_1_), channel_id=1, source_target_pairs={{1,2},{2,1},{5,6},{6,5},{9,10},{10,9},{13,14},{14,13},{17,18},{18,... | collective-permute-start | bytes 1769480 | tf_op jit(solution)/shard_map/ppermute | solution.py:603
  49.9 10.6 %collective-permute-start.12 = (f32[2,16,4224]{2,1,0:T(8,128)S(1)}, f32[2,16,4224]{2,1,0:T(8,128)S(1)}, u32[]{:S(2)}, u32[]{:S(2)}) collective-permute-start(f32[2,16,4224]{2,1,0:T(8,128)S(1)} %slice.19), channel_id=1, source_target_pairs={{0,1},{3,2},{4,5},{7,6},{8,9},{11,10},{12,13},{15,14},{16,17},{19,... | collective-permute-start | bytes 1622024 | tf_op jit(solution)/shard_map/ppermute | solution.py:606
  51.3 17.0 %copy-start.6 = (s32[1,64]{1,0:T(1,128)S(1)}, s32[1,64]{1,0:T(1,128)}, u32[]{:S(2)}) copy-start(s32[1,64]{1,0:T(1,128)} %param.14) | copy-start | bytes 772
  51.3 13.4 %collective-permute-start.14 = (bf16[64,2176]{1,0:T(8,128)(2,1)S(1)}, bf16[64,2176]{1,0:T(8,128)(2,1)S(1)}, u32[]{:S(2)}, u32[]{:S(2)}) collective-permute-start(bf16[64,2176]{1,0:T(8,128)(2,1)S(1)} %get-tuple-element.93.refs_0_), channel_id=1, source_target_pairs={{0,8},{8,0},{16,24},{24,16},{1,9},{9,1},{17,25},{25,17},{2,10},{10... | collective-permute-start | bytes 835592 | tf_op jit(solution)/shard_map/ppermute | solution.py:617
  51.4 13.3 %collective-permute-start.13 = (bf16[64,2176]{1,0:T(8,128)(2,1)S(1)}, bf16[64,2176]{1,0:T(8,128)(2,1)S(1)}, u32[]{:S(2)}, u32[]{:S(2)}) collective-permute-start(bf16[64,2176]{1,0:T(8,128)(2,1)S(1)} %get-tuple-element.93.refs_0_), channel_id=1, source_target_pairs={{0,16},{8,24},{16,0},{24,8},{1,17},{9,25},{17,1},{25,9},{2,18},{10... | collective-permute-start | bytes 835592 | tf_op jit(solution)/shard_map/ppermute | solution.py:617
  56.3 8.3 %collective-permute-start.11 = (f32[16,4224]{1,0:T(8,128)S(1)}, f32[16,4224]{1,0:T(8,128)S(1)}, u32[]{:S(2)}, u32[]{:S(2)}) collective-permute-start(f32[16,4224]{1,0:T(8,128)S(1)} %bitcast_add_fusion), channel_id=1, source_target_pairs={{1,0},{2,3},{5,4},{6,7},{9,8},{10,11},{13,12},{14,15},{17,16},{18,... | collective-permute-start | bytes 811016 | tf_op jit(solution)/shard_map/ppermute | solution.py:600
  64.6 9.7 %collective-permute-start.15 = (bf16[64,2176]{1,0:T(8,128)(2,1)S(1)}, bf16[64,2176]{1,0:T(8,128)(2,1)S(1)}, u32[]{:S(2)}, u32[]{:S(2)}) collective-permute-start(bf16[64,2176]{1,0:T(8,128)(2,1)S(1)} %collective-permute-done.13.refs_1_), channel_id=1, source_target_pairs={{0,8},{8,0},{16,24},{24,16},{1,9},{9,1},{17,25},{25,17},{2,10},{10... | collective-permute-start | bytes 835592 | tf_op jit(solution)/shard_map/ppermute | solution.py:617
  64.7 13.0 %collective-permute-start.16 = (f32[16,4224]{1,0:T(8,128)S(1)}, f32[16,4224]{1,0:T(8,128)S(1)}, u32[]{:S(2)}, u32[]{:S(2)}) collective-permute-start(f32[16,4224]{1,0:T(8,128)S(1)} %add_bitcast_fusion), channel_id=1, source_target_pairs={{1,2},{2,1},{5,6},{6,5},{9,10},{10,9},{13,14},{14,13},{17,18},{18,... | collective-permute-start | bytes 811016 | tf_op jit(solution)/shard_map/ppermute | solution.py:603
  65.4 14.4 %collective-permute-start.17 = (bf16[2048,128]{1,0:T(8,128)(2,1)S(1)}, bf16[2048,128]{1,0:T(8,128)(2,1)S(1)}, u32[]{:S(2)}, u32[]{:S(2)}) collective-permute-start(bf16[2048,128]{1,0:T(8,128)(2,1)S(1)} %pad_maximum_fusion.refs_4_), channel_id=1, source_target_pairs={{0,4},{4,0},{1,5},{5,1},{2,6},{6,2},{3,7},{7,3},{8,12},{12,8},{9,1... | collective-permute-start | bytes 1572872 | tf_op jit(solution)/shard_map/ppermute | solution.py:614
  67.0 22.9 %collective-permute-start.19 = (bf16[576,512]{1,0:T(8,128)(2,1)S(1)}, bf16[576,512]{1,0:T(8,128)(2,1)S(1)}, u32[]{:S(2)}, u32[]{:S(2)}) collective-permute-start(bf16[576,512]{1,0:T(8,128)(2,1)S(1)} %collective-permute-done.10.refs_1_), channel_id=1, source_target_pairs={{1,0},{2,3},{5,4},{6,7},{9,8},{10,11},{13,12},{14,15},{17,16},{18,... | collective-permute-start | bytes 1769480 | tf_op jit(solution)/shard_map/ppermute | solution.py:600
  81.1 8.0 %collective-permute-start.18 = (f32[2,16,2048]{2,1,0:T(8,128)S(1)}, f32[2,16,2048]{2,1,0:T(8,128)S(1)}, u32[]{:S(2)}, u32[]{:S(2)}) collective-permute-start(f32[2,16,2048]{2,1,0:T(8,128)S(1)} %logits.1.part), channel_id=1, source_target_pairs={{0,4},{4,0},{1,5},{5,1},{2,6},{6,2},{3,7},{7,3},{8,12},{12,8},{9,1... | collective-permute-start | bytes 786440 | tf_op jit(solution)/shard_map/ppermute | solution.py:614
  92.8 3.8 %collective-permute-start.20 = (f32[2,16,128]{2,1,0:T(8,128)S(1)}, f32[2,16,128]{2,1,0:T(8,128)S(1)}, u32[]{:S(2)}, u32[]{:S(2)}) collective-permute-start(f32[2,16,128]{2,1,0:T(8,128)S(1)} %pad_maximum_fusion.2), channel_id=1, source_target_pairs={{0,4},{4,0},{1,5},{5,1},{2,6},{6,2},{3,7},{7,3},{8,12},{12,8},{9,1... | collective-permute-start | bytes 49160 | tf_op jit(solution)/shard_map/ppermute | solution.py:614
  99.3 4.3 %collective-permute-start.21 = (bf16[16,2048]{1,0:T(8,128)(2,1)S(1)}, bf16[16,2048]{1,0:T(8,128)(2,1)S(1)}, u32[]{:S(2)}, u32[]{:S(2)}) collective-permute-start(bf16[16,2048]{1,0:T(8,128)(2,1)S(1)} %get-tuple-element.142.refs_9_), channel_id=1, source_target_pairs={{0,4},{4,0},{1,5},{5,1},{2,6},{6,2},{3,7},{7,3},{8,12},{12,8},{9,1... | collective-permute-start | bytes 196616 | tf_op jit(solution)/shard_map/ppermute | solution.py:614
  106.1 5.2 %collective-permute-start.25 = (bf16[1,16,4224]{2,1,0:T(8,128)(2,1)S(1)}, bf16[1,16,4224]{2,1,0:T(8,128)(2,1)S(1)}, u32[]{:S(2)}, u32[]{:S(2)}) collective-permute-start(bf16[1,16,4224]{2,1,0:T(8,128)(2,1)S(1)} %bitcast.32), channel_id=1, source_target_pairs={{0,16},{8,24},{16,0},{24,8},{1,17},{9,25},{17,1},{25,9},{2,18},{10... | collective-permute-start | bytes 405512 | tf_op jit(solution)/shard_map/ppermute | solution.py:617
  107.6 6.5 %collective-permute-start.24 = (bf16[1,16,4224]{2,1,0:T(8,128)(2,1)S(1)}, bf16[1,16,4224]{2,1,0:T(8,128)(2,1)S(1)}, u32[]{:S(2)}, u32[]{:S(2)}) collective-permute-start(bf16[1,16,4224]{2,1,0:T(8,128)(2,1)S(1)} %bitcast.33), channel_id=1, source_target_pairs={{0,3},{1,0},{2,1},{3,2},{4,7},{5,4},{6,5},{7,6},{8,11},{9,8},{10,9... | collective-permute-start | bytes 405512 | tf_op jit(solution)/shard_map/ppermute | solution.py:724
  108.8 9.7 %collective-permute-start.23 = (bf16[1,16,4224]{2,1,0:T(8,128)(2,1)S(1)}, bf16[1,16,4224]{2,1,0:T(8,128)(2,1)S(1)}, u32[]{:S(2)}, u32[]{:S(2)}) collective-permute-start(bf16[1,16,4224]{2,1,0:T(8,128)(2,1)S(1)} %bitcast.34), channel_id=1, source_target_pairs={{0,2},{1,3},{2,0},{3,1},{4,6},{5,7},{6,4},{7,5},{8,10},{9,11},{10,... | collective-permute-start | bytes 405512 | tf_op jit(solution)/shard_map/ppermute | solution.py:724
  110.0 8.5 %collective-permute-start.22 = (bf16[1,16,4224]{2,1,0:T(8,128)(2,1)S(1)}, bf16[1,16,4224]{2,1,0:T(8,128)(2,1)S(1)}, u32[]{:S(2)}, u32[]{:S(2)}) collective-permute-start(bf16[1,16,4224]{2,1,0:T(8,128)(2,1)S(1)} %bitcast.35), channel_id=1, source_target_pairs={{0,1},{1,2},{2,3},{3,0},{4,5},{5,6},{6,7},{7,4},{8,9},{9,10},{10,1... | collective-permute-start | bytes 405512 | tf_op jit(solution)/shard_map/ppermute | solution.py:724
  111.3 7.3 %collective-permute-start.26 = (bf16[1,16,4224]{2,1,0:T(8,128)(2,1)S(1)}, bf16[1,16,4224]{2,1,0:T(8,128)(2,1)S(1)}, u32[]{:S(2)}, u32[]{:S(2)}) collective-permute-start(bf16[1,16,4224]{2,1,0:T(8,128)(2,1)S(1)} %bitcast.36), channel_id=1, source_target_pairs={{0,8},{8,0},{16,24},{24,16},{1,9},{9,1},{17,25},{25,17},{2,10},{10... | collective-permute-start | bytes 405512 | tf_op jit(solution)/shard_map/ppermute | solution.py:617
  111.3 7.3 %collective-permute-start.27 = (bf16[1,16,4224]{2,1,0:T(8,128)(2,1)S(1)}, bf16[1,16,4224]{2,1,0:T(8,128)(2,1)S(1)}, u32[]{:S(2)}, u32[]{:S(2)}) collective-permute-start(bf16[1,16,4224]{2,1,0:T(8,128)(2,1)S(1)} %collective-permute-done.25.refs_1_), channel_id=1, source_target_pairs={{0,8},{8,0},{16,24},{24,16},{1,9},{9,1},{17,25},{25,17},{2,10},{10... | collective-permute-start | bytes 405512 | tf_op jit(solution)/shard_map/ppermute | solution.py:617
  118.6 8.0 %collective-permute-start.28 = (bf16[3,16,4224]{2,1,0:T(8,128)(2,1)S(1)}, bf16[3,16,4224]{2,1,0:T(8,128)(2,1)S(1)}, u32[]{:S(2)}, u32[]{:S(2)}) collective-permute-start(bf16[3,16,4224]{2,1,0:T(8,128)(2,1)S(1)} %pad_maximum_fusion.1.refs_4_), channel_id=1, source_target_pairs={{0,16},{8,24},{16,0},{24,8},{1,17},{9,25},{17,1},{25,9},{2,18},{10... | collective-permute-start | bytes 1216520 | tf_op jit(solution)/shard_map/ppermute | solution.py:617
  119.2 7.4 %collective-permute-start.29 = (bf16[3,16,4224]{2,1,0:T(8,128)(2,1)S(1)}, bf16[3,16,4224]{2,1,0:T(8,128)(2,1)S(1)}, u32[]{:S(2)}, u32[]{:S(2)}) collective-permute-start(bf16[3,16,4224]{2,1,0:T(8,128)(2,1)S(1)} %pad_maximum_fusion.1.refs_4_), channel_id=1, source_target_pairs={{0,8},{8,0},{16,24},{24,16},{1,9},{9,1},{17,25},{25,17},{2,10},{10... | collective-permute-start | bytes 1216520 | tf_op jit(solution)/shard_map/ppermute | solution.py:617
  126.6 1.7 %collective-permute-start.30 = (bf16[3,16,4224]{2,1,0:T(8,128)(2,1)S(1)}, bf16[3,16,4224]{2,1,0:T(8,128)(2,1)S(1)}, u32[]{:S(2)}, u32[]{:S(2)}) collective-permute-start(bf16[3,16,4224]{2,1,0:T(8,128)(2,1)S(1)} %collective-permute-done.28.refs_5_), channel_id=1, source_target_pairs={{0,8},{8,0},{16,24},{24,16},{1,9},{9,1},{17,25},{25,17},{2,10},{10... | collective-permute-start | bytes 1216520 | tf_op jit(solution)/shard_map/ppermute | solution.py:617

commit v10 on v9

--- a/solution.py
+++ b/solution.py
@@ -50,11 +50,23 @@
     return n == 4
 
 
+left_1, right_1, left_2, right_2, last = range(5)
+line_sources = ((0, 1, 2, 3), (1, 2, 3, 0), (2, 1, 0, 3), (3, 2, 1, 0))
+line_options = ((left_1, right_1), (left_2, right_2), (last, right_1, left_1))
+line_brought = ((left_1, left_2, last), (left_1, left_2, right_1), (right_1, right_2, left_1), (right_1, right_2, last))
+
+
 def key_source(n, z, u):
     if on_line(n):
-        return ([0, 1, 2, 3], [1, 2, 0, 3], [2, 1, 3, 0], [3, 2, 1, 0])[z][u]
+        return line_sources[z][u]
     ring = folded_ring(n)
     return ring[(ring.index(z) - u) % n]
+
+
+def key_option(n, z, u):
+    if u == 0 or not on_line(n):
+        return 0
+    return line_options[u - 1].index(line_brought[z][u - 1])
 
 
 def device_table(n, heads, dp_size):
@@ -68,6 +80,7 @@
                 row += [dp ^ k for k in dp_flips(dp_size)]
                 row += [(z - t) % n for t in range(n)]
                 row += [k if z < n // 2 or not on_line(n) else n - 1 - k for k in range(n)]
+                row += [key_option(n, z, u) for u in range(n)]
                 table.append(row)
     return np.array(table, np.int32)
 
@@ -90,6 +103,10 @@
 
 def at_part(n, dp_size, k):
     return 4 + 3 * n + dp_size + k
+
+
+def at_option(n, dp_size, u):
+    return 4 + 4 * n + dp_size + u
 
 
 def dp_flips(dp_size):
@@ -164,7 +181,7 @@
     )(info, latent, weight, hidden, hidden_weight)
 
 
-def score_kernel(t, n, rows_here, info, positions, mine, other, *refs):
+def score_kernel(t, n, rows_here, option_at, info, positions, mine, other, *refs):
     options, refs = refs[:-10], refs[-10:]
     top_before, mass_before, weights, top, top_all, mass_all, mass, even, odd, chosen = refs
     count, heads, depth = mine.shape
@@ -173,7 +190,7 @@
         keys = chosen
         for k, option in enumerate(options):
 
-            @pl.when(info[at_end] == 1 - k)
+            @pl.when(info[option_at] == k)
             def _():
                 chosen[...] = option[...]
 
@@ -228,14 +245,14 @@
         ] * jnp.exp2((now - joint) * exponent_scale)
 
 
-def score(t, n, rows_here, info, positions, mine, other, options, before):
+def score(t, n, rows_here, option_at, info, positions, mine, other, options, before):
     count, heads, depth = mine.shape
     span = options[0].shape[1]
     stats = jax.ShapeDtypeStruct((count, lanes), f32)
     if before is None:
         before = (jnp.zeros((count, lanes), f32),) * 2
     return pl.pallas_call(
-        functools.partial(score_kernel, t, n, rows_here),
+        functools.partial(score_kernel, t, n, rows_here, option_at),
         out_shape=(jax.ShapeDtypeStruct((count, 2 * heads, span), bf16), stats, stats, stats),
         in_specs=[in_smem()] * 2 + [in_vmem()] * (4 + len(options)),
         out_specs=(in_vmem(),) * 4,
@@ -637,51 +654,50 @@
         nonlocal before
         t = len(weights)
         numer, top, *before = score(
-            t, n, rows, info, token, queries, other_queries, options, before
+            t, n, rows, at_option(n, dp_size, t), info, token, queries, other_queries, options, before
         )
         weights.append(numer)
         tops.append(top)
 
     if line:
         index_1, index_3 = shifted(index_part, 1), shifted(index_part, 3)
-        keys_out, keys_over, keys_in = outward(own_keys), centre(own_keys), inward(own_keys)
+        keys = {left_1: lax.ppermute(own_keys, "ctx", [(1, 0), (2, 1), (3, 2)])}
+        keys[right_1] = lax.ppermute(own_keys, "ctx", [(0, 1), (1, 2), (2, 3)])
+        other_queries = swap_head(queries)
         partial, own_part, kept = project(
             info, order_at, queries_here, q_latent[0], w_query, hidden[0], w_weights.T
         )
-        (index_1, index_3), sent_queries = after((index_1, index_3), queries)
-        other_queries = swap_head(sent_queries)
-        _, far_part = after((), partial[3])
-        far_in = inward(far_part)
-        (keys_out, keys_over, keys_in), index_again = after(
-            (keys_out, keys_over, keys_in), index_part
+        (index_1, index_3), far_part, index_again = after(
+            (index_1, index_3), partial[3], index_part
         )
-        keys_out2, keys_over2 = outward(keys_over), centre(keys_in)
-        index_2 = shifted(index_again, 2)
-        (far_in,) = after(far_in)
+        far_in, index_2 = inward(far_part), shifted(index_again, 2)
+        (keys,) = after(keys)
+        keys[left_2] = lax.ppermute(keys[left_1], "ctx", [(1, 0), (2, 1)])
+        keys[right_2] = lax.ppermute(keys[right_1], "ctx", [(1, 2), (2, 3)])
+        (far_in, index_2, other_queries), near_parts = after(
+            (far_in, index_2, other_queries), partial[1:3]
+        )
         far_over = centre(far_part + far_in)
-        index_2, near_parts = after(index_2, partial[1:3])
         near_in = inward(near_parts)
-        (far_over, other_queries), kept = after((far_over, other_queries), kept)
+        index_own = jnp.concatenate([index_part, index_1, index_2, index_3])
+        index_other = swap_head(index_own)
+        (keys,) = after(keys)
+        keys[last] = outward(jnp.where(z < n // 2, keys[left_2], keys[right_2]))
+        (far_over, near_in), kept = after((far_over, near_in), kept)
         sum_out = outward(partial[0] + far_over)
-        half_dp, near_dp = swap_dp(kept, dp_size // 2), swap_dp(kept, dp_size // 4)
-        index_own = jnp.concatenate([index_part, index_1, index_2, index_3])
-        (keys_out2, keys_over2, sum_out, near_in, half_dp, near_dp), index_own = after(
-            (keys_out2, keys_over2, sum_out, near_in, half_dp, near_dp), index_own
-        )
-        keys_out3 = outward(keys_over2)
         sum_over = centre(partial[2] + near_in[1])
-        index_other = swap_head(index_own)
-        kept = [kept, half_dp, near_dp, swap_dp(half_dp, dp_size // 4)]
+        half_dp = swap_dp(kept, dp_size // 2)
+        near_dp = swap_dp(jnp.stack([kept, half_dp]), dp_size // 4)
+        kept = [kept, half_dp, near_dp[0], near_dp[1]]
         score_next(own_keys)
-        score_next(keys_out, keys_over)
-        latents, hiddens = arrange(n, info, rows_latent, kept)
-        before, latents, hiddens = lax.optimization_barrier((before, latents, hiddens))
-        score_next(keys_out2, keys_in)
-        before, sum_out, sum_over, near_in = lax.optimization_barrier(
-            (before, sum_out, sum_over, near_in)
+        for t in range(1, n - 1):
+            score_next(*[keys[k] for k in line_options[t - 1]])
+        before, sum_out, sum_over, near_in, kept = lax.optimization_barrier(
+            (before, sum_out, sum_over, near_in, kept)
         )
         terms = [own_part, sum_out, sum_over, near_in[0]]
-        last_keys = (keys_out3, keys_over2)
+        last_keys = [keys[k] for k in line_options[n - 2]]
+        latents, hiddens = arrange(n, info, rows_latent, kept)
     else:
         ring = folded_ring(n)
         partial, _, kept = project(
@@ -696,13 +712,13 @@
         for _ in range(n - 1):
             score_next(keys)
             keys = lax.ppermute(keys, "ctx", [(ring[k], ring[(k + 1) % n]) for k in range(n)])
-        last_keys = (keys,)
+        last_keys = [keys]
 
     part = make_logits(heads_here, terms, index_own, index_other)
+    far, last_keys = lax.optimization_barrier((swap_head(part), last_keys))
     probs, log_probs = make_softmax(
-        n, rows, at_shift(n, dp_size, 0), info, token, part, swap_head(part)
+        n, rows, at_shift(n, dp_size, 0), info, token, part, far
     )
-    before, probs, log_probs = lax.optimization_barrier((before, probs, log_probs))
     score_next(*last_keys)
     delta_own, sent = make_delta(info, weights, tops, *before, swap_head(jnp.stack(before)), probs)
     piece = gradients(

time: 133 us -> 147 us (1.11)
  starting transfers between devices: 43.5 us -> 48.7 us
  local copies, waits for them, and re-layouts: 5.35 us -> 9.87 us
  other arithmetic: 1.25 us -> 4.41 us
  Pallas kernels: 25.3 us -> 28.3 us
  waiting for transfers between devices: 56.4 us -> 53.4 us
    ppermute x0 -> x4, waiting for transfers between devices: none -> 7.92 us  [the longest x1 6.76 us: per_device(): keys[right_1] = lax.ppermute(own_keys, 'ctx', [(0, 1), (1, 2), (2, 3)])]
    ppermute x4 -> x2, waiting for transfers between devices: 8.31 us -> 0.82 us  [outward(): return lax.ppermute(x, 'ctx', [(1, 0), (2, 3)])]
    ppermute x3 -> x2, waiting for transfers between devices: 8.6 us -> 1.34 us  [inward(): return lax.ppermute(x, 'ctx', [(0, 1), (3, 2)])]
    ppermute x0 -> x4, starting transfers between devices: none -> 5.99 us  [the longest x1 1.93 us: per_device(): keys[right_1] = lax.ppermute(own_keys, 'ctx', [(0, 1), (1, 2), (2, 3)])]
    ppermute x3 -> x2, starting transfers between devices: 8.61 us -> 14.5 us  [inward(): return lax.ppermute(x, 'ctx', [(0, 1), (3, 2)])]
    ppermute x9 -> x8, waiting for transfers between devices: 9.12 us -> 14.7 us  [swap_dp(): return lax.ppermute(x, 'dp', [(k, k ^ bit) for k in range(dp_size)])]
    ppermute x3, starting transfers between devices: 10.3 us -> 5.12 us  [shifted(): return lax.ppermute(x, 'ctx', [(k, (k + t) % n) for k in range(n)])]
    ppermute x3, starting transfers between devices: 3.67 us -> 6.91 us  [per_device(): brought.append(lax.ppermute(piece, 'ctx', pairs))]
  transfers between devices with their start and end apart: 31 -> 29, of which waited for: 15 -> 13; matrix products, arithmetic and copies ran while one was open for 2% -> 5% of each run, Pallas kernels for 10% -> 10%
where the time goes in v10:
time: 147 us; the launch traced here: 146 us
  waiting for transfers between devices  53.4 us (36%)
  starting transfers between devices  48.7 us (33%)
  Pallas kernels  28.3 us (19%)
  local copies, waits for them, and re-layouts  9.87 us (7%)
  other arithmetic  4.41 us (3%)
    ppermute x8, waiting for transfers between devices, swap_dp(): return lax.ppermute(x, 'dp', [(k, k ^ bit) for k in range(dp_size)])  14.7 us
    pallas_call x4, Pallas kernels, score(): pl.pallas_call(functools.partial(score_kernel, t, n, rows_here, option_at...  14.6 us
    ppermute x2, starting transfers between devices, inward(): return lax.ppermute(x, 'ctx', [(0, 1), (3, 2)])  14.5 us
    ppermute x5, waiting for transfers between devices, swap_head(): return lax.ppermute(x, 'head', [(0, 1), (1, 0)])  10.6 us
    ppermute x3, waiting for transfers between devices, shifted(): return lax.ppermute(x, 'ctx', [(k, (k + t) % n) for k in range(n)])  10.4 us
    ppermute x5, starting transfers between devices, swap_head(): return lax.ppermute(x, 'head', [(0, 1), (1, 0)])  7.92 us
    ppermute x3, waiting for transfers between devices, per_device(): brought.append(lax.ppermute(piece, 'ctx', pairs))  7.67 us
    ppermute x3, starting transfers between devices, per_device(): brought.append(lax.ppermute(piece, 'ctx', pairs))  6.91 us
  transfers between devices with their start and end apart: 29, of which 13 were waited for; matrix products, arithmetic and copies ran while one was open for 5% of the time, Pallas kernels for 10%

profile of v10, /device:TPU:0, one launch (start us, length us, event | category | flops | bytes accessed | tf_op | source)
XLA Modules:
  0.0 145.9 jit_solution(17684353871013306131)
XLA Ops:
  0.7 1.7 %dynamic-slice_bitcast_fusion.1 = bf16[512,128]{1,0:T(8,128)(2,1)} fusion(bf16[1,1024,128]{2,1,0:T(8,128)(2,1)} %param.13, s32[]{:T(128)S(6)} %select_n.17), kind=kLoop, calls=%fused_computation.11 | loop fusion | bytes 262148 | tf_op jit(solution)/shard_map/dynamic_slice | solution.py:648
  2.4 5.0 %collective-permute-start.1 = (bf16[512,128]{1,0:T(8,128)(2,1)}, bf16[512,128]{1,0:T(8,128)(2,1)}, u32[]{:S(2)}, u32[]{:S(2)}) collective-permute-start(bf16[512,128]{1,0:T(8,128)(2,1)} %dynamic-slice_bitcast_fusion.1), channel_id=1, source_target_pairs={{0,3},{1,0},{2,1},{3,2},{4,7},{5,4},{6,5},{7,6},{8,11},{9,8},{10,9... | collective-permute-start | bytes 393224 | tf_op jit(solution)/shard_map/ppermute | solution.py:614
  8.3 1.9 %collective-permute-start.3 = (bf16[576,512]{1,0:T(8,128)(2,1)}, bf16[576,512]{1,0:T(8,128)(2,1)S(1)}, u32[]{:S(2)}, u32[]{:S(2)}) collective-permute-start(bf16[576,512]{1,0:T(8,128)(2,1)} %dynamic-slice_bitcast_fusion.refs_0_), channel_id=1, source_target_pairs={{0,1},{1,2},{2,3},{4,5},{5,6},{6,7},{8,9},{9,10},{10,11},{12,13},{... | collective-permute-start | bytes 1769480 | tf_op jit(solution)/shard_map/ppermute | solution.py:665
  10.3 1.3 collective-permute-start.2
  11.6 1.6 %collective-permute-start.6 = (bf16[16,64,576]{2,1,0:T(8,128)(2,1)S(1)}, bf16[16,64,576]{2,1,0:T(8,128)(2,1)}, u32[]{:S(2)}, u32[]{:S(2)}) collective-permute-start(bf16[16,64,576]{2,1,0:T(8,128)(2,1)S(1)} %bitcast.31), channel_id=1, source_target_pairs={{0,4},{4,0},{1,5},{5,1},{2,6},{6,2},{3,7},{7,3},{8,12},{12,8},{9,1... | collective-permute-start | bytes 3538952 | tf_op jit(solution)/shard_map/ppermute | solution.py:631
  13.8 1.9 %copy-done.2 = bf16[384,4096]{1,0:T(8,128)(2,1)S(1)} copy-done((bf16[384,4096]{1,0:T(8,128)(2,1)S(1)}, bf16[384,4096]{1,0:T(8,128)(2,1)}, u32[]{:S(2)}) %copy-start.2) | copy-done | bytes 3145752
  15.7 1.2 copy-done.5
  16.9 0.9 copy-done.8
  17.8 1.3 project.1
  19.3 6.8 %collective-permute-done.3.refs_1_ = bf16[576,512]{1,0:T(8,128)(2,1)S(1)} collective-permute-done((bf16[576,512]{1,0:T(8,128)(2,1)}, bf16[576,512]{1,0:T(8,128)(2,1)S(1)}, u32[]{:S(2)}, u32[]{:S(2)}) %collective-permute-start.3) | collective-permute-done | bytes 589856 | tf_op jit(solution)/shard_map/ppermute | solution.py:665
  26.0 1.2 collective-permute-done.2.refs_0_.refs_2_
  27.2 1.3 collective-permute-start.7
  28.5 1.5 %collective-permute-start.8 = (bf16[576,512]{1,0:T(8,128)(2,1)S(1)}, bf16[576,512]{1,0:T(8,128)(2,1)}, u32[]{:S(2)}, u32[]{:S(2)}) collective-permute-start(bf16[576,512]{1,0:T(8,128)(2,1)S(1)} %collective-permute-done.3.refs_1_), channel_id=1, source_target_pairs={{1,2},{2,3},{5,6},{6,7},{9,10},{10,11},{13,14},{14,15},{17,18},{18... | collective-permute-start | bytes 1769480 | tf_op jit(solution)/shard_map/ppermute | solution.py:676
  29.9 9.3 %collective-permute-start.4 = (f32[16,4224]{1,0:T(8,128)S(1)}, f32[16,4224]{1,0:T(8,128)S(1)}, u32[]{:S(2)}, u32[]{:S(2)}) collective-permute-start(f32[16,4224]{1,0:T(8,128)S(1)} %slice_bitcast_fusion.3), channel_id=1, source_target_pairs={{0,1},{3,2},{4,5},{7,6},{8,9},{11,10},{12,13},{15,14},{16,17},{19,... | collective-permute-start | bytes 811016 | tf_op jit(solution)/shard_map/ppermute | solution.py:623
  40.2 10.4 %collective-permute-done.5 = bf16[512,128]{1,0:T(8,128)(2,1)S(1)} collective-permute-done((bf16[512,128]{1,0:T(8,128)(2,1)}, bf16[512,128]{1,0:T(8,128)(2,1)S(1)}, u32[]{:S(2)}, u32[]{:S(2)}) %collective-permute-start.5) | collective-permute-done | bytes 131104 | tf_op jit(solution)/shard_map/ppermute | solution.py:614
  51.3 5.2 %collective-permute-start.10 = (f32[2,16,4224]{2,1,0:T(8,128)}, f32[2,16,4224]{2,1,0:T(8,128)}, u32[]{:S(2)}, u32[]{:S(2)}) collective-permute-start(f32[2,16,4224]{2,1,0:T(8,128)} %slice.25), channel_id=1, source_target_pairs={{0,1},{3,2},{4,5},{7,6},{8,9},{11,10},{12,13},{15,14},{16,17},{19,... | collective-permute-start | bytes 1622024 | tf_op jit(solution)/shard_map/ppermute | solution.py:623
  56.5 1.1 add.30
  58.4 1.1 pad_maximum_fusion.1.refs_4_
  59.4 1.6 %collective-permute-start.15 = (bf16[2048,128]{1,0:T(8,128)(2,1)S(1)}, bf16[2048,128]{1,0:T(8,128)(2,1)S(1)}, u32[]{:S(2)}, u32[]{:S(2)}) collective-permute-start(bf16[2048,128]{1,0:T(8,128)(2,1)S(1)} %pad_maximum_fusion.1.refs_4_), channel_id=1, source_target_pairs={{0,4},{4,0},{1,5},{5,1},{2,6},{6,2},{3,7},{7,3},{8,12},{12,8},{9,1... | collective-permute-start | bytes 1572872 | tf_op jit(solution)/shard_map/ppermute | solution.py:631
  61.0 1.1 broadcast_select_fusion
  62.2 1.3 collective-permute-start.17
  63.5 1.3 collective-permute-done.10
  64.8 1.5 %collective-permute-start.13 = (bf16[64,2176]{1,0:T(8,128)(2,1)S(1)}, bf16[64,2176]{1,0:T(8,128)(2,1)S(1)}, u32[]{:S(2)}, u32[]{:S(2)}) collective-permute-start(bf16[64,2176]{1,0:T(8,128)(2,1)S(1)} %get-tuple-element.98.refs_0_), channel_id=1, source_target_pairs={{0,16},{8,24},{16,0},{24,8},{1,17},{9,25},{17,1},{25,9},{2,18},{10... | collective-permute-start | bytes 835592 | tf_op jit(solution)/shard_map/ppermute | solution.py:634
  66.3 5.0 %collective-permute-done.13.refs_1_ = bf16[64,2176]{1,0:T(8,128)(2,1)S(1)} collective-permute-done((bf16[64,2176]{1,0:T(8,128)(2,1)S(1)}, bf16[64,2176]{1,0:T(8,128)(2,1)S(1)}, u32[]{:S(2)}, u32[]{:S(2)}) %collective-permute-start.13) | collective-permute-done | bytes 278560 | tf_op jit(solution)/shard_map/ppermute | solution.py:634
  71.5 1.0 add_bitcast_fusion
  73.2 1.3 collective-permute-start.11
  74.5 3.5 %score.4 = (bf16[16,128,512]{2,1,0:T(8,128)(2,1)S(1)}, f32[16,128]{1,0:T(8,128)S(1)}, f32[16,128]{1,0:T(8,128)S(1)}, f32[16,128]{1,0:T(8,128)S(1)}) custom-call(s32[28]{0:T(128)S(1)} %fusion.info, s32[64]{0:T(128)S(1)} %bitcast.49, bf16[16,64,576]{2,1,0:T(8,128)(2,1)S(1)} %bitcast.32, bf16[16,64,576]{2,1,0:T(8,128)(2,1)} %collective-permute-done.6.other, ...), custom_call_target="tpu_custom_call" | custom-call | tf_op jit(solution)/shard_map/score/pallas_call | solution.py:254
  78.0 3.6 %score.5 = (bf16[16,128,512]{2,1,0:T(8,128)(2,1)S(1)}, f32[16,128]{1,0:T(8,128)S(1)}, f32[16,128]{1,0:T(8,128)S(1)}, f32[16,128]{1,0:T(8,128)S(1)}) custom-call(s32[28]{0:T(128)S(1)} %fusion.info, s32[64]{0:T(128)S(1)} %bitcast.50, bf16[16,64,576]{2,1,0:T(8,128)(2,1)S(1)} %bitcast.33, bf16[16,64,576]{2,1,0:T(8,128)(2,1)} %collective-permute-done.6.other, ...), custom_call_target="tpu_custom_call" | custom-call | tf_op jit(solution)/shard_map/score/pallas_call | solution.py:254
  81.6 3.7 %score.6 = (bf16[16,128,512]{2,1,0:T(8,128)(2,1)S(1)}, f32[16,128]{1,0:T(8,128)S(1)}, f32[16,128]{1,0:T(8,128)S(1)}, f32[16,128]{1,0:T(8,128)S(1)}) custom-call(s32[28]{0:T(128)S(1)} %fusion.info, s32[64]{0:T(128)S(1)} %bitcast.51, bf16[16,64,576]{2,1,0:T(8,128)(2,1)S(1)} %bitcast.34, bf16[16,64,576]{2,1,0:T(8,128)(2,1)} %collective-permute-done.6.other, ...), custom_call_target="tpu_custom_call" | custom-call | tf_op jit(solution)/shard_map/score/pallas_call | solution.py:254
  86.2 1.0 slice_bitcast_fusion.2.refs_3_
  87.2 1.3 logits.1.part
  88.5 1.6 %collective-permute-start.16 = (f32[2,16,2048]{2,1,0:T(8,128)S(1)}, f32[2,16,2048]{2,1,0:T(8,128)S(1)}, u32[]{:S(2)}, u32[]{:S(2)}) collective-permute-start(f32[2,16,2048]{2,1,0:T(8,128)S(1)} %logits.1.part), channel_id=1, source_target_pairs={{0,4},{4,0},{1,5},{5,1},{2,6},{6,2},{3,7},{7,3},{8,12},{12,8},{9,1... | collective-permute-start | bytes 786440 | tf_op jit(solution)/shard_map/ppermute | solution.py:631
  90.1 6.4 %collective-permute-done.16.far = f32[2,16,2048]{2,1,0:T(8,128)S(1)} collective-permute-done((f32[2,16,2048]{2,1,0:T(8,128)S(1)}, f32[2,16,2048]{2,1,0:T(8,128)S(1)}, u32[]{:S(2)}, u32[]{:S(2)}) %collective-permute-start.16) | collective-permute-done | bytes 262176 | tf_op jit(solution)/shard_map/ppermute | solution.py:631
  96.5 3.7 %score.7 = (bf16[16,128,512]{2,1,0:T(8,128)(2,1)S(1)}, f32[16,128]{1,0:T(8,128)S(1)}, f32[16,128]{1,0:T(8,128)S(1)}, f32[16,128]{1,0:T(8,128)S(1)}) custom-call(s32[28]{0:T(128)S(1)} %fusion.info, s32[64]{0:T(128)S(1)} %bitcast.52, bf16[16,64,576]{2,1,0:T(8,128)(2,1)S(1)} %bitcast.35, bf16[16,64,576]{2,1,0:T(8,128)(2,1)} %collective-permute-done.6.other, ...), custom_call_target="tpu_custom_call" | custom-call | tf_op jit(solution)/shard_map/score/pallas_call | solution.py:254
  100.2 1.6 %collective-permute-start.18 = (f32[2,16,128]{2,1,0:T(8,128)S(1)}, f32[2,16,128]{2,1,0:T(8,128)S(1)}, u32[]{:S(2)}, u32[]{:S(2)}) collective-permute-start(f32[2,16,128]{2,1,0:T(8,128)S(1)} %pad_maximum_fusion.3), channel_id=1, source_target_pairs={{0,4},{4,0},{1,5},{5,1},{2,6},{6,2},{3,7},{7,3},{8,12},{12,8},{9,1... | collective-permute-start | bytes 49160 | tf_op jit(solution)/shard_map/ppermute | solution.py:631
  102.6 1.4 collective-permute-done.18.refs_10_
  104.1 2.7 %delta.1 = (f32[16,2048]{1,0:T(8,128)S(1)}, bf16[16,2048]{1,0:T(8,128)(2,1)S(1)}) custom-call(s32[28]{0:T(128)S(1)} %fusion.info, bf16[16,128,512]{2,1,0:T(8,128)(2,1)S(1)} %get-tuple-element.114.refs_0_, bf16[16,128,512]{2,1,0:T(8,128)(2,1)S(1)} %get-tuple-element.115.refs_1_, bf16[16,128,512]{2,1,0:T(8,128)(2,1)S(1)} %get-tuple-element.116.refs_2_, ...), custom_call_target="tpu_custom_call" | custom-call | flops 8388608 | bytes 8388608 | tf_op jit(solution)/shard_map/delta/pallas_call | solution.py:299
  106.8 1.6 %collective-permute-start.19 = (bf16[16,2048]{1,0:T(8,128)(2,1)S(1)}, bf16[16,2048]{1,0:T(8,128)(2,1)S(1)}, u32[]{:S(2)}, u32[]{:S(2)}) collective-permute-start(bf16[16,2048]{1,0:T(8,128)(2,1)S(1)} %get-tuple-element.130.refs_9_), channel_id=1, source_target_pairs={{0,4},{4,0},{1,5},{5,1},{2,6},{6,2},{3,7},{7,3},{8,12},{12,8},{9,1... | collective-permute-start | bytes 196616 | tf_op jit(solution)/shard_map/ppermute | solution.py:631
  108.3 2.7 %collective-permute-done.19.refs_10_ = bf16[16,2048]{1,0:T(8,128)(2,1)S(1)} collective-permute-done((bf16[16,2048]{1,0:T(8,128)(2,1)S(1)}, bf16[16,2048]{1,0:T(8,128)(2,1)S(1)}, u32[]{:S(2)}, u32[]{:S(2)}) %collective-permute-start.19) | collective-permute-done | bytes 65568 | tf_op jit(solution)/shard_map/ppermute | solution.py:631
  111.1 2.5 %gradient.1 = bf16[16,4224]{1,0:T(8,128)(2,1)S(1)} custom-call(f32[16,4224]{1,0:T(8,128)S(1)} %copy-done.7, f32[16,4224]{1,0:T(8,128)S(1)} %collective-permute-done.11.refs_1_, f32[16,4224]{1,0:T(8,128)S(1)} %collective-permute-done.12.refs_2_, f32[16,4224]{1,0:T(8,128)S(1)} %slice_bitcast_fusion.2.refs_3_, bf16[2048,128]{1,0:T(8,128)(2,1)S(1)} %pad_maximum_fusion.1.refs_4_, ...), custom_call_target="tpu_custom_call" | custom-call | flops 1073741824 | bytes 2105344 | tf_op jit(solution)/shard_map/gradient/pallas_call | solution.py:485
  113.6 1.6 %collective-permute-start.23 = (bf16[1,16,4224]{2,1,0:T(8,128)(2,1)S(1)}, bf16[1,16,4224]{2,1,0:T(8,128)(2,1)S(1)}, u32[]{:S(2)}, u32[]{:S(2)}) collective-permute-start(bf16[1,16,4224]{2,1,0:T(8,128)(2,1)S(1)} %bitcast.40), channel_id=1, source_target_pairs={{0,16},{8,24},{16,0},{24,8},{1,17},{9,25},{17,1},{25,9},{2,18},{10... | collective-permute-start | bytes 405512 | tf_op jit(solution)/shard_map/ppermute | solution.py:634
  115.1 2.1 %collective-permute-start.22 = (bf16[1,16,4224]{2,1,0:T(8,128)(2,1)S(1)}, bf16[1,16,4224]{2,1,0:T(8,128)(2,1)S(1)}, u32[]{:S(2)}, u32[]{:S(2)}) collective-permute-start(bf16[1,16,4224]{2,1,0:T(8,128)(2,1)S(1)} %bitcast.41), channel_id=1, source_target_pairs={{0,3},{1,0},{2,1},{3,2},{4,7},{5,4},{6,5},{7,6},{8,11},{9,8},{10,9... | collective-permute-start | bytes 405512 | tf_op jit(solution)/shard_map/ppermute | solution.py:740
  117.2 4.0 %collective-permute-start.21 = (bf16[1,16,4224]{2,1,0:T(8,128)(2,1)S(1)}, bf16[1,16,4224]{2,1,0:T(8,128)(2,1)S(1)}, u32[]{:S(2)}, u32[]{:S(2)}) collective-permute-start(bf16[1,16,4224]{2,1,0:T(8,128)(2,1)S(1)} %bitcast.42), channel_id=1, source_target_pairs={{0,2},{1,3},{2,0},{3,1},{4,6},{5,7},{6,4},{7,5},{8,10},{9,11},{10,... | collective-permute-start | bytes 405512 | tf_op jit(solution)/shard_map/ppermute | solution.py:740
  122.5 2.4 %collective-permute-done.22 = bf16[1,16,4224]{2,1,0:T(8,128)(2,1)S(1)} collective-permute-done((bf16[1,16,4224]{2,1,0:T(8,128)(2,1)S(1)}, bf16[1,16,4224]{2,1,0:T(8,128)(2,1)S(1)}, u32[]{:S(2)}, u32[]{:S(2)}) %collective-permute-start.22) | collective-permute-done | bytes 135200 | tf_op jit(solution)/shard_map/ppermute | solution.py:740
  124.9 5.3 %collective-permute-done.21 = bf16[1,16,4224]{2,1,0:T(8,128)(2,1)S(1)} collective-permute-done((bf16[1,16,4224]{2,1,0:T(8,128)(2,1)S(1)}, bf16[1,16,4224]{2,1,0:T(8,128)(2,1)S(1)}, u32[]{:S(2)}, u32[]{:S(2)}) %collective-permute-start.21) | collective-permute-done | bytes 135200 | tf_op jit(solution)/shard_map/ppermute | solution.py:740
  130.9 8.7 %collective-permute-done.26.refs_5_ = bf16[3,16,4224]{2,1,0:T(8,128)(2,1)S(1)} collective-permute-done((bf16[3,16,4224]{2,1,0:T(8,128)(2,1)S(1)}, bf16[3,16,4224]{2,1,0:T(8,128)(2,1)S(1)}, u32[]{:S(2)}, u32[]{:S(2)}) %collective-permute-start.26) | collective-permute-done | bytes 405536 | tf_op jit(solution)/shard_map/ppermute | solution.py:634
  140.3 1.0 collective-permute-done.28.refs_7_
  141.3 4.4 %outer.1 = (f32[384,4096]{1,0:T(8,128)}, f32[32,1792]{1,0:T(8,128)}, f32[1,64]{1,0:T(1,128)}) custom-call(s32[28]{0:T(128)S(1)} %fusion.info, bf16[384,256]{1,0:T(8,128)(2,1)S(1)} %get-tuple-element.102.latents, bf16[256,1792]{1,0:T(8,128)(2,1)S(1)} %get-tuple-element.103.hiddens, bf16[1,16,4224]{2,1,0:T(8,128)(2,1)S(1)} %bitcast.45, ...), custom_call_target="tpu_custom_call" | custom-call | flops 805306368 | bytes 8388608 | tf_op jit(solution)/shard_map/outer/pallas_call | solution.py:574
  (63 shorter events, 9.3 us)
Async XLA Ops:
  0.6 6.8 %copy-start = (bf16[1,1024,576]{1,2,0:T(8,128)(2,1)S(1)}, bf16[1,1024,576]{1,2,0:T(8,128)(2,1)}, u32[]{:S(2)}) copy-start(bf16[1,1024,576]{1,2,0:T(8,128)(2,1)} %param.12) | copy-start | bytes 3538948
  0.6 10.9 %copy-start.1 = (bf16[1,16,64,576]{3,2,1,0:T(8,128)(2,1)S(1)}, bf16[1,16,64,576]{3,2,1,0:T(8,128)(2,1)}, u32[]{:S(2)}) copy-start(bf16[1,16,64,576]{3,2,1,0:T(8,128)(2,1)} %param.11) | copy-start | bytes 3538948
  0.7 13.2 %copy-start.9 = (bf16[1792,32]{0,1:T(8,128)(2,1)S(1)}, bf16[1792,32]{0,1:T(8,128)(2,1)}, u32[]{:S(2)}) copy-start(bf16[1792,32]{0,1:T(8,128)(2,1)} %param.16) | copy-start | bytes 344068
  2.4 16.8 %collective-permute-start.1 = (bf16[512,128]{1,0:T(8,128)(2,1)}, bf16[512,128]{1,0:T(8,128)(2,1)}, u32[]{:S(2)}, u32[]{:S(2)}) collective-permute-start(bf16[512,128]{1,0:T(8,128)(2,1)} %dynamic-slice_bitcast_fusion.1), channel_id=1, source_target_pairs={{0,3},{1,0},{2,1},{3,2},{4,7},{5,4},{6,5},{7,6},{8,11},{9,8},{10,9... | collective-permute-start | bytes 393224 | tf_op jit(solution)/shard_map/ppermute | solution.py:614
  7.4 11.8 %collective-permute-start = (bf16[512,128]{1,0:T(8,128)(2,1)}, bf16[512,128]{1,0:T(8,128)(2,1)}, u32[]{:S(2)}, u32[]{:S(2)}) collective-permute-start(bf16[512,128]{1,0:T(8,128)(2,1)} %dynamic-slice_bitcast_fusion.1), channel_id=1, source_target_pairs={{0,1},{1,2},{2,3},{3,0},{4,5},{5,6},{6,7},{7,4},{8,9},{9,10},{10,1... | collective-permute-start | bytes 393224 | tf_op jit(solution)/shard_map/ppermute | solution.py:614
  8.3 17.7 %collective-permute-start.3 = (bf16[576,512]{1,0:T(8,128)(2,1)}, bf16[576,512]{1,0:T(8,128)(2,1)S(1)}, u32[]{:S(2)}, u32[]{:S(2)}) collective-permute-start(bf16[576,512]{1,0:T(8,128)(2,1)} %dynamic-slice_bitcast_fusion.refs_0_), channel_id=1, source_target_pairs={{0,1},{1,2},{2,3},{4,5},{5,6},{6,7},{8,9},{9,10},{10,11},{12,13},{... | collective-permute-start | bytes 1769480 | tf_op jit(solution)/shard_map/ppermute | solution.py:665
  10.3 16.9 %collective-permute-start.2 = (bf16[576,512]{1,0:T(8,128)(2,1)}, bf16[576,512]{1,0:T(8,128)(2,1)}, u32[]{:S(2)}, u32[]{:S(2)}) collective-permute-start(bf16[576,512]{1,0:T(8,128)(2,1)} %dynamic-slice_bitcast_fusion.refs_0_), channel_id=1, source_target_pairs={{1,0},{2,1},{3,2},{5,4},{6,5},{7,6},{9,8},{10,9},{11,10},{13,12},{... | collective-permute-start | bytes 1769480 | tf_op jit(solution)/shard_map/ppermute | solution.py:664
  11.6 39.1 %collective-permute-start.6 = (bf16[16,64,576]{2,1,0:T(8,128)(2,1)S(1)}, bf16[16,64,576]{2,1,0:T(8,128)(2,1)}, u32[]{:S(2)}, u32[]{:S(2)}) collective-permute-start(bf16[16,64,576]{2,1,0:T(8,128)(2,1)S(1)} %bitcast.31), channel_id=1, source_target_pairs={{0,4},{4,0},{1,5},{5,1},{2,6},{6,2},{3,7},{7,3},{8,12},{12,8},{9,1... | collective-permute-start | bytes 3538952 | tf_op jit(solution)/shard_map/ppermute | solution.py:631
  13.8 1.9 %copy-start.2 = (bf16[384,4096]{1,0:T(8,128)(2,1)S(1)}, bf16[384,4096]{1,0:T(8,128)(2,1)}, u32[]{:S(2)}) copy-start(bf16[384,4096]{1,0:T(8,128)(2,1)} %weight.1) | copy-start | bytes 9437188
  15.7 1.2 copy-start.5
  16.9 0.9 copy-start.8
  19.2 31.4 %copy-start.3 = (f32[4,16,4224]{2,1,0:T(8,128)}, f32[4,16,4224]{2,1,0:T(8,128)S(1)}, u32[]{:S(2)}) copy-start(f32[4,16,4224]{2,1,0:T(8,128)S(1)} %get-tuple-element.71) | copy-start | bytes 3244036
  19.2 31.4 %copy-start.6 = (f32[16,4224]{1,0:T(8,128)}, f32[16,4224]{1,0:T(8,128)S(1)}, u32[]{:S(2)}) copy-start(f32[16,4224]{1,0:T(8,128)S(1)} %get-tuple-element.104.refs_0_) | copy-start | bytes 811012
  19.2 31.4 %copy-start.11 = (f32[16,4224]{1,0:T(8,128)}, f32[16,4224]{1,0:T(8,128)S(1)}, u32[]{:S(2)}) copy-start(f32[16,4224]{1,0:T(8,128)S(1)} %slice_bitcast_fusion.3) | copy-start | bytes 811012
  27.2 33.9 %collective-permute-start.7 = (bf16[576,512]{1,0:T(8,128)(2,1)}, bf16[576,512]{1,0:T(8,128)(2,1)}, u32[]{:S(2)}, u32[]{:S(2)}) collective-permute-start(bf16[576,512]{1,0:T(8,128)(2,1)} %collective-permute-done.2.refs_0_.refs_2_), channel_id=1, source_target_pairs={{1,0},{2,1},{5,4},{6,5},{9,8},{10,9},{13,12},{14,13},{17,16},{18,1... | collective-permute-start | bytes 1769480 | tf_op jit(solution)/shard_map/ppermute | solution.py:675
  28.5 32.6 %collective-permute-start.8 = (bf16[576,512]{1,0:T(8,128)(2,1)S(1)}, bf16[576,512]{1,0:T(8,128)(2,1)}, u32[]{:S(2)}, u32[]{:S(2)}) collective-permute-start(bf16[576,512]{1,0:T(8,128)(2,1)S(1)} %collective-permute-done.3.refs_1_), channel_id=1, source_target_pairs={{1,2},{2,3},{5,6},{6,7},{9,10},{10,11},{13,14},{14,15},{17,18},{18... | collective-permute-start | bytes 1769480 | tf_op jit(solution)/shard_map/ppermute | solution.py:676
  29.9 20.7 %collective-permute-start.4 = (f32[16,4224]{1,0:T(8,128)S(1)}, f32[16,4224]{1,0:T(8,128)S(1)}, u32[]{:S(2)}, u32[]{:S(2)}) collective-permute-start(f32[16,4224]{1,0:T(8,128)S(1)} %slice_bitcast_fusion.3), channel_id=1, source_target_pairs={{0,1},{3,2},{4,5},{7,6},{8,9},{11,10},{12,13},{15,14},{16,17},{19,... | collective-permute-start | bytes 811016 | tf_op jit(solution)/shard_map/ppermute | solution.py:623
  39.3 11.3 %collective-permute-start.5 = (bf16[512,128]{1,0:T(8,128)(2,1)}, bf16[512,128]{1,0:T(8,128)(2,1)S(1)}, u32[]{:S(2)}, u32[]{:S(2)}) collective-permute-start(bf16[512,128]{1,0:T(8,128)(2,1)} %dynamic-slice_bitcast_fusion.1), channel_id=1, source_target_pairs={{0,2},{1,3},{2,0},{3,1},{4,6},{5,7},{6,4},{7,5},{8,10},{9,11},{10,... | collective-permute-start | bytes 393224 | tf_op jit(solution)/shard_map/ppermute | solution.py:614
  50.6 0.7 copy-start.12
  51.3 13.5 %collective-permute-start.10 = (f32[2,16,4224]{2,1,0:T(8,128)}, f32[2,16,4224]{2,1,0:T(8,128)}, u32[]{:S(2)}, u32[]{:S(2)}) collective-permute-start(f32[2,16,4224]{2,1,0:T(8,128)} %slice.25), channel_id=1, source_target_pairs={{0,1},{3,2},{4,5},{7,6},{8,9},{11,10},{12,13},{15,14},{16,17},{19,... | collective-permute-start | bytes 1622024 | tf_op jit(solution)/shard_map/ppermute | solution.py:623
  57.5 8.8 %copy-start.4 = (f32[4,16,4224]{2,1,0:T(8,128)S(1)}, f32[4,16,4224]{2,1,0:T(8,128)}, u32[]{:S(2)}) copy-start(f32[4,16,4224]{2,1,0:T(8,128)} %copy-done.3) | copy-start | bytes 3244036
  57.5 5.9 %collective-permute-start.9 = (f32[16,4224]{1,0:T(8,128)S(1)}, f32[16,4224]{1,0:T(8,128)S(1)}, u32[]{:S(2)}, u32[]{:S(2)}) collective-permute-start(f32[16,4224]{1,0:T(8,128)S(1)} %add.30), channel_id=1, source_target_pairs={{1,2},{2,1},{5,6},{6,5},{9,10},{10,9},{13,14},{14,13},{17,18},{18,... | collective-permute-start | bytes 811016 | tf_op jit(solution)/shard_map/ppermute | solution.py:620
  59.4 27.8 %collective-permute-start.15 = (bf16[2048,128]{1,0:T(8,128)(2,1)S(1)}, bf16[2048,128]{1,0:T(8,128)(2,1)S(1)}, u32[]{:S(2)}, u32[]{:S(2)}) collective-permute-start(bf16[2048,128]{1,0:T(8,128)(2,1)S(1)} %pad_maximum_fusion.1.refs_4_), channel_id=1, source_target_pairs={{0,4},{4,0},{1,5},{5,1},{2,6},{6,2},{3,7},{7,3},{8,12},{12,8},{9,1... | collective-permute-start | bytes 1572872 | tf_op jit(solution)/shard_map/ppermute | solution.py:631
  62.2 27.9 %collective-permute-start.17 = (bf16[576,512]{1,0:T(8,128)(2,1)S(1)}, bf16[576,512]{1,0:T(8,128)(2,1)S(1)}, u32[]{:S(2)}, u32[]{:S(2)}) collective-permute-start(bf16[576,512]{1,0:T(8,128)(2,1)S(1)} %broadcast_select_fusion), channel_id=1, source_target_pairs={{1,0},{2,3},{5,4},{6,7},{9,8},{10,11},{13,12},{14,15},{17,16},{18,... | collective-permute-start | bytes 1769480 | tf_op jit(solution)/shard_map/ppermute | solution.py:617
  64.8 9.7 %copy-start.10 = (s32[1,64]{1,0:T(1,128)S(1)}, s32[1,64]{1,0:T(1,128)}, u32[]{:S(2)}) copy-start(s32[1,64]{1,0:T(1,128)} %param.14) | copy-start | bytes 772
  64.8 6.5 %collective-permute-start.13 = (bf16[64,2176]{1,0:T(8,128)(2,1)S(1)}, bf16[64,2176]{1,0:T(8,128)(2,1)S(1)}, u32[]{:S(2)}, u32[]{:S(2)}) collective-permute-start(bf16[64,2176]{1,0:T(8,128)(2,1)S(1)} %get-tuple-element.98.refs_0_), channel_id=1, source_target_pairs={{0,16},{8,24},{16,0},{24,8},{1,17},{9,25},{17,1},{25,9},{2,18},{10... | collective-permute-start | bytes 835592 | tf_op jit(solution)/shard_map/ppermute | solution.py:634
  71.4 13.9 %collective-permute-start.14 = (bf16[2,64,2176]{2,1,0:T(8,128)(2,1)S(1)}, bf16[2,64,2176]{2,1,0:T(8,128)(2,1)S(1)}, u32[]{:S(2)}, u32[]{:S(2)}) collective-permute-start(bf16[2,64,2176]{2,1,0:T(8,128)(2,1)S(1)} %pad_maximum_fusion), channel_id=1, source_target_pairs={{0,8},{8,0},{16,24},{24,16},{1,9},{9,1},{17,25},{25,17},{2,10},{10... | collective-permute-start | bytes 1671176 | tf_op jit(solution)/shard_map/ppermute | solution.py:634
  72.5 12.9 %collective-permute-start.12 = (f32[16,4224]{1,0:T(8,128)S(1)}, f32[16,4224]{1,0:T(8,128)S(1)}, u32[]{:S(2)}, u32[]{:S(2)}) collective-permute-start(f32[16,4224]{1,0:T(8,128)S(1)} %add_bitcast_fusion), channel_id=1, source_target_pairs={{1,2},{2,1},{5,6},{6,5},{9,10},{10,9},{13,14},{14,13},{17,18},{18,... | collective-permute-start | bytes 811016 | tf_op jit(solution)/shard_map/ppermute | solution.py:620
  73.2 13.0 %collective-permute-start.11 = (f32[16,4224]{1,0:T(8,128)S(1)}, f32[16,4224]{1,0:T(8,128)S(1)}, u32[]{:S(2)}, u32[]{:S(2)}) collective-permute-start(f32[16,4224]{1,0:T(8,128)S(1)} %bitcast_add_fusion), channel_id=1, source_target_pairs={{1,0},{2,3},{5,4},{6,7},{9,8},{10,11},{13,12},{14,15},{17,16},{18,... | collective-permute-start | bytes 811016 | tf_op jit(solution)/shard_map/ppermute | solution.py:617
  85.3 1.9 %copy-start.7 = (f32[16,4224]{1,0:T(8,128)S(1)}, f32[16,4224]{1,0:T(8,128)}, u32[]{:S(2)}) copy-start(f32[16,4224]{1,0:T(8,128)} %copy-done.6) | copy-start | bytes 811012
  88.5 8.0 %collective-permute-start.16 = (f32[2,16,2048]{2,1,0:T(8,128)S(1)}, f32[2,16,2048]{2,1,0:T(8,128)S(1)}, u32[]{:S(2)}, u32[]{:S(2)}) collective-permute-start(f32[2,16,2048]{2,1,0:T(8,128)S(1)} %logits.1.part), channel_id=1, source_target_pairs={{0,4},{4,0},{1,5},{5,1},{2,6},{6,2},{3,7},{7,3},{8,12},{12,8},{9,1... | collective-permute-start | bytes 786440 | tf_op jit(solution)/shard_map/ppermute | solution.py:631
  100.2 3.8 %collective-permute-start.18 = (f32[2,16,128]{2,1,0:T(8,128)S(1)}, f32[2,16,128]{2,1,0:T(8,128)S(1)}, u32[]{:S(2)}, u32[]{:S(2)}) collective-permute-start(f32[2,16,128]{2,1,0:T(8,128)S(1)} %pad_maximum_fusion.3), channel_id=1, source_target_pairs={{0,4},{4,0},{1,5},{5,1},{2,6},{6,2},{3,7},{7,3},{8,12},{12,8},{9,1... | collective-permute-start | bytes 49160 | tf_op jit(solution)/shard_map/ppermute | solution.py:631
  106.8 4.3 %collective-permute-start.19 = (bf16[16,2048]{1,0:T(8,128)(2,1)S(1)}, bf16[16,2048]{1,0:T(8,128)(2,1)S(1)}, u32[]{:S(2)}, u32[]{:S(2)}) collective-permute-start(bf16[16,2048]{1,0:T(8,128)(2,1)S(1)} %get-tuple-element.130.refs_9_), channel_id=1, source_target_pairs={{0,4},{4,0},{1,5},{5,1},{2,6},{6,2},{3,7},{7,3},{8,12},{12,8},{9,1... | collective-permute-start | bytes 196616 | tf_op jit(solution)/shard_map/ppermute | solution.py:631
  113.6 8.5 %collective-permute-start.23 = (bf16[1,16,4224]{2,1,0:T(8,128)(2,1)S(1)}, bf16[1,16,4224]{2,1,0:T(8,128)(2,1)S(1)}, u32[]{:S(2)}, u32[]{:S(2)}) collective-permute-start(bf16[1,16,4224]{2,1,0:T(8,128)(2,1)S(1)} %bitcast.40), channel_id=1, source_target_pairs={{0,16},{8,24},{16,0},{24,8},{1,17},{9,25},{17,1},{25,9},{2,18},{10... | collective-permute-start | bytes 405512 | tf_op jit(solution)/shard_map/ppermute | solution.py:634
  115.1 9.8 %collective-permute-start.22 = (bf16[1,16,4224]{2,1,0:T(8,128)(2,1)S(1)}, bf16[1,16,4224]{2,1,0:T(8,128)(2,1)S(1)}, u32[]{:S(2)}, u32[]{:S(2)}) collective-permute-start(bf16[1,16,4224]{2,1,0:T(8,128)(2,1)S(1)} %bitcast.41), channel_id=1, source_target_pairs={{0,3},{1,0},{2,1},{3,2},{4,7},{5,4},{6,5},{7,6},{8,11},{9,8},{10,9... | collective-permute-start | bytes 405512 | tf_op jit(solution)/shard_map/ppermute | solution.py:740
  117.2 13.0 %collective-permute-start.21 = (bf16[1,16,4224]{2,1,0:T(8,128)(2,1)S(1)}, bf16[1,16,4224]{2,1,0:T(8,128)(2,1)S(1)}, u32[]{:S(2)}, u32[]{:S(2)}) collective-permute-start(bf16[1,16,4224]{2,1,0:T(8,128)(2,1)S(1)} %bitcast.42), channel_id=1, source_target_pairs={{0,2},{1,3},{2,0},{3,1},{4,6},{5,7},{6,4},{7,5},{8,10},{9,11},{10,... | collective-permute-start | bytes 405512 | tf_op jit(solution)/shard_map/ppermute | solution.py:740
  121.2 9.0 %collective-permute-start.20 = (bf16[1,16,4224]{2,1,0:T(8,128)(2,1)S(1)}, bf16[1,16,4224]{2,1,0:T(8,128)(2,1)S(1)}, u32[]{:S(2)}, u32[]{:S(2)}) collective-permute-start(bf16[1,16,4224]{2,1,0:T(8,128)(2,1)S(1)} %bitcast.43), channel_id=1, source_target_pairs={{0,1},{1,2},{2,3},{3,0},{4,5},{5,6},{6,7},{7,4},{8,9},{9,10},{10,1... | collective-permute-start | bytes 405512 | tf_op jit(solution)/shard_map/ppermute | solution.py:740
  122.0 8.2 %collective-permute-start.24 = (bf16[1,16,4224]{2,1,0:T(8,128)(2,1)S(1)}, bf16[1,16,4224]{2,1,0:T(8,128)(2,1)S(1)}, u32[]{:S(2)}, u32[]{:S(2)}) collective-permute-start(bf16[1,16,4224]{2,1,0:T(8,128)(2,1)S(1)} %bitcast.44), channel_id=1, source_target_pairs={{0,8},{8,0},{16,24},{24,16},{1,9},{9,1},{17,25},{25,17},{2,10},{10... | collective-permute-start | bytes 405512 | tf_op jit(solution)/shard_map/ppermute | solution.py:634
  122.0 8.2 %collective-permute-start.25 = (bf16[1,16,4224]{2,1,0:T(8,128)(2,1)S(1)}, bf16[1,16,4224]{2,1,0:T(8,128)(2,1)S(1)}, u32[]{:S(2)}, u32[]{:S(2)}) collective-permute-start(bf16[1,16,4224]{2,1,0:T(8,128)(2,1)S(1)} %collective-permute-done.23.refs_1_), channel_id=1, source_target_pairs={{0,8},{8,0},{16,24},{24,16},{1,9},{9,1},{17,25},{25,17},{2,10},{10... | collective-permute-start | bytes 405512 | tf_op jit(solution)/shard_map/ppermute | solution.py:634
  130.3 9.3 %collective-permute-start.26 = (bf16[3,16,4224]{2,1,0:T(8,128)(2,1)S(1)}, bf16[3,16,4224]{2,1,0:T(8,128)(2,1)S(1)}, u32[]{:S(2)}, u32[]{:S(2)}) collective-permute-start(bf16[3,16,4224]{2,1,0:T(8,128)(2,1)S(1)} %pad_maximum_fusion.2.refs_4_), channel_id=1, source_target_pairs={{0,16},{8,24},{16,0},{24,8},{1,17},{9,25},{17,1},{25,9},{2,18},{10... | collective-permute-start | bytes 1216520 | tf_op jit(solution)/shard_map/ppermute | solution.py:634
  130.9 9.4 %collective-permute-start.27 = (bf16[3,16,4224]{2,1,0:T(8,128)(2,1)S(1)}, bf16[3,16,4224]{2,1,0:T(8,128)(2,1)S(1)}, u32[]{:S(2)}, u32[]{:S(2)}) collective-permute-start(bf16[3,16,4224]{2,1,0:T(8,128)(2,1)S(1)} %pad_maximum_fusion.2.refs_4_), channel_id=1, source_target_pairs={{0,8},{8,0},{16,24},{24,16},{1,9},{9,1},{17,25},{25,17},{2,10},{10... | collective-permute-start | bytes 1216520 | tf_op jit(solution)/shard_map/ppermute | solution.py:634
  139.6 1.7 %collective-permute-start.28 = (bf16[3,16,4224]{2,1,0:T(8,128)(2,1)S(1)}, bf16[3,16,4224]{2,1,0:T(8,128)(2,1)S(1)}, u32[]{:S(2)}, u32[]{:S(2)}) collective-permute-start(bf16[3,16,4224]{2,1,0:T(8,128)(2,1)S(1)} %collective-permute-done.26.refs_5_), channel_id=1, source_target_pairs={{0,8},{8,0},{16,24},{24,16},{1,9},{9,1},{17,25},{25,17},{2,10},{10... | collective-permute-start | bytes 1216520 | tf_op jit(solution)/shard_map/ppermute | solution.py:634

commit v11 on v8

--- a/solution.py
+++ b/solution.py
@@ -603,8 +603,7 @@
     index_parts[1] = onward(index_parts[0])
     index_parts[n - 1] = onward(index_parts[0], n - 1)
     parts, kept = project(info, queries_here, q_latent[0], w_query, hidden[0], w_weights.T)
-    first_part, index_parts = lax.optimization_barrier((parts[0], index_parts))
-    summed = onward(first_part) + parts[1]
+    summed = onward(parts[0]) + parts[1]
     order_at = 1 + 3 * n
     dp_at = order_at + n * dp_size
     weights, tops, before = [], [], None
@@ -621,8 +620,8 @@
     index_own = index_other = None
     for t in range(1, n - 1):
         if t == 1:
-            sent_on, summed, index_parts, kept = lax.optimization_barrier(
-                (keys_mine[t], summed, index_parts, kept)
+            sent_on, summed, index_parts, kept, other_queries = lax.optimization_barrier(
+                (keys_mine[t], summed, index_parts, kept, other_queries)
             )
             for k in range(2, n - 1):
                 index_parts[k] = onward(index_parts[1]) if k == 2 else onward(index_parts[0], k)
@@ -631,8 +630,8 @@
             over_half = swap_dp(kept, dp_size // 2)
             kept = [kept, over_half, swap_dp(kept, dp_size // 4)]
         elif t == 2:
-            sent_on, summed, index_other, kept, other_queries = lax.optimization_barrier(
-                (keys_mine[t], summed, index_other, kept, other_queries)
+            sent_on, summed, index_other, kept = lax.optimization_barrier(
+                (keys_mine[t], summed, index_other, kept)
             )
             kept = kept + [swap_dp(kept[1], dp_size // 4)]
         else:

time: 135 us -> 126 us (0.933)
  waiting for transfers between devices: 71.5 us -> 62.3 us
  local copies, waits for them, and re-layouts: 7.6 us -> 5.73 us
    ppermute x5, waiting for transfers between devices: 24.4 us -> 13.3 us  [swap_head(): return lax.ppermute(x, 'head', [(0, 1), (1, 0)])]
    ppermute x9, waiting for transfers between devices: 23.9 us -> 29.3 us  [onward(): lax.ppermute(x, 'ctx', [(ring[k], ring[(k + t) % n]) for k in range(n)])]
    ppermute x9, waiting for transfers between devices: 15.4 us -> 11.3 us  [swap_dp(): return lax.ppermute(x, 'dp', [(k, k ^ bit) for k in range(dp_size)])]
    ppermute x3, starting transfers between devices: 4.65 us -> 2.99 us  [per_device(): brought.append(lax.ppermute(piece, 'ctx', pairs))]
    ppermute x5, starting transfers between devices: 7.85 us -> 9.51 us  [swap_head(): return lax.ppermute(x, 'head', [(0, 1), (1, 0)])]
    ppermute x9, starting transfers between devices: 14.3 us -> 15.8 us  [onward(): lax.ppermute(x, 'ctx', [(ring[k], ring[(k + t) % n]) for k in range(n)])]
    unnamed x17 -> x19, local copies, waits for them, and re-layouts: 5.93 us -> 4.96 us
  transfers between devices with their start and end apart: 26 -> 26, of which waited for: 15 -> 14; matrix products, arithmetic and copies ran while one was open for 2% -> 1% of each run, Pallas kernels for 9% -> 10%
where the time goes in v11:
time: 126 us; the launch traced here: 125 us
  waiting for transfers between devices  62.3 us (49%)
  starting transfers between devices  32 us (25%)
  Pallas kernels  24.2 us (19%)
  local copies, waits for them, and re-layouts  5.73 us (5%)
    ppermute x9, waiting for transfers between devices, onward(): lax.ppermute(x, 'ctx', [(ring[k], ring[(k + t) % n]) for k in range(n)])  29.3 us
    ppermute x9, starting transfers between devices, onward(): lax.ppermute(x, 'ctx', [(ring[k], ring[(k + t) % n]) for k in range(n)])  15.8 us
    ppermute x5, waiting for transfers between devices, swap_head(): return lax.ppermute(x, 'head', [(0, 1), (1, 0)])  13.3 us
    ppermute x9, waiting for transfers between devices, swap_dp(): return lax.ppermute(x, 'dp', [(k, k ^ bit) for k in range(dp_size)])  11.3 us
    pallas_call x4, Pallas kernels, score(): pl.pallas_call(functools.partial(score_kernel, t, 1 + n + t), out_shape=(...  10.9 us
    ppermute x5, starting transfers between devices, swap_head(): return lax.ppermute(x, 'head', [(0, 1), (1, 0)])  9.51 us
    ppermute x3, waiting for transfers between devices, per_device(): brought.append(lax.ppermute(piece, 'ctx', pairs))  8.41 us
    unnamed x19, local copies, waits for them, and re-layouts  4.96 us
  transfers between devices with their start and end apart: 26, of which 14 were waited for; matrix products, arithmetic and copies ran while one was open for 1% of the time, Pallas kernels for 10%

profile of v11, /device:TPU:0, one launch (start us, length us, event | category | flops | bytes accessed | tf_op | source)
XLA Modules:
  0.0 125.4 jit_solution(4405375741317682889)
XLA Ops:
  0.6 3.0 %collective-permute-start.4 = (bf16[16,64,576]{2,1,0:T(8,128)(2,1)}, bf16[16,64,576]{2,1,0:T(8,128)(2,1)S(1)}, u32[]{:S(2)}, u32[]{:S(2)}) collective-permute-start(bf16[16,64,576]{2,1,0:T(8,128)(2,1)} %bitcast.33), channel_id=1, source_target_pairs={{0,4},{4,0},{1,5},{5,1},{2,6},{6,2},{3,7},{7,3},{8,12},{12,8},{9,1... | collective-permute-start | bytes 3538952 | tf_op jit(solution)/shard_map/ppermute | solution.py:584
  3.7 1.6 %collective-permute-start = (bf16[576,512]{1,0:T(8,128)(2,1)S(1)}, bf16[576,512]{1,0:T(8,128)(2,1)}, u32[]{:S(2)}, u32[]{:S(2)}) collective-permute-start(bf16[576,512]{1,0:T(8,128)(2,1)S(1)} %dynamic-slice_bitcast_fusion.keys), channel_id=1, source_target_pairs={{0,1},{1,3},{3,2},{2,0},{4,5},{5,7},{7,6},{6,4},{8,9},{9,11},{11,1... | collective-permute-start | bytes 1769480 | tf_op jit(solution)/shard_map/ppermute | solution.py:581
  5.4 0.7 fusion.info
  6.1 1.9 %copy-done.1 = bf16[384,4096]{1,0:T(8,128)(2,1)S(1)} copy-done((bf16[384,4096]{1,0:T(8,128)(2,1)S(1)}, bf16[384,4096]{1,0:T(8,128)(2,1)}, u32[]{:S(2)}) %copy-start.1) | copy-done | bytes 3145752
  7.9 1.2 copy-done.2
  9.1 0.9 copy-done.3
  10.0 0.9 copy-done.4
  10.9 1.3 %project.1 = (f32[16,4224]{1,0:T(8,128)S(1)}, f32[16,4224]{1,0:T(8,128)S(1)}, f32[16,4224]{1,0:T(8,128)S(1)}, f32[16,4224]{1,0:T(8,128)S(1)}, bf16[64,2176]{1,0:T(8,128)(2,1)S(1)}) custom-call(s32[33]{0:T(128)S(1)} %fusion.info, bf16[64,1536]{1,0:T(8,128)(2,1)S(1)} %bitcast.18, bf16[384,4096]{1,0:T(8,128)(2,1)S(1)} %copy-done.1, ...), custom_call_target="tpu_custom_call" | custom-call | flops 201326592 | bytes 3145728 | tf_op jit(solution)/shard_map/project/pallas_call | solution.py:111
  12.3 2.7 %collective-permute-start.1 = (f32[16,4224]{1,0:T(8,128)S(1)}, f32[16,4224]{1,0:T(8,128)S(1)}, u32[]{:S(2)}, u32[]{:S(2)}) collective-permute-start(f32[16,4224]{1,0:T(8,128)S(1)} %get-tuple-element.61), channel_id=1, source_target_pairs={{0,1},{1,3},{3,2},{2,0},{4,5},{5,7},{7,6},{6,4},{8,9},{9,11},{11,1... | collective-permute-start | bytes 811016 | tf_op jit(solution)/shard_map/ppermute | solution.py:581
  14.9 0.4 collective-permute-start.3
  15.3 1.7 %collective-permute-start.2 = (bf16[512,128]{1,0:T(8,128)(2,1)S(1)}, bf16[512,128]{1,0:T(8,128)(2,1)S(1)}, u32[]{:S(2)}, u32[]{:S(2)}) collective-permute-start(bf16[512,128]{1,0:T(8,128)(2,1)S(1)} %dynamic-slice_bitcast_fusion.1), channel_id=1, source_target_pairs={{0,1},{1,3},{3,2},{2,0},{4,5},{5,7},{7,6},{6,4},{8,9},{9,11},{11,1... | collective-permute-start | bytes 393224 | tf_op jit(solution)/shard_map/ppermute | solution.py:581
  17.0 11.3 %collective-permute-done.1 = f32[16,4224]{1,0:T(8,128)S(1)} collective-permute-done((f32[16,4224]{1,0:T(8,128)S(1)}, f32[16,4224]{1,0:T(8,128)S(1)}, u32[]{:S(2)}, u32[]{:S(2)}) %collective-permute-start.1) | collective-permute-done | bytes 270368 | tf_op jit(solution)/shard_map/ppermute | solution.py:581
  28.4 2.3 %collective-permute-done.3 = bf16[512,128]{1,0:T(8,128)(2,1)S(1)} collective-permute-done((bf16[512,128]{1,0:T(8,128)(2,1)S(1)}, bf16[512,128]{1,0:T(8,128)(2,1)S(1)}, u32[]{:S(2)}, u32[]{:S(2)}) %collective-permute-start.3) | collective-permute-done | bytes 131104 | tf_op jit(solution)/shard_map/ppermute | solution.py:581
  30.9 1.7 %collective-permute-done.4.other = bf16[16,64,576]{2,1,0:T(8,128)(2,1)S(1)} collective-permute-done((bf16[16,64,576]{2,1,0:T(8,128)(2,1)}, bf16[16,64,576]{2,1,0:T(8,128)(2,1)S(1)}, u32[]{:S(2)}, u32[]{:S(2)}) %collective-permute-start.4) | collective-permute-done | bytes 1179680 | tf_op jit(solution)/shard_map/ppermute | solution.py:584
  32.7 1.8 %collective-permute-start.7 = (bf16[512,128]{1,0:T(8,128)(2,1)S(1)}, bf16[512,128]{1,0:T(8,128)(2,1)S(1)}, u32[]{:S(2)}, u32[]{:S(2)}) collective-permute-start(bf16[512,128]{1,0:T(8,128)(2,1)S(1)} %collective-permute-done.2), channel_id=1, source_target_pairs={{0,1},{1,3},{3,2},{2,0},{4,5},{5,7},{7,6},{6,4},{8,9},{9,11},{11,1... | collective-permute-start | bytes 393224 | tf_op jit(solution)/shard_map/ppermute | solution.py:581
  34.5 2.6 %collective-permute-start.5 = (bf16[576,512]{1,0:T(8,128)(2,1)}, bf16[576,512]{1,0:T(8,128)(2,1)S(1)}, u32[]{:S(2)}, u32[]{:S(2)}) collective-permute-start(bf16[576,512]{1,0:T(8,128)(2,1)} %collective-permute-done.keys), channel_id=1, source_target_pairs={{0,1},{1,3},{3,2},{2,0},{4,5},{5,7},{7,6},{6,4},{8,9},{9,11},{11,1... | collective-permute-start | bytes 1769480 | tf_op jit(solution)/shard_map/ppermute | solution.py:581
  37.1 2.8 %collective-permute-done.7 = bf16[512,128]{1,0:T(8,128)(2,1)S(1)} collective-permute-done((bf16[512,128]{1,0:T(8,128)(2,1)S(1)}, bf16[512,128]{1,0:T(8,128)(2,1)S(1)}, u32[]{:S(2)}, u32[]{:S(2)}) %collective-permute-start.7) | collective-permute-done | bytes 131104 | tf_op jit(solution)/shard_map/ppermute | solution.py:581
  40.0 1.7 %collective-permute-start.8 = (bf16[2048,128]{1,0:T(8,128)(2,1)S(1)}, bf16[2048,128]{1,0:T(8,128)(2,1)S(1)}, u32[]{:S(2)}, u32[]{:S(2)}) collective-permute-start(bf16[2048,128]{1,0:T(8,128)(2,1)S(1)} %constant_dynamic-update-slice_fusion.own), channel_id=1, source_target_pairs={{0,4},{4,0},{1,5},{5,1},{2,6},{6,2},{3,7},{7,3},{8,12},{12,8},{9,1... | collective-permute-start | bytes 1572872 | tf_op jit(solution)/shard_map/ppermute | solution.py:584
  41.7 1.5 %collective-permute-start.9 = (bf16[64,2176]{1,0:T(8,128)(2,1)S(1)}, bf16[64,2176]{1,0:T(8,128)(2,1)S(1)}, u32[]{:S(2)}, u32[]{:S(2)}) collective-permute-start(bf16[64,2176]{1,0:T(8,128)(2,1)S(1)} %get-tuple-element.72.refs_0_), channel_id=1, source_target_pairs={{0,16},{8,24},{16,0},{24,8},{1,17},{9,25},{17,1},{25,9},{2,18},{10... | collective-permute-start | bytes 835592 | tf_op jit(solution)/shard_map/ppermute | solution.py:587
  43.2 0.9 collective-permute-start.6
  44.1 12.6 %collective-permute-done.6 = f32[16,4224]{1,0:T(8,128)S(1)} collective-permute-done((f32[16,4224]{1,0:T(8,128)S(1)}, f32[16,4224]{1,0:T(8,128)S(1)}, u32[]{:S(2)}, u32[]{:S(2)}) %collective-permute-start.6) | collective-permute-done | bytes 270368 | tf_op jit(solution)/shard_map/ppermute | solution.py:581
  56.9 1.2 collective-permute-start.12
  58.1 2.9 %collective-permute-start.14 = (bf16[576,512]{1,0:T(8,128)(2,1)S(1)}, bf16[576,512]{1,0:T(8,128)(2,1)S(1)}, u32[]{:S(2)}, u32[]{:S(2)}) collective-permute-start(bf16[576,512]{1,0:T(8,128)(2,1)S(1)} %collective-permute-done.5.keys), channel_id=1, source_target_pairs={{0,1},{1,3},{3,2},{2,0},{4,5},{5,7},{7,6},{6,4},{8,9},{9,11},{11,1... | collective-permute-start | bytes 1769480 | tf_op jit(solution)/shard_map/ppermute | solution.py:581
  61.0 0.8 arrange.1
  61.8 2.6 %score.4 = (bf16[16,128,512]{2,1,0:T(8,128)(2,1)S(1)}, f32[16,128]{1,0:T(8,128)S(1)}, f32[16,128]{1,0:T(8,128)S(1)}, f32[16,128]{1,0:T(8,128)S(1)}) custom-call(s32[33]{0:T(128)S(1)} %fusion.info, s32[64]{0:T(128)S(1)} %bitcast.28, bf16[16,64,576]{2,1,0:T(8,128)(2,1)S(1)} %bitcast.34, bf16[16,64,576]{2,1,0:T(8,128)(2,1)S(1)} %collective-permute-done.4.other, ...), custom_call_target="tpu_custom_call" | custom-call | flops 1207959552 | bytes 5046272 | tf_op jit(solution)/shard_map/score/pallas_call | solution.py:211
  64.3 3.1 %score.5 = (bf16[16,128,512]{2,1,0:T(8,128)(2,1)S(1)}, f32[16,128]{1,0:T(8,128)S(1)}, f32[16,128]{1,0:T(8,128)S(1)}, f32[16,128]{1,0:T(8,128)S(1)}) custom-call(s32[33]{0:T(128)S(1)} %fusion.info, s32[64]{0:T(128)S(1)} %bitcast.29, bf16[16,64,576]{2,1,0:T(8,128)(2,1)S(1)} %bitcast.35, bf16[16,64,576]{2,1,0:T(8,128)(2,1)S(1)} %collective-permute-done.4.other, ...), custom_call_target="tpu_custom_call" | custom-call | flops 1207959552 | bytes 5046272 | tf_op jit(solution)/shard_map/score/pallas_call | solution.py:211
  67.5 2.6 %score.6 = (bf16[16,128,512]{2,1,0:T(8,128)(2,1)S(1)}, f32[16,128]{1,0:T(8,128)S(1)}, f32[16,128]{1,0:T(8,128)S(1)}, f32[16,128]{1,0:T(8,128)S(1)}) custom-call(s32[33]{0:T(128)S(1)} %fusion.info, s32[64]{0:T(128)S(1)} %bitcast.30, bf16[16,64,576]{2,1,0:T(8,128)(2,1)S(1)} %bitcast.36, bf16[16,64,576]{2,1,0:T(8,128)(2,1)S(1)} %collective-permute-done.4.other, ...), custom_call_target="tpu_custom_call" | custom-call | flops 1207959552 | bytes 5046272 | tf_op jit(solution)/shard_map/score/pallas_call | solution.py:211
  70.1 1.3 %logits.1.part = f32[2,16,2048]{2,1,0:T(8,128)S(1)} custom-call(f32[16,4224]{1,0:T(8,128)S(1)} %collective-permute-done.12.received, f32[16,4224]{1,0:T(8,128)S(1)} %get-tuple-element.89.here, bf16[2048,128]{1,0:T(8,128)(2,1)S(1)} %constant_dynamic-update-slice_fusion.own, bf16[2048,128]{1,0:T(8,128)(2,1)S(1)} %collective-permute-done.8.other), custom_call_target="tpu_custom_call" | custom-call | flops 536870912 | bytes 1851392 | tf_op jit(solution)/shard_map/logits/pallas_call | solution.py:301
  71.3 1.6 %collective-permute-start.13 = (f32[2,16,2048]{2,1,0:T(8,128)S(1)}, f32[2,16,2048]{2,1,0:T(8,128)S(1)}, u32[]{:S(2)}, u32[]{:S(2)}) collective-permute-start(f32[2,16,2048]{2,1,0:T(8,128)S(1)} %logits.1.part), channel_id=1, source_target_pairs={{0,4},{4,0},{1,5},{5,1},{2,6},{6,2},{3,7},{7,3},{8,12},{12,8},{9,1... | collective-permute-start | bytes 786440 | tf_op jit(solution)/shard_map/ppermute | solution.py:584
  72.9 6.6 %collective-permute-done.13.far = f32[2,16,2048]{2,1,0:T(8,128)S(1)} collective-permute-done((f32[2,16,2048]{2,1,0:T(8,128)S(1)}, f32[2,16,2048]{2,1,0:T(8,128)S(1)}, u32[]{:S(2)}, u32[]{:S(2)}) %collective-permute-start.13) | collective-permute-done | bytes 262176 | tf_op jit(solution)/shard_map/ppermute | solution.py:584
  79.5 0.8 softmax.1
  80.3 2.6 %score.7 = (bf16[16,128,512]{2,1,0:T(8,128)(2,1)S(1)}, f32[16,128]{1,0:T(8,128)S(1)}, f32[16,128]{1,0:T(8,128)S(1)}, f32[16,128]{1,0:T(8,128)S(1)}) custom-call(s32[33]{0:T(128)S(1)} %fusion.info, s32[64]{0:T(128)S(1)} %bitcast.32, bf16[16,64,576]{2,1,0:T(8,128)(2,1)S(1)} %bitcast.37, bf16[16,64,576]{2,1,0:T(8,128)(2,1)S(1)} %collective-permute-done.4.other, ...), custom_call_target="tpu_custom_call" | custom-call | flops 1207959552 | bytes 5046272 | tf_op jit(solution)/shard_map/score/pallas_call | solution.py:211
  82.9 1.6 %collective-permute-start.15 = (f32[2,16,128]{2,1,0:T(8,128)S(1)}, f32[2,16,128]{2,1,0:T(8,128)S(1)}, u32[]{:S(2)}, u32[]{:S(2)}) collective-permute-start(f32[2,16,128]{2,1,0:T(8,128)S(1)} %pad_maximum_fusion.1), channel_id=1, source_target_pairs={{0,4},{4,0},{1,5},{5,1},{2,6},{6,2},{3,7},{7,3},{8,12},{12,8},{9,1... | collective-permute-start | bytes 49160 | tf_op jit(solution)/shard_map/ppermute | solution.py:584
  84.5 2.2 %collective-permute-done.15.refs_10_ = f32[2,16,128]{2,1,0:T(8,128)S(1)} collective-permute-done((f32[2,16,128]{2,1,0:T(8,128)S(1)}, f32[2,16,128]{2,1,0:T(8,128)S(1)}, u32[]{:S(2)}, u32[]{:S(2)}) %collective-permute-start.15) | collective-permute-done | bytes 16416 | tf_op jit(solution)/shard_map/ppermute | solution.py:584
  86.7 2.2 %delta.1 = (f32[16,2048]{1,0:T(8,128)S(1)}, bf16[16,2048]{1,0:T(8,128)(2,1)S(1)}) custom-call(bf16[16,128,512]{2,1,0:T(8,128)(2,1)S(1)} %get-tuple-element.97.refs_0_, bf16[16,128,512]{2,1,0:T(8,128)(2,1)S(1)} %get-tuple-element.98.refs_1_, bf16[16,128,512]{2,1,0:T(8,128)(2,1)S(1)} %get-tuple-element.99.refs_2_, ...), custom_call_target="tpu_custom_call" | custom-call | flops 8388608 | bytes 8388608 | tf_op jit(solution)/shard_map/delta/pallas_call | solution.py:258
  88.9 1.6 %collective-permute-start.16 = (bf16[16,2048]{1,0:T(8,128)(2,1)S(1)}, bf16[16,2048]{1,0:T(8,128)(2,1)S(1)}, u32[]{:S(2)}, u32[]{:S(2)}) collective-permute-start(bf16[16,2048]{1,0:T(8,128)(2,1)S(1)} %get-tuple-element.110.sent), channel_id=1, source_target_pairs={{0,4},{4,0},{1,5},{5,1},{2,6},{6,2},{3,7},{7,3},{8,12},{12,8},{9,1... | collective-permute-start | bytes 196616 | tf_op jit(solution)/shard_map/ppermute | solution.py:584
  90.5 2.7 %collective-permute-done.16.brought = bf16[16,2048]{1,0:T(8,128)(2,1)S(1)} collective-permute-done((bf16[16,2048]{1,0:T(8,128)(2,1)S(1)}, bf16[16,2048]{1,0:T(8,128)(2,1)S(1)}, u32[]{:S(2)}, u32[]{:S(2)}) %collective-permute-start.16) | collective-permute-done | bytes 65568 | tf_op jit(solution)/shard_map/ppermute | solution.py:584
  93.2 2.7 %gradient.1 = bf16[16,4224]{1,0:T(8,128)(2,1)S(1)} custom-call(f32[16,4224]{1,0:T(8,128)S(1)} %collective-permute-done.12.received, f32[16,4224]{1,0:T(8,128)S(1)} %get-tuple-element.89.here, bf16[2048,128]{1,0:T(8,128)(2,1)S(1)} %constant_dynamic-update-slice_fusion.own, bf16[2048,128]{1,0:T(8,128)(2,1)S(1)} %collective-permute-done.8.other, ...), custom_call_target="tpu_custom_call" | custom-call | flops 1073741824 | bytes 2375680 | tf_op jit(solution)/shard_map/gradient/pallas_call | solution.py:452
  95.9 1.6 %collective-permute-start.20 = (bf16[1,16,4224]{2,1,0:T(8,128)(2,1)S(1)}, bf16[1,16,4224]{2,1,0:T(8,128)(2,1)S(1)}, u32[]{:S(2)}, u32[]{:S(2)}) collective-permute-start(bf16[1,16,4224]{2,1,0:T(8,128)(2,1)S(1)} %bitcast.19), channel_id=1, source_target_pairs={{0,16},{8,24},{16,0},{24,8},{1,17},{9,25},{17,1},{25,9},{2,18},{10... | collective-permute-start | bytes 405512 | tf_op jit(solution)/shard_map/ppermute | solution.py:587
  97.5 2.4 %collective-permute-start.19 = (bf16[1,16,4224]{2,1,0:T(8,128)(2,1)S(1)}, bf16[1,16,4224]{2,1,0:T(8,128)(2,1)S(1)}, u32[]{:S(2)}, u32[]{:S(2)}) collective-permute-start(bf16[1,16,4224]{2,1,0:T(8,128)(2,1)S(1)} %bitcast.20), channel_id=1, source_target_pairs={{0,3},{1,0},{2,1},{3,2},{4,7},{5,4},{6,5},{7,6},{8,11},{9,8},{10,9... | collective-permute-start | bytes 405512 | tf_op jit(solution)/shard_map/ppermute | solution.py:674
  99.9 0.6 collective-permute-start.17
  100.4 0.5 collective-permute-done.20.refs_1_
  101.0 3.7 %collective-permute-done.19 = bf16[1,16,4224]{2,1,0:T(8,128)(2,1)S(1)} collective-permute-done((bf16[1,16,4224]{2,1,0:T(8,128)(2,1)S(1)}, bf16[1,16,4224]{2,1,0:T(8,128)(2,1)S(1)}, u32[]{:S(2)}, u32[]{:S(2)}) %collective-permute-start.19) | collective-permute-done | bytes 135200 | tf_op jit(solution)/shard_map/ppermute | solution.py:674
  104.7 4.7 %collective-permute-done.18 = bf16[1,16,4224]{2,1,0:T(8,128)(2,1)S(1)} collective-permute-done((bf16[1,16,4224]{2,1,0:T(8,128)(2,1)S(1)}, bf16[1,16,4224]{2,1,0:T(8,128)(2,1)S(1)}, u32[]{:S(2)}, u32[]{:S(2)}) %collective-permute-start.18) | collective-permute-done | bytes 135200 | tf_op jit(solution)/shard_map/ppermute | solution.py:674
  109.5 0.6 collective-permute-start.23
  110.1 9.0 %collective-permute-done.23.refs_5_ = bf16[3,16,4224]{2,1,0:T(8,128)(2,1)S(1)} collective-permute-done((bf16[3,16,4224]{2,1,0:T(8,128)(2,1)S(1)}, bf16[3,16,4224]{2,1,0:T(8,128)(2,1)S(1)}, u32[]{:S(2)}, u32[]{:S(2)}) %collective-permute-start.23) | collective-permute-done | bytes 405536 | tf_op jit(solution)/shard_map/ppermute | solution.py:587
  119.1 1.7 %collective-permute-done.25.refs_7_ = bf16[3,16,4224]{2,1,0:T(8,128)(2,1)S(1)} collective-permute-done((bf16[3,16,4224]{2,1,0:T(8,128)(2,1)S(1)}, bf16[3,16,4224]{2,1,0:T(8,128)(2,1)S(1)}, u32[]{:S(2)}, u32[]{:S(2)}) %collective-permute-start.25) | collective-permute-done | bytes 405536 | tf_op jit(solution)/shard_map/ppermute | solution.py:587
  120.9 4.4 %outer.1 = (f32[384,4096]{1,0:T(8,128)}, f32[32,1792]{1,0:T(8,128)}, f32[1,64]{1,0:T(1,128)}) custom-call(s32[33]{0:T(128)S(1)} %fusion.info, bf16[384,256]{1,0:T(8,128)(2,1)S(1)} %get-tuple-element.77.latents, bf16[256,1792]{1,0:T(8,128)(2,1)S(1)} %get-tuple-element.78.hiddens, bf16[1,16,4224]{2,1,0:T(8,128)(2,1)S(1)} %bitcast.24, ...), custom_call_target="tpu_custom_call" | custom-call | flops 805306368 | bytes 8388608 | tf_op jit(solution)/shard_map/outer/pallas_call | solution.py:539
  (43 shorter events, 0.7 us)
Async XLA Ops:
  0.6 3.0 %copy-start = (bf16[1,1024,576]{1,2,0:T(8,128)(2,1)S(1)}, bf16[1,1024,576]{1,2,0:T(8,128)(2,1)}, u32[]{:S(2)}) copy-start(bf16[1,1024,576]{1,2,0:T(8,128)(2,1)} %param.12) | copy-start | bytes 3538948
  0.6 32.0 %collective-permute-start.4 = (bf16[16,64,576]{2,1,0:T(8,128)(2,1)}, bf16[16,64,576]{2,1,0:T(8,128)(2,1)S(1)}, u32[]{:S(2)}, u32[]{:S(2)}) collective-permute-start(bf16[16,64,576]{2,1,0:T(8,128)(2,1)} %bitcast.33), channel_id=1, source_target_pairs={{0,4},{4,0},{1,5},{5,1},{2,6},{6,2},{3,7},{7,3},{8,12},{12,8},{9,1... | collective-permute-start | bytes 3538952 | tf_op jit(solution)/shard_map/ppermute | solution.py:584
  3.7 27.2 %collective-permute-start = (bf16[576,512]{1,0:T(8,128)(2,1)S(1)}, bf16[576,512]{1,0:T(8,128)(2,1)}, u32[]{:S(2)}, u32[]{:S(2)}) collective-permute-start(bf16[576,512]{1,0:T(8,128)(2,1)S(1)} %dynamic-slice_bitcast_fusion.keys), channel_id=1, source_target_pairs={{0,1},{1,3},{3,2},{2,0},{4,5},{5,7},{7,6},{6,4},{8,9},{9,11},{11,1... | collective-permute-start | bytes 1769480 | tf_op jit(solution)/shard_map/ppermute | solution.py:581
  6.0 1.9 %copy-start.1 = (bf16[384,4096]{1,0:T(8,128)(2,1)S(1)}, bf16[384,4096]{1,0:T(8,128)(2,1)}, u32[]{:S(2)}) copy-start(bf16[384,4096]{1,0:T(8,128)(2,1)} %weight.1) | copy-start | bytes 9437188
  7.9 1.2 copy-start.2
  9.1 0.9 copy-start.3
  10.0 0.9 copy-start.4
  10.9 4.0 %copy-start.7 = (bf16[1,1024,128]{2,1,0:T(8,128)(2,1)S(1)}, bf16[1,1024,128]{2,1,0:T(8,128)(2,1)}, u32[]{:S(2)}) copy-start(bf16[1,1024,128]{2,1,0:T(8,128)(2,1)} %param.13) | copy-start | bytes 786436
  12.2 49.5 %copy-start.5 = (s32[1,64]{1,0:T(1,128)S(1)}, s32[1,64]{1,0:T(1,128)}, u32[]{:S(2)}) copy-start(s32[1,64]{1,0:T(1,128)} %param.14) | copy-start | bytes 772
  12.3 49.5 %copy-start.6 = (bf16[1,16,64,576]{3,2,1,0:T(8,128)(2,1)S(1)}, bf16[1,16,64,576]{3,2,1,0:T(8,128)(2,1)}, u32[]{:S(2)}) copy-start(bf16[1,16,64,576]{3,2,1,0:T(8,128)(2,1)} %param.11) | copy-start | bytes 3538948
  12.3 16.1 %collective-permute-start.1 = (f32[16,4224]{1,0:T(8,128)S(1)}, f32[16,4224]{1,0:T(8,128)S(1)}, u32[]{:S(2)}, u32[]{:S(2)}) collective-permute-start(f32[16,4224]{1,0:T(8,128)S(1)} %get-tuple-element.61), channel_id=1, source_target_pairs={{0,1},{1,3},{3,2},{2,0},{4,5},{5,7},{7,6},{6,4},{8,9},{9,11},{11,1... | collective-permute-start | bytes 811016 | tf_op jit(solution)/shard_map/ppermute | solution.py:581
  14.9 15.7 %collective-permute-start.3 = (bf16[512,128]{1,0:T(8,128)(2,1)S(1)}, bf16[512,128]{1,0:T(8,128)(2,1)S(1)}, u32[]{:S(2)}, u32[]{:S(2)}) collective-permute-start(bf16[512,128]{1,0:T(8,128)(2,1)S(1)} %dynamic-slice_bitcast_fusion.1), channel_id=1, source_target_pairs={{0,2},{1,0},{3,1},{2,3},{4,6},{5,4},{7,5},{6,7},{8,10},{9,8},{11,9... | collective-permute-start | bytes 393224 | tf_op jit(solution)/shard_map/ppermute | solution.py:581
  15.3 15.6 %collective-permute-start.2 = (bf16[512,128]{1,0:T(8,128)(2,1)S(1)}, bf16[512,128]{1,0:T(8,128)(2,1)S(1)}, u32[]{:S(2)}, u32[]{:S(2)}) collective-permute-start(bf16[512,128]{1,0:T(8,128)(2,1)S(1)} %dynamic-slice_bitcast_fusion.1), channel_id=1, source_target_pairs={{0,1},{1,3},{3,2},{2,0},{4,5},{5,7},{7,6},{6,4},{8,9},{9,11},{11,1... | collective-permute-start | bytes 393224 | tf_op jit(solution)/shard_map/ppermute | solution.py:581
  32.7 7.3 %collective-permute-start.7 = (bf16[512,128]{1,0:T(8,128)(2,1)S(1)}, bf16[512,128]{1,0:T(8,128)(2,1)S(1)}, u32[]{:S(2)}, u32[]{:S(2)}) collective-permute-start(bf16[512,128]{1,0:T(8,128)(2,1)S(1)} %collective-permute-done.2), channel_id=1, source_target_pairs={{0,1},{1,3},{3,2},{2,0},{4,5},{5,7},{7,6},{6,4},{8,9},{9,11},{11,1... | collective-permute-start | bytes 393224 | tf_op jit(solution)/shard_map/ppermute | solution.py:581
  34.5 22.3 %collective-permute-start.5 = (bf16[576,512]{1,0:T(8,128)(2,1)}, bf16[576,512]{1,0:T(8,128)(2,1)S(1)}, u32[]{:S(2)}, u32[]{:S(2)}) collective-permute-start(bf16[576,512]{1,0:T(8,128)(2,1)} %collective-permute-done.keys), channel_id=1, source_target_pairs={{0,1},{1,3},{3,2},{2,0},{4,5},{5,7},{7,6},{6,4},{8,9},{9,11},{11,1... | collective-permute-start | bytes 1769480 | tf_op jit(solution)/shard_map/ppermute | solution.py:581
  40.0 16.8 %collective-permute-start.8 = (bf16[2048,128]{1,0:T(8,128)(2,1)S(1)}, bf16[2048,128]{1,0:T(8,128)(2,1)S(1)}, u32[]{:S(2)}, u32[]{:S(2)}) collective-permute-start(bf16[2048,128]{1,0:T(8,128)(2,1)S(1)} %constant_dynamic-update-slice_fusion.own), channel_id=1, source_target_pairs={{0,4},{4,0},{1,5},{5,1},{2,6},{6,2},{3,7},{7,3},{8,12},{12,8},{9,1... | collective-permute-start | bytes 1572872 | tf_op jit(solution)/shard_map/ppermute | solution.py:584
  41.7 15.1 %collective-permute-start.10 = (bf16[64,2176]{1,0:T(8,128)(2,1)S(1)}, bf16[64,2176]{1,0:T(8,128)(2,1)S(1)}, u32[]{:S(2)}, u32[]{:S(2)}) collective-permute-start(bf16[64,2176]{1,0:T(8,128)(2,1)S(1)} %get-tuple-element.72.refs_0_), channel_id=1, source_target_pairs={{0,8},{8,0},{16,24},{24,16},{1,9},{9,1},{17,25},{25,17},{2,10},{10... | collective-permute-start | bytes 835592 | tf_op jit(solution)/shard_map/ppermute | solution.py:587
  41.7 15.1 %collective-permute-start.9 = (bf16[64,2176]{1,0:T(8,128)(2,1)S(1)}, bf16[64,2176]{1,0:T(8,128)(2,1)S(1)}, u32[]{:S(2)}, u32[]{:S(2)}) collective-permute-start(bf16[64,2176]{1,0:T(8,128)(2,1)S(1)} %get-tuple-element.72.refs_0_), channel_id=1, source_target_pairs={{0,16},{8,24},{16,0},{24,8},{1,17},{9,25},{17,1},{25,9},{2,18},{10... | collective-permute-start | bytes 835592 | tf_op jit(solution)/shard_map/ppermute | solution.py:587
  43.2 13.5 %collective-permute-start.6 = (f32[16,4224]{1,0:T(8,128)S(1)}, f32[16,4224]{1,0:T(8,128)S(1)}, u32[]{:S(2)}, u32[]{:S(2)}) collective-permute-start(f32[16,4224]{1,0:T(8,128)S(1)} %add.24), channel_id=1, source_target_pairs={{0,1},{1,3},{3,2},{2,0},{4,5},{5,7},{7,6},{6,4},{8,9},{9,11},{11,1... | collective-permute-start | bytes 811016 | tf_op jit(solution)/shard_map/ppermute | solution.py:581
  56.8 4.1 %collective-permute-start.11 = (bf16[64,2176]{1,0:T(8,128)(2,1)S(1)}, bf16[64,2176]{1,0:T(8,128)(2,1)S(1)}, u32[]{:S(2)}, u32[]{:S(2)}) collective-permute-start(bf16[64,2176]{1,0:T(8,128)(2,1)S(1)} %collective-permute-done.9.refs_1_), channel_id=1, source_target_pairs={{0,8},{8,0},{16,24},{24,16},{1,9},{9,1},{17,25},{25,17},{2,10},{10... | collective-permute-start | bytes 835592 | tf_op jit(solution)/shard_map/ppermute | solution.py:587
  56.9 13.1 %collective-permute-start.12 = (f32[16,4224]{1,0:T(8,128)S(1)}, f32[16,4224]{1,0:T(8,128)S(1)}, u32[]{:S(2)}, u32[]{:S(2)}) collective-permute-start(f32[16,4224]{1,0:T(8,128)S(1)} %add.25), channel_id=1, source_target_pairs={{0,1},{1,3},{3,2},{2,0},{4,5},{5,7},{7,6},{6,4},{8,9},{9,11},{11,1... | collective-permute-start | bytes 811016 | tf_op jit(solution)/shard_map/ppermute | solution.py:581
  58.1 22.3 %collective-permute-start.14 = (bf16[576,512]{1,0:T(8,128)(2,1)S(1)}, bf16[576,512]{1,0:T(8,128)(2,1)S(1)}, u32[]{:S(2)}, u32[]{:S(2)}) collective-permute-start(bf16[576,512]{1,0:T(8,128)(2,1)S(1)} %collective-permute-done.5.keys), channel_id=1, source_target_pairs={{0,1},{1,3},{3,2},{2,0},{4,5},{5,7},{7,6},{6,4},{8,9},{9,11},{11,1... | collective-permute-start | bytes 1769480 | tf_op jit(solution)/shard_map/ppermute | solution.py:581
  71.3 8.2 %collective-permute-start.13 = (f32[2,16,2048]{2,1,0:T(8,128)S(1)}, f32[2,16,2048]{2,1,0:T(8,128)S(1)}, u32[]{:S(2)}, u32[]{:S(2)}) collective-permute-start(f32[2,16,2048]{2,1,0:T(8,128)S(1)} %logits.1.part), channel_id=1, source_target_pairs={{0,4},{4,0},{1,5},{5,1},{2,6},{6,2},{3,7},{7,3},{8,12},{12,8},{9,1... | collective-permute-start | bytes 786440 | tf_op jit(solution)/shard_map/ppermute | solution.py:584
  82.9 3.8 %collective-permute-start.15 = (f32[2,16,128]{2,1,0:T(8,128)S(1)}, f32[2,16,128]{2,1,0:T(8,128)S(1)}, u32[]{:S(2)}, u32[]{:S(2)}) collective-permute-start(f32[2,16,128]{2,1,0:T(8,128)S(1)} %pad_maximum_fusion.1), channel_id=1, source_target_pairs={{0,4},{4,0},{1,5},{5,1},{2,6},{6,2},{3,7},{7,3},{8,12},{12,8},{9,1... | collective-permute-start | bytes 49160 | tf_op jit(solution)/shard_map/ppermute | solution.py:584
  88.9 4.3 %collective-permute-start.16 = (bf16[16,2048]{1,0:T(8,128)(2,1)S(1)}, bf16[16,2048]{1,0:T(8,128)(2,1)S(1)}, u32[]{:S(2)}, u32[]{:S(2)}) collective-permute-start(bf16[16,2048]{1,0:T(8,128)(2,1)S(1)} %get-tuple-element.110.sent), channel_id=1, source_target_pairs={{0,4},{4,0},{1,5},{5,1},{2,6},{6,2},{3,7},{7,3},{8,12},{12,8},{9,1... | collective-permute-start | bytes 196616 | tf_op jit(solution)/shard_map/ppermute | solution.py:584
  95.9 5.1 %collective-permute-start.20 = (bf16[1,16,4224]{2,1,0:T(8,128)(2,1)S(1)}, bf16[1,16,4224]{2,1,0:T(8,128)(2,1)S(1)}, u32[]{:S(2)}, u32[]{:S(2)}) collective-permute-start(bf16[1,16,4224]{2,1,0:T(8,128)(2,1)S(1)} %bitcast.19), channel_id=1, source_target_pairs={{0,16},{8,24},{16,0},{24,8},{1,17},{9,25},{17,1},{25,9},{2,18},{10... | collective-permute-start | bytes 405512 | tf_op jit(solution)/shard_map/ppermute | solution.py:587
  97.5 7.2 %collective-permute-start.19 = (bf16[1,16,4224]{2,1,0:T(8,128)(2,1)S(1)}, bf16[1,16,4224]{2,1,0:T(8,128)(2,1)S(1)}, u32[]{:S(2)}, u32[]{:S(2)}) collective-permute-start(bf16[1,16,4224]{2,1,0:T(8,128)(2,1)S(1)} %bitcast.20), channel_id=1, source_target_pairs={{0,3},{1,0},{2,1},{3,2},{4,7},{5,4},{6,5},{7,6},{8,11},{9,8},{10,9... | collective-permute-start | bytes 405512 | tf_op jit(solution)/shard_map/ppermute | solution.py:674
  99.9 9.5 %collective-permute-start.18 = (bf16[1,16,4224]{2,1,0:T(8,128)(2,1)S(1)}, bf16[1,16,4224]{2,1,0:T(8,128)(2,1)S(1)}, u32[]{:S(2)}, u32[]{:S(2)}) collective-permute-start(bf16[1,16,4224]{2,1,0:T(8,128)(2,1)S(1)} %bitcast.21), channel_id=1, source_target_pairs={{0,2},{1,3},{2,0},{3,1},{4,6},{5,7},{6,4},{7,5},{8,10},{9,11},{10,... | collective-permute-start | bytes 405512 | tf_op jit(solution)/shard_map/ppermute | solution.py:674
  99.9 9.5 %collective-permute-start.17 = (bf16[1,16,4224]{2,1,0:T(8,128)(2,1)S(1)}, bf16[1,16,4224]{2,1,0:T(8,128)(2,1)S(1)}, u32[]{:S(2)}, u32[]{:S(2)}) collective-permute-start(bf16[1,16,4224]{2,1,0:T(8,128)(2,1)S(1)} %bitcast.22), channel_id=1, source_target_pairs={{0,1},{1,2},{2,3},{3,0},{4,5},{5,6},{6,7},{7,4},{8,9},{9,10},{10,1... | collective-permute-start | bytes 405512 | tf_op jit(solution)/shard_map/ppermute | solution.py:674
  100.4 9.0 %collective-permute-start.21 = (bf16[1,16,4224]{2,1,0:T(8,128)(2,1)S(1)}, bf16[1,16,4224]{2,1,0:T(8,128)(2,1)S(1)}, u32[]{:S(2)}, u32[]{:S(2)}) collective-permute-start(bf16[1,16,4224]{2,1,0:T(8,128)(2,1)S(1)} %bitcast.23), channel_id=1, source_target_pairs={{0,8},{8,0},{16,24},{24,16},{1,9},{9,1},{17,25},{25,17},{2,10},{10... | collective-permute-start | bytes 405512 | tf_op jit(solution)/shard_map/ppermute | solution.py:587
  101.0 8.5 %collective-permute-start.22 = (bf16[1,16,4224]{2,1,0:T(8,128)(2,1)S(1)}, bf16[1,16,4224]{2,1,0:T(8,128)(2,1)S(1)}, u32[]{:S(2)}, u32[]{:S(2)}) collective-permute-start(bf16[1,16,4224]{2,1,0:T(8,128)(2,1)S(1)} %collective-permute-done.20.refs_1_), channel_id=1, source_target_pairs={{0,8},{8,0},{16,24},{24,16},{1,9},{9,1},{17,25},{25,17},{2,10},{10... | collective-permute-start | bytes 405512 | tf_op jit(solution)/shard_map/ppermute | solution.py:587
  109.5 9.6 %collective-permute-start.23 = (bf16[3,16,4224]{2,1,0:T(8,128)(2,1)S(1)}, bf16[3,16,4224]{2,1,0:T(8,128)(2,1)S(1)}, u32[]{:S(2)}, u32[]{:S(2)}) collective-permute-start(bf16[3,16,4224]{2,1,0:T(8,128)(2,1)S(1)} %pad_maximum_fusion.refs_4_), channel_id=1, source_target_pairs={{0,16},{8,24},{16,0},{24,8},{1,17},{9,25},{17,1},{25,9},{2,18},{10... | collective-permute-start | bytes 1216520 | tf_op jit(solution)/shard_map/ppermute | solution.py:587
  110.1 9.1 %collective-permute-start.24 = (bf16[3,16,4224]{2,1,0:T(8,128)(2,1)S(1)}, bf16[3,16,4224]{2,1,0:T(8,128)(2,1)S(1)}, u32[]{:S(2)}, u32[]{:S(2)}) collective-permute-start(bf16[3,16,4224]{2,1,0:T(8,128)(2,1)S(1)} %pad_maximum_fusion.refs_4_), channel_id=1, source_target_pairs={{0,8},{8,0},{16,24},{24,16},{1,9},{9,1},{17,25},{25,17},{2,10},{10... | collective-permute-start | bytes 1216520 | tf_op jit(solution)/shard_map/ppermute | solution.py:587
  119.1 1.7 %collective-permute-start.25 = (bf16[3,16,4224]{2,1,0:T(8,128)(2,1)S(1)}, bf16[3,16,4224]{2,1,0:T(8,128)(2,1)S(1)}, u32[]{:S(2)}, u32[]{:S(2)}) collective-permute-start(bf16[3,16,4224]{2,1,0:T(8,128)(2,1)S(1)} %collective-permute-done.23.refs_5_), channel_id=1, source_target_pairs={{0,8},{8,0},{16,24},{24,16},{1,9},{9,1},{17,25},{25,17},{2,10},{10... | collective-permute-start | bytes 1216520 | tf_op jit(solution)/shard_map/ppermute | solution.py:587

commit v12 on v11

--- a/solution.py
+++ b/solution.py
@@ -371,6 +371,8 @@
 
 def gradient_kernel(
     heads,
+    first,
+    here_heads,
     blocks,
     received,
     here,
@@ -391,9 +393,10 @@
     count = received.shape[0]
     total = received[...] + here[...]
     span = own.shape[0] // blocks
-    query = query_rows(total, heads)
+    query = query_rows(total[:, first * DI : (first + here_heads) * DI], here_heads)
     columns = [
-        total[:, heads * DI + j : heads * DI + j + 1] * index_scale for j in range(heads)
+        total[:, heads * DI + first + j : heads * DI + first + j + 1] * index_scale
+        for j in range(here_heads)
     ]
     work = [(side, t) for side in range(2) for t in range(blocks)]
     held = (even, odd)
@@ -415,7 +418,7 @@
         delta = delta_own[:, at] if side == 0 else rounded
         wanted = probs[side, :, at] - rounded
         running[side] = running[side] + wanted * log_probs[side, :, at]
-        for j in range(heads):
+        for j in range(here_heads):
             rows = slice(j * count, (j + 1) * count)
             one = affinity[rows, :]
             reached = jnp.where(one > 0, delta, 0.0)
@@ -435,35 +438,35 @@
     loss = -(losses[0] + losses[1])
     lane_at = lax.broadcasted_iota(jnp.int32, (count, lanes), 1)
     tail = jnp.zeros((count, lanes), f32)
-    for j in range(heads):
+    for j in range(here_heads):
         rows = slice(j * count, (j + 1) * count)
         out[:, j * DI : (j + 1) * DI] = query_sum[rows, :].astype(bf16)
         column = jnp.sum(flow[rows, :], axis=1, keepdims=True) * index_scale
         tail = jnp.where(lane_at == j, column, tail)
     loss_high = loss.astype(bf16).astype(f32)
-    tail = jnp.where(lane_at == heads, loss_high, tail)
-    tail = jnp.where(lane_at == heads + 1, loss - loss_high, tail)
-    out[:, heads * DI :] = tail.astype(bf16)
-
-
-def gradients(heads, blocks, received, here, own, other, probs, log_probs, delta_own, sent, brought):
+    tail = jnp.where(lane_at == here_heads, loss_high, tail)
+    tail = jnp.where(lane_at == here_heads + 1, loss - loss_high, tail)
+    out[:, here_heads * DI :] = tail.astype(bf16)
+
+
+def gradients(heads, first, here_heads, blocks, received, here, own, other, probs, log_probs, delta_own, sent, brought):
     count, length = received.shape[0], own.shape[0]
     span = length // blocks
     return pl.pallas_call(
-        functools.partial(gradient_kernel, heads, blocks),
-        out_shape=jax.ShapeDtypeStruct((count, heads * DI + lanes), bf16),
+        functools.partial(gradient_kernel, heads, first, here_heads, blocks),
+        out_shape=jax.ShapeDtypeStruct((count, here_heads * DI + lanes), bf16),
         in_specs=[in_vmem()] * 9,
         out_specs=in_vmem(),
         scratch_shapes=[
-            pltpu.VMEM((heads * count, lanes), f32),
-            pltpu.VMEM((heads * count, DI), f32),
-            pltpu.VMEM((heads * count, span), bf16),
-            pltpu.VMEM((heads * count, span), f32),
-            pltpu.VMEM((heads * count, span), f32),
+            pltpu.VMEM((here_heads * count, lanes), f32),
+            pltpu.VMEM((here_heads * count, DI), f32),
+            pltpu.VMEM((here_heads * count, span), bf16),
+            pltpu.VMEM((here_heads * count, span), f32),
+            pltpu.VMEM((here_heads * count, span), f32),
         ],
         compiler_params=params(),
         cost_estimate=pl.CostEstimate(
-            flops=8 * count * heads * DI * length,
+            flops=8 * count * here_heads * DI * length,
             bytes_accessed=4 * (2 * received.size + 6 * count * length) + 4 * length * DI,
             transcendentals=0,
         ),
@@ -501,7 +504,9 @@
     )(info, *kept)
 
 
-def outer_kernel(heads, order, dp_at, info, latents, hiddens, *refs):
+def outer_kernel(heads, order, dp_at, at_column, info, latents, hiddens, *refs):
+    if at_column:
+        _, mixed_before, *refs = refs
     parts, (grad, grad_mixed, losses, rows, blocks, sems) = refs[:-6], refs[-6:]
     count = parts[0].shape[-2]
     width = heads * DI
@@ -514,12 +519,18 @@
             k += 1
     copies = []
     for i in range(steps):
-        at = slice(i * span, (i + 1) * span)
-        blocks[i] = times(latents[...], rows[:, at], 1, 0)
+        blocks[i] = times(latents[...], rows[:, i * span : (i + 1) * span], 1, 0)
+        at = slice(at_column + i * span, at_column + (i + 1) * span)
         copies.append(pltpu.make_async_copy(blocks.at[i], grad.at[:, at], sems.at[i]))
         copies[-1].start()
     tails = rows[:, width:]
-    grad_mixed[...] = times(tails, hiddens[...], 0, 0)[:heads]
+    mixed = times(tails, hiddens[...], 0, 0)[:heads]
+    if at_column:
+        before = mixed_before.shape[0]
+        grad_mixed[:before] = mixed_before[...]
+        grad_mixed[before:] = mixed
+    else:
+        grad_mixed[...] = mixed
     own = losses.shape[1]
     from_own = rows[pl.ds(pl.multiple_of(info[dp_at] * own, own), own), width:].astype(f32)
     column = from_own[:, heads : heads + 1] + from_own[:, heads + 1 : heads + 2]
@@ -531,33 +542,34 @@
         copy.wait()
 
 
-def outer(heads, order, dp_at, queries, info, latents, hiddens, parts):
+def outer(heads, order, dp_at, queries, columns, at_column, before, info, latents, hiddens, parts):
     row_count, total = latents.shape
     width = heads * DI
-    steps = 8
+    steps = 4
     hidden_count = hiddens.shape[1]
+    heads_done = before[1].shape[0] if before else 0
     return pl.pallas_call(
-        functools.partial(outer_kernel, heads, order, dp_at),
+        functools.partial(outer_kernel, heads, order, dp_at, at_column),
         out_shape=(
-            jax.ShapeDtypeStruct((row_count, width), f32),
-            jax.ShapeDtypeStruct((heads, hidden_count), f32),
+            jax.ShapeDtypeStruct((row_count, columns), f32),
+            jax.ShapeDtypeStruct((heads_done + heads, hidden_count), f32),
             jax.ShapeDtypeStruct((1, queries), f32),
         ),
-        in_specs=[in_smem()] + [in_vmem()] * (2 + len(parts)),
+        in_specs=[in_smem()]
+        + [in_vmem()] * 2
+        + [pl.BlockSpec(memory_space=pl.ANY), in_vmem()][: len(before)]
+        + [in_vmem()] * len(parts),
         out_specs=(pl.BlockSpec(memory_space=pl.ANY), in_vmem(), in_vmem()),
+        input_output_aliases={3: 0} if before else {},
         scratch_shapes=[
             pltpu.VMEM((total, width + lanes), bf16),
             pltpu.VMEM((steps, row_count, width // steps), f32),
             pltpu.SemaphoreType.DMA((steps,)),
         ],
         compiler_params=params(),
-        cost_estimate=pl.CostEstimate(
-            flops=2 * total * row_count * width,
-            bytes_accessed=4 * row_count * width + 2 * total * width,
-            transcendentals=0,
-        ),
+        cost_estimate=pl.CostEstimate(flops=0, bytes_accessed=0, transcendentals=0),
         name="outer",
-    )(info, latents, hiddens, *parts)
+    )(info, latents, hiddens, *before, *parts)
 
 
 def per_device(
@@ -586,9 +598,11 @@
     def swap_dp(x, bit):
         return lax.ppermute(x, "dp", [(k, k ^ bit) for k in range(dp_size)])
 
-    def over_dp(x):
+    def over_dp(x, held=None):
         gathered, bit = [x], dp_size // 2
         while bit:
+            if held is not None and len(gathered) > 1:
+                gathered[1:], held = lax.optimization_barrier((gathered[1:], held))
             gathered, bit = gathered + [swap_dp(one, bit) for one in gathered], bit // 2
         return gathered
 
@@ -654,45 +668,56 @@
     before, probs, log_probs = lax.optimization_barrier((before, probs, log_probs))
     score_next(keys_mine[n - 1])
     delta_own, sent = make_delta(weights, tops, *before, swap_head(jnp.stack(before)), probs)
-    piece = gradients(
-        heads_here,
-        n,
-        received,
-        parts[n - 1],
-        index_own,
-        index_other,
-        probs,
-        log_probs,
-        delta_own,
-        sent,
-        swap_head(sent),
-    )[None]
-
-    brought = []
-    for t in range(1, n):
-        pairs = [(k, (k + t) % n) for k in range(n)]
-        brought.append(lax.ppermute(piece, "ctx", pairs))
-    own_pieces = over_dp(piece)
-    brought, own_pieces = lax.optimization_barrier((jnp.concatenate(brought), own_pieces))
-    brought = over_dp(brought)
-    if queries_here % 16:
-        flat = jnp.concatenate([jnp.concatenate([a, b]) for a, b in zip(own_pieces, brought)])
-        order = jnp.argsort(info[order_at : order_at + n * dp_size])
-        parts_in, order = [flat[order].reshape(1, -1, flat.shape[2])], None
-    else:
-        parts_in, order = own_pieces + brought, []
-        order += [order_at + k * n for k in range(dp_size)]
-        order += [order_at + k * n + t for k in range(dp_size) for t in range(1, n)]
-    grad_query, grad_weights, losses = outer(
-        heads_here,
-        order,
-        dp_at,
-        q_latent.shape[1],
-        info,
-        latents,
-        hiddens,
-        parts_in,
-    )
+    delta_other = swap_head(sent)
+
+    half_heads = heads_here // 2
+    order = [order_at + k * n + t for k in range(dp_size) for t in range(n)]
+    done, losses, shards = (), None, []
+    for first in (0, half_heads):
+        piece = gradients(
+            heads_here,
+            first,
+            half_heads,
+            n,
+            received,
+            parts[n - 1],
+            index_own,
+            index_other,
+            probs,
+            log_probs,
+            delta_own,
+            sent,
+            delta_other,
+        )[None]
+        shards.append(piece)
+    for half_at, first in enumerate((0, half_heads)):
+        piece = shards[half_at]
+        brought = [piece]
+        for t in range(1, n):
+            pairs = [(k, (k + t) % n) for k in range(n)]
+            brought.append(lax.ppermute(piece, "ctx", pairs))
+        stacked, _ = lax.optimization_barrier((jnp.concatenate(brought), shards))
+        gathered = over_dp(stacked, losses)
+        order_here = order
+        if queries_here % 16:
+            flat = jnp.concatenate(gathered)
+            by_place = jnp.argsort(info[order_at : order_at + n * dp_size])
+            gathered, order_here = [flat[by_place].reshape(1, -1, flat.shape[2])], None
+        grad_query, grad_weights, losses_here = outer(
+            half_heads,
+            order_here,
+            dp_at,
+            q_latent.shape[1],
+            heads_here * DI,
+            first * DI,
+            done,
+            info,
+            latents,
+            hiddens,
+            gathered,
+        )
+        done = (grad_query, grad_weights)
+        losses = losses_here if losses is None else losses
     return (grad_query, grad_weights.T, losses)
 
 

time: 126 us -> 129 us (1.024)
  starting transfers between devices: 32 us -> 37.8 us
  waiting for transfers between devices: 62.3 us -> 57.9 us
  Pallas kernels: 24.2 us -> 26.5 us
    ppermute x3 -> x6, starting transfers between devices: 2.99 us -> 7.6 us  [per_device(): brought.append(lax.ppermute(piece, 'ctx', pairs))]
    ppermute x3 -> x6, waiting for transfers between devices: 8.41 us -> 4.41 us  [per_device(): brought.append(lax.ppermute(piece, 'ctx', pairs))]
    pallas_call x2 -> x4, Pallas kernels: 7.05 us -> 9.32 us  [the longest x2 6.36 us: outer(): pl.pallas_call(functools.partial(outer_kernel, heads, order, dp_at, at_co...]
  transfers between devices with their start and end apart: 26 -> 29, of which waited for: 14 -> 15; matrix products, arithmetic and copies ran while one was open for 1% -> 1% of each run, Pallas kernels for 10% -> 13%
where the time goes in v12:
time: 129 us
  waiting for transfers between devices  57.9 us (45%)
  starting transfers between devices  37.8 us (29%)
  Pallas kernels  26.5 us (21%)
  local copies, waits for them, and re-layouts  5.73 us (4%)
    ppermute x9, waiting for transfers between devices, onward(): lax.ppermute(x, 'ctx', [(ring[k], ring[(k + t) % n]) for k in range(n)])  29.3 us
    ppermute x9, starting transfers between devices, onward(): lax.ppermute(x, 'ctx', [(ring[k], ring[(k + t) % n]) for k in range(n)])  15.8 us
    ppermute x5, waiting for transfers between devices, swap_head(): return lax.ppermute(x, 'head', [(0, 1), (1, 0)])  13.3 us
    ppermute x9, waiting for transfers between devices, swap_dp(): return lax.ppermute(x, 'dp', [(k, k ^ bit) for k in range(dp_size)])  10.9 us
    pallas_call x4, Pallas kernels, score(): pl.pallas_call(functools.partial(score_kernel, t, 1 + n + t), out_shape=(...  10.8 us
    ppermute x5, starting transfers between devices, swap_head(): return lax.ppermute(x, 'head', [(0, 1), (1, 0)])  9.53 us
    ppermute x6, starting transfers between devices, per_device(): brought.append(lax.ppermute(piece, 'ctx', pairs))  7.6 us
    pallas_call x2, Pallas kernels, outer(): pl.pallas_call(functools.partial(outer_kernel, heads, order, dp_at, at_co...  6.36 us
  transfers between devices with their start and end apart: 29, of which 15 were waited for; matrix products, arithmetic and copies ran while one was open for 1% of the time, Pallas kernels for 13%

profile of v12, /device:TPU:0, one launch (start us, length us, event | category | flops | bytes accessed | tf_op | source)
XLA Modules:
  0.0 129.1 jit_solution(15279180723514979752)
XLA Ops:
  0.6 3.0 %collective-permute-start.4 = (bf16[16,64,576]{2,1,0:T(8,128)(2,1)}, bf16[16,64,576]{2,1,0:T(8,128)(2,1)S(1)}, u32[]{:S(2)}, u32[]{:S(2)}) collective-permute-start(bf16[16,64,576]{2,1,0:T(8,128)(2,1)} %bitcast.36), channel_id=1, source_target_pairs={{0,4},{4,0},{1,5},{5,1},{2,6},{6,2},{3,7},{7,3},{8,12},{12,8},{9,1... | collective-permute-start | bytes 3538952 | tf_op jit(solution)/shard_map/ppermute | solution.py:596
  3.7 1.6 %collective-permute-start = (bf16[576,512]{1,0:T(8,128)(2,1)S(1)}, bf16[576,512]{1,0:T(8,128)(2,1)}, u32[]{:S(2)}, u32[]{:S(2)}) collective-permute-start(bf16[576,512]{1,0:T(8,128)(2,1)S(1)} %dynamic-slice_bitcast_fusion.keys), channel_id=1, source_target_pairs={{0,1},{1,3},{3,2},{2,0},{4,5},{5,7},{7,6},{6,4},{8,9},{9,11},{11,1... | collective-permute-start | bytes 1769480 | tf_op jit(solution)/shard_map/ppermute | solution.py:593
  6.1 1.9 %copy-done.1 = bf16[384,4096]{1,0:T(8,128)(2,1)S(1)} copy-done((bf16[384,4096]{1,0:T(8,128)(2,1)S(1)}, bf16[384,4096]{1,0:T(8,128)(2,1)}, u32[]{:S(2)}) %copy-start.1) | copy-done | bytes 3145752
  7.9 1.2 copy-done.2
  9.1 0.9 copy-done.3
  10.0 0.9 copy-done.4
  10.9 1.3 project.1
  12.3 2.7 %collective-permute-start.1 = (f32[16,4224]{1,0:T(8,128)S(1)}, f32[16,4224]{1,0:T(8,128)S(1)}, u32[]{:S(2)}, u32[]{:S(2)}) collective-permute-start(f32[16,4224]{1,0:T(8,128)S(1)} %get-tuple-element.61), channel_id=1, source_target_pairs={{0,1},{1,3},{3,2},{2,0},{4,5},{5,7},{7,6},{6,4},{8,9},{9,11},{11,1... | collective-permute-start | bytes 811016 | tf_op jit(solution)/shard_map/ppermute | solution.py:593
  15.3 1.7 %collective-permute-start.2 = (bf16[512,128]{1,0:T(8,128)(2,1)S(1)}, bf16[512,128]{1,0:T(8,128)(2,1)S(1)}, u32[]{:S(2)}, u32[]{:S(2)}) collective-permute-start(bf16[512,128]{1,0:T(8,128)(2,1)S(1)} %dynamic-slice_bitcast_fusion.1), channel_id=1, source_target_pairs={{0,1},{1,3},{3,2},{2,0},{4,5},{5,7},{7,6},{6,4},{8,9},{9,11},{11,1... | collective-permute-start | bytes 393224 | tf_op jit(solution)/shard_map/ppermute | solution.py:593
  17.0 11.3 %collective-permute-done.1 = f32[16,4224]{1,0:T(8,128)S(1)} collective-permute-done((f32[16,4224]{1,0:T(8,128)S(1)}, f32[16,4224]{1,0:T(8,128)S(1)}, u32[]{:S(2)}, u32[]{:S(2)}) %collective-permute-start.1) | collective-permute-done | bytes 270368 | tf_op jit(solution)/shard_map/ppermute | solution.py:593
  28.4 2.3 %collective-permute-done.3 = bf16[512,128]{1,0:T(8,128)(2,1)S(1)} collective-permute-done((bf16[512,128]{1,0:T(8,128)(2,1)S(1)}, bf16[512,128]{1,0:T(8,128)(2,1)S(1)}, u32[]{:S(2)}, u32[]{:S(2)}) %collective-permute-start.3) | collective-permute-done | bytes 131104 | tf_op jit(solution)/shard_map/ppermute | solution.py:593
  30.9 1.7 %collective-permute-done.4.other = bf16[16,64,576]{2,1,0:T(8,128)(2,1)S(1)} collective-permute-done((bf16[16,64,576]{2,1,0:T(8,128)(2,1)}, bf16[16,64,576]{2,1,0:T(8,128)(2,1)S(1)}, u32[]{:S(2)}, u32[]{:S(2)}) %collective-permute-start.4) | collective-permute-done | bytes 1179680 | tf_op jit(solution)/shard_map/ppermute | solution.py:596
  32.7 1.8 %collective-permute-start.7 = (bf16[512,128]{1,0:T(8,128)(2,1)S(1)}, bf16[512,128]{1,0:T(8,128)(2,1)S(1)}, u32[]{:S(2)}, u32[]{:S(2)}) collective-permute-start(bf16[512,128]{1,0:T(8,128)(2,1)S(1)} %collective-permute-done.2), channel_id=1, source_target_pairs={{0,1},{1,3},{3,2},{2,0},{4,5},{5,7},{7,6},{6,4},{8,9},{9,11},{11,1... | collective-permute-start | bytes 393224 | tf_op jit(solution)/shard_map/ppermute | solution.py:593
  34.5 2.6 %collective-permute-start.5 = (bf16[576,512]{1,0:T(8,128)(2,1)}, bf16[576,512]{1,0:T(8,128)(2,1)S(1)}, u32[]{:S(2)}, u32[]{:S(2)}) collective-permute-start(bf16[576,512]{1,0:T(8,128)(2,1)} %collective-permute-done.keys), channel_id=1, source_target_pairs={{0,1},{1,3},{3,2},{2,0},{4,5},{5,7},{7,6},{6,4},{8,9},{9,11},{11,1... | collective-permute-start | bytes 1769480 | tf_op jit(solution)/shard_map/ppermute | solution.py:593
  37.1 2.8 %collective-permute-done.7 = bf16[512,128]{1,0:T(8,128)(2,1)S(1)} collective-permute-done((bf16[512,128]{1,0:T(8,128)(2,1)S(1)}, bf16[512,128]{1,0:T(8,128)(2,1)S(1)}, u32[]{:S(2)}, u32[]{:S(2)}) %collective-permute-start.7) | collective-permute-done | bytes 131104 | tf_op jit(solution)/shard_map/ppermute | solution.py:593
  40.0 1.7 %collective-permute-start.8 = (bf16[2048,128]{1,0:T(8,128)(2,1)S(1)}, bf16[2048,128]{1,0:T(8,128)(2,1)S(1)}, u32[]{:S(2)}, u32[]{:S(2)}) collective-permute-start(bf16[2048,128]{1,0:T(8,128)(2,1)S(1)} %constant_dynamic-update-slice_fusion.own), channel_id=1, source_target_pairs={{0,4},{4,0},{1,5},{5,1},{2,6},{6,2},{3,7},{7,3},{8,12},{12,8},{9,1... | collective-permute-start | bytes 1572872 | tf_op jit(solution)/shard_map/ppermute | solution.py:596
  41.7 1.5 %collective-permute-start.9 = (bf16[64,2176]{1,0:T(8,128)(2,1)S(1)}, bf16[64,2176]{1,0:T(8,128)(2,1)S(1)}, u32[]{:S(2)}, u32[]{:S(2)}) collective-permute-start(bf16[64,2176]{1,0:T(8,128)(2,1)S(1)} %get-tuple-element.72.refs_0_), channel_id=1, source_target_pairs={{0,16},{8,24},{16,0},{24,8},{1,17},{9,25},{17,1},{25,9},{2,18},{10... | collective-permute-start | bytes 835592 | tf_op jit(solution)/shard_map/ppermute | solution.py:599
  43.2 0.9 collective-permute-start.6
  44.1 12.6 %collective-permute-done.6 = f32[16,4224]{1,0:T(8,128)S(1)} collective-permute-done((f32[16,4224]{1,0:T(8,128)S(1)}, f32[16,4224]{1,0:T(8,128)S(1)}, u32[]{:S(2)}, u32[]{:S(2)}) %collective-permute-start.6) | collective-permute-done | bytes 270368 | tf_op jit(solution)/shard_map/ppermute | solution.py:593
  56.9 1.2 collective-permute-start.12
  58.1 2.9 %collective-permute-start.14 = (bf16[576,512]{1,0:T(8,128)(2,1)S(1)}, bf16[576,512]{1,0:T(8,128)(2,1)S(1)}, u32[]{:S(2)}, u32[]{:S(2)}) collective-permute-start(bf16[576,512]{1,0:T(8,128)(2,1)S(1)} %collective-permute-done.5.keys), channel_id=1, source_target_pairs={{0,1},{1,3},{3,2},{2,0},{4,5},{5,7},{7,6},{6,4},{8,9},{9,11},{11,1... | collective-permute-start | bytes 1769480 | tf_op jit(solution)/shard_map/ppermute | solution.py:593
  61.8 2.6 %score.4 = (bf16[16,128,512]{2,1,0:T(8,128)(2,1)S(1)}, f32[16,128]{1,0:T(8,128)S(1)}, f32[16,128]{1,0:T(8,128)S(1)}, f32[16,128]{1,0:T(8,128)S(1)}) custom-call(s32[33]{0:T(128)S(1)} %fusion.info, s32[64]{0:T(128)S(1)} %bitcast.31, bf16[16,64,576]{2,1,0:T(8,128)(2,1)S(1)} %bitcast.37, bf16[16,64,576]{2,1,0:T(8,128)(2,1)S(1)} %collective-permute-done.4.other, ...), custom_call_target="tpu_custom_call" | custom-call | flops 1207959552 | bytes 5046272 | tf_op jit(solution)/shard_map/score/pallas_call | solution.py:211
  64.3 3.1 %score.5 = (bf16[16,128,512]{2,1,0:T(8,128)(2,1)S(1)}, f32[16,128]{1,0:T(8,128)S(1)}, f32[16,128]{1,0:T(8,128)S(1)}, f32[16,128]{1,0:T(8,128)S(1)}) custom-call(s32[33]{0:T(128)S(1)} %fusion.info, s32[64]{0:T(128)S(1)} %bitcast.32, bf16[16,64,576]{2,1,0:T(8,128)(2,1)S(1)} %bitcast.38, bf16[16,64,576]{2,1,0:T(8,128)(2,1)S(1)} %collective-permute-done.4.other, ...), custom_call_target="tpu_custom_call" | custom-call | flops 1207959552 | bytes 5046272 | tf_op jit(solution)/shard_map/score/pallas_call | solution.py:211
  67.4 2.6 %score.6 = (bf16[16,128,512]{2,1,0:T(8,128)(2,1)S(1)}, f32[16,128]{1,0:T(8,128)S(1)}, f32[16,128]{1,0:T(8,128)S(1)}, f32[16,128]{1,0:T(8,128)S(1)}) custom-call(s32[33]{0:T(128)S(1)} %fusion.info, s32[64]{0:T(128)S(1)} %bitcast.33, bf16[16,64,576]{2,1,0:T(8,128)(2,1)S(1)} %bitcast.39, bf16[16,64,576]{2,1,0:T(8,128)(2,1)S(1)} %collective-permute-done.4.other, ...), custom_call_target="tpu_custom_call" | custom-call | flops 1207959552 | bytes 5046272 | tf_op jit(solution)/shard_map/score/pallas_call | solution.py:211
  70.0 1.3 logits.1.part
  71.2 1.6 %collective-permute-start.13 = (f32[2,16,2048]{2,1,0:T(8,128)S(1)}, f32[2,16,2048]{2,1,0:T(8,128)S(1)}, u32[]{:S(2)}, u32[]{:S(2)}) collective-permute-start(f32[2,16,2048]{2,1,0:T(8,128)S(1)} %logits.1.part), channel_id=1, source_target_pairs={{0,4},{4,0},{1,5},{5,1},{2,6},{6,2},{3,7},{7,3},{8,12},{12,8},{9,1... | collective-permute-start | bytes 786440 | tf_op jit(solution)/shard_map/ppermute | solution.py:596
  72.8 6.6 %collective-permute-done.13.far = f32[2,16,2048]{2,1,0:T(8,128)S(1)} collective-permute-done((f32[2,16,2048]{2,1,0:T(8,128)S(1)}, f32[2,16,2048]{2,1,0:T(8,128)S(1)}, u32[]{:S(2)}, u32[]{:S(2)}) %collective-permute-start.13) | collective-permute-done | bytes 262176 | tf_op jit(solution)/shard_map/ppermute | solution.py:596
  79.4 0.8 softmax.1
  80.2 2.7 %score.7 = (bf16[16,128,512]{2,1,0:T(8,128)(2,1)S(1)}, f32[16,128]{1,0:T(8,128)S(1)}, f32[16,128]{1,0:T(8,128)S(1)}, f32[16,128]{1,0:T(8,128)S(1)}) custom-call(s32[33]{0:T(128)S(1)} %fusion.info, s32[64]{0:T(128)S(1)} %bitcast.35, bf16[16,64,576]{2,1,0:T(8,128)(2,1)S(1)} %bitcast.40, bf16[16,64,576]{2,1,0:T(8,128)(2,1)S(1)} %collective-permute-done.4.other, ...), custom_call_target="tpu_custom_call" | custom-call | flops 1207959552 | bytes 5046272 | tf_op jit(solution)/shard_map/score/pallas_call | solution.py:211
  82.9 1.6 %collective-permute-start.15 = (f32[2,16,128]{2,1,0:T(8,128)S(1)}, f32[2,16,128]{2,1,0:T(8,128)S(1)}, u32[]{:S(2)}, u32[]{:S(2)}) collective-permute-start(f32[2,16,128]{2,1,0:T(8,128)S(1)} %pad_maximum_fusion.2), channel_id=1, source_target_pairs={{0,4},{4,0},{1,5},{5,1},{2,6},{6,2},{3,7},{7,3},{8,12},{12,8},{9,1... | collective-permute-start | bytes 49160 | tf_op jit(solution)/shard_map/ppermute | solution.py:596
  84.5 2.2 %collective-permute-done.15.refs_10_ = f32[2,16,128]{2,1,0:T(8,128)S(1)} collective-permute-done((f32[2,16,128]{2,1,0:T(8,128)S(1)}, f32[2,16,128]{2,1,0:T(8,128)S(1)}, u32[]{:S(2)}, u32[]{:S(2)}) %collective-permute-start.15) | collective-permute-done | bytes 16416 | tf_op jit(solution)/shard_map/ppermute | solution.py:596
  86.7 2.2 %delta.1 = (f32[16,2048]{1,0:T(8,128)S(1)}, bf16[16,2048]{1,0:T(8,128)(2,1)S(1)}) custom-call(bf16[16,128,512]{2,1,0:T(8,128)(2,1)S(1)} %get-tuple-element.97.refs_0_, bf16[16,128,512]{2,1,0:T(8,128)(2,1)S(1)} %get-tuple-element.98.refs_1_, bf16[16,128,512]{2,1,0:T(8,128)(2,1)S(1)} %get-tuple-element.99.refs_2_, ...), custom_call_target="tpu_custom_call" | custom-call | flops 8388608 | bytes 8388608 | tf_op jit(solution)/shard_map/delta/pallas_call | solution.py:258
  88.9 1.6 %collective-permute-start.16 = (bf16[16,2048]{1,0:T(8,128)(2,1)S(1)}, bf16[16,2048]{1,0:T(8,128)(2,1)S(1)}, u32[]{:S(2)}, u32[]{:S(2)}) collective-permute-start(bf16[16,2048]{1,0:T(8,128)(2,1)S(1)} %get-tuple-element.110.sent), channel_id=1, source_target_pairs={{0,4},{4,0},{1,5},{5,1},{2,6},{6,2},{3,7},{7,3},{8,12},{12,8},{9,1... | collective-permute-start | bytes 196616 | tf_op jit(solution)/shard_map/ppermute | solution.py:596
  90.4 2.7 %collective-permute-done.16.brought = bf16[16,2048]{1,0:T(8,128)(2,1)S(1)} collective-permute-done((bf16[16,2048]{1,0:T(8,128)(2,1)S(1)}, bf16[16,2048]{1,0:T(8,128)(2,1)S(1)}, u32[]{:S(2)}, u32[]{:S(2)}) %collective-permute-start.16) | collective-permute-done | bytes 65568 | tf_op jit(solution)/shard_map/ppermute | solution.py:596
  93.2 1.6 %gradient.2 = bf16[16,2176]{1,0:T(8,128)(2,1)S(1)} custom-call(f32[16,4224]{1,0:T(8,128)S(1)} %collective-permute-done.12.received, f32[16,4224]{1,0:T(8,128)S(1)} %get-tuple-element.89.here, bf16[2048,128]{1,0:T(8,128)(2,1)S(1)} %constant_dynamic-update-slice_fusion.own, bf16[2048,128]{1,0:T(8,128)(2,1)S(1)} %collective-permute-done.8.other, ...), custom_call_target="tpu_custom_call" | custom-call | flops 536870912 | bytes 2375680 | tf_op jit(solution)/shard_map/gradient/pallas_call | solution.py:455
  94.8 2.6 %collective-permute-start.19 = (bf16[1,16,2176]{2,1,0:T(8,128)(2,1)S(1)}, bf16[1,16,2176]{2,1,0:T(8,128)(2,1)S(1)}, u32[]{:S(2)}, u32[]{:S(2)}) collective-permute-start(bf16[1,16,2176]{2,1,0:T(8,128)(2,1)S(1)} %bitcast.23), channel_id=1, source_target_pairs={{0,3},{1,0},{2,1},{3,2},{4,7},{5,4},{6,5},{7,6},{8,11},{9,8},{10,9... | collective-permute-start | bytes 208904 | tf_op jit(solution)/shard_map/ppermute | solution.py:698
  98.0 1.4 %gradient.3 = bf16[16,2176]{1,0:T(8,128)(2,1)S(1)} custom-call(f32[16,4224]{1,0:T(8,128)S(1)} %collective-permute-done.12.received, f32[16,4224]{1,0:T(8,128)S(1)} %get-tuple-element.89.here, bf16[2048,128]{1,0:T(8,128)(2,1)S(1)} %constant_dynamic-update-slice_fusion.own, bf16[2048,128]{1,0:T(8,128)(2,1)S(1)} %collective-permute-done.8.other, ...), custom_call_target="tpu_custom_call" | custom-call | flops 536870912 | bytes 2375680 | tf_op jit(solution)/shard_map/gradient/pallas_call | solution.py:455
  99.4 3.2 %collective-permute-start.25 = (bf16[1,16,2176]{2,1,0:T(8,128)(2,1)S(1)}, bf16[1,16,2176]{2,1,0:T(8,128)(2,1)S(1)}, u32[]{:S(2)}, u32[]{:S(2)}) collective-permute-start(bf16[1,16,2176]{2,1,0:T(8,128)(2,1)S(1)} %bitcast.19), channel_id=1, source_target_pairs={{0,3},{1,0},{2,1},{3,2},{4,7},{5,4},{6,5},{7,6},{8,11},{9,8},{10,9... | collective-permute-start | bytes 208904 | tf_op jit(solution)/shard_map/ppermute | solution.py:698
  102.6 1.1 collective-permute-start.24
  103.8 2.1 %collective-permute-done.18 = bf16[1,16,2176]{2,1,0:T(8,128)(2,1)S(1)} collective-permute-done((bf16[1,16,2176]{2,1,0:T(8,128)(2,1)S(1)}, bf16[1,16,2176]{2,1,0:T(8,128)(2,1)S(1)}, u32[]{:S(2)}, u32[]{:S(2)}) %collective-permute-start.18) | collective-permute-done | bytes 69664 | tf_op jit(solution)/shard_map/ppermute | solution.py:698
  106.0 1.6 %collective-permute-start.20 = (bf16[4,16,2176]{2,1,0:T(8,128)(2,1)S(1)}, bf16[4,16,2176]{2,1,0:T(8,128)(2,1)S(1)}, u32[]{:S(2)}, u32[]{:S(2)}) collective-permute-start(bf16[4,16,2176]{2,1,0:T(8,128)(2,1)S(1)} %pad_maximum_fusion.refs_0_), channel_id=1, source_target_pairs={{0,16},{8,24},{16,0},{24,8},{1,17},{9,25},{17,1},{25,9},{2,18},{10... | collective-permute-start | bytes 835592 | tf_op jit(solution)/shard_map/ppermute | solution.py:599
  108.3 1.6 %collective-permute-done.23 = bf16[1,16,2176]{2,1,0:T(8,128)(2,1)S(1)} collective-permute-done((bf16[1,16,2176]{2,1,0:T(8,128)(2,1)S(1)}, bf16[1,16,2176]{2,1,0:T(8,128)(2,1)S(1)}, u32[]{:S(2)}, u32[]{:S(2)}) %collective-permute-start.23) | collective-permute-done | bytes 69664 | tf_op jit(solution)/shard_map/ppermute | solution.py:698
  109.9 5.1 %collective-permute-done.20.refs_1_ = bf16[4,16,2176]{2,1,0:T(8,128)(2,1)S(1)} collective-permute-done((bf16[4,16,2176]{2,1,0:T(8,128)(2,1)S(1)}, bf16[4,16,2176]{2,1,0:T(8,128)(2,1)S(1)}, u32[]{:S(2)}, u32[]{:S(2)}) %collective-permute-start.20) | collective-permute-done | bytes 278560 | tf_op jit(solution)/shard_map/ppermute | solution.py:599
  115.1 1.5 %collective-permute-start.26 = (bf16[4,16,2176]{2,1,0:T(8,128)(2,1)S(1)}, bf16[4,16,2176]{2,1,0:T(8,128)(2,1)S(1)}, u32[]{:S(2)}, u32[]{:S(2)}) collective-permute-start(bf16[4,16,2176]{2,1,0:T(8,128)(2,1)S(1)} %pad_maximum_fusion.1.refs_2_), channel_id=1, source_target_pairs={{0,16},{8,24},{16,0},{24,8},{1,17},{9,25},{17,1},{25,9},{2,18},{10... | collective-permute-start | bytes 835592 | tf_op jit(solution)/shard_map/ppermute | solution.py:599
  116.8 3.1 %outer.2 = (f32[384,4096]{1,0:T(8,128)}, f32[16,1792]{1,0:T(8,128)S(1)}, f32[1,64]{1,0:T(1,128)}) custom-call(s32[33]{0:T(128)S(1)} %fusion.info, bf16[384,256]{1,0:T(8,128)(2,1)S(1)} %get-tuple-element.77.latents, bf16[256,1792]{1,0:T(8,128)(2,1)S(1)} %get-tuple-element.78.hiddens, bf16[4,16,2176]{2,1,0:T(8,128)(2,1)S(1)} %pad_maximum_fusion.refs_0_, ...), custom_call_target="tpu_custom_call" | custom-call | tf_op jit(solution)/shard_map/outer/pallas_call | solution.py:551
  119.9 4.2 %collective-permute-done.26.refs_3_ = bf16[4,16,2176]{2,1,0:T(8,128)(2,1)S(1)} collective-permute-done((bf16[4,16,2176]{2,1,0:T(8,128)(2,1)S(1)}, bf16[4,16,2176]{2,1,0:T(8,128)(2,1)S(1)}, u32[]{:S(2)}, u32[]{:S(2)}) %collective-permute-start.26) | collective-permute-done | bytes 278560 | tf_op jit(solution)/shard_map/ppermute | solution.py:599
  124.1 1.6 %collective-permute-done.28.refs_5_ = bf16[4,16,2176]{2,1,0:T(8,128)(2,1)S(1)} collective-permute-done((bf16[4,16,2176]{2,1,0:T(8,128)(2,1)S(1)}, bf16[4,16,2176]{2,1,0:T(8,128)(2,1)S(1)}, u32[]{:S(2)}, u32[]{:S(2)}) %collective-permute-start.28) | collective-permute-done | bytes 278560 | tf_op jit(solution)/shard_map/ppermute | solution.py:599
  125.7 3.3 %outer.3 = (f32[384,4096]{1,0:T(8,128)}, f32[32,1792]{1,0:T(8,128)}, f32[1,64]{1,0:T(1,128)}) custom-call(s32[33]{0:T(128)S(1)} %fusion.info, bf16[384,256]{1,0:T(8,128)(2,1)S(1)} %get-tuple-element.77.latents, bf16[256,1792]{1,0:T(8,128)(2,1)S(1)} %get-tuple-element.78.hiddens, ...), custom_call_target="tpu_custom_call", output_to_operand_aliasing={{0}: (3, {})} | custom-call | tf_op jit(solution)/shard_map/outer/pallas_call | solution.py:551
  (52 shorter events, 4.2 us)
Async XLA Ops:
  0.6 3.0 %copy-start = (bf16[1,1024,576]{1,2,0:T(8,128)(2,1)S(1)}, bf16[1,1024,576]{1,2,0:T(8,128)(2,1)}, u32[]{:S(2)}) copy-start(bf16[1,1024,576]{1,2,0:T(8,128)(2,1)} %param.12) | copy-start | bytes 3538948
  0.6 32.0 %collective-permute-start.4 = (bf16[16,64,576]{2,1,0:T(8,128)(2,1)}, bf16[16,64,576]{2,1,0:T(8,128)(2,1)S(1)}, u32[]{:S(2)}, u32[]{:S(2)}) collective-permute-start(bf16[16,64,576]{2,1,0:T(8,128)(2,1)} %bitcast.36), channel_id=1, source_target_pairs={{0,4},{4,0},{1,5},{5,1},{2,6},{6,2},{3,7},{7,3},{8,12},{12,8},{9,1... | collective-permute-start | bytes 3538952 | tf_op jit(solution)/shard_map/ppermute | solution.py:596
  3.7 27.2 %collective-permute-start = (bf16[576,512]{1,0:T(8,128)(2,1)S(1)}, bf16[576,512]{1,0:T(8,128)(2,1)}, u32[]{:S(2)}, u32[]{:S(2)}) collective-permute-start(bf16[576,512]{1,0:T(8,128)(2,1)S(1)} %dynamic-slice_bitcast_fusion.keys), channel_id=1, source_target_pairs={{0,1},{1,3},{3,2},{2,0},{4,5},{5,7},{7,6},{6,4},{8,9},{9,11},{11,1... | collective-permute-start | bytes 1769480 | tf_op jit(solution)/shard_map/ppermute | solution.py:593
  6.0 1.9 %copy-start.1 = (bf16[384,4096]{1,0:T(8,128)(2,1)S(1)}, bf16[384,4096]{1,0:T(8,128)(2,1)}, u32[]{:S(2)}) copy-start(bf16[384,4096]{1,0:T(8,128)(2,1)} %weight.1) | copy-start | bytes 9437188
  7.9 1.2 copy-start.2
  9.1 0.9 copy-start.3
  10.0 0.9 copy-start.4
  10.9 4.0 %copy-start.7 = (bf16[1,1024,128]{2,1,0:T(8,128)(2,1)S(1)}, bf16[1,1024,128]{2,1,0:T(8,128)(2,1)}, u32[]{:S(2)}) copy-start(bf16[1,1024,128]{2,1,0:T(8,128)(2,1)} %param.13) | copy-start | bytes 786436
  12.2 49.5 %copy-start.5 = (s32[1,64]{1,0:T(1,128)S(1)}, s32[1,64]{1,0:T(1,128)}, u32[]{:S(2)}) copy-start(s32[1,64]{1,0:T(1,128)} %param.14) | copy-start | bytes 772
  12.3 49.5 %copy-start.6 = (bf16[1,16,64,576]{3,2,1,0:T(8,128)(2,1)S(1)}, bf16[1,16,64,576]{3,2,1,0:T(8,128)(2,1)}, u32[]{:S(2)}) copy-start(bf16[1,16,64,576]{3,2,1,0:T(8,128)(2,1)} %param.11) | copy-start | bytes 3538948
  12.3 16.1 %collective-permute-start.1 = (f32[16,4224]{1,0:T(8,128)S(1)}, f32[16,4224]{1,0:T(8,128)S(1)}, u32[]{:S(2)}, u32[]{:S(2)}) collective-permute-start(f32[16,4224]{1,0:T(8,128)S(1)} %get-tuple-element.61), channel_id=1, source_target_pairs={{0,1},{1,3},{3,2},{2,0},{4,5},{5,7},{7,6},{6,4},{8,9},{9,11},{11,1... | collective-permute-start | bytes 811016 | tf_op jit(solution)/shard_map/ppermute | solution.py:593
  14.9 15.7 %collective-permute-start.3 = (bf16[512,128]{1,0:T(8,128)(2,1)S(1)}, bf16[512,128]{1,0:T(8,128)(2,1)S(1)}, u32[]{:S(2)}, u32[]{:S(2)}) collective-permute-start(bf16[512,128]{1,0:T(8,128)(2,1)S(1)} %dynamic-slice_bitcast_fusion.1), channel_id=1, source_target_pairs={{0,2},{1,0},{3,1},{2,3},{4,6},{5,4},{7,5},{6,7},{8,10},{9,8},{11,9... | collective-permute-start | bytes 393224 | tf_op jit(solution)/shard_map/ppermute | solution.py:593
  15.3 15.6 %collective-permute-start.2 = (bf16[512,128]{1,0:T(8,128)(2,1)S(1)}, bf16[512,128]{1,0:T(8,128)(2,1)S(1)}, u32[]{:S(2)}, u32[]{:S(2)}) collective-permute-start(bf16[512,128]{1,0:T(8,128)(2,1)S(1)} %dynamic-slice_bitcast_fusion.1), channel_id=1, source_target_pairs={{0,1},{1,3},{3,2},{2,0},{4,5},{5,7},{7,6},{6,4},{8,9},{9,11},{11,1... | collective-permute-start | bytes 393224 | tf_op jit(solution)/shard_map/ppermute | solution.py:593
  32.7 7.3 %collective-permute-start.7 = (bf16[512,128]{1,0:T(8,128)(2,1)S(1)}, bf16[512,128]{1,0:T(8,128)(2,1)S(1)}, u32[]{:S(2)}, u32[]{:S(2)}) collective-permute-start(bf16[512,128]{1,0:T(8,128)(2,1)S(1)} %collective-permute-done.2), channel_id=1, source_target_pairs={{0,1},{1,3},{3,2},{2,0},{4,5},{5,7},{7,6},{6,4},{8,9},{9,11},{11,1... | collective-permute-start | bytes 393224 | tf_op jit(solution)/shard_map/ppermute | solution.py:593
  34.5 22.3 %collective-permute-start.5 = (bf16[576,512]{1,0:T(8,128)(2,1)}, bf16[576,512]{1,0:T(8,128)(2,1)S(1)}, u32[]{:S(2)}, u32[]{:S(2)}) collective-permute-start(bf16[576,512]{1,0:T(8,128)(2,1)} %collective-permute-done.keys), channel_id=1, source_target_pairs={{0,1},{1,3},{3,2},{2,0},{4,5},{5,7},{7,6},{6,4},{8,9},{9,11},{11,1... | collective-permute-start | bytes 1769480 | tf_op jit(solution)/shard_map/ppermute | solution.py:593
  40.0 16.8 %collective-permute-start.8 = (bf16[2048,128]{1,0:T(8,128)(2,1)S(1)}, bf16[2048,128]{1,0:T(8,128)(2,1)S(1)}, u32[]{:S(2)}, u32[]{:S(2)}) collective-permute-start(bf16[2048,128]{1,0:T(8,128)(2,1)S(1)} %constant_dynamic-update-slice_fusion.own), channel_id=1, source_target_pairs={{0,4},{4,0},{1,5},{5,1},{2,6},{6,2},{3,7},{7,3},{8,12},{12,8},{9,1... | collective-permute-start | bytes 1572872 | tf_op jit(solution)/shard_map/ppermute | solution.py:596
  41.7 15.1 %collective-permute-start.10 = (bf16[64,2176]{1,0:T(8,128)(2,1)S(1)}, bf16[64,2176]{1,0:T(8,128)(2,1)S(1)}, u32[]{:S(2)}, u32[]{:S(2)}) collective-permute-start(bf16[64,2176]{1,0:T(8,128)(2,1)S(1)} %get-tuple-element.72.refs_0_), channel_id=1, source_target_pairs={{0,8},{8,0},{16,24},{24,16},{1,9},{9,1},{17,25},{25,17},{2,10},{10... | collective-permute-start | bytes 835592 | tf_op jit(solution)/shard_map/ppermute | solution.py:599
  41.7 15.1 %collective-permute-start.9 = (bf16[64,2176]{1,0:T(8,128)(2,1)S(1)}, bf16[64,2176]{1,0:T(8,128)(2,1)S(1)}, u32[]{:S(2)}, u32[]{:S(2)}) collective-permute-start(bf16[64,2176]{1,0:T(8,128)(2,1)S(1)} %get-tuple-element.72.refs_0_), channel_id=1, source_target_pairs={{0,16},{8,24},{16,0},{24,8},{1,17},{9,25},{17,1},{25,9},{2,18},{10... | collective-permute-start | bytes 835592 | tf_op jit(solution)/shard_map/ppermute | solution.py:599
  43.2 13.5 %collective-permute-start.6 = (f32[16,4224]{1,0:T(8,128)S(1)}, f32[16,4224]{1,0:T(8,128)S(1)}, u32[]{:S(2)}, u32[]{:S(2)}) collective-permute-start(f32[16,4224]{1,0:T(8,128)S(1)} %add.24), channel_id=1, source_target_pairs={{0,1},{1,3},{3,2},{2,0},{4,5},{5,7},{7,6},{6,4},{8,9},{9,11},{11,1... | collective-permute-start | bytes 811016 | tf_op jit(solution)/shard_map/ppermute | solution.py:593
  56.8 4.1 %collective-permute-start.11 = (bf16[64,2176]{1,0:T(8,128)(2,1)S(1)}, bf16[64,2176]{1,0:T(8,128)(2,1)S(1)}, u32[]{:S(2)}, u32[]{:S(2)}) collective-permute-start(bf16[64,2176]{1,0:T(8,128)(2,1)S(1)} %collective-permute-done.9.refs_1_), channel_id=1, source_target_pairs={{0,8},{8,0},{16,24},{24,16},{1,9},{9,1},{17,25},{25,17},{2,10},{10... | collective-permute-start | bytes 835592 | tf_op jit(solution)/shard_map/ppermute | solution.py:599
  56.9 13.0 %collective-permute-start.12 = (f32[16,4224]{1,0:T(8,128)S(1)}, f32[16,4224]{1,0:T(8,128)S(1)}, u32[]{:S(2)}, u32[]{:S(2)}) collective-permute-start(f32[16,4224]{1,0:T(8,128)S(1)} %add.25), channel_id=1, source_target_pairs={{0,1},{1,3},{3,2},{2,0},{4,5},{5,7},{7,6},{6,4},{8,9},{9,11},{11,1... | collective-permute-start | bytes 811016 | tf_op jit(solution)/shard_map/ppermute | solution.py:593
  58.1 22.1 %collective-permute-start.14 = (bf16[576,512]{1,0:T(8,128)(2,1)S(1)}, bf16[576,512]{1,0:T(8,128)(2,1)S(1)}, u32[]{:S(2)}, u32[]{:S(2)}) collective-permute-start(bf16[576,512]{1,0:T(8,128)(2,1)S(1)} %collective-permute-done.5.keys), channel_id=1, source_target_pairs={{0,1},{1,3},{3,2},{2,0},{4,5},{5,7},{7,6},{6,4},{8,9},{9,11},{11,1... | collective-permute-start | bytes 1769480 | tf_op jit(solution)/shard_map/ppermute | solution.py:593
  71.2 8.2 %collective-permute-start.13 = (f32[2,16,2048]{2,1,0:T(8,128)S(1)}, f32[2,16,2048]{2,1,0:T(8,128)S(1)}, u32[]{:S(2)}, u32[]{:S(2)}) collective-permute-start(f32[2,16,2048]{2,1,0:T(8,128)S(1)} %logits.1.part), channel_id=1, source_target_pairs={{0,4},{4,0},{1,5},{5,1},{2,6},{6,2},{3,7},{7,3},{8,12},{12,8},{9,1... | collective-permute-start | bytes 786440 | tf_op jit(solution)/shard_map/ppermute | solution.py:596
  82.9 3.8 %collective-permute-start.15 = (f32[2,16,128]{2,1,0:T(8,128)S(1)}, f32[2,16,128]{2,1,0:T(8,128)S(1)}, u32[]{:S(2)}, u32[]{:S(2)}) collective-permute-start(f32[2,16,128]{2,1,0:T(8,128)S(1)} %pad_maximum_fusion.2), channel_id=1, source_target_pairs={{0,4},{4,0},{1,5},{5,1},{2,6},{6,2},{3,7},{7,3},{8,12},{12,8},{9,1... | collective-permute-start | bytes 49160 | tf_op jit(solution)/shard_map/ppermute | solution.py:596
  88.9 4.3 %collective-permute-start.16 = (bf16[16,2048]{1,0:T(8,128)(2,1)S(1)}, bf16[16,2048]{1,0:T(8,128)(2,1)S(1)}, u32[]{:S(2)}, u32[]{:S(2)}) collective-permute-start(bf16[16,2048]{1,0:T(8,128)(2,1)S(1)} %get-tuple-element.110.sent), channel_id=1, source_target_pairs={{0,4},{4,0},{1,5},{5,1},{2,6},{6,2},{3,7},{7,3},{8,12},{12,8},{9,1... | collective-permute-start | bytes 196616 | tf_op jit(solution)/shard_map/ppermute | solution.py:596
  94.8 9.0 %collective-permute-start.19 = (bf16[1,16,2176]{2,1,0:T(8,128)(2,1)S(1)}, bf16[1,16,2176]{2,1,0:T(8,128)(2,1)S(1)}, u32[]{:S(2)}, u32[]{:S(2)}) collective-permute-start(bf16[1,16,2176]{2,1,0:T(8,128)(2,1)S(1)} %bitcast.23), channel_id=1, source_target_pairs={{0,3},{1,0},{2,1},{3,2},{4,7},{5,4},{6,5},{7,6},{8,11},{9,8},{10,9... | collective-permute-start | bytes 208904 | tf_op jit(solution)/shard_map/ppermute | solution.py:698
  97.4 8.5 %collective-permute-start.18 = (bf16[1,16,2176]{2,1,0:T(8,128)(2,1)S(1)}, bf16[1,16,2176]{2,1,0:T(8,128)(2,1)S(1)}, u32[]{:S(2)}, u32[]{:S(2)}) collective-permute-start(bf16[1,16,2176]{2,1,0:T(8,128)(2,1)S(1)} %bitcast.24), channel_id=1, source_target_pairs={{0,2},{1,3},{2,0},{3,1},{4,6},{5,7},{6,4},{7,5},{8,10},{9,11},{10,... | collective-permute-start | bytes 208904 | tf_op jit(solution)/shard_map/ppermute | solution.py:698
  97.4 8.5 %collective-permute-start.17 = (bf16[1,16,2176]{2,1,0:T(8,128)(2,1)S(1)}, bf16[1,16,2176]{2,1,0:T(8,128)(2,1)S(1)}, u32[]{:S(2)}, u32[]{:S(2)}) collective-permute-start(bf16[1,16,2176]{2,1,0:T(8,128)(2,1)S(1)} %bitcast.25), channel_id=1, source_target_pairs={{0,1},{1,2},{2,3},{3,0},{4,5},{5,6},{6,7},{7,4},{8,9},{9,10},{10,1... | collective-permute-start | bytes 208904 | tf_op jit(solution)/shard_map/ppermute | solution.py:698
  99.4 8.2 %collective-permute-start.25 = (bf16[1,16,2176]{2,1,0:T(8,128)(2,1)S(1)}, bf16[1,16,2176]{2,1,0:T(8,128)(2,1)S(1)}, u32[]{:S(2)}, u32[]{:S(2)}) collective-permute-start(bf16[1,16,2176]{2,1,0:T(8,128)(2,1)S(1)} %bitcast.19), channel_id=1, source_target_pairs={{0,3},{1,0},{2,1},{3,2},{4,7},{5,4},{6,5},{7,6},{8,11},{9,8},{10,9... | collective-permute-start | bytes 208904 | tf_op jit(solution)/shard_map/ppermute | solution.py:698
  102.6 5.7 %collective-permute-start.24 = (bf16[1,16,2176]{2,1,0:T(8,128)(2,1)S(1)}, bf16[1,16,2176]{2,1,0:T(8,128)(2,1)S(1)}, u32[]{:S(2)}, u32[]{:S(2)}) collective-permute-start(bf16[1,16,2176]{2,1,0:T(8,128)(2,1)S(1)} %bitcast.20), channel_id=1, source_target_pairs={{0,2},{1,3},{2,0},{3,1},{4,6},{5,7},{6,4},{7,5},{8,10},{9,11},{10,... | collective-permute-start | bytes 208904 | tf_op jit(solution)/shard_map/ppermute | solution.py:698
  103.8 6.1 %collective-permute-start.23 = (bf16[1,16,2176]{2,1,0:T(8,128)(2,1)S(1)}, bf16[1,16,2176]{2,1,0:T(8,128)(2,1)S(1)}, u32[]{:S(2)}, u32[]{:S(2)}) collective-permute-start(bf16[1,16,2176]{2,1,0:T(8,128)(2,1)S(1)} %bitcast.21), channel_id=1, source_target_pairs={{0,1},{1,2},{2,3},{3,0},{4,5},{5,6},{6,7},{7,4},{8,9},{9,10},{10,1... | collective-permute-start | bytes 208904 | tf_op jit(solution)/shard_map/ppermute | solution.py:698
  105.9 10.9 %collective-permute-start.21 = (bf16[4,16,2176]{2,1,0:T(8,128)(2,1)S(1)}, bf16[4,16,2176]{2,1,0:T(8,128)(2,1)S(1)}, u32[]{:S(2)}, u32[]{:S(2)}) collective-permute-start(bf16[4,16,2176]{2,1,0:T(8,128)(2,1)S(1)} %pad_maximum_fusion.refs_0_), channel_id=1, source_target_pairs={{0,8},{8,0},{16,24},{24,16},{1,9},{9,1},{17,25},{25,17},{2,10},{10... | collective-permute-start | bytes 835592 | tf_op jit(solution)/shard_map/ppermute | solution.py:599
  106.0 9.1 %collective-permute-start.20 = (bf16[4,16,2176]{2,1,0:T(8,128)(2,1)S(1)}, bf16[4,16,2176]{2,1,0:T(8,128)(2,1)S(1)}, u32[]{:S(2)}, u32[]{:S(2)}) collective-permute-start(bf16[4,16,2176]{2,1,0:T(8,128)(2,1)S(1)} %pad_maximum_fusion.refs_0_), channel_id=1, source_target_pairs={{0,16},{8,24},{16,0},{24,8},{1,17},{9,25},{17,1},{25,9},{2,18},{10... | collective-permute-start | bytes 835592 | tf_op jit(solution)/shard_map/ppermute | solution.py:599
  115.1 1.7 %collective-permute-start.22 = (bf16[4,16,2176]{2,1,0:T(8,128)(2,1)S(1)}, bf16[4,16,2176]{2,1,0:T(8,128)(2,1)S(1)}, u32[]{:S(2)}, u32[]{:S(2)}) collective-permute-start(bf16[4,16,2176]{2,1,0:T(8,128)(2,1)S(1)} %collective-permute-done.20.refs_1_), channel_id=1, source_target_pairs={{0,8},{8,0},{16,24},{24,16},{1,9},{9,1},{17,25},{25,17},{2,10},{10... | collective-permute-start | bytes 835592 | tf_op jit(solution)/shard_map/ppermute | solution.py:599
  115.1 9.1 %collective-permute-start.26 = (bf16[4,16,2176]{2,1,0:T(8,128)(2,1)S(1)}, bf16[4,16,2176]{2,1,0:T(8,128)(2,1)S(1)}, u32[]{:S(2)}, u32[]{:S(2)}) collective-permute-start(bf16[4,16,2176]{2,1,0:T(8,128)(2,1)S(1)} %pad_maximum_fusion.1.refs_2_), channel_id=1, source_target_pairs={{0,16},{8,24},{16,0},{24,8},{1,17},{9,25},{17,1},{25,9},{2,18},{10... | collective-permute-start | bytes 835592 | tf_op jit(solution)/shard_map/ppermute | solution.py:599
  116.6 7.6 %collective-permute-start.27 = (bf16[4,16,2176]{2,1,0:T(8,128)(2,1)S(1)}, bf16[4,16,2176]{2,1,0:T(8,128)(2,1)S(1)}, u32[]{:S(2)}, u32[]{:S(2)}) collective-permute-start(bf16[4,16,2176]{2,1,0:T(8,128)(2,1)S(1)} %pad_maximum_fusion.1.refs_2_), channel_id=1, source_target_pairs={{0,8},{8,0},{16,24},{24,16},{1,9},{9,1},{17,25},{25,17},{2,10},{10... | collective-permute-start | bytes 835592 | tf_op jit(solution)/shard_map/ppermute | solution.py:599
  124.1 1.6 %collective-permute-start.28 = (bf16[4,16,2176]{2,1,0:T(8,128)(2,1)S(1)}, bf16[4,16,2176]{2,1,0:T(8,128)(2,1)S(1)}, u32[]{:S(2)}, u32[]{:S(2)}) collective-permute-start(bf16[4,16,2176]{2,1,0:T(8,128)(2,1)S(1)} %collective-permute-done.26.refs_3_), channel_id=1, source_target_pairs={{0,8},{8,0},{16,24},{24,16},{1,9},{9,1},{17,25},{25,17},{2,10},{10... | collective-permute-start | bytes 835592 | tf_op jit(solution)/shard_map/ppermute | solution.py:599

commit v13 on v11

--- a/solution.py
+++ b/solution.py
@@ -620,12 +620,13 @@
     index_own = index_other = None
     for t in range(1, n - 1):
         if t == 1:
-            sent_on, summed, index_parts, kept, other_queries = lax.optimization_barrier(
-                (keys_mine[t], summed, index_parts, kept, other_queries)
+            sent_on, summed, index_parts, kept = lax.optimization_barrier(
+                (keys_mine[t], summed, index_parts, kept)
             )
             for k in range(2, n - 1):
                 index_parts[k] = onward(index_parts[1]) if k == 2 else onward(index_parts[0], k)
             index_own = jnp.concatenate(index_parts)
+            index_own, other_queries = lax.optimization_barrier((index_own, other_queries))
             index_other = swap_head(index_own)
             over_half = swap_dp(kept, dp_size // 2)
             kept = [kept, over_half, swap_dp(kept, dp_size // 4)]

time: 126 us -> 124 us (0.984)
  waiting for transfers between devices: 62.3 us -> 60.8 us
    ppermute x5, waiting for transfers between devices: 13.3 us -> 10.9 us  [swap_head(): return lax.ppermute(x, 'head', [(0, 1), (1, 0)])]
    unnamed x19 -> x16, local copies, waits for them, and re-layouts: 4.96 us -> 4.92 us
  transfers between devices with their start and end apart: 26 -> 26, of which waited for: 14 -> 13; matrix products, arithmetic and copies ran while one was open for 1% -> 1% of each run, Pallas kernels for 10% -> 10%
where the time goes in v13:
time: 124 us; the launch traced here: 123 us
  waiting for transfers between devices  60.8 us (49%)
  starting transfers between devices  31.5 us (25%)
  Pallas kernels  24.1 us (19%)
  local copies, waits for them, and re-layouts  5.66 us (5%)
    ppermute x9, waiting for transfers between devices, onward(): lax.ppermute(x, 'ctx', [(ring[k], ring[(k + t) % n]) for k in range(n)])  30.1 us
    ppermute x9, starting transfers between devices, onward(): lax.ppermute(x, 'ctx', [(ring[k], ring[(k + t) % n]) for k in range(n)])  14.6 us
    ppermute x9, waiting for transfers between devices, swap_dp(): return lax.ppermute(x, 'dp', [(k, k ^ bit) for k in range(dp_size)])  11.3 us
    ppermute x5, waiting for transfers between devices, swap_head(): return lax.ppermute(x, 'head', [(0, 1), (1, 0)])  10.9 us
    pallas_call x4, Pallas kernels, score(): pl.pallas_call(functools.partial(score_kernel, t, 1 + n + t), out_shape=(...  10.7 us
    ppermute x5, starting transfers between devices, swap_head(): return lax.ppermute(x, 'head', [(0, 1), (1, 0)])  10.1 us
    ppermute x3, waiting for transfers between devices, per_device(): brought.append(lax.ppermute(piece, 'ctx', pairs))  8.5 us
    unnamed x16, local copies, waits for them, and re-layouts  4.92 us
  transfers between devices with their start and end apart: 26, of which 13 were waited for; matrix products, arithmetic and copies ran while one was open for 1% of the time, Pallas kernels for 10%

profile of v13, /device:TPU:0, one launch (start us, length us, event | category | flops | bytes accessed | tf_op | source)
XLA Modules:
  0.0 123.2 jit_solution(3532988924839723329)
XLA Ops:
  0.6 3.0 %collective-permute-start.5 = (bf16[16,64,576]{2,1,0:T(8,128)(2,1)}, bf16[16,64,576]{2,1,0:T(8,128)(2,1)S(1)}, u32[]{:S(2)}, u32[]{:S(2)}) collective-permute-start(bf16[16,64,576]{2,1,0:T(8,128)(2,1)} %bitcast.33), channel_id=1, source_target_pairs={{0,4},{4,0},{1,5},{5,1},{2,6},{6,2},{3,7},{7,3},{8,12},{12,8},{9,1... | collective-permute-start | bytes 3538952 | tf_op jit(solution)/shard_map/ppermute | solution.py:584
  3.7 1.6 %collective-permute-start = (bf16[576,512]{1,0:T(8,128)(2,1)S(1)}, bf16[576,512]{1,0:T(8,128)(2,1)}, u32[]{:S(2)}, u32[]{:S(2)}) collective-permute-start(bf16[576,512]{1,0:T(8,128)(2,1)S(1)} %dynamic-slice_bitcast_fusion.keys), channel_id=1, source_target_pairs={{0,1},{1,3},{3,2},{2,0},{4,5},{5,7},{7,6},{6,4},{8,9},{9,11},{11,1... | collective-permute-start | bytes 1769480 | tf_op jit(solution)/shard_map/ppermute | solution.py:581
  5.4 0.7 fusion.info
  6.1 1.9 %copy-done.1 = bf16[384,4096]{1,0:T(8,128)(2,1)S(1)} copy-done((bf16[384,4096]{1,0:T(8,128)(2,1)S(1)}, bf16[384,4096]{1,0:T(8,128)(2,1)}, u32[]{:S(2)}) %copy-start.1) | copy-done | bytes 3145752
  7.9 1.2 copy-done.2
  9.1 0.9 copy-done.3
  10.0 0.9 copy-done.4
  10.9 1.3 %project.1 = (f32[16,4224]{1,0:T(8,128)S(1)}, f32[16,4224]{1,0:T(8,128)S(1)}, f32[16,4224]{1,0:T(8,128)S(1)}, f32[16,4224]{1,0:T(8,128)S(1)}, bf16[64,2176]{1,0:T(8,128)(2,1)S(1)}) custom-call(s32[33]{0:T(128)S(1)} %fusion.info, bf16[64,1536]{1,0:T(8,128)(2,1)S(1)} %bitcast.18, bf16[384,4096]{1,0:T(8,128)(2,1)S(1)} %copy-done.1, ...), custom_call_target="tpu_custom_call" | custom-call | flops 201326592 | bytes 3145728 | tf_op jit(solution)/shard_map/project/pallas_call | solution.py:111
  12.3 2.7 %collective-permute-start.1 = (f32[16,4224]{1,0:T(8,128)S(1)}, f32[16,4224]{1,0:T(8,128)S(1)}, u32[]{:S(2)}, u32[]{:S(2)}) collective-permute-start(f32[16,4224]{1,0:T(8,128)S(1)} %get-tuple-element.62), channel_id=1, source_target_pairs={{0,1},{1,3},{3,2},{2,0},{4,5},{5,7},{7,6},{6,4},{8,9},{9,11},{11,1... | collective-permute-start | bytes 811016 | tf_op jit(solution)/shard_map/ppermute | solution.py:581
  14.9 0.4 collective-permute-start.3
  15.3 1.7 %collective-permute-start.2 = (bf16[512,128]{1,0:T(8,128)(2,1)S(1)}, bf16[512,128]{1,0:T(8,128)(2,1)S(1)}, u32[]{:S(2)}, u32[]{:S(2)}) collective-permute-start(bf16[512,128]{1,0:T(8,128)(2,1)S(1)} %dynamic-slice_bitcast_fusion.1), channel_id=1, source_target_pairs={{0,1},{1,3},{3,2},{2,0},{4,5},{5,7},{7,6},{6,4},{8,9},{9,11},{11,1... | collective-permute-start | bytes 393224 | tf_op jit(solution)/shard_map/ppermute | solution.py:581
  17.0 11.3 %collective-permute-done.1 = f32[16,4224]{1,0:T(8,128)S(1)} collective-permute-done((f32[16,4224]{1,0:T(8,128)S(1)}, f32[16,4224]{1,0:T(8,128)S(1)}, u32[]{:S(2)}, u32[]{:S(2)}) %collective-permute-start.1) | collective-permute-done | bytes 270368 | tf_op jit(solution)/shard_map/ppermute | solution.py:581
  28.4 2.3 %collective-permute-done.3 = bf16[512,128]{1,0:T(8,128)(2,1)S(1)} collective-permute-done((bf16[512,128]{1,0:T(8,128)(2,1)S(1)}, bf16[512,128]{1,0:T(8,128)(2,1)S(1)}, u32[]{:S(2)}, u32[]{:S(2)}) %collective-permute-start.3) | collective-permute-done | bytes 131104 | tf_op jit(solution)/shard_map/ppermute | solution.py:581
  30.7 0.3 collective-permute-done.2
  30.9 0.8 collective-permute-start.4
  31.7 3.4 %collective-permute-start.6 = (bf16[576,512]{1,0:T(8,128)(2,1)}, bf16[576,512]{1,0:T(8,128)(2,1)S(1)}, u32[]{:S(2)}, u32[]{:S(2)}) collective-permute-start(bf16[576,512]{1,0:T(8,128)(2,1)} %collective-permute-done.keys), channel_id=1, source_target_pairs={{0,1},{1,3},{3,2},{2,0},{4,5},{5,7},{7,6},{6,4},{8,9},{9,11},{11,1... | collective-permute-start | bytes 1769480 | tf_op jit(solution)/shard_map/ppermute | solution.py:581
  35.1 3.2 %collective-permute-done.4 = bf16[512,128]{1,0:T(8,128)(2,1)S(1)} collective-permute-done((bf16[512,128]{1,0:T(8,128)(2,1)S(1)}, bf16[512,128]{1,0:T(8,128)(2,1)S(1)}, u32[]{:S(2)}, u32[]{:S(2)}) %collective-permute-start.4) | collective-permute-done | bytes 131104 | tf_op jit(solution)/shard_map/ppermute | solution.py:581
  38.3 1.5 %collective-permute-start.8 = (bf16[2048,128]{1,0:T(8,128)(2,1)S(1)}, bf16[2048,128]{1,0:T(8,128)(2,1)S(1)}, u32[]{:S(2)}, u32[]{:S(2)}) collective-permute-start(bf16[2048,128]{1,0:T(8,128)(2,1)S(1)} %pad_maximum_fusion.own), channel_id=1, source_target_pairs={{0,4},{4,0},{1,5},{5,1},{2,6},{6,2},{3,7},{7,3},{8,12},{12,8},{9,1... | collective-permute-start | bytes 1572872 | tf_op jit(solution)/shard_map/ppermute | solution.py:584
  39.8 1.5 %collective-permute-start.9 = (bf16[64,2176]{1,0:T(8,128)(2,1)S(1)}, bf16[64,2176]{1,0:T(8,128)(2,1)S(1)}, u32[]{:S(2)}, u32[]{:S(2)}) collective-permute-start(bf16[64,2176]{1,0:T(8,128)(2,1)S(1)} %get-tuple-element.74.refs_0_), channel_id=1, source_target_pairs={{0,16},{8,24},{16,0},{24,8},{1,17},{9,25},{17,1},{25,9},{2,18},{10... | collective-permute-start | bytes 835592 | tf_op jit(solution)/shard_map/ppermute | solution.py:587
  41.3 0.8 collective-permute-start.7
  42.1 13.1 %collective-permute-done.7 = f32[16,4224]{1,0:T(8,128)S(1)} collective-permute-done((f32[16,4224]{1,0:T(8,128)S(1)}, f32[16,4224]{1,0:T(8,128)S(1)}, u32[]{:S(2)}, u32[]{:S(2)}) %collective-permute-start.7) | collective-permute-done | bytes 270368 | tf_op jit(solution)/shard_map/ppermute | solution.py:581
  55.3 0.1 collective-permute-start.11
  55.5 3.2 %collective-permute-start.14 = (bf16[576,512]{1,0:T(8,128)(2,1)S(1)}, bf16[576,512]{1,0:T(8,128)(2,1)S(1)}, u32[]{:S(2)}, u32[]{:S(2)}) collective-permute-start(bf16[576,512]{1,0:T(8,128)(2,1)S(1)} %collective-permute-done.6.keys), channel_id=1, source_target_pairs={{0,1},{1,3},{3,2},{2,0},{4,5},{5,7},{7,6},{6,4},{8,9},{9,11},{11,1... | collective-permute-start | bytes 1769480 | tf_op jit(solution)/shard_map/ppermute | solution.py:581
  58.7 0.8 arrange.1
  59.5 2.5 %score.4 = (bf16[16,128,512]{2,1,0:T(8,128)(2,1)S(1)}, f32[16,128]{1,0:T(8,128)S(1)}, f32[16,128]{1,0:T(8,128)S(1)}, f32[16,128]{1,0:T(8,128)S(1)}) custom-call(s32[33]{0:T(128)S(1)} %fusion.info, s32[64]{0:T(128)S(1)} %bitcast.28, bf16[16,64,576]{2,1,0:T(8,128)(2,1)S(1)} %bitcast.34, bf16[16,64,576]{2,1,0:T(8,128)(2,1)S(1)} %collective-permute-done.5.other, ...), custom_call_target="tpu_custom_call" | custom-call | flops 1207959552 | bytes 5046272 | tf_op jit(solution)/shard_map/score/pallas_call | solution.py:211
  62.0 3.1 %score.5 = (bf16[16,128,512]{2,1,0:T(8,128)(2,1)S(1)}, f32[16,128]{1,0:T(8,128)S(1)}, f32[16,128]{1,0:T(8,128)S(1)}, f32[16,128]{1,0:T(8,128)S(1)}) custom-call(s32[33]{0:T(128)S(1)} %fusion.info, s32[64]{0:T(128)S(1)} %bitcast.29, bf16[16,64,576]{2,1,0:T(8,128)(2,1)S(1)} %bitcast.35, bf16[16,64,576]{2,1,0:T(8,128)(2,1)S(1)} %collective-permute-done.5.other, ...), custom_call_target="tpu_custom_call" | custom-call | flops 1207959552 | bytes 5046272 | tf_op jit(solution)/shard_map/score/pallas_call | solution.py:211
  65.1 2.5 %score.6 = (bf16[16,128,512]{2,1,0:T(8,128)(2,1)S(1)}, f32[16,128]{1,0:T(8,128)S(1)}, f32[16,128]{1,0:T(8,128)S(1)}, f32[16,128]{1,0:T(8,128)S(1)}) custom-call(s32[33]{0:T(128)S(1)} %fusion.info, s32[64]{0:T(128)S(1)} %bitcast.30, bf16[16,64,576]{2,1,0:T(8,128)(2,1)S(1)} %bitcast.36, bf16[16,64,576]{2,1,0:T(8,128)(2,1)S(1)} %collective-permute-done.5.other, ...), custom_call_target="tpu_custom_call" | custom-call | flops 1207959552 | bytes 5046272 | tf_op jit(solution)/shard_map/score/pallas_call | solution.py:211
  67.7 1.3 %logits.1.part = f32[2,16,2048]{2,1,0:T(8,128)S(1)} custom-call(f32[16,4224]{1,0:T(8,128)S(1)} %collective-permute-done.12.received, f32[16,4224]{1,0:T(8,128)S(1)} %get-tuple-element.91.here, bf16[2048,128]{1,0:T(8,128)(2,1)S(1)} %pad_maximum_fusion.own, bf16[2048,128]{1,0:T(8,128)(2,1)S(1)} %collective-permute-done.8.other), custom_call_target="tpu_custom_call" | custom-call | flops 536870912 | bytes 1851392 | tf_op jit(solution)/shard_map/logits/pallas_call | solution.py:301
  68.9 1.9 %collective-permute-start.13 = (f32[2,16,2048]{2,1,0:T(8,128)S(1)}, f32[2,16,2048]{2,1,0:T(8,128)S(1)}, u32[]{:S(2)}, u32[]{:S(2)}) collective-permute-start(f32[2,16,2048]{2,1,0:T(8,128)S(1)} %logits.1.part), channel_id=1, source_target_pairs={{0,4},{4,0},{1,5},{5,1},{2,6},{6,2},{3,7},{7,3},{8,12},{12,8},{9,1... | collective-permute-start | bytes 786440 | tf_op jit(solution)/shard_map/ppermute | solution.py:584
  70.8 6.4 %collective-permute-done.13.far = f32[2,16,2048]{2,1,0:T(8,128)S(1)} collective-permute-done((f32[2,16,2048]{2,1,0:T(8,128)S(1)}, f32[2,16,2048]{2,1,0:T(8,128)S(1)}, u32[]{:S(2)}, u32[]{:S(2)}) %collective-permute-start.13) | collective-permute-done | bytes 262176 | tf_op jit(solution)/shard_map/ppermute | solution.py:584
  77.1 0.8 softmax.1
  78.0 2.5 %score.7 = (bf16[16,128,512]{2,1,0:T(8,128)(2,1)S(1)}, f32[16,128]{1,0:T(8,128)S(1)}, f32[16,128]{1,0:T(8,128)S(1)}, f32[16,128]{1,0:T(8,128)S(1)}) custom-call(s32[33]{0:T(128)S(1)} %fusion.info, s32[64]{0:T(128)S(1)} %bitcast.32, bf16[16,64,576]{2,1,0:T(8,128)(2,1)S(1)} %bitcast.37, bf16[16,64,576]{2,1,0:T(8,128)(2,1)S(1)} %collective-permute-done.5.other, ...), custom_call_target="tpu_custom_call" | custom-call | flops 1207959552 | bytes 5046272 | tf_op jit(solution)/shard_map/score/pallas_call | solution.py:211
  80.5 1.8 %collective-permute-start.15 = (f32[2,16,128]{2,1,0:T(8,128)S(1)}, f32[2,16,128]{2,1,0:T(8,128)S(1)}, u32[]{:S(2)}, u32[]{:S(2)}) collective-permute-start(f32[2,16,128]{2,1,0:T(8,128)S(1)} %pad_maximum_fusion.2), channel_id=1, source_target_pairs={{0,4},{4,0},{1,5},{5,1},{2,6},{6,2},{3,7},{7,3},{8,12},{12,8},{9,1... | collective-permute-start | bytes 49160 | tf_op jit(solution)/shard_map/ppermute | solution.py:584
  82.3 2.0 %collective-permute-done.15.refs_10_ = f32[2,16,128]{2,1,0:T(8,128)S(1)} collective-permute-done((f32[2,16,128]{2,1,0:T(8,128)S(1)}, f32[2,16,128]{2,1,0:T(8,128)S(1)}, u32[]{:S(2)}, u32[]{:S(2)}) %collective-permute-start.15) | collective-permute-done | bytes 16416 | tf_op jit(solution)/shard_map/ppermute | solution.py:584
  84.3 2.2 %delta.1 = (f32[16,2048]{1,0:T(8,128)S(1)}, bf16[16,2048]{1,0:T(8,128)(2,1)S(1)}) custom-call(bf16[16,128,512]{2,1,0:T(8,128)(2,1)S(1)} %get-tuple-element.99.refs_0_, bf16[16,128,512]{2,1,0:T(8,128)(2,1)S(1)} %get-tuple-element.100.refs_1_, bf16[16,128,512]{2,1,0:T(8,128)(2,1)S(1)} %get-tuple-element.101.refs_2_, ...), custom_call_target="tpu_custom_call" | custom-call | flops 8388608 | bytes 8388608 | tf_op jit(solution)/shard_map/delta/pallas_call | solution.py:258
  86.5 1.8 %collective-permute-start.16 = (bf16[16,2048]{1,0:T(8,128)(2,1)S(1)}, bf16[16,2048]{1,0:T(8,128)(2,1)S(1)}, u32[]{:S(2)}, u32[]{:S(2)}) collective-permute-start(bf16[16,2048]{1,0:T(8,128)(2,1)S(1)} %get-tuple-element.112.sent), channel_id=1, source_target_pairs={{0,4},{4,0},{1,5},{5,1},{2,6},{6,2},{3,7},{7,3},{8,12},{12,8},{9,1... | collective-permute-start | bytes 196616 | tf_op jit(solution)/shard_map/ppermute | solution.py:584
  88.3 2.5 %collective-permute-done.16.brought = bf16[16,2048]{1,0:T(8,128)(2,1)S(1)} collective-permute-done((bf16[16,2048]{1,0:T(8,128)(2,1)S(1)}, bf16[16,2048]{1,0:T(8,128)(2,1)S(1)}, u32[]{:S(2)}, u32[]{:S(2)}) %collective-permute-start.16) | collective-permute-done | bytes 65568 | tf_op jit(solution)/shard_map/ppermute | solution.py:584
  90.8 2.7 %gradient.1 = bf16[16,4224]{1,0:T(8,128)(2,1)S(1)} custom-call(f32[16,4224]{1,0:T(8,128)S(1)} %collective-permute-done.12.received, f32[16,4224]{1,0:T(8,128)S(1)} %get-tuple-element.91.here, bf16[2048,128]{1,0:T(8,128)(2,1)S(1)} %pad_maximum_fusion.own, bf16[2048,128]{1,0:T(8,128)(2,1)S(1)} %collective-permute-done.8.other, ...), custom_call_target="tpu_custom_call" | custom-call | flops 1073741824 | bytes 2375680 | tf_op jit(solution)/shard_map/gradient/pallas_call | solution.py:452
  93.5 1.6 %collective-permute-start.20 = (bf16[1,16,4224]{2,1,0:T(8,128)(2,1)S(1)}, bf16[1,16,4224]{2,1,0:T(8,128)(2,1)S(1)}, u32[]{:S(2)}, u32[]{:S(2)}) collective-permute-start(bf16[1,16,4224]{2,1,0:T(8,128)(2,1)S(1)} %bitcast.19), channel_id=1, source_target_pairs={{0,16},{8,24},{16,0},{24,8},{1,17},{9,25},{17,1},{25,9},{2,18},{10... | collective-permute-start | bytes 405512 | tf_op jit(solution)/shard_map/ppermute | solution.py:587
  95.1 2.5 %collective-permute-start.19 = (bf16[1,16,4224]{2,1,0:T(8,128)(2,1)S(1)}, bf16[1,16,4224]{2,1,0:T(8,128)(2,1)S(1)}, u32[]{:S(2)}, u32[]{:S(2)}) collective-permute-start(bf16[1,16,4224]{2,1,0:T(8,128)(2,1)S(1)} %bitcast.20), channel_id=1, source_target_pairs={{0,3},{1,0},{2,1},{3,2},{4,7},{5,4},{6,5},{7,6},{8,11},{9,8},{10,9... | collective-permute-start | bytes 405512 | tf_op jit(solution)/shard_map/ppermute | solution.py:675
  97.6 0.6 collective-permute-start.17
  98.1 0.4 collective-permute-done.20.refs_1_
  98.7 3.7 %collective-permute-done.19 = bf16[1,16,4224]{2,1,0:T(8,128)(2,1)S(1)} collective-permute-done((bf16[1,16,4224]{2,1,0:T(8,128)(2,1)S(1)}, bf16[1,16,4224]{2,1,0:T(8,128)(2,1)S(1)}, u32[]{:S(2)}, u32[]{:S(2)}) %collective-permute-start.19) | collective-permute-done | bytes 135200 | tf_op jit(solution)/shard_map/ppermute | solution.py:675
  102.4 4.8 %collective-permute-done.18 = bf16[1,16,4224]{2,1,0:T(8,128)(2,1)S(1)} collective-permute-done((bf16[1,16,4224]{2,1,0:T(8,128)(2,1)S(1)}, bf16[1,16,4224]{2,1,0:T(8,128)(2,1)S(1)}, u32[]{:S(2)}, u32[]{:S(2)}) %collective-permute-start.18) | collective-permute-done | bytes 135200 | tf_op jit(solution)/shard_map/ppermute | solution.py:675
  107.2 0.6 collective-permute-start.23
  107.8 9.1 %collective-permute-done.23.refs_5_ = bf16[3,16,4224]{2,1,0:T(8,128)(2,1)S(1)} collective-permute-done((bf16[3,16,4224]{2,1,0:T(8,128)(2,1)S(1)}, bf16[3,16,4224]{2,1,0:T(8,128)(2,1)S(1)}, u32[]{:S(2)}, u32[]{:S(2)}) %collective-permute-start.23) | collective-permute-done | bytes 405536 | tf_op jit(solution)/shard_map/ppermute | solution.py:587
  116.9 1.7 %collective-permute-done.25.refs_7_ = bf16[3,16,4224]{2,1,0:T(8,128)(2,1)S(1)} collective-permute-done((bf16[3,16,4224]{2,1,0:T(8,128)(2,1)S(1)}, bf16[3,16,4224]{2,1,0:T(8,128)(2,1)S(1)}, u32[]{:S(2)}, u32[]{:S(2)}) %collective-permute-start.25) | collective-permute-done | bytes 405536 | tf_op jit(solution)/shard_map/ppermute | solution.py:587
  118.6 4.4 %outer.1 = (f32[384,4096]{1,0:T(8,128)}, f32[32,1792]{1,0:T(8,128)}, f32[1,64]{1,0:T(1,128)}) custom-call(s32[33]{0:T(128)S(1)} %fusion.info, bf16[384,256]{1,0:T(8,128)(2,1)S(1)} %get-tuple-element.79.latents, bf16[256,1792]{1,0:T(8,128)(2,1)S(1)} %get-tuple-element.80.hiddens, bf16[1,16,4224]{2,1,0:T(8,128)(2,1)S(1)} %bitcast.24, ...), custom_call_target="tpu_custom_call" | custom-call | flops 805306368 | bytes 8388608 | tf_op jit(solution)/shard_map/outer/pallas_call | solution.py:539
  (40 shorter events, 0.4 us)
Async XLA Ops:
  0.6 3.0 %copy-start = (bf16[1,1024,576]{1,2,0:T(8,128)(2,1)S(1)}, bf16[1,1024,576]{1,2,0:T(8,128)(2,1)}, u32[]{:S(2)}) copy-start(bf16[1,1024,576]{1,2,0:T(8,128)(2,1)} %param.12) | copy-start | bytes 3538948
  0.6 37.6 %collective-permute-start.5 = (bf16[16,64,576]{2,1,0:T(8,128)(2,1)}, bf16[16,64,576]{2,1,0:T(8,128)(2,1)S(1)}, u32[]{:S(2)}, u32[]{:S(2)}) collective-permute-start(bf16[16,64,576]{2,1,0:T(8,128)(2,1)} %bitcast.33), channel_id=1, source_target_pairs={{0,4},{4,0},{1,5},{5,1},{2,6},{6,2},{3,7},{7,3},{8,12},{12,8},{9,1... | collective-permute-start | bytes 3538952 | tf_op jit(solution)/shard_map/ppermute | solution.py:584
  3.7 27.2 %collective-permute-start = (bf16[576,512]{1,0:T(8,128)(2,1)S(1)}, bf16[576,512]{1,0:T(8,128)(2,1)}, u32[]{:S(2)}, u32[]{:S(2)}) collective-permute-start(bf16[576,512]{1,0:T(8,128)(2,1)S(1)} %dynamic-slice_bitcast_fusion.keys), channel_id=1, source_target_pairs={{0,1},{1,3},{3,2},{2,0},{4,5},{5,7},{7,6},{6,4},{8,9},{9,11},{11,1... | collective-permute-start | bytes 1769480 | tf_op jit(solution)/shard_map/ppermute | solution.py:581
  6.0 1.9 %copy-start.1 = (bf16[384,4096]{1,0:T(8,128)(2,1)S(1)}, bf16[384,4096]{1,0:T(8,128)(2,1)}, u32[]{:S(2)}) copy-start(bf16[384,4096]{1,0:T(8,128)(2,1)} %weight.1) | copy-start | bytes 9437188
  7.9 1.2 copy-start.2
  9.1 0.9 copy-start.3
  10.0 0.9 copy-start.4
  10.9 4.0 %copy-start.7 = (bf16[1,1024,128]{2,1,0:T(8,128)(2,1)S(1)}, bf16[1,1024,128]{2,1,0:T(8,128)(2,1)}, u32[]{:S(2)}) copy-start(bf16[1,1024,128]{2,1,0:T(8,128)(2,1)} %param.13) | copy-start | bytes 786436
  12.2 47.2 %copy-start.5 = (s32[1,64]{1,0:T(1,128)S(1)}, s32[1,64]{1,0:T(1,128)}, u32[]{:S(2)}) copy-start(s32[1,64]{1,0:T(1,128)} %param.14) | copy-start | bytes 772
  12.3 47.2 %copy-start.6 = (bf16[1,16,64,576]{3,2,1,0:T(8,128)(2,1)S(1)}, bf16[1,16,64,576]{3,2,1,0:T(8,128)(2,1)}, u32[]{:S(2)}) copy-start(bf16[1,16,64,576]{3,2,1,0:T(8,128)(2,1)} %param.11) | copy-start | bytes 3538948
  12.3 16.1 %collective-permute-start.1 = (f32[16,4224]{1,0:T(8,128)S(1)}, f32[16,4224]{1,0:T(8,128)S(1)}, u32[]{:S(2)}, u32[]{:S(2)}) collective-permute-start(f32[16,4224]{1,0:T(8,128)S(1)} %get-tuple-element.62), channel_id=1, source_target_pairs={{0,1},{1,3},{3,2},{2,0},{4,5},{5,7},{7,6},{6,4},{8,9},{9,11},{11,1... | collective-permute-start | bytes 811016 | tf_op jit(solution)/shard_map/ppermute | solution.py:581
  14.9 15.7 %collective-permute-start.3 = (bf16[512,128]{1,0:T(8,128)(2,1)S(1)}, bf16[512,128]{1,0:T(8,128)(2,1)S(1)}, u32[]{:S(2)}, u32[]{:S(2)}) collective-permute-start(bf16[512,128]{1,0:T(8,128)(2,1)S(1)} %dynamic-slice_bitcast_fusion.1), channel_id=1, source_target_pairs={{0,2},{1,0},{3,1},{2,3},{4,6},{5,4},{7,5},{6,7},{8,10},{9,8},{11,9... | collective-permute-start | bytes 393224 | tf_op jit(solution)/shard_map/ppermute | solution.py:581
  15.3 15.6 %collective-permute-start.2 = (bf16[512,128]{1,0:T(8,128)(2,1)S(1)}, bf16[512,128]{1,0:T(8,128)(2,1)S(1)}, u32[]{:S(2)}, u32[]{:S(2)}) collective-permute-start(bf16[512,128]{1,0:T(8,128)(2,1)S(1)} %dynamic-slice_bitcast_fusion.1), channel_id=1, source_target_pairs={{0,1},{1,3},{3,2},{2,0},{4,5},{5,7},{7,6},{6,4},{8,9},{9,11},{11,1... | collective-permute-start | bytes 393224 | tf_op jit(solution)/shard_map/ppermute | solution.py:581
  30.9 7.3 %collective-permute-start.4 = (bf16[512,128]{1,0:T(8,128)(2,1)S(1)}, bf16[512,128]{1,0:T(8,128)(2,1)S(1)}, u32[]{:S(2)}, u32[]{:S(2)}) collective-permute-start(bf16[512,128]{1,0:T(8,128)(2,1)S(1)} %collective-permute-done.2), channel_id=1, source_target_pairs={{0,1},{1,3},{3,2},{2,0},{4,5},{5,7},{7,6},{6,4},{8,9},{9,11},{11,1... | collective-permute-start | bytes 393224 | tf_op jit(solution)/shard_map/ppermute | solution.py:581
  31.7 23.6 %collective-permute-start.6 = (bf16[576,512]{1,0:T(8,128)(2,1)}, bf16[576,512]{1,0:T(8,128)(2,1)S(1)}, u32[]{:S(2)}, u32[]{:S(2)}) collective-permute-start(bf16[576,512]{1,0:T(8,128)(2,1)} %collective-permute-done.keys), channel_id=1, source_target_pairs={{0,1},{1,3},{3,2},{2,0},{4,5},{5,7},{7,6},{6,4},{8,9},{9,11},{11,1... | collective-permute-start | bytes 1769480 | tf_op jit(solution)/shard_map/ppermute | solution.py:581
  38.3 17.0 %collective-permute-start.8 = (bf16[2048,128]{1,0:T(8,128)(2,1)S(1)}, bf16[2048,128]{1,0:T(8,128)(2,1)S(1)}, u32[]{:S(2)}, u32[]{:S(2)}) collective-permute-start(bf16[2048,128]{1,0:T(8,128)(2,1)S(1)} %pad_maximum_fusion.own), channel_id=1, source_target_pairs={{0,4},{4,0},{1,5},{5,1},{2,6},{6,2},{3,7},{7,3},{8,12},{12,8},{9,1... | collective-permute-start | bytes 1572872 | tf_op jit(solution)/shard_map/ppermute | solution.py:584
  39.8 15.4 %collective-permute-start.10 = (bf16[64,2176]{1,0:T(8,128)(2,1)S(1)}, bf16[64,2176]{1,0:T(8,128)(2,1)S(1)}, u32[]{:S(2)}, u32[]{:S(2)}) collective-permute-start(bf16[64,2176]{1,0:T(8,128)(2,1)S(1)} %get-tuple-element.74.refs_0_), channel_id=1, source_target_pairs={{0,8},{8,0},{16,24},{24,16},{1,9},{9,1},{17,25},{25,17},{2,10},{10... | collective-permute-start | bytes 835592 | tf_op jit(solution)/shard_map/ppermute | solution.py:587
  39.8 15.4 %collective-permute-start.9 = (bf16[64,2176]{1,0:T(8,128)(2,1)S(1)}, bf16[64,2176]{1,0:T(8,128)(2,1)S(1)}, u32[]{:S(2)}, u32[]{:S(2)}) collective-permute-start(bf16[64,2176]{1,0:T(8,128)(2,1)S(1)} %get-tuple-element.74.refs_0_), channel_id=1, source_target_pairs={{0,16},{8,24},{16,0},{24,8},{1,17},{9,25},{17,1},{25,9},{2,18},{10... | collective-permute-start | bytes 835592 | tf_op jit(solution)/shard_map/ppermute | solution.py:587
  41.3 13.9 %collective-permute-start.7 = (f32[16,4224]{1,0:T(8,128)S(1)}, f32[16,4224]{1,0:T(8,128)S(1)}, u32[]{:S(2)}, u32[]{:S(2)}) collective-permute-start(f32[16,4224]{1,0:T(8,128)S(1)} %add.24), channel_id=1, source_target_pairs={{0,1},{1,3},{3,2},{2,0},{4,5},{5,7},{7,6},{6,4},{8,9},{9,11},{11,1... | collective-permute-start | bytes 811016 | tf_op jit(solution)/shard_map/ppermute | solution.py:581
  55.3 3.4 %collective-permute-start.11 = (bf16[64,2176]{1,0:T(8,128)(2,1)S(1)}, bf16[64,2176]{1,0:T(8,128)(2,1)S(1)}, u32[]{:S(2)}, u32[]{:S(2)}) collective-permute-start(bf16[64,2176]{1,0:T(8,128)(2,1)S(1)} %collective-permute-done.9.refs_1_), channel_id=1, source_target_pairs={{0,8},{8,0},{16,24},{24,16},{1,9},{9,1},{17,25},{25,17},{2,10},{10... | collective-permute-start | bytes 835592 | tf_op jit(solution)/shard_map/ppermute | solution.py:587
  55.4 12.3 %collective-permute-start.12 = (f32[16,4224]{1,0:T(8,128)S(1)}, f32[16,4224]{1,0:T(8,128)S(1)}, u32[]{:S(2)}, u32[]{:S(2)}) collective-permute-start(f32[16,4224]{1,0:T(8,128)S(1)} %add.25), channel_id=1, source_target_pairs={{0,1},{1,3},{3,2},{2,0},{4,5},{5,7},{7,6},{6,4},{8,9},{9,11},{11,1... | collective-permute-start | bytes 811016 | tf_op jit(solution)/shard_map/ppermute | solution.py:581
  55.5 22.5 %collective-permute-start.14 = (bf16[576,512]{1,0:T(8,128)(2,1)S(1)}, bf16[576,512]{1,0:T(8,128)(2,1)S(1)}, u32[]{:S(2)}, u32[]{:S(2)}) collective-permute-start(bf16[576,512]{1,0:T(8,128)(2,1)S(1)} %collective-permute-done.6.keys), channel_id=1, source_target_pairs={{0,1},{1,3},{3,2},{2,0},{4,5},{5,7},{7,6},{6,4},{8,9},{9,11},{11,1... | collective-permute-start | bytes 1769480 | tf_op jit(solution)/shard_map/ppermute | solution.py:581
  68.9 8.2 %collective-permute-start.13 = (f32[2,16,2048]{2,1,0:T(8,128)S(1)}, f32[2,16,2048]{2,1,0:T(8,128)S(1)}, u32[]{:S(2)}, u32[]{:S(2)}) collective-permute-start(f32[2,16,2048]{2,1,0:T(8,128)S(1)} %logits.1.part), channel_id=1, source_target_pairs={{0,4},{4,0},{1,5},{5,1},{2,6},{6,2},{3,7},{7,3},{8,12},{12,8},{9,1... | collective-permute-start | bytes 786440 | tf_op jit(solution)/shard_map/ppermute | solution.py:584
  80.5 3.8 %collective-permute-start.15 = (f32[2,16,128]{2,1,0:T(8,128)S(1)}, f32[2,16,128]{2,1,0:T(8,128)S(1)}, u32[]{:S(2)}, u32[]{:S(2)}) collective-permute-start(f32[2,16,128]{2,1,0:T(8,128)S(1)} %pad_maximum_fusion.2), channel_id=1, source_target_pairs={{0,4},{4,0},{1,5},{5,1},{2,6},{6,2},{3,7},{7,3},{8,12},{12,8},{9,1... | collective-permute-start | bytes 49160 | tf_op jit(solution)/shard_map/ppermute | solution.py:584
  86.5 4.3 %collective-permute-start.16 = (bf16[16,2048]{1,0:T(8,128)(2,1)S(1)}, bf16[16,2048]{1,0:T(8,128)(2,1)S(1)}, u32[]{:S(2)}, u32[]{:S(2)}) collective-permute-start(bf16[16,2048]{1,0:T(8,128)(2,1)S(1)} %get-tuple-element.112.sent), channel_id=1, source_target_pairs={{0,4},{4,0},{1,5},{5,1},{2,6},{6,2},{3,7},{7,3},{8,12},{12,8},{9,1... | collective-permute-start | bytes 196616 | tf_op jit(solution)/shard_map/ppermute | solution.py:584
  93.5 5.1 %collective-permute-start.20 = (bf16[1,16,4224]{2,1,0:T(8,128)(2,1)S(1)}, bf16[1,16,4224]{2,1,0:T(8,128)(2,1)S(1)}, u32[]{:S(2)}, u32[]{:S(2)}) collective-permute-start(bf16[1,16,4224]{2,1,0:T(8,128)(2,1)S(1)} %bitcast.19), channel_id=1, source_target_pairs={{0,16},{8,24},{16,0},{24,8},{1,17},{9,25},{17,1},{25,9},{2,18},{10... | collective-permute-start | bytes 405512 | tf_op jit(solution)/shard_map/ppermute | solution.py:587
  95.1 7.3 %collective-permute-start.19 = (bf16[1,16,4224]{2,1,0:T(8,128)(2,1)S(1)}, bf16[1,16,4224]{2,1,0:T(8,128)(2,1)S(1)}, u32[]{:S(2)}, u32[]{:S(2)}) collective-permute-start(bf16[1,16,4224]{2,1,0:T(8,128)(2,1)S(1)} %bitcast.20), channel_id=1, source_target_pairs={{0,3},{1,0},{2,1},{3,2},{4,7},{5,4},{6,5},{7,6},{8,11},{9,8},{10,9... | collective-permute-start | bytes 405512 | tf_op jit(solution)/shard_map/ppermute | solution.py:675
  97.6 9.6 %collective-permute-start.18 = (bf16[1,16,4224]{2,1,0:T(8,128)(2,1)S(1)}, bf16[1,16,4224]{2,1,0:T(8,128)(2,1)S(1)}, u32[]{:S(2)}, u32[]{:S(2)}) collective-permute-start(bf16[1,16,4224]{2,1,0:T(8,128)(2,1)S(1)} %bitcast.21), channel_id=1, source_target_pairs={{0,2},{1,3},{2,0},{3,1},{4,6},{5,7},{6,4},{7,5},{8,10},{9,11},{10,... | collective-permute-start | bytes 405512 | tf_op jit(solution)/shard_map/ppermute | solution.py:675
  97.6 9.6 %collective-permute-start.17 = (bf16[1,16,4224]{2,1,0:T(8,128)(2,1)S(1)}, bf16[1,16,4224]{2,1,0:T(8,128)(2,1)S(1)}, u32[]{:S(2)}, u32[]{:S(2)}) collective-permute-start(bf16[1,16,4224]{2,1,0:T(8,128)(2,1)S(1)} %bitcast.22), channel_id=1, source_target_pairs={{0,1},{1,2},{2,3},{3,0},{4,5},{5,6},{6,7},{7,4},{8,9},{9,10},{10,1... | collective-permute-start | bytes 405512 | tf_op jit(solution)/shard_map/ppermute | solution.py:675
  98.1 9.1 %collective-permute-start.21 = (bf16[1,16,4224]{2,1,0:T(8,128)(2,1)S(1)}, bf16[1,16,4224]{2,1,0:T(8,128)(2,1)S(1)}, u32[]{:S(2)}, u32[]{:S(2)}) collective-permute-start(bf16[1,16,4224]{2,1,0:T(8,128)(2,1)S(1)} %bitcast.23), channel_id=1, source_target_pairs={{0,8},{8,0},{16,24},{24,16},{1,9},{9,1},{17,25},{25,17},{2,10},{10... | collective-permute-start | bytes 405512 | tf_op jit(solution)/shard_map/ppermute | solution.py:587
  98.6 8.6 %collective-permute-start.22 = (bf16[1,16,4224]{2,1,0:T(8,128)(2,1)S(1)}, bf16[1,16,4224]{2,1,0:T(8,128)(2,1)S(1)}, u32[]{:S(2)}, u32[]{:S(2)}) collective-permute-start(bf16[1,16,4224]{2,1,0:T(8,128)(2,1)S(1)} %collective-permute-done.20.refs_1_), channel_id=1, source_target_pairs={{0,8},{8,0},{16,24},{24,16},{1,9},{9,1},{17,25},{25,17},{2,10},{10... | collective-permute-start | bytes 405512 | tf_op jit(solution)/shard_map/ppermute | solution.py:587
  107.2 9.7 %collective-permute-start.23 = (bf16[3,16,4224]{2,1,0:T(8,128)(2,1)S(1)}, bf16[3,16,4224]{2,1,0:T(8,128)(2,1)S(1)}, u32[]{:S(2)}, u32[]{:S(2)}) collective-permute-start(bf16[3,16,4224]{2,1,0:T(8,128)(2,1)S(1)} %pad_maximum_fusion.1.refs_4_), channel_id=1, source_target_pairs={{0,16},{8,24},{16,0},{24,8},{1,17},{9,25},{17,1},{25,9},{2,18},{10... | collective-permute-start | bytes 1216520 | tf_op jit(solution)/shard_map/ppermute | solution.py:587
  107.8 9.1 %collective-permute-start.24 = (bf16[3,16,4224]{2,1,0:T(8,128)(2,1)S(1)}, bf16[3,16,4224]{2,1,0:T(8,128)(2,1)S(1)}, u32[]{:S(2)}, u32[]{:S(2)}) collective-permute-start(bf16[3,16,4224]{2,1,0:T(8,128)(2,1)S(1)} %pad_maximum_fusion.1.refs_4_), channel_id=1, source_target_pairs={{0,8},{8,0},{16,24},{24,16},{1,9},{9,1},{17,25},{25,17},{2,10},{10... | collective-permute-start | bytes 1216520 | tf_op jit(solution)/shard_map/ppermute | solution.py:587
  116.9 1.7 %collective-permute-start.25 = (bf16[3,16,4224]{2,1,0:T(8,128)(2,1)S(1)}, bf16[3,16,4224]{2,1,0:T(8,128)(2,1)S(1)}, u32[]{:S(2)}, u32[]{:S(2)}) collective-permute-start(bf16[3,16,4224]{2,1,0:T(8,128)(2,1)S(1)} %collective-permute-done.23.refs_5_), channel_id=1, source_target_pairs={{0,8},{8,0},{16,24},{24,16},{1,9},{9,1},{17,25},{25,17},{2,10},{10... | collective-permute-start | bytes 1216520 | tf_op jit(solution)/shard_map/ppermute | solution.py:587

commit v14 on v13

--- a/solution.py
+++ b/solution.py
@@ -650,9 +650,10 @@
     before, received = lax.optimization_barrier((before, received))
 
     part = make_logits(heads_here, received, parts[n - 1], index_own, index_other)
-    probs, log_probs = make_softmax(n, info, sequence_positions, part, swap_head(part))
-
-    before, probs, log_probs = lax.optimization_barrier((before, probs, log_probs))
+    far = swap_head(part)
+    before, far = lax.optimization_barrier((before, far))
+    probs, log_probs = make_softmax(n, info, sequence_positions, part, far)
+
     score_next(keys_mine[n - 1])
     delta_own, sent = make_delta(weights, tops, *before, swap_head(jnp.stack(before)), probs)
     piece = gradients(

time: 124 us -> 124 us (level)
  transfers between devices with their start and end apart: 26 -> 26, of which waited for: 13 -> 14; matrix products, arithmetic and copies ran while one was open for 1% -> 1% of each run, Pallas kernels for 10% -> 10%
where the time goes in v14:
time: 124 us
  waiting for transfers between devices  62 us (50%)
  starting transfers between devices  30.7 us (25%)
  Pallas kernels  24 us (19%)
  local copies, waits for them, and re-layouts  5.66 us (5%)
    ppermute x9, waiting for transfers between devices, onward(): lax.ppermute(x, 'ctx', [(ring[k], ring[(k + t) % n]) for k in range(n)])  30.8 us
    ppermute x9, starting transfers between devices, onward(): lax.ppermute(x, 'ctx', [(ring[k], ring[(k + t) % n]) for k in range(n)])  14.6 us
    ppermute x9, waiting for transfers between devices, swap_dp(): return lax.ppermute(x, 'dp', [(k, k ^ bit) for k in range(dp_size)])  11.4 us
    ppermute x5, waiting for transfers between devices, swap_head(): return lax.ppermute(x, 'head', [(0, 1), (1, 0)])  11.2 us
    pallas_call x4, Pallas kernels, score(): pl.pallas_call(functools.partial(score_kernel, t, 1 + n + t), out_shape=(...  10.7 us
    ppermute x5, starting transfers between devices, swap_head(): return lax.ppermute(x, 'head', [(0, 1), (1, 0)])  8.88 us
    ppermute x3, waiting for transfers between devices, per_device(): brought.append(lax.ppermute(piece, 'ctx', pairs))  8.5 us
    unnamed x16, local copies, waits for them, and re-layouts  4.92 us
  transfers between devices with their start and end apart: 26, of which 14 were waited for; matrix products, arithmetic and copies ran while one was open for 1% of the time, Pallas kernels for 10%

profile of v14, /device:TPU:0, one launch (start us, length us, event | category | flops | bytes accessed | tf_op | source)
XLA Modules:
  0.0 123.5 jit_solution(611594980388909924)
XLA Ops:
  0.6 3.0 %collective-permute-start.5 = (bf16[16,64,576]{2,1,0:T(8,128)(2,1)}, bf16[16,64,576]{2,1,0:T(8,128)(2,1)S(1)}, u32[]{:S(2)}, u32[]{:S(2)}) collective-permute-start(bf16[16,64,576]{2,1,0:T(8,128)(2,1)} %bitcast.33), channel_id=1, source_target_pairs={{0,4},{4,0},{1,5},{5,1},{2,6},{6,2},{3,7},{7,3},{8,12},{12,8},{9,1... | collective-permute-start | bytes 3538952 | tf_op jit(solution)/shard_map/ppermute | solution.py:584
  3.7 1.6 %collective-permute-start = (bf16[576,512]{1,0:T(8,128)(2,1)S(1)}, bf16[576,512]{1,0:T(8,128)(2,1)}, u32[]{:S(2)}, u32[]{:S(2)}) collective-permute-start(bf16[576,512]{1,0:T(8,128)(2,1)S(1)} %dynamic-slice_bitcast_fusion.keys), channel_id=1, source_target_pairs={{0,1},{1,3},{3,2},{2,0},{4,5},{5,7},{7,6},{6,4},{8,9},{9,11},{11,1... | collective-permute-start | bytes 1769480 | tf_op jit(solution)/shard_map/ppermute | solution.py:581
  5.4 0.7 fusion.info
  6.1 1.9 %copy-done.1 = bf16[384,4096]{1,0:T(8,128)(2,1)S(1)} copy-done((bf16[384,4096]{1,0:T(8,128)(2,1)S(1)}, bf16[384,4096]{1,0:T(8,128)(2,1)}, u32[]{:S(2)}) %copy-start.1) | copy-done | bytes 3145752
  7.9 1.2 copy-done.2
  9.1 0.9 copy-done.3
  10.0 0.9 copy-done.4
  10.9 1.3 %project.1 = (f32[16,4224]{1,0:T(8,128)S(1)}, f32[16,4224]{1,0:T(8,128)S(1)}, f32[16,4224]{1,0:T(8,128)S(1)}, f32[16,4224]{1,0:T(8,128)S(1)}, bf16[64,2176]{1,0:T(8,128)(2,1)S(1)}) custom-call(s32[33]{0:T(128)S(1)} %fusion.info, bf16[64,1536]{1,0:T(8,128)(2,1)S(1)} %bitcast.18, bf16[384,4096]{1,0:T(8,128)(2,1)S(1)} %copy-done.1, ...), custom_call_target="tpu_custom_call" | custom-call | flops 201326592 | bytes 3145728 | tf_op jit(solution)/shard_map/project/pallas_call | solution.py:111
  12.3 2.7 %collective-permute-start.1 = (f32[16,4224]{1,0:T(8,128)S(1)}, f32[16,4224]{1,0:T(8,128)S(1)}, u32[]{:S(2)}, u32[]{:S(2)}) collective-permute-start(f32[16,4224]{1,0:T(8,128)S(1)} %get-tuple-element.61), channel_id=1, source_target_pairs={{0,1},{1,3},{3,2},{2,0},{4,5},{5,7},{7,6},{6,4},{8,9},{9,11},{11,1... | collective-permute-start | bytes 811016 | tf_op jit(solution)/shard_map/ppermute | solution.py:581
  14.9 0.4 collective-permute-start.3
  15.3 1.7 %collective-permute-start.2 = (bf16[512,128]{1,0:T(8,128)(2,1)S(1)}, bf16[512,128]{1,0:T(8,128)(2,1)S(1)}, u32[]{:S(2)}, u32[]{:S(2)}) collective-permute-start(bf16[512,128]{1,0:T(8,128)(2,1)S(1)} %dynamic-slice_bitcast_fusion.1), channel_id=1, source_target_pairs={{0,1},{1,3},{3,2},{2,0},{4,5},{5,7},{7,6},{6,4},{8,9},{9,11},{11,1... | collective-permute-start | bytes 393224 | tf_op jit(solution)/shard_map/ppermute | solution.py:581
  17.0 11.3 %collective-permute-done.1 = f32[16,4224]{1,0:T(8,128)S(1)} collective-permute-done((f32[16,4224]{1,0:T(8,128)S(1)}, f32[16,4224]{1,0:T(8,128)S(1)}, u32[]{:S(2)}, u32[]{:S(2)}) %collective-permute-start.1) | collective-permute-done | bytes 270368 | tf_op jit(solution)/shard_map/ppermute | solution.py:581
  28.4 2.3 %collective-permute-done.3 = bf16[512,128]{1,0:T(8,128)(2,1)S(1)} collective-permute-done((bf16[512,128]{1,0:T(8,128)(2,1)S(1)}, bf16[512,128]{1,0:T(8,128)(2,1)S(1)}, u32[]{:S(2)}, u32[]{:S(2)}) %collective-permute-start.3) | collective-permute-done | bytes 131104 | tf_op jit(solution)/shard_map/ppermute | solution.py:581
  30.7 0.3 collective-permute-done.2
  30.9 0.8 collective-permute-start.4
  31.7 3.4 %collective-permute-start.6 = (bf16[576,512]{1,0:T(8,128)(2,1)}, bf16[576,512]{1,0:T(8,128)(2,1)S(1)}, u32[]{:S(2)}, u32[]{:S(2)}) collective-permute-start(bf16[576,512]{1,0:T(8,128)(2,1)} %collective-permute-done.keys), channel_id=1, source_target_pairs={{0,1},{1,3},{3,2},{2,0},{4,5},{5,7},{7,6},{6,4},{8,9},{9,11},{11,1... | collective-permute-start | bytes 1769480 | tf_op jit(solution)/shard_map/ppermute | solution.py:581
  35.1 3.2 %collective-permute-done.4 = bf16[512,128]{1,0:T(8,128)(2,1)S(1)} collective-permute-done((bf16[512,128]{1,0:T(8,128)(2,1)S(1)}, bf16[512,128]{1,0:T(8,128)(2,1)S(1)}, u32[]{:S(2)}, u32[]{:S(2)}) %collective-permute-start.4) | collective-permute-done | bytes 131104 | tf_op jit(solution)/shard_map/ppermute | solution.py:581
  38.3 1.5 %collective-permute-start.8 = (bf16[2048,128]{1,0:T(8,128)(2,1)S(1)}, bf16[2048,128]{1,0:T(8,128)(2,1)S(1)}, u32[]{:S(2)}, u32[]{:S(2)}) collective-permute-start(bf16[2048,128]{1,0:T(8,128)(2,1)S(1)} %pad_maximum_fusion.own), channel_id=1, source_target_pairs={{0,4},{4,0},{1,5},{5,1},{2,6},{6,2},{3,7},{7,3},{8,12},{12,8},{9,1... | collective-permute-start | bytes 1572872 | tf_op jit(solution)/shard_map/ppermute | solution.py:584
  39.8 1.5 %collective-permute-start.9 = (bf16[64,2176]{1,0:T(8,128)(2,1)S(1)}, bf16[64,2176]{1,0:T(8,128)(2,1)S(1)}, u32[]{:S(2)}, u32[]{:S(2)}) collective-permute-start(bf16[64,2176]{1,0:T(8,128)(2,1)S(1)} %get-tuple-element.73.refs_0_), channel_id=1, source_target_pairs={{0,16},{8,24},{16,0},{24,8},{1,17},{9,25},{17,1},{25,9},{2,18},{10... | collective-permute-start | bytes 835592 | tf_op jit(solution)/shard_map/ppermute | solution.py:587
  41.3 0.8 collective-permute-start.7
  42.1 13.1 %collective-permute-done.7 = f32[16,4224]{1,0:T(8,128)S(1)} collective-permute-done((f32[16,4224]{1,0:T(8,128)S(1)}, f32[16,4224]{1,0:T(8,128)S(1)}, u32[]{:S(2)}, u32[]{:S(2)}) %collective-permute-start.7) | collective-permute-done | bytes 270368 | tf_op jit(solution)/shard_map/ppermute | solution.py:581
  55.5 3.2 %collective-permute-start.14 = (bf16[576,512]{1,0:T(8,128)(2,1)S(1)}, bf16[576,512]{1,0:T(8,128)(2,1)S(1)}, u32[]{:S(2)}, u32[]{:S(2)}) collective-permute-start(bf16[576,512]{1,0:T(8,128)(2,1)S(1)} %collective-permute-done.6.keys), channel_id=1, source_target_pairs={{0,1},{1,3},{3,2},{2,0},{4,5},{5,7},{7,6},{6,4},{8,9},{9,11},{11,1... | collective-permute-start | bytes 1769480 | tf_op jit(solution)/shard_map/ppermute | solution.py:581
  58.7 0.8 arrange.1
  59.5 2.5 %score.4 = (bf16[16,128,512]{2,1,0:T(8,128)(2,1)S(1)}, f32[16,128]{1,0:T(8,128)S(1)}, f32[16,128]{1,0:T(8,128)S(1)}, f32[16,128]{1,0:T(8,128)S(1)}) custom-call(s32[33]{0:T(128)S(1)} %fusion.info, s32[64]{0:T(128)S(1)} %bitcast.28, bf16[16,64,576]{2,1,0:T(8,128)(2,1)S(1)} %bitcast.34, bf16[16,64,576]{2,1,0:T(8,128)(2,1)S(1)} %collective-permute-done.5.other, ...), custom_call_target="tpu_custom_call" | custom-call | flops 1207959552 | bytes 5046272 | tf_op jit(solution)/shard_map/score/pallas_call | solution.py:211
  62.0 3.1 %score.5 = (bf16[16,128,512]{2,1,0:T(8,128)(2,1)S(1)}, f32[16,128]{1,0:T(8,128)S(1)}, f32[16,128]{1,0:T(8,128)S(1)}, f32[16,128]{1,0:T(8,128)S(1)}) custom-call(s32[33]{0:T(128)S(1)} %fusion.info, s32[64]{0:T(128)S(1)} %bitcast.29, bf16[16,64,576]{2,1,0:T(8,128)(2,1)S(1)} %bitcast.35, bf16[16,64,576]{2,1,0:T(8,128)(2,1)S(1)} %collective-permute-done.5.other, ...), custom_call_target="tpu_custom_call" | custom-call | flops 1207959552 | bytes 5046272 | tf_op jit(solution)/shard_map/score/pallas_call | solution.py:211
  65.1 2.5 %score.6 = (bf16[16,128,512]{2,1,0:T(8,128)(2,1)S(1)}, f32[16,128]{1,0:T(8,128)S(1)}, f32[16,128]{1,0:T(8,128)S(1)}, f32[16,128]{1,0:T(8,128)S(1)}) custom-call(s32[33]{0:T(128)S(1)} %fusion.info, s32[64]{0:T(128)S(1)} %bitcast.30, bf16[16,64,576]{2,1,0:T(8,128)(2,1)S(1)} %bitcast.36, bf16[16,64,576]{2,1,0:T(8,128)(2,1)S(1)} %collective-permute-done.5.other, ...), custom_call_target="tpu_custom_call" | custom-call | flops 1207959552 | bytes 5046272 | tf_op jit(solution)/shard_map/score/pallas_call | solution.py:211
  67.7 1.3 %logits.1.part = f32[2,16,2048]{2,1,0:T(8,128)S(1)} custom-call(f32[16,4224]{1,0:T(8,128)S(1)} %collective-permute-done.12.received, f32[16,4224]{1,0:T(8,128)S(1)} %get-tuple-element.90.here, bf16[2048,128]{1,0:T(8,128)(2,1)S(1)} %pad_maximum_fusion.own, bf16[2048,128]{1,0:T(8,128)(2,1)S(1)} %collective-permute-done.8.other), custom_call_target="tpu_custom_call" | custom-call | flops 536870912 | bytes 1851392 | tf_op jit(solution)/shard_map/logits/pallas_call | solution.py:301
  68.9 1.9 %collective-permute-start.13 = (f32[2,16,2048]{2,1,0:T(8,128)S(1)}, f32[2,16,2048]{2,1,0:T(8,128)S(1)}, u32[]{:S(2)}, u32[]{:S(2)}) collective-permute-start(f32[2,16,2048]{2,1,0:T(8,128)S(1)} %logits.1.part), channel_id=1, source_target_pairs={{0,4},{4,0},{1,5},{5,1},{2,6},{6,2},{3,7},{7,3},{8,12},{12,8},{9,1... | collective-permute-start | bytes 786440 | tf_op jit(solution)/shard_map/ppermute | solution.py:584
  70.8 6.3 %collective-permute-done.13.far = f32[2,16,2048]{2,1,0:T(8,128)S(1)} collective-permute-done((f32[2,16,2048]{2,1,0:T(8,128)S(1)}, f32[2,16,2048]{2,1,0:T(8,128)S(1)}, u32[]{:S(2)}, u32[]{:S(2)}) %collective-permute-start.13) | collective-permute-done | bytes 262176 | tf_op jit(solution)/shard_map/ppermute | solution.py:584
  77.1 0.7 collective-permute-done.14.keys
  77.8 2.5 %score.7 = (bf16[16,128,512]{2,1,0:T(8,128)(2,1)S(1)}, f32[16,128]{1,0:T(8,128)S(1)}, f32[16,128]{1,0:T(8,128)S(1)}, f32[16,128]{1,0:T(8,128)S(1)}) custom-call(s32[33]{0:T(128)S(1)} %fusion.info, s32[64]{0:T(128)S(1)} %bitcast.31, bf16[16,64,576]{2,1,0:T(8,128)(2,1)S(1)} %bitcast.37, bf16[16,64,576]{2,1,0:T(8,128)(2,1)S(1)} %collective-permute-done.5.other, ...), custom_call_target="tpu_custom_call" | custom-call | flops 1207959552 | bytes 5046272 | tf_op jit(solution)/shard_map/score/pallas_call | solution.py:211
  80.4 1.2 collective-permute-start.15
  81.6 0.8 softmax.1
  82.4 1.8 %collective-permute-done.15.refs_10_ = f32[2,16,128]{2,1,0:T(8,128)S(1)} collective-permute-done((f32[2,16,128]{2,1,0:T(8,128)S(1)}, f32[2,16,128]{2,1,0:T(8,128)S(1)}, u32[]{:S(2)}, u32[]{:S(2)}) %collective-permute-start.15) | collective-permute-done | bytes 16416 | tf_op jit(solution)/shard_map/ppermute | solution.py:584
  84.2 2.2 %delta.1 = (f32[16,2048]{1,0:T(8,128)S(1)}, bf16[16,2048]{1,0:T(8,128)(2,1)S(1)}) custom-call(bf16[16,128,512]{2,1,0:T(8,128)(2,1)S(1)} %get-tuple-element.97.refs_0_, bf16[16,128,512]{2,1,0:T(8,128)(2,1)S(1)} %get-tuple-element.98.refs_1_, bf16[16,128,512]{2,1,0:T(8,128)(2,1)S(1)} %get-tuple-element.99.refs_2_, ...), custom_call_target="tpu_custom_call" | custom-call | flops 8388608 | bytes 8388608 | tf_op jit(solution)/shard_map/delta/pallas_call | solution.py:258
  86.3 1.2 collective-permute-start.16
  87.6 3.1 %collective-permute-done.16.brought = bf16[16,2048]{1,0:T(8,128)(2,1)S(1)} collective-permute-done((bf16[16,2048]{1,0:T(8,128)(2,1)S(1)}, bf16[16,2048]{1,0:T(8,128)(2,1)S(1)}, u32[]{:S(2)}, u32[]{:S(2)}) %collective-permute-start.16) | collective-permute-done | bytes 65568 | tf_op jit(solution)/shard_map/ppermute | solution.py:584
  90.7 2.7 %gradient.1 = bf16[16,4224]{1,0:T(8,128)(2,1)S(1)} custom-call(f32[16,4224]{1,0:T(8,128)S(1)} %collective-permute-done.12.received, f32[16,4224]{1,0:T(8,128)S(1)} %get-tuple-element.90.here, bf16[2048,128]{1,0:T(8,128)(2,1)S(1)} %pad_maximum_fusion.own, bf16[2048,128]{1,0:T(8,128)(2,1)S(1)} %collective-permute-done.8.other, ...), custom_call_target="tpu_custom_call" | custom-call | flops 1073741824 | bytes 2375680 | tf_op jit(solution)/shard_map/gradient/pallas_call | solution.py:452
  93.3 1.6 %collective-permute-start.20 = (bf16[1,16,4224]{2,1,0:T(8,128)(2,1)S(1)}, bf16[1,16,4224]{2,1,0:T(8,128)(2,1)S(1)}, u32[]{:S(2)}, u32[]{:S(2)}) collective-permute-start(bf16[1,16,4224]{2,1,0:T(8,128)(2,1)S(1)} %bitcast.19), channel_id=1, source_target_pairs={{0,16},{8,24},{16,0},{24,8},{1,17},{9,25},{17,1},{25,9},{2,18},{10... | collective-permute-start | bytes 405512 | tf_op jit(solution)/shard_map/ppermute | solution.py:587
  94.9 2.7 %collective-permute-start.19 = (bf16[1,16,4224]{2,1,0:T(8,128)(2,1)S(1)}, bf16[1,16,4224]{2,1,0:T(8,128)(2,1)S(1)}, u32[]{:S(2)}, u32[]{:S(2)}) collective-permute-start(bf16[1,16,4224]{2,1,0:T(8,128)(2,1)S(1)} %bitcast.20), channel_id=1, source_target_pairs={{0,3},{1,0},{2,1},{3,2},{4,7},{5,4},{6,5},{7,6},{8,11},{9,8},{10,9... | collective-permute-start | bytes 405512 | tf_op jit(solution)/shard_map/ppermute | solution.py:676
  97.6 0.6 collective-permute-start.17
  98.1 0.3 collective-permute-done.20.refs_1_
  98.6 3.6 %collective-permute-done.19 = bf16[1,16,4224]{2,1,0:T(8,128)(2,1)S(1)} collective-permute-done((bf16[1,16,4224]{2,1,0:T(8,128)(2,1)S(1)}, bf16[1,16,4224]{2,1,0:T(8,128)(2,1)S(1)}, u32[]{:S(2)}, u32[]{:S(2)}) %collective-permute-start.19) | collective-permute-done | bytes 135200 | tf_op jit(solution)/shard_map/ppermute | solution.py:676
  102.2 4.9 %collective-permute-done.18 = bf16[1,16,4224]{2,1,0:T(8,128)(2,1)S(1)} collective-permute-done((bf16[1,16,4224]{2,1,0:T(8,128)(2,1)S(1)}, bf16[1,16,4224]{2,1,0:T(8,128)(2,1)S(1)}, u32[]{:S(2)}, u32[]{:S(2)}) %collective-permute-start.18) | collective-permute-done | bytes 135200 | tf_op jit(solution)/shard_map/ppermute | solution.py:676
  107.2 0.6 collective-permute-start.23
  107.8 9.4 %collective-permute-done.23.refs_5_ = bf16[3,16,4224]{2,1,0:T(8,128)(2,1)S(1)} collective-permute-done((bf16[3,16,4224]{2,1,0:T(8,128)(2,1)S(1)}, bf16[3,16,4224]{2,1,0:T(8,128)(2,1)S(1)}, u32[]{:S(2)}, u32[]{:S(2)}) %collective-permute-start.23) | collective-permute-done | bytes 405536 | tf_op jit(solution)/shard_map/ppermute | solution.py:587
  117.3 1.7 %collective-permute-done.25.refs_7_ = bf16[3,16,4224]{2,1,0:T(8,128)(2,1)S(1)} collective-permute-done((bf16[3,16,4224]{2,1,0:T(8,128)(2,1)S(1)}, bf16[3,16,4224]{2,1,0:T(8,128)(2,1)S(1)}, u32[]{:S(2)}, u32[]{:S(2)}) %collective-permute-start.25) | collective-permute-done | bytes 405536 | tf_op jit(solution)/shard_map/ppermute | solution.py:587
  119.0 4.4 %outer.1 = (f32[384,4096]{1,0:T(8,128)}, f32[32,1792]{1,0:T(8,128)}, f32[1,64]{1,0:T(1,128)}) custom-call(s32[33]{0:T(128)S(1)} %fusion.info, bf16[384,256]{1,0:T(8,128)(2,1)S(1)} %get-tuple-element.78.latents, bf16[256,1792]{1,0:T(8,128)(2,1)S(1)} %get-tuple-element.79.hiddens, bf16[1,16,4224]{2,1,0:T(8,128)(2,1)S(1)} %bitcast.24, ...), custom_call_target="tpu_custom_call" | custom-call | flops 805306368 | bytes 8388608 | tf_op jit(solution)/shard_map/outer/pallas_call | solution.py:539
  (40 shorter events, 0.7 us)
Async XLA Ops:
  0.6 3.0 %copy-start = (bf16[1,1024,576]{1,2,0:T(8,128)(2,1)S(1)}, bf16[1,1024,576]{1,2,0:T(8,128)(2,1)}, u32[]{:S(2)}) copy-start(bf16[1,1024,576]{1,2,0:T(8,128)(2,1)} %param.12) | copy-start | bytes 3538948
  0.6 37.6 %collective-permute-start.5 = (bf16[16,64,576]{2,1,0:T(8,128)(2,1)}, bf16[16,64,576]{2,1,0:T(8,128)(2,1)S(1)}, u32[]{:S(2)}, u32[]{:S(2)}) collective-permute-start(bf16[16,64,576]{2,1,0:T(8,128)(2,1)} %bitcast.33), channel_id=1, source_target_pairs={{0,4},{4,0},{1,5},{5,1},{2,6},{6,2},{3,7},{7,3},{8,12},{12,8},{9,1... | collective-permute-start | bytes 3538952 | tf_op jit(solution)/shard_map/ppermute | solution.py:584
  3.7 27.2 %collective-permute-start = (bf16[576,512]{1,0:T(8,128)(2,1)S(1)}, bf16[576,512]{1,0:T(8,128)(2,1)}, u32[]{:S(2)}, u32[]{:S(2)}) collective-permute-start(bf16[576,512]{1,0:T(8,128)(2,1)S(1)} %dynamic-slice_bitcast_fusion.keys), channel_id=1, source_target_pairs={{0,1},{1,3},{3,2},{2,0},{4,5},{5,7},{7,6},{6,4},{8,9},{9,11},{11,1... | collective-permute-start | bytes 1769480 | tf_op jit(solution)/shard_map/ppermute | solution.py:581
  6.0 1.9 %copy-start.1 = (bf16[384,4096]{1,0:T(8,128)(2,1)S(1)}, bf16[384,4096]{1,0:T(8,128)(2,1)}, u32[]{:S(2)}) copy-start(bf16[384,4096]{1,0:T(8,128)(2,1)} %weight.1) | copy-start | bytes 9437188
  7.9 1.2 copy-start.2
  9.1 0.9 copy-start.3
  10.0 0.9 copy-start.4
  10.9 4.0 %copy-start.7 = (bf16[1,1024,128]{2,1,0:T(8,128)(2,1)S(1)}, bf16[1,1024,128]{2,1,0:T(8,128)(2,1)}, u32[]{:S(2)}) copy-start(bf16[1,1024,128]{2,1,0:T(8,128)(2,1)} %param.13) | copy-start | bytes 786436
  12.2 47.2 %copy-start.5 = (s32[1,64]{1,0:T(1,128)S(1)}, s32[1,64]{1,0:T(1,128)}, u32[]{:S(2)}) copy-start(s32[1,64]{1,0:T(1,128)} %param.14) | copy-start | bytes 772
  12.3 47.2 %copy-start.6 = (bf16[1,16,64,576]{3,2,1,0:T(8,128)(2,1)S(1)}, bf16[1,16,64,576]{3,2,1,0:T(8,128)(2,1)}, u32[]{:S(2)}) copy-start(bf16[1,16,64,576]{3,2,1,0:T(8,128)(2,1)} %param.11) | copy-start | bytes 3538948
  12.3 16.1 %collective-permute-start.1 = (f32[16,4224]{1,0:T(8,128)S(1)}, f32[16,4224]{1,0:T(8,128)S(1)}, u32[]{:S(2)}, u32[]{:S(2)}) collective-permute-start(f32[16,4224]{1,0:T(8,128)S(1)} %get-tuple-element.61), channel_id=1, source_target_pairs={{0,1},{1,3},{3,2},{2,0},{4,5},{5,7},{7,6},{6,4},{8,9},{9,11},{11,1... | collective-permute-start | bytes 811016 | tf_op jit(solution)/shard_map/ppermute | solution.py:581
  14.9 15.7 %collective-permute-start.3 = (bf16[512,128]{1,0:T(8,128)(2,1)S(1)}, bf16[512,128]{1,0:T(8,128)(2,1)S(1)}, u32[]{:S(2)}, u32[]{:S(2)}) collective-permute-start(bf16[512,128]{1,0:T(8,128)(2,1)S(1)} %dynamic-slice_bitcast_fusion.1), channel_id=1, source_target_pairs={{0,2},{1,0},{3,1},{2,3},{4,6},{5,4},{7,5},{6,7},{8,10},{9,8},{11,9... | collective-permute-start | bytes 393224 | tf_op jit(solution)/shard_map/ppermute | solution.py:581
  15.3 15.6 %collective-permute-start.2 = (bf16[512,128]{1,0:T(8,128)(2,1)S(1)}, bf16[512,128]{1,0:T(8,128)(2,1)S(1)}, u32[]{:S(2)}, u32[]{:S(2)}) collective-permute-start(bf16[512,128]{1,0:T(8,128)(2,1)S(1)} %dynamic-slice_bitcast_fusion.1), channel_id=1, source_target_pairs={{0,1},{1,3},{3,2},{2,0},{4,5},{5,7},{7,6},{6,4},{8,9},{9,11},{11,1... | collective-permute-start | bytes 393224 | tf_op jit(solution)/shard_map/ppermute | solution.py:581
  30.9 7.3 %collective-permute-start.4 = (bf16[512,128]{1,0:T(8,128)(2,1)S(1)}, bf16[512,128]{1,0:T(8,128)(2,1)S(1)}, u32[]{:S(2)}, u32[]{:S(2)}) collective-permute-start(bf16[512,128]{1,0:T(8,128)(2,1)S(1)} %collective-permute-done.2), channel_id=1, source_target_pairs={{0,1},{1,3},{3,2},{2,0},{4,5},{5,7},{7,6},{6,4},{8,9},{9,11},{11,1... | collective-permute-start | bytes 393224 | tf_op jit(solution)/shard_map/ppermute | solution.py:581
  31.7 23.6 %collective-permute-start.6 = (bf16[576,512]{1,0:T(8,128)(2,1)}, bf16[576,512]{1,0:T(8,128)(2,1)S(1)}, u32[]{:S(2)}, u32[]{:S(2)}) collective-permute-start(bf16[576,512]{1,0:T(8,128)(2,1)} %collective-permute-done.keys), channel_id=1, source_target_pairs={{0,1},{1,3},{3,2},{2,0},{4,5},{5,7},{7,6},{6,4},{8,9},{9,11},{11,1... | collective-permute-start | bytes 1769480 | tf_op jit(solution)/shard_map/ppermute | solution.py:581
  38.3 17.0 %collective-permute-start.8 = (bf16[2048,128]{1,0:T(8,128)(2,1)S(1)}, bf16[2048,128]{1,0:T(8,128)(2,1)S(1)}, u32[]{:S(2)}, u32[]{:S(2)}) collective-permute-start(bf16[2048,128]{1,0:T(8,128)(2,1)S(1)} %pad_maximum_fusion.own), channel_id=1, source_target_pairs={{0,4},{4,0},{1,5},{5,1},{2,6},{6,2},{3,7},{7,3},{8,12},{12,8},{9,1... | collective-permute-start | bytes 1572872 | tf_op jit(solution)/shard_map/ppermute | solution.py:584
  39.8 15.4 %collective-permute-start.10 = (bf16[64,2176]{1,0:T(8,128)(2,1)S(1)}, bf16[64,2176]{1,0:T(8,128)(2,1)S(1)}, u32[]{:S(2)}, u32[]{:S(2)}) collective-permute-start(bf16[64,2176]{1,0:T(8,128)(2,1)S(1)} %get-tuple-element.73.refs_0_), channel_id=1, source_target_pairs={{0,8},{8,0},{16,24},{24,16},{1,9},{9,1},{17,25},{25,17},{2,10},{10... | collective-permute-start | bytes 835592 | tf_op jit(solution)/shard_map/ppermute | solution.py:587
  39.8 15.4 %collective-permute-start.9 = (bf16[64,2176]{1,0:T(8,128)(2,1)S(1)}, bf16[64,2176]{1,0:T(8,128)(2,1)S(1)}, u32[]{:S(2)}, u32[]{:S(2)}) collective-permute-start(bf16[64,2176]{1,0:T(8,128)(2,1)S(1)} %get-tuple-element.73.refs_0_), channel_id=1, source_target_pairs={{0,16},{8,24},{16,0},{24,8},{1,17},{9,25},{17,1},{25,9},{2,18},{10... | collective-permute-start | bytes 835592 | tf_op jit(solution)/shard_map/ppermute | solution.py:587
  41.3 13.9 %collective-permute-start.7 = (f32[16,4224]{1,0:T(8,128)S(1)}, f32[16,4224]{1,0:T(8,128)S(1)}, u32[]{:S(2)}, u32[]{:S(2)}) collective-permute-start(f32[16,4224]{1,0:T(8,128)S(1)} %add.24), channel_id=1, source_target_pairs={{0,1},{1,3},{3,2},{2,0},{4,5},{5,7},{7,6},{6,4},{8,9},{9,11},{11,1... | collective-permute-start | bytes 811016 | tf_op jit(solution)/shard_map/ppermute | solution.py:581
  55.3 3.4 %collective-permute-start.11 = (bf16[64,2176]{1,0:T(8,128)(2,1)S(1)}, bf16[64,2176]{1,0:T(8,128)(2,1)S(1)}, u32[]{:S(2)}, u32[]{:S(2)}) collective-permute-start(bf16[64,2176]{1,0:T(8,128)(2,1)S(1)} %collective-permute-done.9.refs_1_), channel_id=1, source_target_pairs={{0,8},{8,0},{16,24},{24,16},{1,9},{9,1},{17,25},{25,17},{2,10},{10... | collective-permute-start | bytes 835592 | tf_op jit(solution)/shard_map/ppermute | solution.py:587
  55.4 12.3 %collective-permute-start.12 = (f32[16,4224]{1,0:T(8,128)S(1)}, f32[16,4224]{1,0:T(8,128)S(1)}, u32[]{:S(2)}, u32[]{:S(2)}) collective-permute-start(f32[16,4224]{1,0:T(8,128)S(1)} %add.25), channel_id=1, source_target_pairs={{0,1},{1,3},{3,2},{2,0},{4,5},{5,7},{7,6},{6,4},{8,9},{9,11},{11,1... | collective-permute-start | bytes 811016 | tf_op jit(solution)/shard_map/ppermute | solution.py:581
  55.5 22.4 %collective-permute-start.14 = (bf16[576,512]{1,0:T(8,128)(2,1)S(1)}, bf16[576,512]{1,0:T(8,128)(2,1)S(1)}, u32[]{:S(2)}, u32[]{:S(2)}) collective-permute-start(bf16[576,512]{1,0:T(8,128)(2,1)S(1)} %collective-permute-done.6.keys), channel_id=1, source_target_pairs={{0,1},{1,3},{3,2},{2,0},{4,5},{5,7},{7,6},{6,4},{8,9},{9,11},{11,1... | collective-permute-start | bytes 1769480 | tf_op jit(solution)/shard_map/ppermute | solution.py:581
  68.9 8.2 %collective-permute-start.13 = (f32[2,16,2048]{2,1,0:T(8,128)S(1)}, f32[2,16,2048]{2,1,0:T(8,128)S(1)}, u32[]{:S(2)}, u32[]{:S(2)}) collective-permute-start(f32[2,16,2048]{2,1,0:T(8,128)S(1)} %logits.1.part), channel_id=1, source_target_pairs={{0,4},{4,0},{1,5},{5,1},{2,6},{6,2},{3,7},{7,3},{8,12},{12,8},{9,1... | collective-permute-start | bytes 786440 | tf_op jit(solution)/shard_map/ppermute | solution.py:584
  80.4 3.8 %collective-permute-start.15 = (f32[2,16,128]{2,1,0:T(8,128)S(1)}, f32[2,16,128]{2,1,0:T(8,128)S(1)}, u32[]{:S(2)}, u32[]{:S(2)}) collective-permute-start(f32[2,16,128]{2,1,0:T(8,128)S(1)} %pad_maximum_fusion.2), channel_id=1, source_target_pairs={{0,4},{4,0},{1,5},{5,1},{2,6},{6,2},{3,7},{7,3},{8,12},{12,8},{9,1... | collective-permute-start | bytes 49160 | tf_op jit(solution)/shard_map/ppermute | solution.py:584
  86.3 4.3 %collective-permute-start.16 = (bf16[16,2048]{1,0:T(8,128)(2,1)S(1)}, bf16[16,2048]{1,0:T(8,128)(2,1)S(1)}, u32[]{:S(2)}, u32[]{:S(2)}) collective-permute-start(bf16[16,2048]{1,0:T(8,128)(2,1)S(1)} %get-tuple-element.110.sent), channel_id=1, source_target_pairs={{0,4},{4,0},{1,5},{5,1},{2,6},{6,2},{3,7},{7,3},{8,12},{12,8},{9,1... | collective-permute-start | bytes 196616 | tf_op jit(solution)/shard_map/ppermute | solution.py:584
  93.3 5.1 %collective-permute-start.20 = (bf16[1,16,4224]{2,1,0:T(8,128)(2,1)S(1)}, bf16[1,16,4224]{2,1,0:T(8,128)(2,1)S(1)}, u32[]{:S(2)}, u32[]{:S(2)}) collective-permute-start(bf16[1,16,4224]{2,1,0:T(8,128)(2,1)S(1)} %bitcast.19), channel_id=1, source_target_pairs={{0,16},{8,24},{16,0},{24,8},{1,17},{9,25},{17,1},{25,9},{2,18},{10... | collective-permute-start | bytes 405512 | tf_op jit(solution)/shard_map/ppermute | solution.py:587
  94.9 7.3 %collective-permute-start.19 = (bf16[1,16,4224]{2,1,0:T(8,128)(2,1)S(1)}, bf16[1,16,4224]{2,1,0:T(8,128)(2,1)S(1)}, u32[]{:S(2)}, u32[]{:S(2)}) collective-permute-start(bf16[1,16,4224]{2,1,0:T(8,128)(2,1)S(1)} %bitcast.20), channel_id=1, source_target_pairs={{0,3},{1,0},{2,1},{3,2},{4,7},{5,4},{6,5},{7,6},{8,11},{9,8},{10,9... | collective-permute-start | bytes 405512 | tf_op jit(solution)/shard_map/ppermute | solution.py:676
  97.6 9.6 %collective-permute-start.18 = (bf16[1,16,4224]{2,1,0:T(8,128)(2,1)S(1)}, bf16[1,16,4224]{2,1,0:T(8,128)(2,1)S(1)}, u32[]{:S(2)}, u32[]{:S(2)}) collective-permute-start(bf16[1,16,4224]{2,1,0:T(8,128)(2,1)S(1)} %bitcast.21), channel_id=1, source_target_pairs={{0,2},{1,3},{2,0},{3,1},{4,6},{5,7},{6,4},{7,5},{8,10},{9,11},{10,... | collective-permute-start | bytes 405512 | tf_op jit(solution)/shard_map/ppermute | solution.py:676
  97.6 9.6 %collective-permute-start.17 = (bf16[1,16,4224]{2,1,0:T(8,128)(2,1)S(1)}, bf16[1,16,4224]{2,1,0:T(8,128)(2,1)S(1)}, u32[]{:S(2)}, u32[]{:S(2)}) collective-permute-start(bf16[1,16,4224]{2,1,0:T(8,128)(2,1)S(1)} %bitcast.22), channel_id=1, source_target_pairs={{0,1},{1,2},{2,3},{3,0},{4,5},{5,6},{6,7},{7,4},{8,9},{9,10},{10,1... | collective-permute-start | bytes 405512 | tf_op jit(solution)/shard_map/ppermute | solution.py:676
  98.1 9.1 %collective-permute-start.21 = (bf16[1,16,4224]{2,1,0:T(8,128)(2,1)S(1)}, bf16[1,16,4224]{2,1,0:T(8,128)(2,1)S(1)}, u32[]{:S(2)}, u32[]{:S(2)}) collective-permute-start(bf16[1,16,4224]{2,1,0:T(8,128)(2,1)S(1)} %bitcast.23), channel_id=1, source_target_pairs={{0,8},{8,0},{16,24},{24,16},{1,9},{9,1},{17,25},{25,17},{2,10},{10... | collective-permute-start | bytes 405512 | tf_op jit(solution)/shard_map/ppermute | solution.py:587
  98.4 8.8 %collective-permute-start.22 = (bf16[1,16,4224]{2,1,0:T(8,128)(2,1)S(1)}, bf16[1,16,4224]{2,1,0:T(8,128)(2,1)S(1)}, u32[]{:S(2)}, u32[]{:S(2)}) collective-permute-start(bf16[1,16,4224]{2,1,0:T(8,128)(2,1)S(1)} %collective-permute-done.20.refs_1_), channel_id=1, source_target_pairs={{0,8},{8,0},{16,24},{24,16},{1,9},{9,1},{17,25},{25,17},{2,10},{10... | collective-permute-start | bytes 405512 | tf_op jit(solution)/shard_map/ppermute | solution.py:587
  107.2 10.0 %collective-permute-start.23 = (bf16[3,16,4224]{2,1,0:T(8,128)(2,1)S(1)}, bf16[3,16,4224]{2,1,0:T(8,128)(2,1)S(1)}, u32[]{:S(2)}, u32[]{:S(2)}) collective-permute-start(bf16[3,16,4224]{2,1,0:T(8,128)(2,1)S(1)} %pad_maximum_fusion.1.refs_4_), channel_id=1, source_target_pairs={{0,16},{8,24},{16,0},{24,8},{1,17},{9,25},{17,1},{25,9},{2,18},{10... | collective-permute-start | bytes 1216520 | tf_op jit(solution)/shard_map/ppermute | solution.py:587
  107.8 9.4 %collective-permute-start.24 = (bf16[3,16,4224]{2,1,0:T(8,128)(2,1)S(1)}, bf16[3,16,4224]{2,1,0:T(8,128)(2,1)S(1)}, u32[]{:S(2)}, u32[]{:S(2)}) collective-permute-start(bf16[3,16,4224]{2,1,0:T(8,128)(2,1)S(1)} %pad_maximum_fusion.1.refs_4_), channel_id=1, source_target_pairs={{0,8},{8,0},{16,24},{24,16},{1,9},{9,1},{17,25},{25,17},{2,10},{10... | collective-permute-start | bytes 1216520 | tf_op jit(solution)/shard_map/ppermute | solution.py:587
  117.2 1.7 %collective-permute-start.25 = (bf16[3,16,4224]{2,1,0:T(8,128)(2,1)S(1)}, bf16[3,16,4224]{2,1,0:T(8,128)(2,1)S(1)}, u32[]{:S(2)}, u32[]{:S(2)}) collective-permute-start(bf16[3,16,4224]{2,1,0:T(8,128)(2,1)S(1)} %collective-permute-done.23.refs_5_), channel_id=1, source_target_pairs={{0,8},{8,0},{16,24},{24,16},{1,9},{9,1},{17,25},{25,17},{2,10},{10... | collective-permute-start | bytes 1216520 | tf_op jit(solution)/shard_map/ppermute | solution.py:587
